TPU v7x, 32 devices: a whole 2x2x4 slice. The times are simulated.
32 devices in a mesh: dp: 2 (over core), expert: 16 (over z, y, x).
Axes of the slice: x: 2, y: 2, z: 4, core: 2. Of those that a mesh axis runs over, the one named last changes fastest.
Arguments:
- hidden_saved: bfloat16 [2, 16, 448, 1024], P('dp', 'expert'), may hold values from -6 to 6
- down_weight: bfloat16 [16, 1024, 3584], P('expert', 'dp'), may hold values from -0.1875 to 0.1875
- route_device: int32 [4096, 4], P(('dp', 'expert')), may hold values from 0 to 15, all different within a row; in each aligned block of 128 rows (0 to 127, 128 to 255, ...) at most 40 rows name the same one
- replica_flag: int32 [4096, 4], P(('dp', 'expert')), may hold values 0 or 1
- gate_values: float32 [4096, 4], P(('dp', 'expert')), may hold values from 0.05 to 1
- grad_out: bfloat16 [4096, 3584], P(('dp', 'expert')), may hold values from -6 to 6
Outputs:
- layer_out: bfloat16 [4096, 3584], P(('dp', 'expert'))
- grad_hidden: bfloat16 [2, 16, 448, 1024], P('dp', 'expert')
- grad_weight: bfloat16 [16, 1024, 3584], P('expert', 'dp')
Inputs may be any that keep to these rules, and one draw needn't show every extreme that they name: `route_device`: the 4 numbers of a row differ; the rows of one device name any one device at most 40 times, and some device exactly 40 times.
All inputs are finite; a program needn't handle non-finite values. No bound on the sum of `replica_flag` on one device may be relied on, other than what follows from the above.
Results may differ from a plain program's by a relative error of at most 0.012.
Values may be sent and summed in bfloat16 or wider, within the bound.
No kernel may reach another device: no remote copies, remote signals or barrier semaphores. Data moves between devices by JAX's collectives and lax.ppermute only.
A program may use at most 192 MiB of HBM per device.

v0:
```python
import functools
import jax
import jax.numpy as jnp
from jax import lax
from jax.experimental import pallas as pl
from jax.experimental.pallas import tpu as pltpu
from jax.sharding import PartitionSpec as P

F32, BF16, I32 = jnp.float32, jnp.bfloat16, jnp.int32
LANES = 128
VMEM_LIMIT = 60 * 1024 * 1024


def swapped(value, axis, distance):
    count = lax.axis_size(axis)
    pairs = [(source, (source + distance) % count) for source in range(count)]
    return lax.ppermute(value, axis, pairs)


def dot(left, right, left_dim=1, right_dim=0):
    contract = (((left_dim,), (right_dim,)), ((), ()))
    return lax.dot_general(left, right, contract, preferred_element_type=F32)


def iota(shape, dim):
    return lax.broadcasted_iota(I32, shape, dim).astype(F32)


def row_of(rows, cap, lanes):
    row = iota((rows, lanes), 0)
    group = jnp.floor((row + 0.5) * (1.0 / cap))
    return group, row - group * cap


def before_mask(size):
    return (iota((size, size), 0) < iota((size, size), 1)).astype(BF16)


def bf16(*shape):
    return jax.ShapeDtypeStruct(shape, BF16)


def f32(*shape):
    return jax.ShapeDtypeStruct(shape, F32)


def call(body, grid, ins, outs, scratch=(), after=(), alias=None):
    single = not isinstance(outs, list)
    pairs = [outs] if single else outs
    specs = [spec for _, spec in pairs]
    shapes = [shape for shape, _ in pairs]
    count = len(ins)

    def kernel(*refs):
        body(*refs[:count], *refs[count + len(after) :])

    return pl.pallas_call(
        kernel,
        grid=(grid,),
        in_specs=[spec for _, spec in ins] + [anywhere()] * len(after),
        out_specs=specs[0] if single else specs,
        out_shape=shapes[0] if single else shapes,
        scratch_shapes=list(scratch),
        input_output_aliases=alias or {},
        compiler_params=pltpu.CompilerParams(vmem_limit_bytes=VMEM_LIMIT),
        cost_estimate=pl.CostEstimate(flops=0, bytes_accessed=0, transcendentals=0),
    )(*[array for array, _ in ins], *after)


def anywhere():
    return pl.BlockSpec(memory_space=pl.ANY)


def whole(array):
    return pl.BlockSpec(array.shape, lambda step: (0,) * len(array.shape))


def columns(array, tile):
    return pl.BlockSpec((array.shape[0], tile), lambda step: (0, step))


def entire(*arrays):
    return [(array, whole(array)) for array in arrays]


def by_columns(tile, *arrays):
    return [(array, columns(array, tile)) for array in arrays]


def head_kernel(device_ref, flag_ref, gate_ref, hidden_ref, meta_ref, spare_ref):
    top = device_ref.shape[0]
    codes = (device_ref[...] * 2 + flag_ref[...]).astype(F32)
    count = meta_ref.shape[0]
    meta_ref[:, :top, :] = jnp.broadcast_to(codes[None], (count, *codes.shape))
    meta_ref[:, top:, :] = jnp.broadcast_to(gate_ref[...][None], (count, *codes.shape))
    spare_ref[...] = hidden_ref[...]


def head(devices, flags, gates, hidden, spare, count):
    top, tok = devices.shape
    slots, hid = hidden.shape
    last = pl.BlockSpec((spare, hid), lambda step: (slots // spare - 1, 0))
    outs = entire(f32(count, 2 * top, tok), bf16(spare, hid))
    return call(head_kernel, 1, entire(devices, flags, gates) + [(hidden, last)], outs)


def copy_kernel(source_ref, target_ref, done):
    copy = pltpu.make_async_copy(source_ref, target_ref, done)
    copy.start()
    copy.wait()


def copied(array, *after):
    shape = jax.ShapeDtypeStruct(array.shape, array.dtype)
    return call(
        copy_kernel, 1, [(array, anywhere())], (shape, anywhere()), [pltpu.SemaphoreType.DMA], after
    )


def plan_rows(meta, cap, half, sel_ref, gate_ref, mix_ref):
    rows, tok = sel_ref.shape
    top = meta.shape[0] // 2
    me = lax.axis_index("expert")
    first = (lax.div(me, half) * half).astype(F32)
    dest = iota((LANES, tok), 0)
    inside = dest < half
    dest = dest + first
    hit = jnp.zeros((LANES, tok), F32)
    gate = jnp.zeros((LANES, tok), F32)
    for k in range(top):
        device = jnp.floor(meta[k : k + 1] * 0.5)
        named = (dest == device) & inside
        hit = jnp.where(named, 1.0, hit)
        gate = jnp.where(named, meta[top + k : top + k + 1], gate)
    place = dot(hit.astype(BF16), before_mask(tok))
    place = jnp.where(hit > 0.5, place, -1.0)
    group, at = row_of(rows, cap, LANES)
    spread = (iota((rows, LANES), 1) == group).astype(BF16)
    to_rows = lambda table: dot(spread, table.astype(BF16))
    chosen = jnp.where(to_rows(place) == at, 1.0, jnp.zeros((rows, tok), F32))
    high = gate.astype(BF16).astype(F32)
    mid = (gate - high).astype(BF16).astype(F32)
    low = gate - high - mid
    high, mid, low = to_rows(high), to_rows(mid), to_rows(low)
    scale = jnp.sum(chosen * (high + mid + low), axis=1, keepdims=True)
    sel_ref[...] = chosen.astype(BF16)
    gate_ref[...] = jnp.broadcast_to(scale, (rows, LANES))
    mix_ref[:tok] = (chosen * high).T.astype(BF16)
    mix_ref[tok:] = (chosen * mid).T.astype(BF16)


def packed_rows(sel_ref, gate_ref, tokens_ref, packed_ref):
    packed_ref[...] = (dot(sel_ref[...], tokens_ref[...]) * gate_ref[:, :1]).astype(BF16)


def pack_own_kernel(cap, half, meta_ref, tokens_ref, packed_ref, mix_ref, sel_ref, gate_ref):
    @pl.when(pl.program_id(0) == 0)
    def _():
        plan_rows(meta_ref[0], cap, half, sel_ref, gate_ref, mix_ref)

    packed_rows(sel_ref, gate_ref, tokens_ref, packed_ref)


def pack_own(meta, tokens, cap, half, tile, *after):
    tok, width = tokens.shape
    rows = half * cap
    first = pl.BlockSpec((1, *meta.shape[1:]), lambda step: (0, 0, 0))
    return call(
        functools.partial(pack_own_kernel, cap, half),
        width // tile,
        [(meta, first)] + by_columns(tile, tokens),
        by_columns(tile, bf16(rows, width)) + entire(bf16(2 * tok, rows)),
        [pltpu.VMEM((rows, tok), BF16), pltpu.VMEM((rows, LANES), F32)],
        after,
    )


def pack(sel, gate, tokens, tile, *after):
    rows, width = sel.shape[0], tokens.shape[1]
    return call(
        packed_rows,
        width // tile,
        entire(sel, gate) + by_columns(tile, tokens),
        by_columns(tile, bf16(rows, width))[0],
        after=after,
    )


def plan_kernel(cap, half, main, metas_ref, sel_ref, gate_ref, mix_ref, *slot_refs):
    count, tops, tok = metas_ref.shape
    top = tops // 2
    rows, slots = slot_refs[0].shape
    spare = slots - main
    me = lax.axis_index("expert")
    mirror = lax.rem(me + half, count)
    plan_rows(metas_ref[mirror], cap, half, sel_ref, gate_ref, mix_ref)

    mine, other = me.astype(F32), mirror.astype(F32)
    none = jnp.zeros((count, tok), F32)
    here, flag, clash = none, none, none
    for k in range(top):
        code = metas_ref[:, k, :]
        device = jnp.floor(code * 0.5)
        here = jnp.where(device == mine, 1.0, here)
        flag = jnp.where(device == mine, code - 2.0 * device, flag)
        clash = jnp.where(device == other, 1.0, clash)
    at_spare = here * flag * (1.0 - clash)
    at_main = here - at_spare
    before = before_mask(tok)
    ones = jnp.ones((tok, LANES), BF16)
    lower = (iota((count, count), 1) < iota((count, count), 0)).astype(BF16)

    def rank(flags):
        flags = flags.astype(BF16)
        return dot(flags, before) + dot(lower, dot(flags, ones).astype(BF16))

    rank_main, rank_spare = rank(at_main), rank(at_spare)
    slot = jnp.where((at_main > 0.5) & (rank_main < main), rank_main + 1.0, none)
    slot = jnp.where((at_spare > 0.5) & (rank_spare < spare), rank_spare + (main + 1.0), slot)
    place = jnp.where(here > 0.5, dot(here.astype(BF16), before), -1.0).astype(BF16)
    tens = jnp.floor(slot * (1.0 / 32.0))
    units = (slot - tens * 32.0).astype(BF16)
    tens = tens.astype(BF16)
    group, _ = row_of(rows, cap, count)
    _, at = row_of(rows, cap, tok)
    start = lax.div(me, half) * half
    for side, base in enumerate((start, lax.rem(start + half, count))):
        spread = (iota((rows, count), 1) == group + base.astype(F32)).astype(BF16)
        chosen = dot(spread, place) == at
        number = dot(spread, tens) * 32.0 + dot(spread, units)
        number = jnp.sum(jnp.where(chosen, number, 0.0), axis=1, keepdims=True)
        give_ref, take_ref = slot_refs[2 * side : 2 * side + 2]
        give_ref[...] = (iota((rows, slots), 1) + 1.0 == number).astype(BF16)
        number = jnp.broadcast_to(number, (rows, LANES)).T[0:1]
        take_ref[...] = (iota((slots, rows), 0) + 1.0 == number).astype(BF16)


def plan(metas, cap, half, main, slots):
    tok = metas.shape[2]
    rows = half * cap
    sides = [bf16(rows, slots), bf16(slots, rows)] * 2
    outs = entire(bf16(rows, tok), f32(rows, LANES), bf16(2 * tok, rows), *sides)
    return call(functools.partial(plan_kernel, cap, half, main), 1, entire(metas), outs)


def project_kernel(hidden_ref, spare_ref, near_ref, far_ref, main_out, spare_out, near_turned, far_turned, stack_ref):
    main, half = main_out.shape[0], near_ref.shape[0]

    @pl.when(pl.program_id(0) == 0)
    def _():
        core = lax.axis_index("dp")
        for at, which, turned_ref in ((0, core, near_turned), (half, 1 - core, far_turned)):
            start = pl.multiple_of(which * half, LANES)
            stack_ref[:main, at : at + half] = hidden_ref[:main, pl.ds(start, half)]
            stack_ref[main:, at : at + half] = spare_ref[:, pl.ds(start, half)]
            turned_ref[...] = stack_ref[:, at : at + half].T

    total = dot(stack_ref[:, :half], near_ref[...]) + dot(stack_ref[:, half:], far_ref[...])
    total = total.astype(BF16)
    main_out[...] = total[:main]
    spare_out[...] = total[main:]


def project(hidden, spare_hidden, near, far, tile, *after):
    half, width = near.shape
    spare = spare_hidden.shape[0]
    slots = hidden.shape[0]
    turned = [bf16(half, slots), bf16(half, slots)]
    return call(
        project_kernel,
        width // tile,
        entire(hidden, spare_hidden) + by_columns(tile, near, far),
        by_columns(tile, bf16(slots - spare, width), bf16(spare, width)) + entire(*turned),
        [pltpu.VMEM(hidden.shape, BF16)],
        after,
    )


def give_kernel(own_slot, mirror_slot, main_ref, spare_ref, own_ref, mirror_ref):
    main = main_ref.shape[0]
    for slot_ref, out_ref in ((own_slot, own_ref), (mirror_slot, mirror_ref)):
        packed = dot(slot_ref[:, :main], main_ref[...]) + dot(slot_ref[:, main:], spare_ref[...])
        out_ref[...] = packed.astype(BF16)


def give(own_slot, mirror_slot, out_main, out_spare, tile):
    rows, width = own_slot.shape[0], out_main.shape[1]
    return call(
        give_kernel,
        width // tile,
        entire(own_slot, mirror_slot) + by_columns(tile, out_main, out_spare),
        by_columns(tile, bf16(rows, width), bf16(rows, width)),
    )


def take_kernel(own_slot, mirror_slot, own_ref, mirror_ref, main_ref, spare_ref):
    total = dot(own_slot[...], own_ref[...]) + dot(mirror_slot[...], mirror_ref[...])
    total = total.astype(BF16)
    main = main_ref.shape[0]
    main_ref[...] = total[:main]
    spare_ref[...] = total[main:]


def take(own_slot, mirror_slot, own, mirror, main, tile, *after):
    slots, width = own_slot.shape[0], own.shape[1]
    return call(
        take_kernel,
        width // tile,
        entire(own_slot, mirror_slot) + by_columns(tile, own, mirror),
        by_columns(tile, bf16(main, width), bf16(slots - main, width)),
        after=after,
    )


def mixed(mix_ref, rows_ref):
    both = dot(mix_ref[...], rows_ref[...])
    tok = both.shape[0] // 2
    return both[:tok] + both[tok:]


def part_kernel(mix_ref, rows_ref, part_ref):
    part_ref[...] = mixed(mix_ref, rows_ref).astype(BF16)


def total_kernel(mix_ref, rows_ref, other_ref, total_ref):
    total_ref[...] = (mixed(mix_ref, rows_ref) + other_ref[...].astype(F32)).astype(BF16)


def combine(mix, rows, others, tile, *after):
    width = rows.shape[1]
    return call(
        total_kernel if others else part_kernel,
        width // tile,
        entire(mix) + by_columns(tile, rows, *others),
        by_columns(tile, bf16(mix.shape[0] // 2, width))[0],
        after=after,
    )


def stack_grads(main_ref, spare_ref, grads_ref):
    main = main_ref.shape[0]
    grads_ref[:main] = main_ref[...]
    grads_ref[main:] = spare_ref[...]


def weight_kernel(turned, other_turned, main_ref, spare_ref, other_main, other_spare, out_ref, grads_ref):
    stack_grads(main_ref, spare_ref, grads_ref)
    total = dot(turned[...], grads_ref[...])
    stack_grads(other_main, other_spare, grads_ref)
    out_ref[...] = (total + dot(other_turned[...], grads_ref[...])).astype(BF16)


def weight_grad(turned, other_turned, grads, other_grads, tile, *after):
    half, slots = turned.shape
    width = grads[0].shape[1]
    return call(
        weight_kernel,
        width // tile,
        entire(turned, other_turned) + by_columns(tile, *grads, *other_grads),
        by_columns(tile, bf16(half, width))[0],
        [pltpu.VMEM((slots, tile), BF16)],
        after,
    )


def back_kernel(main_ref, grad_ref, near_ref, far_ref, back_ref, spare_ref, sum_ref, grads_ref):
    step = pl.program_id(0)
    half = near_ref.shape[0]
    main = main_ref.shape[0]

    @pl.when(step == 0)
    def _():
        sum_ref[...] = jnp.zeros_like(sum_ref)

    stack_grads(main_ref, grad_ref, grads_ref)
    sum_ref[:, :half] += dot(grads_ref[...], near_ref[...], 1, 1)
    sum_ref[:, half:] += dot(grads_ref[...], far_ref[...], 1, 1)

    @pl.when(step == pl.num_programs(0) - 1)
    def _():
        core = lax.axis_index("dp")
        for at, which in ((0, core), (half, 1 - core)):
            start = pl.multiple_of(which * half, LANES)
            total = sum_ref[:, at : at + half].astype(BF16)
            back_ref[:, pl.ds(start, half)] = total
            spare_ref[:, pl.ds(start, half)] = total[main:]


def project_back(grads_main, grads_spare, near, far, tile, *after):
    main, width = grads_main.shape
    spare = grads_spare.shape[0]
    half = near.shape[0]
    slots = main + spare
    return call(
        back_kernel,
        width // tile,
        by_columns(tile, grads_main, grads_spare, near, far),
        entire(bf16(slots, 2 * half), bf16(spare, 2 * half)),
        [pltpu.VMEM((slots, 2 * half), F32), pltpu.VMEM((slots, tile), BF16)],
        after,
    )


def place_kernel(back_ref, spare_ref, out_ref):
    out_ref[...] = spare_ref[...]


def with_spare(back, back_spare, *after):
    slots, hid = back.shape
    spare = back_spare.shape[0]
    last = pl.BlockSpec((spare, hid), lambda step: (slots // spare - 1, 0))
    ins = [(back, anywhere())] + entire(back_spare)
    return call(place_kernel, 1, ins, (bf16(slots, hid), last), (), after, {0: 0})


def local(hidden_saved, down_weight, route_device, replica_flag, gate_values, grad_out):
    count = lax.axis_size("expert")
    half = count // 2
    tok, top = route_device.shape
    width = grad_out.shape[1]
    cap = 5 * tok * top // (4 * count)
    main = 3 * tok * top // 4
    hidden = hidden_saved[0, 0]
    near = down_weight[0]
    slots = hidden.shape[0]
    tile = width // 4
    groups = [list(range(half)), list(range(half, count))]

    def to_half(rows):
        return lax.all_to_all(
            rows.reshape(half, cap, width), "expert", 0, 0, axis_index_groups=groups, tiled=True
        ).reshape(half * cap, width)

    far = swapped(near, "dp", 1)
    meta, spare_hidden = head(
        route_device.T, replica_flag.T, gate_values.T, hidden, slots - main, count
    )
    spare_hidden = swapped(spare_hidden, "expert", half)
    metas = lax.all_to_all(meta, "expert", 0, 0, tiled=True)
    mirror = swapped(copied(grad_out, metas, spare_hidden), "expert", half)
    packed_own, mix_own = pack_own(meta, grad_out, cap, half, tile)
    arrived_own = to_half(packed_own)
    sel, gate, mix_mirror, give_own, take_own, give_mirror, take_mirror = plan(
        metas, cap, half, main, slots
    )
    out_main, out_spare, turned, far_turned = project(
        hidden, spare_hidden, near, far, tile, mix_own
    )
    other_turned = swapped(far_turned, "dp", 1)
    packed_mirror = pack(sel, gate, mirror, tile, out_spare)
    out_spare = swapped(out_spare, "expert", half)
    arrived_mirror = to_half(packed_mirror)
    given_own, given_mirror = give(give_own, give_mirror, out_main, out_spare, tile)
    returned_mirror = to_half(given_mirror)
    grads_main, grads_spare = take(
        take_own, take_mirror, arrived_own, arrived_mirror, main, tile, given_mirror
    )
    returned_own = to_half(given_own)
    other_main = swapped(grads_main, "dp", 1)
    grads_spare = swapped(grads_spare, "expert", half)
    other_spare = swapped(grads_spare, "dp", 1)
    part = combine(mix_mirror, returned_mirror, [], tile)
    back, back_spare = project_back(grads_main, grads_spare, near, far, tile, part)
    grad_weight = weight_grad(
        turned, other_turned, (grads_main, grads_spare), (other_main, other_spare), tile, back
    )
    part = swapped(part, "expert", half)
    back_spare = swapped(back_spare, "expert", half)
    layer_out = combine(mix_own, returned_own, [part], tile, grad_weight)
    grad_hidden = with_spare(back, back_spare, layer_out)
    return (layer_out, grad_hidden[None, None], grad_weight[None])


def solution(mesh):
    in_specs = (
        P("dp", "expert", None, None),
        P("expert", "dp", None),
        P(("dp", "expert"), None),
        P(("dp", "expert"), None),
        P(("dp", "expert"), None),
        P(("dp", "expert"), None),
    )
    out_specs = (P(("dp", "expert"), None), P("dp", "expert", None, None), P("expert", "dp", None))
    return jax.shard_map(local, mesh=mesh, in_specs=in_specs, out_specs=out_specs, check_vma=False)
```

profile of v0, /device:TPU:0, one launch (start us, length us, event | category | flops | bytes accessed | tf_op | source)
XLA Modules:
  0.0 292.8 jit_solution(18411182484865107762)
XLA Ops:
  0.6 1.6 shard_map.85
  2.3 8.3 %all-to-all-start = ((f32[16,8,128]{2,1,0:T(8,128)}), f32[16,8,128]{2,1,0:T(8,128)S(1)}, u32[]{:S(2)}, u32[]{:S(2)}) async-start(f32[16,8,128]{2,1,0:T(8,128)} %get-tuple-element.24.refs_0_), calls=%async_computation | async-start | bytes 131072 | tf_op jit(solution)/shard_map/all_to_all | solution.py:439
  10.6 4.8 %shard_map.86 = (bf16[320,3584]{1,0:T(8,128)(2,1)}, bf16[256,320]{1,0:T(8,128)(2,1)}) custom-call(f32[16,8,128]{2,1,0:T(8,128)} %get-tuple-element.24.refs_0_, bf16[128,3584]{1,0:T(8,128)(2,1)} %refs_0_.1), custom_call_target="tpu_custom_call" | custom-call | tf_op jit(solution)/shard_map/pallas_call | solution.py:57
  15.4 2.7 all-to-all-done.refs_0_.refs_1_
  18.1 0.0 copy-start.5
  18.1 0.0 copy-start.10
  18.1 0.6 copy-done.5
  18.8 4.4 %all-to-all-start.3 = ((bf16[8,40,3584]{2,1,0:T(8,128)(2,1)}), bf16[8,40,3584]{2,1,0:T(8,128)(2,1)}, u32[]{:S(2)}, u32[]{:S(2)}) async-start(bf16[8,40,3584]{2,1,0:T(8,128)(2,1)} %bitcast.28), calls=%async_computation.3 | async-start | bytes 4587520 | tf_op jit(solution)/shard_map/all_to_all | solution.py:430
  23.1 0.1 collective-permute-start.1
  23.2 0.0 copy-done.10
  23.2 0.8 collective-permute-start
  24.0 25.6 %collective-permute-done.refs_1_.refs_2_ = bf16[64,1024]{1,0:T(8,128)(2,1)S(1)} collective-permute-done((bf16[64,1024]{1,0:T(8,128)(2,1)S(1)}, bf16[64,1024]{1,0:T(8,128)(2,1)S(1)}, u32[]{:S(2)}, u32[]{:S(2)}) %collective-permute-start) | collective-permute-done | bytes 131104 | tf_op jit(solution)/shard_map/ppermute | solution.py:17
  49.6 0.0 copy-start.6
  49.6 0.7 copy-done.6
  50.2 28.9 %shard_map.91 = bf16[128,3584]{1,0:T(8,128)(2,1)} custom-call(bf16[128,3584]{1,0:T(8,128)(2,1)} %refs_0_.1, f32[16,8,128]{2,1,0:T(8,128)} %copy-done.5, bf16[64,1024]{1,0:T(8,128)(2,1)} %copy-done.6), custom_call_target="tpu_custom_call" | custom-call | tf_op jit(solution)/shard_map/pallas_call | solution.py:57
  79.1 3.4 %collective-permute-start.5 = (bf16[128,3584]{1,0:T(8,128)(2,1)}, bf16[128,3584]{1,0:T(8,128)(2,1)}, u32[]{:S(2)}, u32[]{:S(2)}) collective-permute-start(bf16[128,3584]{1,0:T(8,128)(2,1)} %shard_map.91), channel_id=1, source_target_pairs={{0,8},{1,9},{2,10},{3,11},{4,12},{5,13},{6,14},{7,15},{8,0},{9,1},... | collective-permute-start | bytes 2752520 | tf_op jit(solution)/shard_map/ppermute | solution.py:17
  82.6 2.9 %shard_map.87 = (bf16[320,128]{1,0:T(8,128)(2,1)}, f32[320,128]{1,0:T(8,128)}, bf16[256,320]{1,0:T(8,128)(2,1)}, bf16[320,448]{1,0:T(8,128)(2,1)}, bf16[448,320]...) custom-call(f32[16,8,128]{2,1,0:T(8,128)} %copy-done.5), custom_call_target="tpu_custom_call" | custom-call | tf_op jit(solution)/shard_map/pallas_call | solution.py:57
  85.5 0.0 collective-permute-done.1.refs_3_
  85.5 0.0 copy-start
  85.5 1.8 copy-done
  87.4 8.3 %shard_map.88 = (bf16[384,3584]{1,0:T(8,128)(2,1)}, bf16[64,3584]{1,0:T(8,128)(2,1)}, bf16[512,448]{1,0:T(8,128)(2,1)}, bf16[512,448]{1,0:T(8,128)(2,1)}) custom-call(bf16[448,1024]{1,0:T(8,128)(2,1)} %bitcast.25, bf16[64,1024]{1,0:T(8,128)(2,1)} %copy-done.6, bf16[512,3584]{1,0:T(8,128)(2,1)} %bitcast.16, bf16[512,3584]{1,0:T(8,128)(2,1)} %copy-done, ...), custom_call_target="tpu_custom_call" | custom-call | tf_op jit(solution)/shard_map/pallas_call | solution.py:57
  95.6 25.4 %collective-permute-done.5.refs_2_ = bf16[128,3584]{1,0:T(8,128)(2,1)} collective-permute-done((bf16[128,3584]{1,0:T(8,128)(2,1)}, bf16[128,3584]{1,0:T(8,128)(2,1)}, u32[]{:S(2)}, u32[]{:S(2)}) %collective-permute-start.5) | collective-permute-done | bytes 917536 | tf_op jit(solution)/shard_map/ppermute | solution.py:17
  121.0 4.4 %shard_map.92 = bf16[320,3584]{1,0:T(8,128)(2,1)} custom-call(bf16[320,128]{1,0:T(8,128)(2,1)} %get-tuple-element.39.refs_0_, f32[320,128]{1,0:T(8,128)} %get-tuple-element.40.refs_1_, bf16[128,3584]{1,0:T(8,128)(2,1)} %collective-permute-done.5.refs_2_, bf16[64,3584]{1,0:T(8,128)(2,1)} %get-tuple-element.30.refs_3_), custom_call_target="tpu_custom_call" | custom-call | tf_op jit(solution)/shard_map/pallas_call | solution.py:57
  125.4 0.0 all-to-all-done.3
  125.4 0.0 copy-start.7
  125.4 4.2 %all-to-all-start.4 = ((bf16[8,40,3584]{2,1,0:T(8,128)(2,1)}), bf16[8,40,3584]{2,1,0:T(8,128)(2,1)S(1)}, u32[]{:S(2)}, u32[]{:S(2)}) async-start(bf16[8,40,3584]{2,1,0:T(8,128)(2,1)} %bitcast.20), calls=%async_computation.4 | async-start | bytes 4587520 | tf_op jit(solution)/shard_map/all_to_all | solution.py:430
  129.6 0.0 copy-done.7
  129.6 2.9 collective-permute-start.2
  132.5 30.6 %collective-permute-done.2.refs_3_ = bf16[64,3584]{1,0:T(8,128)(2,1)S(1)} collective-permute-done((bf16[64,3584]{1,0:T(8,128)(2,1)S(1)}, bf16[64,3584]{1,0:T(8,128)(2,1)S(1)}, u32[]{:S(2)}, u32[]{:S(2)}) %collective-permute-start.2) | collective-permute-done | bytes 458784 | tf_op jit(solution)/shard_map/ppermute | solution.py:17
  163.1 0.0 copy-start.8
  163.1 0.8 copy-done.8
  163.8 6.8 %shard_map.89 = (bf16[320,3584]{1,0:T(8,128)(2,1)}, bf16[320,3584]{1,0:T(8,128)(2,1)}) custom-call(bf16[320,448]{1,0:T(8,128)(2,1)} %get-tuple-element.26.refs_0_, bf16[320,448]{1,0:T(8,128)(2,1)} %get-tuple-element.27.refs_1_, bf16[384,3584]{1,0:T(8,128)(2,1)} %get-tuple-element.29.refs_2_, bf16[64,3584]{1,0:T(8,128)(2,1)} %copy-done.8), custom_call_target="tpu_custom_call" | custom-call | tf_op jit(solution)/shard_map/pallas_call | solution.py:57
  170.7 0.0 all-to-all-done.4
  170.7 0.0 copy-start.2
  170.7 37.2 %all_to_all.25 = bf16[8,40,3584]{2,1,0:T(8,128)(2,1)} all-to-all(bf16[8,40,3584]{2,1,0:T(8,128)(2,1)} %bitcast.23), channel_id=1, replica_groups={{0,1,2,3,4,5,6,7},{8,9,10,11,12,13,14,15},{16,17,18,19,20,21,22,23},{24..., dimensions={0} | all-to-all | bytes 4587520 | tf_op jit(solution)/shard_map/all_to_all | solution.py:430
  207.9 0.0 copy-done.2
  207.9 3.6 %all-to-all-start.1 = ((bf16[8,40,3584]{2,1,0:T(8,128)(2,1)}), bf16[8,40,3584]{2,1,0:T(8,128)(2,1)S(1)}, u32[]{:S(2)}, u32[]{:S(2)}) async-start(bf16[8,40,3584]{2,1,0:T(8,128)(2,1)} %bitcast.27), calls=%async_computation.1 | async-start | bytes 4587520 | tf_op jit(solution)/shard_map/all_to_all | solution.py:430
  211.5 7.1 %shard_map.93 = (bf16[384,3584]{1,0:T(8,128)(2,1)}, bf16[64,3584]{1,0:T(8,128)(2,1)}) custom-call(bf16[448,320]{1,0:T(8,128)(2,1)} %get-tuple-element.36.refs_0_, bf16[448,320]{1,0:T(8,128)(2,1)} %get-tuple-element.37.refs_1_, bf16[320,3584]{1,0:T(8,128)(2,1)} %bitcast.10.refs_2_, bf16[320,3584]{1,0:T(8,128)(2,1)} %bitcast.22, ...), custom_call_target="tpu_custom_call" | custom-call | tf_op jit(solution)/shard_map/pallas_call | solution.py:57
  218.6 0.0 collective-permute-start.7
  218.6 0.1 collective-permute-start.6
  218.7 4.4 %shard_map.90.refs_4_ = bf16[128,3584]{1,0:T(8,128)(2,1)} custom-call(bf16[256,320]{1,0:T(8,128)(2,1)} %get-tuple-element.32.refs_0_, bf16[320,3584]{1,0:T(8,128)(2,1)} %bitcast.21), custom_call_target="tpu_custom_call" | custom-call | tf_op jit(solution)/shard_map/pallas_call | solution.py:57
  223.1 2.9 collective-permute-start.3
  226.0 0.0 collective-permute-start.4
  226.0 21.5 %collective-permute-done.6.refs_1_.refs_3_ = bf16[64,3584]{1,0:T(8,128)(2,1)S(1)} collective-permute-done((bf16[64,3584]{1,0:T(8,128)(2,1)}, bf16[64,3584]{1,0:T(8,128)(2,1)S(1)}, u32[]{:S(2)}, u32[]{:S(2)}) %collective-permute-start.6) | collective-permute-done | bytes 458784 | tf_op jit(solution)/shard_map/ppermute | solution.py:17
  247.4 0.0 copy-start.3
  247.4 0.0 collective-permute-start.8
  247.4 0.8 copy-done.3
  248.3 8.3 %shard_map.94 = (bf16[448,1024]{1,0:T(8,128)(2,1)}, bf16[64,1024]{1,0:T(8,128)(2,1)}) custom-call(bf16[384,3584]{1,0:T(8,128)(2,1)} %get-tuple-element.41.refs_0_.refs_2_, bf16[64,3584]{1,0:T(8,128)(2,1)} %copy-done.3, bf16[512,3584]{1,0:T(8,128)(2,1)} %bitcast.17, bf16[512,3584]{1,0:T(8,128)(2,1)} %copy-done, bf16[128,3584]{1,0:T(8,128)(2,1)} %shard_map.90.refs_4_), custom_call_target="tpu_custom_call" | custom-call | tf_op jit(solution)/shard_map/pallas_call | solution.py:57
  256.5 3.3 %collective-permute-start.9 = (bf16[64,1024]{1,0:T(8,128)(2,1)}, bf16[64,1024]{1,0:T(8,128)(2,1)S(1)}, u32[]{:S(2)}, u32[]{:S(2)}) collective-permute-start(bf16[64,1024]{1,0:T(8,128)(2,1)} %get-tuple-element.44), channel_id=1, source_target_pairs={{0,8},{1,9},{2,10},{3,11},{4,12},{5,13},{6,14},{7,15},{8,0},{9,1},... | collective-permute-start | bytes 393224 | tf_op jit(solution)/shard_map/ppermute | solution.py:17
  259.9 0.0 collective-permute-done.4.refs_1_
  259.9 0.0 collective-permute-done.8.refs_5_
  259.9 0.0 collective-permute-done.7.refs_4_
  259.9 8.4 %shard_map.95.refs_3_ = bf16[512,3584]{1,0:T(8,128)(2,1)} custom-call(bf16[512,448]{1,0:T(8,128)(2,1)} %get-tuple-element.34.refs_0_, bf16[512,448]{1,0:T(8,128)(2,1)} %collective-permute-done.4.refs_1_, bf16[384,3584]{1,0:T(8,128)(2,1)} %get-tuple-element.41.refs_0_.refs_2_, bf16[64,3584]{1,0:T(8,128)(2,1)} %copy-done.3, ...), custom_call_target="tpu_custom_call" | custom-call | tf_op jit(solution)/shard_map/pallas_call | solution.py:57
  268.3 0.0 all-to-all-done.1
  268.3 0.0 copy-start.1
  268.3 16.8 %collective-permute-done.3.refs_2_ = bf16[128,3584]{1,0:T(8,128)(2,1)S(1)} collective-permute-done((bf16[128,3584]{1,0:T(8,128)(2,1)}, bf16[128,3584]{1,0:T(8,128)(2,1)S(1)}, u32[]{:S(2)}, u32[]{:S(2)}) %collective-permute-start.3) | collective-permute-done | bytes 917536 | tf_op jit(solution)/shard_map/ppermute | solution.py:17
  285.1 0.0 copy-start.4
  285.1 0.0 copy-done.1
  285.1 0.9 copy-done.4
  286.0 4.5 %shard_map.96.refs_2_ = bf16[128,3584]{1,0:T(8,128)(2,1)} custom-call(bf16[256,320]{1,0:T(8,128)(2,1)} %get-tuple-element.25.refs_4_.refs_0_, bf16[320,3584]{1,0:T(8,128)(2,1)} %bitcast.19, bf16[128,3584]{1,0:T(8,128)(2,1)} %copy-done.4, bf16[512,3584]{1,0:T(8,128)(2,1)} %shard_map.95.refs_3_), custom_call_target="tpu_custom_call" | custom-call | tf_op jit(solution)/shard_map/pallas_call | solution.py:57
  290.6 0.0 collective-permute-done.9.refs_1_
  290.6 0.0 copy-start.9
  290.6 0.6 copy-done.9
  291.2 1.6 shard_map.97
Async XLA Ops:
  2.3 15.9 %all-to-all-start = ((f32[16,8,128]{2,1,0:T(8,128)}), f32[16,8,128]{2,1,0:T(8,128)S(1)}, u32[]{:S(2)}, u32[]{:S(2)}) async-start(f32[16,8,128]{2,1,0:T(8,128)} %get-tuple-element.24.refs_0_), calls=%async_computation | async-start | bytes 131072 | tf_op jit(solution)/shard_map/all_to_all | solution.py:439
  18.1 0.6 copy-start.5
  18.1 5.1 %copy-start.10 = (bf16[64,1024]{1,0:T(8,128)(2,1)S(1)}, bf16[64,1024]{1,0:T(8,128)(2,1)}, u32[]{:S(2)}) copy-start(bf16[64,1024]{1,0:T(8,128)(2,1)} %get-tuple-element.28) | copy-start | bytes 393220
  18.8 106.7 %all-to-all-start.3 = ((bf16[8,40,3584]{2,1,0:T(8,128)(2,1)}), bf16[8,40,3584]{2,1,0:T(8,128)(2,1)}, u32[]{:S(2)}, u32[]{:S(2)}) async-start(bf16[8,40,3584]{2,1,0:T(8,128)(2,1)} %bitcast.28), calls=%async_computation.3 | async-start | bytes 4587520 | tf_op jit(solution)/shard_map/all_to_all | solution.py:430
  23.1 62.4 %collective-permute-start.1 = (bf16[512,3584]{1,0:T(8,128)(2,1)}, bf16[512,3584]{1,0:T(8,128)(2,1)S(1)}, u32[]{:S(2)}, u32[]{:S(2)}) collective-permute-start(bf16[512,3584]{1,0:T(8,128)(2,1)} %bitcast.15), channel_id=1, source_target_pairs={{0,16},{16,0},{1,17},{17,1},{2,18},{18,2},{3,19},{19,3},{4,20},{20... | collective-permute-start | bytes 11010056 | tf_op jit(solution)/shard_map/ppermute | solution.py:17
  23.2 26.4 %collective-permute-start = (bf16[64,1024]{1,0:T(8,128)(2,1)S(1)}, bf16[64,1024]{1,0:T(8,128)(2,1)S(1)}, u32[]{:S(2)}, u32[]{:S(2)}) collective-permute-start(bf16[64,1024]{1,0:T(8,128)(2,1)S(1)} %copy-done.10), channel_id=1, source_target_pairs={{0,8},{1,9},{2,10},{3,11},{4,12},{5,13},{6,14},{7,15},{8,0},{9,1},... | collective-permute-start | bytes 393224 | tf_op jit(solution)/shard_map/ppermute | solution.py:17
  49.6 0.7 copy-start.6
  79.1 41.9 %collective-permute-start.5 = (bf16[128,3584]{1,0:T(8,128)(2,1)}, bf16[128,3584]{1,0:T(8,128)(2,1)}, u32[]{:S(2)}, u32[]{:S(2)}) collective-permute-start(bf16[128,3584]{1,0:T(8,128)(2,1)} %shard_map.91), channel_id=1, source_target_pairs={{0,8},{1,9},{2,10},{3,11},{4,12},{5,13},{6,14},{7,15},{8,0},{9,1},... | collective-permute-start | bytes 2752520 | tf_op jit(solution)/shard_map/ppermute | solution.py:17
  85.5 1.8 copy-start
  125.4 4.2 %copy-start.7 = (bf16[64,3584]{1,0:T(8,128)(2,1)S(1)}, bf16[64,3584]{1,0:T(8,128)(2,1)}, u32[]{:S(2)}) copy-start(bf16[64,3584]{1,0:T(8,128)(2,1)} %get-tuple-element.30.refs_3_) | copy-start | bytes 1376260
  125.4 45.2 %all-to-all-start.4 = ((bf16[8,40,3584]{2,1,0:T(8,128)(2,1)}), bf16[8,40,3584]{2,1,0:T(8,128)(2,1)S(1)}, u32[]{:S(2)}, u32[]{:S(2)}) async-start(bf16[8,40,3584]{2,1,0:T(8,128)(2,1)} %bitcast.20), calls=%async_computation.4 | async-start | bytes 4587520 | tf_op jit(solution)/shard_map/all_to_all | solution.py:430
  129.6 33.5 %collective-permute-start.2 = (bf16[64,3584]{1,0:T(8,128)(2,1)S(1)}, bf16[64,3584]{1,0:T(8,128)(2,1)S(1)}, u32[]{:S(2)}, u32[]{:S(2)}) collective-permute-start(bf16[64,3584]{1,0:T(8,128)(2,1)S(1)} %copy-done.7), channel_id=1, source_target_pairs={{0,8},{1,9},{2,10},{3,11},{4,12},{5,13},{6,14},{7,15},{8,0},{9,1},... | collective-permute-start | bytes 1376264 | tf_op jit(solution)/shard_map/ppermute | solution.py:17
  163.1 0.8 copy-start.8
  170.7 37.2 %copy-start.2 = (bf16[8,40,3584]{2,1,0:T(8,128)(2,1)}, bf16[8,40,3584]{2,1,0:T(8,128)(2,1)S(1)}, u32[]{:S(2)}) copy-start(bf16[8,40,3584]{2,1,0:T(8,128)(2,1)S(1)} %all-to-all-done.4) | copy-start | bytes 6881284
  207.9 60.4 %all-to-all-start.1 = ((bf16[8,40,3584]{2,1,0:T(8,128)(2,1)}), bf16[8,40,3584]{2,1,0:T(8,128)(2,1)S(1)}, u32[]{:S(2)}, u32[]{:S(2)}) async-start(bf16[8,40,3584]{2,1,0:T(8,128)(2,1)} %bitcast.27), calls=%async_computation.1 | async-start | bytes 4587520 | tf_op jit(solution)/shard_map/all_to_all | solution.py:430
  218.6 41.3 %collective-permute-start.7 = (bf16[384,3584]{1,0:T(8,128)(2,1)}, bf16[384,3584]{1,0:T(8,128)(2,1)}, u32[]{:S(2)}, u32[]{:S(2)}) collective-permute-start(bf16[384,3584]{1,0:T(8,128)(2,1)} %get-tuple-element.41.refs_0_.refs_2_), channel_id=1, source_target_pairs={{0,16},{16,0},{1,17},{17,1},{2,18},{18,2},{3,19},{19,3},{4,20},{20... | collective-permute-start | bytes 8257544 | tf_op jit(solution)/shard_map/ppermute | solution.py:17
  218.6 28.8 %collective-permute-start.6 = (bf16[64,3584]{1,0:T(8,128)(2,1)}, bf16[64,3584]{1,0:T(8,128)(2,1)S(1)}, u32[]{:S(2)}, u32[]{:S(2)}) collective-permute-start(bf16[64,3584]{1,0:T(8,128)(2,1)} %get-tuple-element.42), channel_id=1, source_target_pairs={{0,8},{1,9},{2,10},{3,11},{4,12},{5,13},{6,14},{7,15},{8,0},{9,1},... | collective-permute-start | bytes 1376264 | tf_op jit(solution)/shard_map/ppermute | solution.py:17
  223.1 62.0 %collective-permute-start.3 = (bf16[128,3584]{1,0:T(8,128)(2,1)}, bf16[128,3584]{1,0:T(8,128)(2,1)S(1)}, u32[]{:S(2)}, u32[]{:S(2)}) collective-permute-start(bf16[128,3584]{1,0:T(8,128)(2,1)} %shard_map.90.refs_4_), channel_id=1, source_target_pairs={{0,8},{1,9},{2,10},{3,11},{4,12},{5,13},{6,14},{7,15},{8,0},{9,1},... | collective-permute-start | bytes 2752520 | tf_op jit(solution)/shard_map/ppermute | solution.py:17
  226.0 33.9 %collective-permute-start.4 = (bf16[512,448]{1,0:T(8,128)(2,1)}, bf16[512,448]{1,0:T(8,128)(2,1)}, u32[]{:S(2)}, u32[]{:S(2)}) collective-permute-start(bf16[512,448]{1,0:T(8,128)(2,1)} %get-tuple-element.35), channel_id=1, source_target_pairs={{0,16},{16,0},{1,17},{17,1},{2,18},{18,2},{3,19},{19,3},{4,20},{20... | collective-permute-start | bytes 1376264 | tf_op jit(solution)/shard_map/ppermute | solution.py:17
  247.4 0.8 copy-start.3
  247.4 12.4 %collective-permute-start.8 = (bf16[64,3584]{1,0:T(8,128)(2,1)S(1)}, bf16[64,3584]{1,0:T(8,128)(2,1)}, u32[]{:S(2)}, u32[]{:S(2)}) collective-permute-start(bf16[64,3584]{1,0:T(8,128)(2,1)S(1)} %collective-permute-done.6.refs_1_.refs_3_), channel_id=1, source_target_pairs={{0,16},{16,0},{1,17},{17,1},{2,18},{18,2},{3,19},{19,3},{4,20},{20... | collective-permute-start | bytes 1376264 | tf_op jit(solution)/shard_map/ppermute | solution.py:17
  256.5 34.0 %collective-permute-start.9 = (bf16[64,1024]{1,0:T(8,128)(2,1)}, bf16[64,1024]{1,0:T(8,128)(2,1)S(1)}, u32[]{:S(2)}, u32[]{:S(2)}) collective-permute-start(bf16[64,1024]{1,0:T(8,128)(2,1)} %get-tuple-element.44), channel_id=1, source_target_pairs={{0,8},{1,9},{2,10},{3,11},{4,12},{5,13},{6,14},{7,15},{8,0},{9,1},... | collective-permute-start | bytes 393224 | tf_op jit(solution)/shard_map/ppermute | solution.py:17
  268.3 16.8 %copy-start.1 = (bf16[8,40,3584]{2,1,0:T(8,128)(2,1)}, bf16[8,40,3584]{2,1,0:T(8,128)(2,1)S(1)}, u32[]{:S(2)}) copy-start(bf16[8,40,3584]{2,1,0:T(8,128)(2,1)S(1)} %all-to-all-done.1) | copy-start | bytes 6881284
  285.1 0.9 copy-start.4
  290.6 0.6 copy-start.9
where the time goes:
time: 294 us; the launch traced here: 293 us
  waiting for transfers between devices  123 us (42%)
  Pallas kernels  92 us (31%)
  blocking collectives  37.2 us (13%)
  starting transfers between devices  34 us (12%)
  local copies, waits for them, and re-layouts  6.29 us (2%)
    ppermute x10, waiting for transfers between devices, swapped(): return lax.ppermute(value, axis, pairs)  120 us
    pallas_call x13, Pallas kernels, call(): pl.pallas_call(kernel, grid=(grid,), in_specs=[spec for _, spec in ins] +...  92 us
    all_to_all x1, blocking collectives, to_half(): lax.all_to_all(rows.reshape(half, cap, width), 'expert', 0, 0, axis_index...  37.2 us
    ppermute x10, starting transfers between devices, swapped(): return lax.ppermute(value, axis, pairs)  13.5 us
    all_to_all x3, starting transfers between devices, to_half(): lax.all_to_all(rows.reshape(half, cap, width), 'expert', 0, 0, axis_index...  12.2 us
    all_to_all x1, starting transfers between devices, local(): metas = lax.all_to_all(meta, 'expert', 0, 0, tiled=True)  8.31 us
    unnamed x22, local copies, waits for them, and re-layouts  6.29 us
  transfers between devices with their start and end apart: 14, of which 6 were waited for; matrix products, arithmetic and copies ran while one was open for 0% of the time, Pallas kernels for 30%

commit v1 on v0

v1 whole, which is shorter than its diff:
```python
import functools
import jax
import jax.numpy as jnp
from jax import lax
from jax.experimental import pallas as pl
from jax.experimental.pallas import tpu as pltpu
from jax.sharding import PartitionSpec as P

F32, BF16, I32 = jnp.float32, jnp.bfloat16, jnp.int32
LANES = 128
VMEM_LIMIT = 60 * 1024 * 1024


def swapped(value, axis, distance):
    count = lax.axis_size(axis)
    pairs = [(source, (source + distance) % count) for source in range(count)]
    return lax.ppermute(value, axis, pairs)


def dot(left, right, left_dim=1, right_dim=0):
    contract = (((left_dim,), (right_dim,)), ((), ()))
    return lax.dot_general(left, right, contract, preferred_element_type=F32)


def iota(shape, dim):
    return lax.broadcasted_iota(I32, shape, dim).astype(F32)


def row_of(rows, cap, lanes):
    row = iota((rows, lanes), 0)
    group = jnp.floor((row + 0.5) * (1.0 / cap))
    return group, row - group * cap


def before_mask(size):
    return (iota((size, size), 0) < iota((size, size), 1)).astype(BF16)


def bf16(*shape):
    return jax.ShapeDtypeStruct(shape, BF16)


def f32(*shape):
    return jax.ShapeDtypeStruct(shape, F32)


def call(body, grid, ins, outs, scratch=(), after=(), alias=None):
    single = not isinstance(outs, list)
    pairs = [outs] if single else outs
    specs = [spec for _, spec in pairs]
    shapes = [shape for shape, _ in pairs]
    count = len(ins)

    def kernel(*refs):
        body(*refs[:count], *refs[count + len(after) :])

    return pl.pallas_call(
        kernel,
        grid=(grid,),
        in_specs=[spec for _, spec in ins] + [anywhere()] * len(after),
        out_specs=specs[0] if single else specs,
        out_shape=shapes[0] if single else shapes,
        scratch_shapes=list(scratch),
        input_output_aliases=alias or {},
        compiler_params=pltpu.CompilerParams(vmem_limit_bytes=VMEM_LIMIT),
        cost_estimate=pl.CostEstimate(flops=0, bytes_accessed=0, transcendentals=0),
    )(*[array for array, _ in ins], *after)


def anywhere():
    return pl.BlockSpec(memory_space=pl.ANY)


def whole(array):
    return pl.BlockSpec(array.shape, lambda step: (0,) * len(array.shape))


def columns(array, tile):
    return pl.BlockSpec((array.shape[0], tile), lambda step: (0, step))


def entire(*arrays):
    return [(array, whole(array)) for array in arrays]


def by_columns(tile, *arrays):
    return [(array, columns(array, tile)) for array in arrays]


def slice_kernel(source_ref, target_ref):
    target_ref[...] = source_ref[...]


def last_rows(array, rows):
    return pl.BlockSpec((rows, array.shape[1]), lambda step: (array.shape[0] // rows - 1, 0))


def tail_of(array, rows):
    return call(slice_kernel, 1, [(array, last_rows(array, rows))], entire(bf16(rows, array.shape[1]))[0])


def touch_kernel(source_ref, target_ref):
    pass


def touched(array, *after):
    shape = jax.ShapeDtypeStruct(array.shape, array.dtype)
    return call(touch_kernel, 1, [(array, anywhere())], (shape, anywhere()), (), after, {0: 0})


def payload_kernel(device_ref, flag_ref, gate_ref, tokens_ref, first_ref, second_ref):
    top, tok = device_ref.shape
    cut = second_ref.shape[1]
    gate = gate_ref[...]
    high = gate.astype(BF16).astype(F32)
    mid = (gate - high).astype(BF16).astype(F32)
    low = gate - high - mid
    parts = [device_ref[...].astype(F32), flag_ref[...].astype(F32), high, mid, low]
    filler = jnp.zeros((LANES - len(parts) * top, tok), F32)
    first_ref[:, :cut] = tokens_ref[:, :cut]
    first_ref[:, cut:] = jnp.concatenate(parts + [filler], axis=0).T.astype(BF16)
    second_ref[...] = tokens_ref[:, cut:]


def payloads(routes, tokens, *after):
    tok, width = tokens.shape
    outs = entire(bf16(tok, width // 2 + LANES), bf16(tok, width // 2))
    return call(payload_kernel, 1, entire(*routes, tokens), outs, (), after)


def plan_rows(part, top, cap, half, sel_ref, gate_ref, kind_ref, mix_ref):
    rows, tok = sel_ref.shape
    me = lax.axis_index("expert")
    first = (lax.div(me, half) * half).astype(F32)
    devices = [part(0, k) for k in range(top)]
    dest = iota((LANES, tok), 0)
    inside = dest < half
    dest = dest + first
    none = jnp.zeros((LANES, tok), F32)
    hit, spare, high, mid, low = none, none, none, none, none
    for k in range(top):
        partner = devices[k] + jnp.where(devices[k] < half, 1.0 * half, -1.0 * half)
        wants = part(1, k)
        for other in devices:
            wants = jnp.where(other == partner, 0.0, wants)
        named = (dest == devices[k]) & inside
        hit = jnp.where(named, 1.0, hit)
        spare = jnp.where(named, wants, spare)
        high = jnp.where(named, part(2, k), high)
        mid = jnp.where(named, part(3, k), mid)
        low = jnp.where(named, part(4, k), low)
    place = dot(hit.astype(BF16), before_mask(tok))
    place = jnp.where(hit > 0.5, place, -1.0)
    group, at = row_of(rows, cap, LANES)
    spread = (iota((rows, LANES), 1) == group).astype(BF16)
    to_rows = lambda table: dot(spread, table.astype(BF16))
    chosen = jnp.where(to_rows(place) == at, 1.0, jnp.zeros((rows, tok), F32))
    of_row = lambda table: jnp.sum(chosen * table, axis=1, keepdims=True)
    high, mid, low = to_rows(high), to_rows(mid), to_rows(low)
    sel_ref[...] = chosen.astype(BF16)
    gate_ref[...] = jnp.broadcast_to(of_row(high + mid + low), (rows, LANES))
    mix_ref[:tok] = (chosen * high).T.astype(BF16)
    mix_ref[tok:] = (chosen * mid).T.astype(BF16)
    is_spare = of_row(to_rows(spare))
    is_main = of_row(1.0) - is_spare
    lane = iota((rows, LANES), 1)
    kind = jnp.where(lane == 0.0, is_main, jnp.where(lane == 1.0, is_spare, 0.0))
    kind_ref[...] = kind.astype(BF16)


def packed_rows(sel_ref, gate_ref, tokens_ref, packed_ref):
    packed_ref[...] = (dot(sel_ref[...], tokens_ref[...]) * gate_ref[:, :1]).astype(BF16)


def pack_steps(tiles, sel_ref, gate_ref, kind_ref, tokens_ref, packed_ref):
    step = pl.program_id(0)

    @pl.when(step < tiles)
    def _():
        packed_rows(sel_ref, gate_ref, tokens_ref, packed_ref)

    @pl.when(step == tiles)
    def _():
        packed_ref[:, :LANES] = kind_ref[...]


def pack_own_kernel(cap, half, tiles, device_ref, flag_ref, gates_ref, tokens_ref, packed_ref, mix_ref, *plan):
    sel_ref, gate_ref, kind_ref = plan
    top = device_ref.shape[0]

    @pl.when(pl.program_id(0) == 0)
    def _():
        gate = gates_ref[...]
        high = gate.astype(BF16).astype(F32)
        mid = (gate - high).astype(BF16).astype(F32)
        tables = (device_ref[...].astype(F32), flag_ref[...].astype(F32), high, mid, gate - high - mid)
        part = lambda which, k: tables[which][k : k + 1]
        plan_rows(part, top, cap, half, sel_ref, gate_ref, kind_ref, mix_ref)

    pack_steps(tiles, sel_ref, gate_ref, kind_ref, tokens_ref, packed_ref)


def up_to(array, tile, tiles):
    return pl.BlockSpec((array.shape[0], tile), lambda step: (0, jnp.minimum(step, tiles - 1)))


def pack_own(routes, tokens, cap, half, tile):
    tok, width = tokens.shape
    rows, tiles = half * cap, width // tile
    return call(
        functools.partial(pack_own_kernel, cap, half, tiles),
        tiles + 1,
        entire(*routes) + [(tokens, up_to(tokens, tile, tiles))],
        by_columns(tile, bf16(rows, width + LANES)) + entire(bf16(2 * tok, rows)),
        [pltpu.VMEM((rows, tok), BF16), pltpu.VMEM((rows, LANES), F32), pltpu.VMEM((rows, LANES), BF16)],
    )


def pack_first_kernel(cap, top, half, tiles, meta_ref, tokens_ref, packed_ref, sel_ref, gate_ref, mix_ref, kind_ref):
    @pl.when(pl.program_id(0) == 0)
    def _():
        meta = meta_ref[...].astype(F32).T
        part = lambda which, k: meta[which * top + k : which * top + k + 1]
        plan_rows(part, top, cap, half, sel_ref, gate_ref, kind_ref, mix_ref)

    pack_steps(tiles, sel_ref, gate_ref, kind_ref, tokens_ref, packed_ref)


def last_columns(array):
    return pl.BlockSpec((array.shape[0], LANES), lambda step: (0, array.shape[1] // LANES - 1))


def pack_first(payload, cap, top, half, tile, *after):
    tok, wide = payload.shape
    rows, tiles = half * cap, (wide - LANES) // tile
    return call(
        functools.partial(pack_first_kernel, cap, top, half, tiles),
        tiles + 1,
        [(payload, last_columns(payload)), (payload, up_to(payload, tile, tiles))],
        by_columns(tile, bf16(rows, wide)) + entire(bf16(rows, tok), f32(rows, LANES), bf16(2 * tok, rows)),
        [pltpu.VMEM((rows, LANES), BF16)],
        after,
    )


def pack(sel, gate, tokens, tile, *after):
    rows, width = sel.shape[0], tokens.shape[1]
    return call(
        packed_rows,
        width // tile,
        entire(sel, gate) + by_columns(tile, tokens),
        by_columns(tile, bf16(rows, width))[0],
        after=after,
    )


def slots_of(kind_ref, other_ref, second, main, spare):
    rows = kind_ref.shape[0]
    kind = kind_ref[...]
    lower = (iota((rows, rows), 1) < iota((rows, rows), 0)).astype(BF16)
    ahead = jnp.sum(other_ref[...].astype(F32), axis=0, keepdims=True)
    rank = dot(lower, kind) + jnp.where(second, ahead, 0.0)
    kind = kind.astype(F32)
    fits = lambda lane, limit: (kind[:, lane : lane + 1] > 0.5) & (rank[:, lane : lane + 1] < limit)
    slot = jnp.where(fits(1, spare), rank[:, 1:2] + (main + 1.0), 0.0)
    return jnp.where(fits(0, main), rank[:, 0:1] + 1.0, slot)


def upper_half(half):
    return lax.axis_index("expert") >= half


def project_kernel(hidden_ref, spare_ref, near_ref, far_ref, main_out, spare_out, near_turned, far_turned, stack_ref):
    main, half = main_out.shape[0], near_ref.shape[0]

    @pl.when(pl.program_id(0) == 0)
    def _():
        core = lax.axis_index("dp")
        for at, which, turned_ref in ((0, core, near_turned), (half, 1 - core, far_turned)):
            start = pl.multiple_of(which * half, LANES)
            stack_ref[:main, at : at + half] = hidden_ref[:main, pl.ds(start, half)]
            stack_ref[main:, at : at + half] = spare_ref[:, pl.ds(start, half)]
            turned_ref[...] = stack_ref[:, at : at + half].T

    total = dot(stack_ref[:, :half], near_ref[...]) + dot(stack_ref[:, half:], far_ref[...])
    total = total.astype(BF16)
    main_out[...] = total[:main]
    spare_out[...] = total[main:]


def project(hidden, spare_hidden, near, far, tile, *after):
    half, width = near.shape
    spare = spare_hidden.shape[0]
    slots = hidden.shape[0]
    turned = [bf16(half, slots), bf16(half, slots)]
    return call(
        project_kernel,
        width // tile,
        entire(hidden, spare_hidden) + by_columns(tile, near, far),
        by_columns(tile, bf16(slots - spare, width), bf16(spare, width)) + entire(*turned),
        [pltpu.VMEM(hidden.shape, BF16)],
        after,
    )


def given_rows(slot_ref, main_ref, spare_ref, out_ref):
    main = main_ref.shape[0]
    packed = dot(slot_ref[:, :main], main_ref[...]) + dot(slot_ref[:, main:], spare_ref[...])
    out_ref[...] = packed.astype(BF16)


def give_plan_kernel(half, mirrored, kind_ref, other_ref, main_ref, spare_ref, out_ref, slot_ref):
    rows, slots = slot_ref.shape
    main, spare = main_ref.shape[0], spare_ref.shape[0]

    @pl.when(pl.program_id(0) == 0)
    def _():
        slot = slots_of(kind_ref, other_ref, upper_half(half) != mirrored, main, spare)
        slot_ref[...] = (iota((rows, slots), 1) + 1.0 == slot).astype(BF16)

    given_rows(slot_ref, main_ref, spare_ref, out_ref)


def give_plan(kind, other, out_main, out_spare, half, mirrored, width, tile, *after):
    main, spare, rows = out_main.shape[0], out_spare.shape[0], kind.shape[0]
    ins = [(kind, last_columns(kind)), (other, last_columns(other))]
    return call(
        functools.partial(give_plan_kernel, half, mirrored),
        width // tile,
        ins + by_columns(tile, out_main, out_spare),
        by_columns(tile, bf16(rows, width)) + entire(bf16(rows, main + spare)),
        after=after,
    )


def later(array, tile, first):
    return pl.BlockSpec((array.shape[0], tile), lambda step: (0, step + first))


def give(slot, out_main, out_spare, first, tile, *after):
    width = out_main.shape[1] - first * tile
    return call(
        given_rows,
        width // tile,
        entire(slot) + [(array, later(array, tile, first)) for array in (out_main, out_spare)],
        by_columns(tile, bf16(slot.shape[0], width))[0],
        after=after,
    )


def take_kernel(half, cut, own_kind, mirror_kind, own_ref, first_ref, second_ref, *rest):
    main_ref, spare_ref, own_slot, mirror_slot = rest
    main, spare = main_ref.shape[0], spare_ref.shape[0]
    slots, rows = own_slot.shape
    step = pl.program_id(0)

    @pl.when(step == 0)
    def _():
        upper = upper_half(half)
        pairs = (
            (own_kind, mirror_kind, upper, own_slot),
            (mirror_kind, own_kind, jnp.logical_not(upper), mirror_slot),
        )
        for kind, other, second, out_ref in pairs:
            slot = slots_of(kind, other, second, main, spare)
            slot = jnp.broadcast_to(slot, (rows, LANES)).T[0:1]
            out_ref[...] = (iota((slots, rows), 0) + 1.0 == slot).astype(BF16)

    mirror = jnp.where(step < cut, first_ref[...], second_ref[...])
    total = dot(own_slot[...], own_ref[...]) + dot(mirror_slot[...], mirror)
    total = total.astype(BF16)
    main_ref[...] = total[:main]
    spare_ref[...] = total[main:]


def from_step(array, tile, first):
    return pl.BlockSpec((array.shape[0], tile), lambda step: (0, jnp.maximum(step - first, 0)))


def take(own, first, second, main, spare, half, tile, *after):
    rows = own.shape[0]
    width = own.shape[1] - LANES
    cut = second.shape[1] // tile
    ins = [(own, last_columns(own)), (first, last_columns(first))] + by_columns(tile, own)
    ins += [(first, up_to(first, tile, cut)), (second, from_step(second, tile, cut))]
    return call(
        functools.partial(take_kernel, half, cut),
        width // tile,
        ins,
        by_columns(tile, bf16(main, width), bf16(spare, width)),
        [pltpu.VMEM((main + spare, rows), BF16), pltpu.VMEM((main + spare, rows), BF16)],
        after,
    )


def mixed(mix_ref, rows_ref):
    both = dot(mix_ref[...], rows_ref[...])
    tok = both.shape[0] // 2
    return both[:tok] + both[tok:]


def part_kernel(mix_ref, rows_ref, part_ref):
    part_ref[...] = mixed(mix_ref, rows_ref).astype(BF16)


def total_kernel(cut, mix_ref, rows_ref, first_ref, second_ref, total_ref):
    other = jnp.where(pl.program_id(0) < cut, first_ref[...], second_ref[...]).astype(F32)
    total_ref[...] = (mixed(mix_ref, rows_ref) + other).astype(BF16)


def combine(mix, rows, others, tile, *after):
    width = rows.shape[1]
    body, more = part_kernel, []
    if others:
        cut = others[1].shape[1] // tile
        body = functools.partial(total_kernel, cut)
        more = [(others[0], up_to(others[0], tile, cut)), (others[1], from_step(others[1], tile, cut))]
    return call(
        body,
        width // tile,
        entire(mix) + by_columns(tile, rows) + more,
        by_columns(tile, bf16(mix.shape[0] // 2, width))[0],
        after=after,
    )


def stack_grads(main_ref, spare_ref, grads_ref):
    main = main_ref.shape[0]
    grads_ref[:main] = main_ref[...]
    grads_ref[main:] = spare_ref[...]


def weight_kernel(turned, other_turned, main_ref, spare_ref, other_main, other_spare, out_ref, grads_ref):
    stack_grads(main_ref, spare_ref, grads_ref)
    total = dot(turned[...], grads_ref[...])
    stack_grads(other_main, other_spare, grads_ref)
    out_ref[...] = (total + dot(other_turned[...], grads_ref[...])).astype(BF16)


def weight_grad(turned, other_turned, grads, other_grads, tile, *after):
    half, slots = turned.shape
    width = grads[0].shape[1]
    return call(
        weight_kernel,
        width // tile,
        entire(turned, other_turned) + by_columns(tile, *grads, *other_grads),
        by_columns(tile, bf16(half, width))[0],
        [pltpu.VMEM((slots, tile), BF16)],
        after,
    )


def back_kernel(main_ref, grad_ref, near_ref, far_ref, back_ref, spare_ref, sum_ref, grads_ref):
    step = pl.program_id(0)
    half = near_ref.shape[0]
    main = main_ref.shape[0]

    @pl.when(step == 0)
    def _():
        sum_ref[...] = jnp.zeros_like(sum_ref)

    stack_grads(main_ref, grad_ref, grads_ref)
    sum_ref[:, :half] += dot(grads_ref[...], near_ref[...], 1, 1)
    sum_ref[:, half:] += dot(grads_ref[...], far_ref[...], 1, 1)

    @pl.when(step == pl.num_programs(0) - 1)
    def _():
        core = lax.axis_index("dp")
        for at, which in ((0, core), (half, 1 - core)):
            start = pl.multiple_of(which * half, LANES)
            total = sum_ref[:, at : at + half].astype(BF16)
            back_ref[:, pl.ds(start, half)] = total
            spare_ref[:, pl.ds(start, half)] = total[main:]


def project_back(grads_main, grads_spare, near, far, tile, *after):
    main, width = grads_main.shape
    spare = grads_spare.shape[0]
    half = near.shape[0]
    slots = main + spare
    return call(
        back_kernel,
        width // tile,
        by_columns(tile, grads_main, grads_spare, near, far),
        entire(bf16(slots, 2 * half), bf16(spare, 2 * half)),
        [pltpu.VMEM((slots, 2 * half), F32), pltpu.VMEM((slots, tile), BF16)],
        after,
    )


def place_kernel(back_ref, spare_ref, out_ref):
    out_ref[...] = spare_ref[...]


def with_spare(back, back_spare, *after):
    slots, hid = back.shape
    spare = back_spare.shape[0]
    last = pl.BlockSpec((spare, hid), lambda step: (slots // spare - 1, 0))
    ins = [(back, anywhere())] + entire(back_spare)
    return call(place_kernel, 1, ins, (bf16(slots, hid), last), (), after, {0: 0})


def local(hidden_saved, down_weight, route_device, replica_flag, gate_values, grad_out):
    count = lax.axis_size("expert")
    half = count // 2
    tok, top = route_device.shape
    width = grad_out.shape[1]
    cap = 5 * tok * top // (4 * count)
    main = 3 * tok * top // 4
    hidden = hidden_saved[0, 0]
    near = down_weight[0]
    slots = hidden.shape[0]
    tile = width // 4
    groups = [list(range(half)), list(range(half, count))]

    def to_half(rows):
        return lax.all_to_all(
            rows.reshape(half, cap, -1), "expert", 0, 0, axis_index_groups=groups, tiled=True
        ).reshape(half * cap, -1)

    spare = slots - main
    routes = (route_device.T, replica_flag.T, gate_values.T)
    spare_hidden = swapped(tail_of(hidden, spare), "expert", half)
    far = swapped(near, "dp", 1)
    packed_own, mix_own = pack_own(routes, grad_out, cap, half, tile)
    arrived_own = to_half(touched(packed_own, spare_hidden))
    mirrors = [swapped(part, "expert", half) for part in payloads(routes, grad_out, spare_hidden)]
    out_main, out_spare, turned, far_turned = project(
        hidden, spare_hidden, near, far, tile, mix_own
    )
    other_turned = swapped(far_turned, "dp", 1)
    packed_first, sel, gate, mix_mirror = pack_first(mirrors[0], cap, top, half, tile, out_spare)
    arrived_first = to_half(packed_first)
    packed_second = pack(sel, gate, mirrors[1], tile)
    out_spare = swapped(out_spare, "expert", half)
    arrived_second = to_half(packed_second)
    given_first, slot_mirror = give_plan(
        arrived_first, arrived_own, out_main, out_spare, half, True, width // 2, tile
    )
    returned_first = to_half(given_first)
    given_second = give(slot_mirror, out_main, out_spare, width // 2 // tile, tile)
    returned_second = to_half(given_second)
    grads_main, grads_spare = take(
        arrived_own, arrived_first, arrived_second, main, spare, half, tile, given_second
    )
    given_own, _ = give_plan(
        arrived_own, arrived_first, out_main, out_spare, half, False, width, tile, grads_spare
    )
    returned_own = to_half(given_own)
    other_main = swapped(grads_main, "dp", 1)
    grads_spare = swapped(grads_spare, "expert", half)
    other_spare = swapped(grads_spare, "dp", 1)
    part_first = combine(mix_mirror, returned_first, [], tile, given_own)
    part_second = combine(mix_mirror, returned_second, [], tile, part_first)
    back, back_spare = project_back(grads_main, grads_spare, near, far, tile, part_second)
    grad_weight = weight_grad(
        turned, other_turned, (grads_main, grads_spare), (other_main, other_spare), tile, back
    )
    parts = [swapped(part, "expert", half) for part in (part_first, part_second)]
    back_spare = swapped(back_spare, "expert", half)
    layer_out = combine(mix_own, returned_own, parts, tile, grad_weight)
    grad_hidden = with_spare(back, back_spare, layer_out)
    return (layer_out, grad_hidden[None, None], grad_weight[None])


def solution(mesh):
    in_specs = (
        P("dp", "expert", None, None),
        P("expert", "dp", None),
        P(("dp", "expert"), None),
        P(("dp", "expert"), None),
        P(("dp", "expert"), None),
        P(("dp", "expert"), None),
    )
    out_specs = (P(("dp", "expert"), None), P("dp", "expert", None, None), P("expert", "dp", None))
    return jax.shard_map(local, mesh=mesh, in_specs=in_specs, out_specs=out_specs, check_vma=False)
```

time: 294 us -> 266 us (0.905)
  blocking collectives: 37.2 us -> 0 us
  starting transfers between devices: 34 us -> 53.9 us
  Pallas kernels: 92 us -> 72.2 us
  waiting for transfers between devices: 123 us -> 132 us
    all_to_all x1 -> x0, blocking collectives: 37.2 us -> none  [to_half(): lax.all_to_all(rows.reshape(half, cap, width), 'expert', 0, 0, axis_index...]
    pallas_call x13 -> x17, Pallas kernels: 92 us -> 72.2 us  [call(): pl.pallas_call(kernel, grid=(grid,), in_specs=[spec for _, spec in ins] +...]
    all_to_all x4 -> x6, starting transfers between devices: 20.5 us -> 37.3 us  [to_half(): lax.all_to_all(rows.reshape(half, cap, -1), 'expert', 0, 0, axis_index_gr...]
    all_to_all x4 -> x6, waiting for transfers between devices: 2.74 us -> 11 us  [to_half(): lax.all_to_all(rows.reshape(half, cap, -1), 'expert', 0, 0, axis_index_gr...]
    ppermute x10 -> x12, starting transfers between devices: 13.5 us -> 16.6 us  [swapped(): return lax.ppermute(value, axis, pairs)]
    ppermute x10 -> x12, waiting for transfers between devices: 120 us -> 122 us  [swapped(): return lax.ppermute(value, axis, pairs)]
    unnamed x22 -> x26, local copies, waits for them, and re-layouts: 6.29 us -> 5.64 us
  transfers between devices with their start and end apart: 14 -> 18, of which waited for: 6 -> 10; matrix products, arithmetic and copies ran while one was open for 0% -> 0% of each run, Pallas kernels for 30% -> 26%
where the time goes in v1:
time: 266 us; the launch traced here: 265 us
  waiting for transfers between devices  132 us (50%)
  Pallas kernels  72.2 us (27%)
  starting transfers between devices  53.9 us (20%)
  local copies, waits for them, and re-layouts  5.64 us (2%)
    ppermute x12, waiting for transfers between devices, swapped(): return lax.ppermute(value, axis, pairs)  122 us
    pallas_call x17, Pallas kernels, call(): pl.pallas_call(kernel, grid=(grid,), in_specs=[spec for _, spec in ins] +...  72.2 us
    all_to_all x6, starting transfers between devices, to_half(): lax.all_to_all(rows.reshape(half, cap, -1), 'expert', 0, 0, axis_index_gr...  37.3 us
    ppermute x12, starting transfers between devices, swapped(): return lax.ppermute(value, axis, pairs)  16.6 us
    all_to_all x6, waiting for transfers between devices, to_half(): lax.all_to_all(rows.reshape(half, cap, -1), 'expert', 0, 0, axis_index_gr...  11 us
    unnamed x26, local copies, waits for them, and re-layouts  5.64 us
  transfers between devices with their start and end apart: 18, of which 10 were waited for; matrix products, arithmetic and copies ran while one was open for 0% of the time, Pallas kernels for 26%

profile of v1, /device:TPU:0, one launch (start us, length us, event | category | flops | bytes accessed | tf_op | source)
XLA Modules:
  0.0 264.9 jit_solution(6836953060886173653)
XLA Ops:
  0.6 1.6 shard_map.86
  2.2 4.0 %collective-permute-start = (bf16[64,1024]{1,0:T(8,128)(2,1)}, bf16[64,1024]{1,0:T(8,128)(2,1)S(1)}, u32[]{:S(2)}, u32[]{:S(2)}) collective-permute-start(bf16[64,1024]{1,0:T(8,128)(2,1)} %shard_map.86), channel_id=1, source_target_pairs={{0,8},{1,9},{2,10},{3,11},{4,12},{5,13},{6,14},{7,15},{8,0},{9,1},... | collective-permute-start | bytes 393224 | tf_op jit(solution)/shard_map/ppermute | solution.py:17
  6.2 5.0 %shard_map.85 = (bf16[320,3712]{1,0:T(8,128)(2,1)}, bf16[256,320]{1,0:T(8,128)(2,1)}) custom-call(s32[4,128]{1,0:T(4,128)} %bitcast.39, s32[4,128]{1,0:T(4,128)} %bitcast.41, f32[4,128]{1,0:T(4,128)} %bitcast.43, bf16[128,3584]{1,0:T(8,128)(2,1)} %refs_3_.3), custom_call_target="tpu_custom_call" | custom-call | tf_op jit(solution)/shard_map/pallas_call | solution.py:57
  11.2 1.5 collective-permute-done.refs_1_.refs_4_
  12.8 0.7 copy-done.8
  13.4 4.0 %all-to-all-start = ((bf16[8,40,3712]{2,1,0:T(8,128)(2,1)}), bf16[8,40,3712]{2,1,0:T(8,128)(2,1)S(1)}, u32[]{:S(2)}, u32[]{:S(2)}) async-start(bf16[8,40,3712]{2,1,0:T(8,128)(2,1)} %bitcast.28), calls=%async_computation | async-start | bytes 4751360 | tf_op jit(solution)/shard_map/all_to_all | solution.py:517
  17.4 0.0 collective-permute-start.2
  17.4 2.2 shard_map.88
  19.6 3.3 %collective-permute-start.1 = (bf16[128,1920]{1,0:T(8,128)(2,1)}, bf16[128,1920]{1,0:T(8,128)(2,1)S(1)}, u32[]{:S(2)}, u32[]{:S(2)}) collective-permute-start(bf16[128,1920]{1,0:T(8,128)(2,1)} %get-tuple-element.24), channel_id=1, source_target_pairs={{0,8},{1,9},{2,10},{3,11},{4,12},{5,13},{6,14},{7,15},{8,0},{9,1},... | collective-permute-start | bytes 1474568 | tf_op jit(solution)/shard_map/ppermute | solution.py:17
  22.9 1.2 collective-permute-done.2.refs_3_
  24.2 8.3 %shard_map.89 = (bf16[384,3584]{1,0:T(8,128)(2,1)}, bf16[64,3584]{1,0:T(8,128)(2,1)}, bf16[512,448]{1,0:T(8,128)(2,1)}, bf16[512,448]{1,0:T(8,128)(2,1)}) custom-call(bf16[448,1024]{1,0:T(8,128)(2,1)} %bitcast.35, bf16[64,1024]{1,0:T(8,128)(2,1)} %copy-done.8, bf16[512,3584]{1,0:T(8,128)(2,1)} %bitcast.25, bf16[512,3584]{1,0:T(8,128)(2,1)} %collective-permute-done.2.refs_3_, ...), custom_call_target="tpu_custom_call" | custom-call | tf_op jit(solution)/shard_map/pallas_call | solution.py:57
  32.4 21.5 %collective-permute-done.1.refs_0_.refs_1_ = bf16[128,1920]{1,0:T(8,128)(2,1)S(1)} collective-permute-done((bf16[128,1920]{1,0:T(8,128)(2,1)}, bf16[128,1920]{1,0:T(8,128)(2,1)S(1)}, u32[]{:S(2)}, u32[]{:S(2)}) %collective-permute-start.1) | collective-permute-done | bytes 491552 | tf_op jit(solution)/shard_map/ppermute | solution.py:17
  54.0 0.8 copy-done.6
  54.7 3.6 %shard_map.90 = (bf16[320,1920]{1,0:T(8,128)(2,1)}, bf16[320,128]{1,0:T(8,128)(2,1)}, f32[320,128]{1,0:T(8,128)}, bf16[256,320]{1,0:T(8,128)(2,1)}) custom-call(bf16[128,1920]{1,0:T(8,128)(2,1)} %copy-done.6, bf16[128,1920]{1,0:T(8,128)(2,1)} %copy-done.6, bf16[64,3584]{1,0:T(8,128)(2,1)} %get-tuple-element.25.refs_2_), custom_call_target="tpu_custom_call" | custom-call | tf_op jit(solution)/shard_map/pallas_call | solution.py:57
  58.4 0.0 all-to-all-done
  58.4 0.0 copy-start
  58.4 12.0 %all-to-all-start.1 = ((bf16[8,40,1920]{2,1,0:T(8,128)(2,1)}), bf16[8,40,1920]{2,1,0:T(8,128)(2,1)}, u32[]{:S(2)}, u32[]{:S(2)}) async-start(bf16[8,40,1920]{2,1,0:T(8,128)(2,1)} %bitcast.37), calls=%async_computation.1 | async-start | bytes 2457600 | tf_op jit(solution)/shard_map/all_to_all | solution.py:517
  70.4 0.0 copy-done.12
  70.4 0.1 collective-permute-start.4
  70.5 22.1 %collective-permute-done.4.refs_2_ = bf16[128,1792]{1,0:T(8,128)(2,1)S(1)} collective-permute-done((bf16[128,1792]{1,0:T(8,128)(2,1)S(1)}, bf16[128,1792]{1,0:T(8,128)(2,1)S(1)}, u32[]{:S(2)}, u32[]{:S(2)}) %collective-permute-start.4) | collective-permute-done | bytes 458784 | tf_op jit(solution)/shard_map/ppermute | solution.py:17
  92.6 0.8 copy-done.10
  93.3 2.6 shard_map.91
  95.9 0.0 all-to-all-done.1
  95.9 0.0 copy-done
  95.9 5.0 %all-to-all-start.2 = ((bf16[8,40,1792]{2,1,0:T(8,128)(2,1)}), bf16[8,40,1792]{2,1,0:T(8,128)(2,1)S(1)}, u32[]{:S(2)}, u32[]{:S(2)}) async-start(bf16[8,40,1792]{2,1,0:T(8,128)(2,1)} %bitcast.31), calls=%async_computation.2 | async-start | bytes 2293760 | tf_op jit(solution)/shard_map/all_to_all | solution.py:517
  101.0 2.3 collective-permute-start.3
  103.3 18.0 %collective-permute-done.3.refs_3_.refs_2_ = bf16[64,3584]{1,0:T(8,128)(2,1)S(1)} collective-permute-done((bf16[64,3584]{1,0:T(8,128)(2,1)}, bf16[64,3584]{1,0:T(8,128)(2,1)S(1)}, u32[]{:S(2)}, u32[]{:S(2)}) %collective-permute-start.3) | collective-permute-done | bytes 458784 | tf_op jit(solution)/shard_map/ppermute | solution.py:17
  121.3 0.8 copy-done.5
  122.1 3.6 %shard_map.92 = (bf16[320,1792]{1,0:T(8,128)(2,1)}, bf16[320,448]{1,0:T(8,128)(2,1)}) custom-call(bf16[320,1920]{1,0:T(8,128)(2,1)} %bitcast.8.refs_0_.refs_1_.refs_3_, bf16[320,3712]{1,0:T(8,128)(2,1)} %bitcast.19, bf16[384,3584]{1,0:T(8,128)(2,1)} %get-tuple-element.27.refs_2_.refs_1_, bf16[64,3584]{1,0:T(8,128)(2,1)} %copy-done.5), custom_call_target="tpu_custom_call" | custom-call | tf_op jit(solution)/shard_map/pallas_call | solution.py:57
  125.7 0.0 all-to-all-done.2
  125.7 8.1 %all-to-all-start.4 = ((bf16[8,40,1792]{2,1,0:T(8,128)(2,1)}), bf16[8,40,1792]{2,1,0:T(8,128)(2,1)S(1)}, u32[]{:S(2)}, u32[]{:S(2)}) async-start(bf16[8,40,1792]{2,1,0:T(8,128)(2,1)} %bitcast.38), calls=%async_computation.4 | async-start | bytes 2293760 | tf_op jit(solution)/shard_map/all_to_all | solution.py:517
  133.8 3.4 %shard_map.93.refs_5_ = bf16[320,1792]{1,0:T(8,128)(2,1)} custom-call(bf16[320,448]{1,0:T(8,128)(2,1)} %get-tuple-element.31.refs_0_, bf16[384,3584]{1,0:T(8,128)(2,1)} %get-tuple-element.27.refs_2_.refs_1_, bf16[64,3584]{1,0:T(8,128)(2,1)} %copy-done.5), custom_call_target="tpu_custom_call" | custom-call | tf_op jit(solution)/shard_map/pallas_call | solution.py:57
  137.2 0.0 copy-done.2
  137.2 9.5 %all-to-all-done.4 = bf16[8,40,1792]{2,1,0:T(8,128)(2,1)S(1)} async-done(((bf16[8,40,1792]{2,1,0:T(8,128)(2,1)}), bf16[8,40,1792]{2,1,0:T(8,128)(2,1)S(1)}, u32[]{:S(2)}, u32[]{:S(2)}) %all-to-all-start.4) | async-done | bytes 1146912 | tf_op jit(solution)/shard_map/all_to_all | solution.py:517
  146.7 1.0 copy-done.4
  147.7 3.6 %all-to-all-start.5 = ((bf16[8,40,1792]{2,1,0:T(8,128)(2,1)}), bf16[8,40,1792]{2,1,0:T(8,128)(2,1)S(1)}, u32[]{:S(2)}, u32[]{:S(2)}) async-start(bf16[8,40,1792]{2,1,0:T(8,128)(2,1)} %bitcast.27), calls=%async_computation.5 | async-start | bytes 2293760 | tf_op jit(solution)/shard_map/all_to_all | solution.py:517
  151.3 7.9 %shard_map.94 = (bf16[384,3584]{1,0:T(8,128)(2,1)}, bf16[64,3584]{1,0:T(8,128)(2,1)}) custom-call(bf16[320,3712]{1,0:T(8,128)(2,1)} %bitcast.20, bf16[320,1920]{1,0:T(8,128)(2,1)} %bitcast.8.refs_0_.refs_1_.refs_3_, bf16[320,3712]{1,0:T(8,128)(2,1)} %bitcast.21, bf16[320,1920]{1,0:T(8,128)(2,1)} %bitcast.8.refs_0_.refs_1_.refs_3_, ...), custom_call_target="tpu_custom_call" | custom-call | tf_op jit(solution)/shard_map/pallas_call | solution.py:57
  159.2 5.7 %shard_map.95 = (bf16[320,3584]{1,0:T(8,128)(2,1)}, bf16[320,448]{1,0:T(8,128)(2,1)}) custom-call(bf16[320,3712]{1,0:T(8,128)(2,1)} %bitcast.22, bf16[320,1920]{1,0:T(8,128)(2,1)} %bitcast.8.refs_0_.refs_1_.refs_3_, bf16[384,3584]{1,0:T(8,128)(2,1)} %get-tuple-element.27.refs_2_.refs_1_, bf16[64,3584]{1,0:T(8,128)(2,1)} %copy-done.5, ...), custom_call_target="tpu_custom_call" | custom-call | tf_op jit(solution)/shard_map/pallas_call | solution.py:57
  164.9 1.4 all-to-all-done.5
  166.3 1.0 copy-done.3
  167.3 4.6 %all-to-all-start.3 = ((bf16[8,40,3584]{2,1,0:T(8,128)(2,1)}), bf16[8,40,3584]{2,1,0:T(8,128)(2,1)}, u32[]{:S(2)}, u32[]{:S(2)}) async-start(bf16[8,40,3584]{2,1,0:T(8,128)(2,1)} %bitcast.29), calls=%async_computation.3 | async-start | bytes 4587520 | tf_op jit(solution)/shard_map/all_to_all | solution.py:517
  172.0 0.0 copy-done.1
  172.0 0.1 collective-permute-start.9
  172.0 0.1 collective-permute-start.8
  172.1 0.4 collective-permute-start.7
  172.5 32.8 %collective-permute-done.8.refs_1_.refs_3_ = bf16[64,3584]{1,0:T(8,128)(2,1)S(1)} collective-permute-done((bf16[64,3584]{1,0:T(8,128)(2,1)}, bf16[64,3584]{1,0:T(8,128)(2,1)S(1)}, u32[]{:S(2)}, u32[]{:S(2)}) %collective-permute-start.8) | collective-permute-done | bytes 458784 | tf_op jit(solution)/shard_map/ppermute | solution.py:17
  205.3 0.0 collective-permute-start.10
  205.4 2.8 %shard_map.96.refs_2_ = bf16[128,1792]{1,0:T(8,128)(2,1)} custom-call(bf16[256,320]{1,0:T(8,128)(2,1)} %get-tuple-element.34.refs_0_, bf16[320,1792]{1,0:T(8,128)(2,1)} %bitcast.33, bf16[320,3584]{1,0:T(8,128)(2,1)} %get-tuple-element.33.refs_2_), custom_call_target="tpu_custom_call" | custom-call | tf_op jit(solution)/shard_map/pallas_call | solution.py:57
  208.2 2.6 shard_map.97.refs_4_
  210.8 3.3 %collective-permute-start.6 = (bf16[128,1792]{1,0:T(8,128)(2,1)}, bf16[128,1792]{1,0:T(8,128)(2,1)}, u32[]{:S(2)}, u32[]{:S(2)}) collective-permute-start(bf16[128,1792]{1,0:T(8,128)(2,1)} %shard_map.97.refs_4_), channel_id=1, source_target_pairs={{0,8},{1,9},{2,10},{3,11},{4,12},{5,13},{6,14},{7,15},{8,0},{9,1},... | collective-permute-start | bytes 1376264 | tf_op jit(solution)/shard_map/ppermute | solution.py:17
  214.1 0.1 collective-permute-start.5
  214.1 8.3 %shard_map.98 = (bf16[448,1024]{1,0:T(8,128)(2,1)}, bf16[64,1024]{1,0:T(8,128)(2,1)}) custom-call(bf16[384,3584]{1,0:T(8,128)(2,1)} %get-tuple-element.38.refs_0_.refs_2_, bf16[64,3584]{1,0:T(8,128)(2,1)} %copy-done.7, bf16[512,3584]{1,0:T(8,128)(2,1)} %bitcast.26, bf16[512,3584]{1,0:T(8,128)(2,1)} %collective-permute-done.2.refs_3_, ...), custom_call_target="tpu_custom_call" | custom-call | tf_op jit(solution)/shard_map/pallas_call | solution.py:57
  222.4 0.0 collective-permute-done.7.refs_1_
  222.4 2.9 %collective-permute-start.11 = (bf16[64,1024]{1,0:T(8,128)(2,1)}, bf16[64,1024]{1,0:T(8,128)(2,1)S(1)}, u32[]{:S(2)}, u32[]{:S(2)}) collective-permute-start(bf16[64,1024]{1,0:T(8,128)(2,1)} %get-tuple-element.40), channel_id=1, source_target_pairs={{0,8},{1,9},{2,10},{3,11},{4,12},{5,13},{6,14},{7,15},{8,0},{9,1},... | collective-permute-start | bytes 393224 | tf_op jit(solution)/shard_map/ppermute | solution.py:17
  225.3 0.0 collective-permute-done.10.refs_5_
  225.3 0.0 collective-permute-done.9.refs_4_
  225.4 8.4 %shard_map.99.refs_4_ = bf16[512,3584]{1,0:T(8,128)(2,1)} custom-call(bf16[512,448]{1,0:T(8,128)(2,1)} %get-tuple-element.36.refs_0_, bf16[512,448]{1,0:T(8,128)(2,1)} %copy-done.9, bf16[384,3584]{1,0:T(8,128)(2,1)} %get-tuple-element.38.refs_0_.refs_2_, bf16[64,3584]{1,0:T(8,128)(2,1)} %copy-done.7, bf16[384,3584]{1,0:T(8,128)(2,1)} %collective-permute-done.9.refs_4_, ...), custom_call_target="tpu_custom_call" | custom-call | tf_op jit(solution)/shard_map/pallas_call | solution.py:57
  233.7 14.4 %collective-permute-done.6.refs_3_ = bf16[128,1792]{1,0:T(8,128)(2,1)} collective-permute-done((bf16[128,1792]{1,0:T(8,128)(2,1)}, bf16[128,1792]{1,0:T(8,128)(2,1)}, u32[]{:S(2)}, u32[]{:S(2)}) %collective-permute-start.6) | collective-permute-done | bytes 458784 | tf_op jit(solution)/shard_map/ppermute | solution.py:17
  248.1 9.8 %collective-permute-done.5.refs_2_ = bf16[128,1792]{1,0:T(8,128)(2,1)} collective-permute-done((bf16[128,1792]{1,0:T(8,128)(2,1)}, bf16[128,1792]{1,0:T(8,128)(2,1)}, u32[]{:S(2)}, u32[]{:S(2)}) %collective-permute-start.5) | collective-permute-done | bytes 458784 | tf_op jit(solution)/shard_map/ppermute | solution.py:17
  258.0 0.0 all-to-all-done.3
  258.0 4.7 %shard_map.100.refs_2_ = bf16[128,3584]{1,0:T(8,128)(2,1)} custom-call(bf16[256,320]{1,0:T(8,128)(2,1)} %get-tuple-element.22.refs_4_.refs_0_, bf16[320,3584]{1,0:T(8,128)(2,1)} %bitcast.12.refs_1_, bf16[128,1792]{1,0:T(8,128)(2,1)} %collective-permute-done.5.refs_2_, bf16[128,1792]{1,0:T(8,128)(2,1)} %collective-permute-done.6.refs_3_, ...), custom_call_target="tpu_custom_call" | custom-call | tf_op jit(solution)/shard_map/pallas_call | solution.py:57
  262.7 0.0 collective-permute-done.11.refs_1_
  262.7 0.6 copy-done.11
  263.3 1.6 shard_map.101
  (15 shorter events, 0.0 us)
Async XLA Ops:
  2.2 10.5 %collective-permute-start = (bf16[64,1024]{1,0:T(8,128)(2,1)}, bf16[64,1024]{1,0:T(8,128)(2,1)S(1)}, u32[]{:S(2)}, u32[]{:S(2)}) collective-permute-start(bf16[64,1024]{1,0:T(8,128)(2,1)} %shard_map.86), channel_id=1, source_target_pairs={{0,8},{1,9},{2,10},{3,11},{4,12},{5,13},{6,14},{7,15},{8,0},{9,1},... | collective-permute-start | bytes 393224 | tf_op jit(solution)/shard_map/ppermute | solution.py:17
  12.8 0.7 copy-start.8
  13.4 45.0 %all-to-all-start = ((bf16[8,40,3712]{2,1,0:T(8,128)(2,1)}), bf16[8,40,3712]{2,1,0:T(8,128)(2,1)S(1)}, u32[]{:S(2)}, u32[]{:S(2)}) async-start(bf16[8,40,3712]{2,1,0:T(8,128)(2,1)} %bitcast.28), calls=%async_computation | async-start | bytes 4751360 | tf_op jit(solution)/shard_map/all_to_all | solution.py:517
  17.4 6.8 %collective-permute-start.2 = (bf16[512,3584]{1,0:T(8,128)(2,1)}, bf16[512,3584]{1,0:T(8,128)(2,1)}, u32[]{:S(2)}, u32[]{:S(2)}) collective-permute-start(bf16[512,3584]{1,0:T(8,128)(2,1)} %bitcast.24), channel_id=1, source_target_pairs={{0,16},{16,0},{1,17},{17,1},{2,18},{18,2},{3,19},{19,3},{4,20},{20... | collective-permute-start | bytes 11010056 | tf_op jit(solution)/shard_map/ppermute | solution.py:17
  19.6 34.3 %collective-permute-start.1 = (bf16[128,1920]{1,0:T(8,128)(2,1)}, bf16[128,1920]{1,0:T(8,128)(2,1)S(1)}, u32[]{:S(2)}, u32[]{:S(2)}) collective-permute-start(bf16[128,1920]{1,0:T(8,128)(2,1)} %get-tuple-element.24), channel_id=1, source_target_pairs={{0,8},{1,9},{2,10},{3,11},{4,12},{5,13},{6,14},{7,15},{8,0},{9,1},... | collective-permute-start | bytes 1474568 | tf_op jit(solution)/shard_map/ppermute | solution.py:17
  32.4 37.9 %copy-start.12 = (bf16[128,1792]{1,0:T(8,128)(2,1)S(1)}, bf16[128,1792]{1,0:T(8,128)(2,1)}, u32[]{:S(2)}) copy-start(bf16[128,1792]{1,0:T(8,128)(2,1)} %get-tuple-element.30) | copy-start | bytes 1376260
  54.0 0.8 copy-start.6
  58.4 37.6 %copy-start = (bf16[8,40,3712]{2,1,0:T(8,128)(2,1)}, bf16[8,40,3712]{2,1,0:T(8,128)(2,1)S(1)}, u32[]{:S(2)}) copy-start(bf16[8,40,3712]{2,1,0:T(8,128)(2,1)S(1)} %all-to-all-done) | copy-start | bytes 7127044
  58.4 37.5 %all-to-all-start.1 = ((bf16[8,40,1920]{2,1,0:T(8,128)(2,1)}), bf16[8,40,1920]{2,1,0:T(8,128)(2,1)}, u32[]{:S(2)}, u32[]{:S(2)}) async-start(bf16[8,40,1920]{2,1,0:T(8,128)(2,1)} %bitcast.37), calls=%async_computation.1 | async-start | bytes 2457600 | tf_op jit(solution)/shard_map/all_to_all | solution.py:517
  70.4 22.2 %collective-permute-start.4 = (bf16[128,1792]{1,0:T(8,128)(2,1)S(1)}, bf16[128,1792]{1,0:T(8,128)(2,1)S(1)}, u32[]{:S(2)}, u32[]{:S(2)}) collective-permute-start(bf16[128,1792]{1,0:T(8,128)(2,1)S(1)} %copy-done.12), channel_id=1, source_target_pairs={{0,8},{1,9},{2,10},{3,11},{4,12},{5,13},{6,14},{7,15},{8,0},{9,1},... | collective-permute-start | bytes 1376264 | tf_op jit(solution)/shard_map/ppermute | solution.py:17
  92.6 0.8 copy-start.10
  95.9 29.8 %all-to-all-start.2 = ((bf16[8,40,1792]{2,1,0:T(8,128)(2,1)}), bf16[8,40,1792]{2,1,0:T(8,128)(2,1)S(1)}, u32[]{:S(2)}, u32[]{:S(2)}) async-start(bf16[8,40,1792]{2,1,0:T(8,128)(2,1)} %bitcast.31), calls=%async_computation.2 | async-start | bytes 2293760 | tf_op jit(solution)/shard_map/all_to_all | solution.py:517
  101.0 20.4 %collective-permute-start.3 = (bf16[64,3584]{1,0:T(8,128)(2,1)}, bf16[64,3584]{1,0:T(8,128)(2,1)S(1)}, u32[]{:S(2)}, u32[]{:S(2)}) collective-permute-start(bf16[64,3584]{1,0:T(8,128)(2,1)} %get-tuple-element.25.refs_2_), channel_id=1, source_target_pairs={{0,8},{1,9},{2,10},{3,11},{4,12},{5,13},{6,14},{7,15},{8,0},{9,1},... | collective-permute-start | bytes 1376264 | tf_op jit(solution)/shard_map/ppermute | solution.py:17
  121.3 0.8 copy-start.5
  125.7 11.5 %copy-start.2 = (bf16[8,40,1792]{2,1,0:T(8,128)(2,1)}, bf16[8,40,1792]{2,1,0:T(8,128)(2,1)S(1)}, u32[]{:S(2)}) copy-start(bf16[8,40,1792]{2,1,0:T(8,128)(2,1)S(1)} %all-to-all-done.2) | copy-start | bytes 3440644
  125.7 21.0 %all-to-all-start.4 = ((bf16[8,40,1792]{2,1,0:T(8,128)(2,1)}), bf16[8,40,1792]{2,1,0:T(8,128)(2,1)S(1)}, u32[]{:S(2)}, u32[]{:S(2)}) async-start(bf16[8,40,1792]{2,1,0:T(8,128)(2,1)} %bitcast.38), calls=%async_computation.4 | async-start | bytes 2293760 | tf_op jit(solution)/shard_map/all_to_all | solution.py:517
  146.7 1.0 copy-start.4
  147.7 18.6 %all-to-all-start.5 = ((bf16[8,40,1792]{2,1,0:T(8,128)(2,1)}), bf16[8,40,1792]{2,1,0:T(8,128)(2,1)S(1)}, u32[]{:S(2)}, u32[]{:S(2)}) async-start(bf16[8,40,1792]{2,1,0:T(8,128)(2,1)} %bitcast.27), calls=%async_computation.5 | async-start | bytes 2293760 | tf_op jit(solution)/shard_map/all_to_all | solution.py:517
  166.3 1.0 copy-start.3
  167.3 4.6 %copy-start.1 = (bf16[384,3584]{1,0:T(8,128)(2,1)S(1)}, bf16[384,3584]{1,0:T(8,128)(2,1)}, u32[]{:S(2)}) copy-start(bf16[384,3584]{1,0:T(8,128)(2,1)} %get-tuple-element.38.refs_0_.refs_2_) | copy-start | bytes 8257540
  167.3 90.6 %all-to-all-start.3 = ((bf16[8,40,3584]{2,1,0:T(8,128)(2,1)}), bf16[8,40,3584]{2,1,0:T(8,128)(2,1)}, u32[]{:S(2)}, u32[]{:S(2)}) async-start(bf16[8,40,3584]{2,1,0:T(8,128)(2,1)} %bitcast.29), calls=%async_computation.3 | async-start | bytes 4587520 | tf_op jit(solution)/shard_map/all_to_all | solution.py:517
  172.0 53.4 %collective-permute-start.9 = (bf16[384,3584]{1,0:T(8,128)(2,1)S(1)}, bf16[384,3584]{1,0:T(8,128)(2,1)}, u32[]{:S(2)}, u32[]{:S(2)}) collective-permute-start(bf16[384,3584]{1,0:T(8,128)(2,1)S(1)} %copy-done.1), channel_id=1, source_target_pairs={{0,16},{16,0},{1,17},{17,1},{2,18},{18,2},{3,19},{19,3},{4,20},{20... | collective-permute-start | bytes 8257544 | tf_op jit(solution)/shard_map/ppermute | solution.py:17
  172.0 33.3 %collective-permute-start.8 = (bf16[64,3584]{1,0:T(8,128)(2,1)}, bf16[64,3584]{1,0:T(8,128)(2,1)S(1)}, u32[]{:S(2)}, u32[]{:S(2)}) collective-permute-start(bf16[64,3584]{1,0:T(8,128)(2,1)} %get-tuple-element.32.refs_4_), channel_id=1, source_target_pairs={{0,8},{1,9},{2,10},{3,11},{4,12},{5,13},{6,14},{7,15},{8,0},{9,1},... | collective-permute-start | bytes 1376264 | tf_op jit(solution)/shard_map/ppermute | solution.py:17
  172.1 50.3 %collective-permute-start.7 = (bf16[512,448]{1,0:T(8,128)(2,1)}, bf16[512,448]{1,0:T(8,128)(2,1)S(1)}, u32[]{:S(2)}, u32[]{:S(2)}) collective-permute-start(bf16[512,448]{1,0:T(8,128)(2,1)} %get-tuple-element.37), channel_id=1, source_target_pairs={{0,16},{16,0},{1,17},{17,1},{2,18},{18,2},{3,19},{19,3},{4,20},{20... | collective-permute-start | bytes 1376264 | tf_op jit(solution)/shard_map/ppermute | solution.py:17
  205.3 5.4 %copy-start.7 = (bf16[64,3584]{1,0:T(8,128)(2,1)}, bf16[64,3584]{1,0:T(8,128)(2,1)S(1)}, u32[]{:S(2)}) copy-start(bf16[64,3584]{1,0:T(8,128)(2,1)S(1)} %collective-permute-done.8.refs_1_.refs_3_) | copy-start | bytes 1376260
  205.3 20.0 %collective-permute-start.10 = (bf16[64,3584]{1,0:T(8,128)(2,1)S(1)}, bf16[64,3584]{1,0:T(8,128)(2,1)}, u32[]{:S(2)}, u32[]{:S(2)}) collective-permute-start(bf16[64,3584]{1,0:T(8,128)(2,1)S(1)} %collective-permute-done.8.refs_1_.refs_3_), channel_id=1, source_target_pairs={{0,16},{16,0},{1,17},{17,1},{2,18},{18,2},{3,19},{19,3},{4,20},{20... | collective-permute-start | bytes 1376264 | tf_op jit(solution)/shard_map/ppermute | solution.py:17
  210.8 37.3 %collective-permute-start.6 = (bf16[128,1792]{1,0:T(8,128)(2,1)}, bf16[128,1792]{1,0:T(8,128)(2,1)}, u32[]{:S(2)}, u32[]{:S(2)}) collective-permute-start(bf16[128,1792]{1,0:T(8,128)(2,1)} %shard_map.97.refs_4_), channel_id=1, source_target_pairs={{0,8},{1,9},{2,10},{3,11},{4,12},{5,13},{6,14},{7,15},{8,0},{9,1},... | collective-permute-start | bytes 1376264 | tf_op jit(solution)/shard_map/ppermute | solution.py:17
  214.1 43.9 %collective-permute-start.5 = (bf16[128,1792]{1,0:T(8,128)(2,1)}, bf16[128,1792]{1,0:T(8,128)(2,1)}, u32[]{:S(2)}, u32[]{:S(2)}) collective-permute-start(bf16[128,1792]{1,0:T(8,128)(2,1)} %shard_map.96.refs_2_), channel_id=1, source_target_pairs={{0,8},{1,9},{2,10},{3,11},{4,12},{5,13},{6,14},{7,15},{8,0},{9,1},... | collective-permute-start | bytes 1376264 | tf_op jit(solution)/shard_map/ppermute | solution.py:17
  222.4 2.9 %copy-start.9 = (bf16[512,448]{1,0:T(8,128)(2,1)}, bf16[512,448]{1,0:T(8,128)(2,1)S(1)}, u32[]{:S(2)}) copy-start(bf16[512,448]{1,0:T(8,128)(2,1)S(1)} %collective-permute-done.7.refs_1_) | copy-start | bytes 1376260
  222.4 40.3 %collective-permute-start.11 = (bf16[64,1024]{1,0:T(8,128)(2,1)}, bf16[64,1024]{1,0:T(8,128)(2,1)S(1)}, u32[]{:S(2)}, u32[]{:S(2)}) collective-permute-start(bf16[64,1024]{1,0:T(8,128)(2,1)} %get-tuple-element.40), channel_id=1, source_target_pairs={{0,8},{1,9},{2,10},{3,11},{4,12},{5,13},{6,14},{7,15},{8,0},{9,1},... | collective-permute-start | bytes 393224 | tf_op jit(solution)/shard_map/ppermute | solution.py:17
  262.7 0.7 copy-start.11

commit v2 on v1

--- a/solution.py
+++ b/solution.py
@@ -8,6 +8,7 @@
 
 F32, BF16, I32 = jnp.float32, jnp.bfloat16, jnp.int32
 LANES = 128
+LONG = 4_000_000_000_000
 VMEM_LIMIT = 60 * 1024 * 1024
 
 
@@ -44,7 +45,7 @@
     return jax.ShapeDtypeStruct(shape, F32)
 
 
-def call(body, grid, ins, outs, scratch=(), after=(), alias=None):
+def call(body, grid, ins, outs, scratch=(), after=(), alias=None, cost=0):
     single = not isinstance(outs, list)
     pairs = [outs] if single else outs
     specs = [spec for _, spec in pairs]
@@ -63,7 +64,7 @@
         scratch_shapes=list(scratch),
         input_output_aliases=alias or {},
         compiler_params=pltpu.CompilerParams(vmem_limit_bytes=VMEM_LIMIT),
-        cost_estimate=pl.CostEstimate(flops=0, bytes_accessed=0, transcendentals=0),
+        cost_estimate=pl.CostEstimate(flops=cost, bytes_accessed=0, transcendentals=0),
     )(*[array for array, _ in ins], *after)
 
 
@@ -251,6 +252,7 @@
         entire(sel, gate) + by_columns(tile, tokens),
         by_columns(tile, bf16(rows, width))[0],
         after=after,
+        cost=LONG,
     )
 
 
@@ -321,7 +323,7 @@
     given_rows(slot_ref, main_ref, spare_ref, out_ref)
 
 
-def give_plan(kind, other, out_main, out_spare, half, mirrored, width, tile, *after):
+def give_plan(kind, other, out_main, out_spare, half, mirrored, width, tile, cost, *after):
     main, spare, rows = out_main.shape[0], out_spare.shape[0], kind.shape[0]
     ins = [(kind, last_columns(kind)), (other, last_columns(other))]
     return call(
@@ -330,6 +332,7 @@
         ins + by_columns(tile, out_main, out_spare),
         by_columns(tile, bf16(rows, width)) + entire(bf16(rows, main + spare)),
         after=after,
+        cost=cost,
     )
 
 
@@ -485,6 +488,7 @@
         entire(bf16(slots, 2 * half), bf16(spare, 2 * half)),
         [pltpu.VMEM((slots, 2 * half), F32), pltpu.VMEM((slots, tile), BF16)],
         after,
+        cost=LONG,
     )
 
 
@@ -535,7 +539,7 @@
     out_spare = swapped(out_spare, "expert", half)
     arrived_second = to_half(packed_second)
     given_first, slot_mirror = give_plan(
-        arrived_first, arrived_own, out_main, out_spare, half, True, width // 2, tile
+        arrived_first, arrived_own, out_main, out_spare, half, True, width // 2, tile, LONG
     )
     returned_first = to_half(given_first)
     given_second = give(slot_mirror, out_main, out_spare, width // 2 // tile, tile)
@@ -544,7 +548,7 @@
         arrived_own, arrived_first, arrived_second, main, spare, half, tile, given_second
     )
     given_own, _ = give_plan(
-        arrived_own, arrived_first, out_main, out_spare, half, False, width, tile, grads_spare
+        arrived_own, arrived_first, out_main, out_spare, half, False, width, tile, 0, grads_spare
     )
     returned_own = to_half(given_own)
     other_main = swapped(grads_main, "dp", 1)

time: 266 us -> 237 us (0.89)
  waiting for transfers between devices: 132 us -> 118 us
  starting transfers between devices: 53.9 us -> 41.9 us
    ppermute x12, waiting for transfers between devices: 122 us -> 58 us  [swapped(): return lax.ppermute(value, axis, pairs)]
    all_to_all x6, waiting for transfers between devices: 11 us -> 59.7 us  [to_half(): lax.all_to_all(rows.reshape(half, cap, -1), 'expert', 0, 0, axis_index_gr...]
    all_to_all x6, starting transfers between devices: 37.3 us -> 27.1 us  [to_half(): lax.all_to_all(rows.reshape(half, cap, -1), 'expert', 0, 0, axis_index_gr...]
    unnamed x26 -> x14, local copies, waits for them, and re-layouts: 5.64 us -> 3.84 us
  transfers between devices with their start and end apart: 18 -> 18, of which waited for: 10 -> 10; matrix products, arithmetic and copies ran while one was open for 0% -> 0% of each run, Pallas kernels for 26% -> 29%
where the time goes in v2:
time: 237 us; the launch traced here: 236 us
  waiting for transfers between devices  118 us (50%)
  Pallas kernels  71.9 us (30%)
  starting transfers between devices  41.9 us (18%)
  local copies, waits for them, and re-layouts  3.84 us (2%)
    pallas_call x17, Pallas kernels, call(): pl.pallas_call(kernel, grid=(grid,), in_specs=[spec for _, spec in ins] +...  71.9 us
    all_to_all x6, waiting for transfers between devices, to_half(): lax.all_to_all(rows.reshape(half, cap, -1), 'expert', 0, 0, axis_index_gr...  59.7 us
    ppermute x12, waiting for transfers between devices, swapped(): return lax.ppermute(value, axis, pairs)  58 us
    all_to_all x6, starting transfers between devices, to_half(): lax.all_to_all(rows.reshape(half, cap, -1), 'expert', 0, 0, axis_index_gr...  27.1 us
    ppermute x12, starting transfers between devices, swapped(): return lax.ppermute(value, axis, pairs)  14.8 us
  transfers between devices with their start and end apart: 18, of which 10 were waited for; matrix products, arithmetic and copies ran while one was open for 0% of the time, Pallas kernels for 29%

profile of v2, /device:TPU:0, one launch (start us, length us, event | category | flops | bytes accessed | tf_op | source)
XLA Modules:
  0.0 236.1 jit_solution(12905942058754107419)
XLA Ops:
  0.6 1.6 shard_map.86
  2.2 4.0 %collective-permute-start = (bf16[64,1024]{1,0:T(8,128)(2,1)}, bf16[64,1024]{1,0:T(8,128)(2,1)S(1)}, u32[]{:S(2)}, u32[]{:S(2)}) collective-permute-start(bf16[64,1024]{1,0:T(8,128)(2,1)} %shard_map.86), channel_id=1, source_target_pairs={{0,8},{1,9},{2,10},{3,11},{4,12},{5,13},{6,14},{7,15},{8,0},{9,1},... | collective-permute-start | bytes 393224 | tf_op jit(solution)/shard_map/ppermute | solution.py:18
  6.2 4.9 %shard_map.85 = (bf16[320,3712]{1,0:T(8,128)(2,1)}, bf16[256,320]{1,0:T(8,128)(2,1)}) custom-call(s32[4,128]{1,0:T(4,128)} %bitcast.37, s32[4,128]{1,0:T(4,128)} %bitcast.39, f32[4,128]{1,0:T(4,128)} %bitcast.41, bf16[128,3584]{1,0:T(8,128)(2,1)} %refs_3_.3), custom_call_target="tpu_custom_call" | custom-call | tf_op jit(solution)/shard_map/pallas_call | solution.py:58
  11.2 1.6 collective-permute-done.refs_1_.refs_4_
  12.8 0.0 copy-start.4
  12.8 0.7 copy-done.4
  13.4 4.0 %all-to-all-start = ((bf16[8,40,3712]{2,1,0:T(8,128)(2,1)}), bf16[8,40,3712]{2,1,0:T(8,128)(2,1)S(1)}, u32[]{:S(2)}, u32[]{:S(2)}) async-start(bf16[8,40,3712]{2,1,0:T(8,128)(2,1)} %bitcast.25), calls=%async_computation | async-start | bytes 4751360 | tf_op jit(solution)/shard_map/all_to_all | solution.py:521
  17.4 0.0 collective-permute-start.2
  17.4 2.2 shard_map.88
  19.6 3.3 %collective-permute-start.1 = (bf16[128,1920]{1,0:T(8,128)(2,1)}, bf16[128,1920]{1,0:T(8,128)(2,1)S(1)}, u32[]{:S(2)}, u32[]{:S(2)}) collective-permute-start(bf16[128,1920]{1,0:T(8,128)(2,1)} %get-tuple-element.24), channel_id=1, source_target_pairs={{0,8},{1,9},{2,10},{3,11},{4,12},{5,13},{6,14},{7,15},{8,0},{9,1},... | collective-permute-start | bytes 1474568 | tf_op jit(solution)/shard_map/ppermute | solution.py:18
  22.9 0.0 collective-permute-start.4
  22.9 1.2 collective-permute-done.2.refs_3_
  24.1 8.3 %shard_map.89 = (bf16[384,3584]{1,0:T(8,128)(2,1)}, bf16[64,3584]{1,0:T(8,128)(2,1)}, bf16[512,448]{1,0:T(8,128)(2,1)}, bf16[512,448]{1,0:T(8,128)(2,1)}) custom-call(bf16[448,1024]{1,0:T(8,128)(2,1)} %bitcast.29, bf16[64,1024]{1,0:T(8,128)(2,1)} %copy-done.4, bf16[512,3584]{1,0:T(8,128)(2,1)} %bitcast.32, bf16[512,3584]{1,0:T(8,128)(2,1)} %collective-permute-done.2.refs_3_, ...), custom_call_target="tpu_custom_call" | custom-call | tf_op jit(solution)/shard_map/pallas_call | solution.py:58
  32.5 3.3 %collective-permute-start.3 = (bf16[64,3584]{1,0:T(8,128)(2,1)}, bf16[64,3584]{1,0:T(8,128)(2,1)}, u32[]{:S(2)}, u32[]{:S(2)}) collective-permute-start(bf16[64,3584]{1,0:T(8,128)(2,1)} %get-tuple-element.25.refs_2_), channel_id=1, source_target_pairs={{0,8},{1,9},{2,10},{3,11},{4,12},{5,13},{6,14},{7,15},{8,0},{9,1},... | collective-permute-start | bytes 1376264 | tf_op jit(solution)/shard_map/ppermute | solution.py:18
  35.7 19.2 %collective-permute-done.1.refs_0_.refs_1_ = bf16[128,1920]{1,0:T(8,128)(2,1)S(1)} collective-permute-done((bf16[128,1920]{1,0:T(8,128)(2,1)}, bf16[128,1920]{1,0:T(8,128)(2,1)S(1)}, u32[]{:S(2)}, u32[]{:S(2)}) %collective-permute-start.1) | collective-permute-done | bytes 491552 | tf_op jit(solution)/shard_map/ppermute | solution.py:18
  54.9 0.0 copy-start.3
  54.9 0.8 copy-done.3
  55.7 3.6 %shard_map.90 = (bf16[320,1920]{1,0:T(8,128)(2,1)}, bf16[320,128]{1,0:T(8,128)(2,1)}, f32[320,128]{1,0:T(8,128)}, bf16[256,320]{1,0:T(8,128)(2,1)}) custom-call(bf16[128,1920]{1,0:T(8,128)(2,1)} %copy-done.3, bf16[128,1920]{1,0:T(8,128)(2,1)} %copy-done.3, bf16[64,3584]{1,0:T(8,128)(2,1)} %get-tuple-element.25.refs_2_), custom_call_target="tpu_custom_call" | custom-call | tf_op jit(solution)/shard_map/pallas_call | solution.py:58
  59.4 9.9 %all-to-all-done = bf16[8,40,3712]{2,1,0:T(8,128)(2,1)S(1)} async-done(((bf16[8,40,3712]{2,1,0:T(8,128)(2,1)}), bf16[8,40,3712]{2,1,0:T(8,128)(2,1)S(1)}, u32[]{:S(2)}, u32[]{:S(2)}) %all-to-all-start) | async-done | bytes 2375712 | tf_op jit(solution)/shard_map/all_to_all | solution.py:521
  69.2 6.6 %all-to-all-start.1 = ((bf16[8,40,1920]{2,1,0:T(8,128)(2,1)}), bf16[8,40,1920]{2,1,0:T(8,128)(2,1)}, u32[]{:S(2)}, u32[]{:S(2)}) async-start(bf16[8,40,1920]{2,1,0:T(8,128)(2,1)} %bitcast.34), calls=%async_computation.1 | async-start | bytes 2457600 | tf_op jit(solution)/shard_map/all_to_all | solution.py:521
  75.9 0.0 collective-permute-done.4.refs_2_
  75.9 0.0 copy-start.6
  75.9 0.8 copy-done.6
  76.7 2.6 %shard_map.91 = bf16[320,1792]{1,0:T(8,128)(2,1)} custom-call(bf16[320,128]{1,0:T(8,128)(2,1)} %get-tuple-element.28.refs_0_, f32[320,128]{1,0:T(8,128)} %get-tuple-element.29.refs_1_, bf16[128,1792]{1,0:T(8,128)(2,1)} %copy-done.6), custom_call_target="tpu_custom_call" | custom-call | flops 3999999983616 | tf_op jit(solution)/shard_map/pallas_call | solution.py:58
  79.2 0.0 copy-done
  79.2 18.4 %all-to-all-done.1 = bf16[8,40,1920]{2,1,0:T(8,128)(2,1)} async-done(((bf16[8,40,1920]{2,1,0:T(8,128)(2,1)}), bf16[8,40,1920]{2,1,0:T(8,128)(2,1)}, u32[]{:S(2)}, u32[]{:S(2)}) %all-to-all-start.1) | async-done | bytes 1228832 | tf_op jit(solution)/shard_map/all_to_all | solution.py:521
  97.6 4.2 %all-to-all-start.2 = ((bf16[8,40,1792]{2,1,0:T(8,128)(2,1)}), bf16[8,40,1792]{2,1,0:T(8,128)(2,1)}, u32[]{:S(2)}, u32[]{:S(2)}) async-start(bf16[8,40,1792]{2,1,0:T(8,128)(2,1)} %bitcast.35), calls=%async_computation.2 | async-start | bytes 2293760 | tf_op jit(solution)/shard_map/all_to_all | solution.py:521
  101.9 0.0 collective-permute-done.3.refs_3_.refs_2_
  101.9 3.7 %shard_map.92 = (bf16[320,1792]{1,0:T(8,128)(2,1)}, bf16[320,448]{1,0:T(8,128)(2,1)}) custom-call(bf16[320,1920]{1,0:T(8,128)(2,1)} %bitcast.8.refs_0_.refs_1_.refs_3_, bf16[320,3712]{1,0:T(8,128)(2,1)} %bitcast.19, bf16[384,3584]{1,0:T(8,128)(2,1)} %get-tuple-element.27.refs_2_.refs_1_, bf16[64,3584]{1,0:T(8,128)(2,1)} %collective-permute-done.3.refs_3_.refs_2_), custom_call_target="tpu_custom_call" | custom-call | flops 3999999983616 | tf_op jit(solution)/shard_map/pallas_call | solution.py:58
  105.6 11.5 %all-to-all-done.2 = bf16[8,40,1792]{2,1,0:T(8,128)(2,1)} async-done(((bf16[8,40,1792]{2,1,0:T(8,128)(2,1)}), bf16[8,40,1792]{2,1,0:T(8,128)(2,1)}, u32[]{:S(2)}, u32[]{:S(2)}) %all-to-all-start.2) | async-done | bytes 1146912 | tf_op jit(solution)/shard_map/all_to_all | solution.py:521
  117.0 3.6 %all-to-all-start.4 = ((bf16[8,40,1792]{2,1,0:T(8,128)(2,1)}), bf16[8,40,1792]{2,1,0:T(8,128)(2,1)S(1)}, u32[]{:S(2)}, u32[]{:S(2)}) async-start(bf16[8,40,1792]{2,1,0:T(8,128)(2,1)} %bitcast.36), calls=%async_computation.4 | async-start | bytes 2293760 | tf_op jit(solution)/shard_map/all_to_all | solution.py:521
  120.6 3.3 %shard_map.93.refs_5_ = bf16[320,1792]{1,0:T(8,128)(2,1)} custom-call(bf16[320,448]{1,0:T(8,128)(2,1)} %get-tuple-element.31.refs_0_, bf16[384,3584]{1,0:T(8,128)(2,1)} %get-tuple-element.27.refs_2_.refs_1_, bf16[64,3584]{1,0:T(8,128)(2,1)} %collective-permute-done.3.refs_3_.refs_2_), custom_call_target="tpu_custom_call" | custom-call | tf_op jit(solution)/shard_map/pallas_call | solution.py:58
  123.9 12.1 %all-to-all-done.4 = bf16[8,40,1792]{2,1,0:T(8,128)(2,1)S(1)} async-done(((bf16[8,40,1792]{2,1,0:T(8,128)(2,1)}), bf16[8,40,1792]{2,1,0:T(8,128)(2,1)S(1)}, u32[]{:S(2)}, u32[]{:S(2)}) %all-to-all-start.4) | async-done | bytes 1146912 | tf_op jit(solution)/shard_map/all_to_all | solution.py:521
  136.0 0.0 copy-start.2
  136.1 3.6 %all-to-all-start.5 = ((bf16[8,40,1792]{2,1,0:T(8,128)(2,1)}), bf16[8,40,1792]{2,1,0:T(8,128)(2,1)S(1)}, u32[]{:S(2)}, u32[]{:S(2)}) async-start(bf16[8,40,1792]{2,1,0:T(8,128)(2,1)} %bitcast.24), calls=%async_computation.5 | async-start | bytes 2293760 | tf_op jit(solution)/shard_map/all_to_all | solution.py:521
  139.6 7.9 %shard_map.94 = (bf16[384,3584]{1,0:T(8,128)(2,1)}, bf16[64,3584]{1,0:T(8,128)(2,1)}) custom-call(bf16[320,3712]{1,0:T(8,128)(2,1)} %bitcast.20, bf16[320,1920]{1,0:T(8,128)(2,1)} %bitcast.8.refs_0_.refs_1_.refs_3_, bf16[320,3712]{1,0:T(8,128)(2,1)} %bitcast.21, bf16[320,1920]{1,0:T(8,128)(2,1)} %bitcast.8.refs_0_.refs_1_.refs_3_, ...), custom_call_target="tpu_custom_call" | custom-call | tf_op jit(solution)/shard_map/pallas_call | solution.py:58
  147.5 0.0 copy-done.2
  147.5 0.7 collective-permute-start.8
  148.2 0.0 collective-permute-start.7
  148.2 0.5 collective-permute-start.9
  148.7 5.7 %shard_map.95 = (bf16[320,3584]{1,0:T(8,128)(2,1)}, bf16[320,448]{1,0:T(8,128)(2,1)}) custom-call(bf16[320,3712]{1,0:T(8,128)(2,1)} %bitcast.22, bf16[320,1920]{1,0:T(8,128)(2,1)} %bitcast.8.refs_0_.refs_1_.refs_3_, bf16[384,3584]{1,0:T(8,128)(2,1)} %get-tuple-element.27.refs_2_.refs_1_, bf16[64,3584]{1,0:T(8,128)(2,1)} %collective-permute-done.3.refs_3_.refs_2_, ...), custom_call_target="tpu_custom_call" | custom-call | tf_op jit(solution)/shard_map/pallas_call | solution.py:58
  154.4 16.2 %collective-permute-done.8.refs_1_.refs_3_ = bf16[64,3584]{1,0:T(8,128)(2,1)} collective-permute-done((bf16[64,3584]{1,0:T(8,128)(2,1)}, bf16[64,3584]{1,0:T(8,128)(2,1)}, u32[]{:S(2)}, u32[]{:S(2)}) %collective-permute-start.8) | collective-permute-done | bytes 458784 | tf_op jit(solution)/shard_map/ppermute | solution.py:18
  170.5 0.0 collective-permute-start.10
  170.5 2.6 %shard_map.96.refs_2_ = bf16[128,1792]{1,0:T(8,128)(2,1)} custom-call(bf16[256,320]{1,0:T(8,128)(2,1)} %get-tuple-element.34.refs_0_, bf16[320,1792]{1,0:T(8,128)(2,1)} %bitcast.27, bf16[320,3584]{1,0:T(8,128)(2,1)} %get-tuple-element.33.refs_2_), custom_call_target="tpu_custom_call" | custom-call | tf_op jit(solution)/shard_map/pallas_call | solution.py:58
  173.2 0.0 collective-permute-start.5
  173.2 0.0 all-to-all-done.5
  173.2 0.0 copy-start.1
  173.2 1.0 copy-done.1
  174.2 5.1 %all-to-all-start.3 = ((bf16[8,40,3584]{2,1,0:T(8,128)(2,1)}), bf16[8,40,3584]{2,1,0:T(8,128)(2,1)}, u32[]{:S(2)}, u32[]{:S(2)}) async-start(bf16[8,40,3584]{2,1,0:T(8,128)(2,1)} %bitcast.11), calls=%async_computation.3 | async-start | bytes 4587520 | tf_op jit(solution)/shard_map/all_to_all | solution.py:521
  179.3 2.6 %shard_map.97.refs_4_ = bf16[128,1792]{1,0:T(8,128)(2,1)} custom-call(bf16[256,320]{1,0:T(8,128)(2,1)} %get-tuple-element.34.refs_0_, bf16[320,1792]{1,0:T(8,128)(2,1)} %bitcast.26, bf16[128,1792]{1,0:T(8,128)(2,1)} %shard_map.96.refs_2_), custom_call_target="tpu_custom_call" | custom-call | tf_op jit(solution)/shard_map/pallas_call | solution.py:58
  181.9 2.2 collective-permute-start.6
  184.1 8.3 %shard_map.98 = (bf16[448,1024]{1,0:T(8,128)(2,1)}, bf16[64,1024]{1,0:T(8,128)(2,1)}) custom-call(bf16[384,3584]{1,0:T(8,128)(2,1)} %get-tuple-element.38.refs_0_.refs_2_, bf16[64,3584]{1,0:T(8,128)(2,1)} %collective-permute-done.8.refs_1_.refs_3_, bf16[512,3584]{1,0:T(8,128)(2,1)} %bitcast.33, bf16[512,3584]{1,0:T(8,128)(2,1)} %collective-permute-done.2.refs_3_, ...), custom_call_target="tpu_custom_call" | custom-call | flops 3999999983616 | tf_op jit(solution)/shard_map/pallas_call | solution.py:58
  192.4 0.0 collective-permute-done.7.refs_1_
  192.4 0.8 collective-permute-start.11
  193.1 0.0 collective-permute-done.10.refs_5_
  193.1 0.0 collective-permute-done.9.refs_4_
  193.1 8.4 %shard_map.99.refs_4_ = bf16[512,3584]{1,0:T(8,128)(2,1)} custom-call(bf16[512,448]{1,0:T(8,128)(2,1)} %get-tuple-element.36.refs_0_, bf16[512,448]{1,0:T(8,128)(2,1)} %collective-permute-done.7.refs_1_, bf16[384,3584]{1,0:T(8,128)(2,1)} %get-tuple-element.38.refs_0_.refs_2_, bf16[64,3584]{1,0:T(8,128)(2,1)} %collective-permute-done.8.refs_1_.refs_3_, ...), custom_call_target="tpu_custom_call" | custom-call | tf_op jit(solution)/shard_map/pallas_call | solution.py:58
  201.5 19.8 %collective-permute-done.6.refs_3_ = bf16[128,1792]{1,0:T(8,128)(2,1)} collective-permute-done((bf16[128,1792]{1,0:T(8,128)(2,1)}, bf16[128,1792]{1,0:T(8,128)(2,1)}, u32[]{:S(2)}, u32[]{:S(2)}) %collective-permute-start.6) | collective-permute-done | bytes 458784 | tf_op jit(solution)/shard_map/ppermute | solution.py:18
  221.4 0.0 collective-permute-done.5.refs_2_
  221.4 7.8 %all-to-all-done.3 = bf16[8,40,3584]{2,1,0:T(8,128)(2,1)} async-done(((bf16[8,40,3584]{2,1,0:T(8,128)(2,1)}), bf16[8,40,3584]{2,1,0:T(8,128)(2,1)}, u32[]{:S(2)}, u32[]{:S(2)}) %all-to-all-start.3) | async-done | bytes 2293792 | tf_op jit(solution)/shard_map/all_to_all | solution.py:521
  229.2 4.7 %shard_map.100.refs_2_ = bf16[128,3584]{1,0:T(8,128)(2,1)} custom-call(bf16[256,320]{1,0:T(8,128)(2,1)} %get-tuple-element.22.refs_4_.refs_0_, bf16[320,3584]{1,0:T(8,128)(2,1)} %bitcast.12.refs_1_, bf16[128,1792]{1,0:T(8,128)(2,1)} %collective-permute-done.5.refs_2_, bf16[128,1792]{1,0:T(8,128)(2,1)} %collective-permute-done.6.refs_3_, ...), custom_call_target="tpu_custom_call" | custom-call | tf_op jit(solution)/shard_map/pallas_call | solution.py:58
  233.9 0.0 collective-permute-done.11.refs_1_
  233.9 0.6 copy-done.5
  234.5 1.6 shard_map.101
  (3 shorter events, 0.0 us)
Async XLA Ops:
  2.2 10.5 %collective-permute-start = (bf16[64,1024]{1,0:T(8,128)(2,1)}, bf16[64,1024]{1,0:T(8,128)(2,1)S(1)}, u32[]{:S(2)}, u32[]{:S(2)}) collective-permute-start(bf16[64,1024]{1,0:T(8,128)(2,1)} %shard_map.86), channel_id=1, source_target_pairs={{0,8},{1,9},{2,10},{3,11},{4,12},{5,13},{6,14},{7,15},{8,0},{9,1},... | collective-permute-start | bytes 393224 | tf_op jit(solution)/shard_map/ppermute | solution.py:18
  12.8 0.7 copy-start.4
  13.4 55.8 %all-to-all-start = ((bf16[8,40,3712]{2,1,0:T(8,128)(2,1)}), bf16[8,40,3712]{2,1,0:T(8,128)(2,1)S(1)}, u32[]{:S(2)}, u32[]{:S(2)}) async-start(bf16[8,40,3712]{2,1,0:T(8,128)(2,1)} %bitcast.25), calls=%async_computation | async-start | bytes 4751360 | tf_op jit(solution)/shard_map/all_to_all | solution.py:521
  17.4 6.8 %collective-permute-start.2 = (bf16[512,3584]{1,0:T(8,128)(2,1)}, bf16[512,3584]{1,0:T(8,128)(2,1)}, u32[]{:S(2)}, u32[]{:S(2)}) collective-permute-start(bf16[512,3584]{1,0:T(8,128)(2,1)} %bitcast.31), channel_id=1, source_target_pairs={{0,16},{16,0},{1,17},{17,1},{2,18},{18,2},{3,19},{19,3},{4,20},{20... | collective-permute-start | bytes 11010056 | tf_op jit(solution)/shard_map/ppermute | solution.py:18
  19.6 35.3 %collective-permute-start.1 = (bf16[128,1920]{1,0:T(8,128)(2,1)}, bf16[128,1920]{1,0:T(8,128)(2,1)S(1)}, u32[]{:S(2)}, u32[]{:S(2)}) collective-permute-start(bf16[128,1920]{1,0:T(8,128)(2,1)} %get-tuple-element.24), channel_id=1, source_target_pairs={{0,8},{1,9},{2,10},{3,11},{4,12},{5,13},{6,14},{7,15},{8,0},{9,1},... | collective-permute-start | bytes 1474568 | tf_op jit(solution)/shard_map/ppermute | solution.py:18
  22.9 53.0 %collective-permute-start.4 = (bf16[128,1792]{1,0:T(8,128)(2,1)}, bf16[128,1792]{1,0:T(8,128)(2,1)S(1)}, u32[]{:S(2)}, u32[]{:S(2)}) collective-permute-start(bf16[128,1792]{1,0:T(8,128)(2,1)} %get-tuple-element.30), channel_id=1, source_target_pairs={{0,8},{1,9},{2,10},{3,11},{4,12},{5,13},{6,14},{7,15},{8,0},{9,1},... | collective-permute-start | bytes 1376264 | tf_op jit(solution)/shard_map/ppermute | solution.py:18
  32.5 69.4 %collective-permute-start.3 = (bf16[64,3584]{1,0:T(8,128)(2,1)}, bf16[64,3584]{1,0:T(8,128)(2,1)}, u32[]{:S(2)}, u32[]{:S(2)}) collective-permute-start(bf16[64,3584]{1,0:T(8,128)(2,1)} %get-tuple-element.25.refs_2_), channel_id=1, source_target_pairs={{0,8},{1,9},{2,10},{3,11},{4,12},{5,13},{6,14},{7,15},{8,0},{9,1},... | collective-permute-start | bytes 1376264 | tf_op jit(solution)/shard_map/ppermute | solution.py:18
  54.9 0.8 copy-start.3
  69.2 10.0 %copy-start = (bf16[8,40,3712]{2,1,0:T(8,128)(2,1)}, bf16[8,40,3712]{2,1,0:T(8,128)(2,1)S(1)}, u32[]{:S(2)}) copy-start(bf16[8,40,3712]{2,1,0:T(8,128)(2,1)S(1)} %all-to-all-done) | copy-start | bytes 7127044
  69.2 28.4 %all-to-all-start.1 = ((bf16[8,40,1920]{2,1,0:T(8,128)(2,1)}), bf16[8,40,1920]{2,1,0:T(8,128)(2,1)}, u32[]{:S(2)}, u32[]{:S(2)}) async-start(bf16[8,40,1920]{2,1,0:T(8,128)(2,1)} %bitcast.34), calls=%async_computation.1 | async-start | bytes 2457600 | tf_op jit(solution)/shard_map/all_to_all | solution.py:521
  75.9 0.8 copy-start.6
  97.6 19.4 %all-to-all-start.2 = ((bf16[8,40,1792]{2,1,0:T(8,128)(2,1)}), bf16[8,40,1792]{2,1,0:T(8,128)(2,1)}, u32[]{:S(2)}, u32[]{:S(2)}) async-start(bf16[8,40,1792]{2,1,0:T(8,128)(2,1)} %bitcast.35), calls=%async_computation.2 | async-start | bytes 2293760 | tf_op jit(solution)/shard_map/all_to_all | solution.py:521
  117.0 19.0 %all-to-all-start.4 = ((bf16[8,40,1792]{2,1,0:T(8,128)(2,1)}), bf16[8,40,1792]{2,1,0:T(8,128)(2,1)S(1)}, u32[]{:S(2)}, u32[]{:S(2)}) async-start(bf16[8,40,1792]{2,1,0:T(8,128)(2,1)} %bitcast.36), calls=%async_computation.4 | async-start | bytes 2293760 | tf_op jit(solution)/shard_map/all_to_all | solution.py:521
  136.0 11.5 %copy-start.2 = (bf16[8,40,1792]{2,1,0:T(8,128)(2,1)}, bf16[8,40,1792]{2,1,0:T(8,128)(2,1)S(1)}, u32[]{:S(2)}) copy-start(bf16[8,40,1792]{2,1,0:T(8,128)(2,1)S(1)} %all-to-all-done.4) | copy-start | bytes 3440644
  136.1 37.1 %all-to-all-start.5 = ((bf16[8,40,1792]{2,1,0:T(8,128)(2,1)}), bf16[8,40,1792]{2,1,0:T(8,128)(2,1)S(1)}, u32[]{:S(2)}, u32[]{:S(2)}) async-start(bf16[8,40,1792]{2,1,0:T(8,128)(2,1)} %bitcast.24), calls=%async_computation.5 | async-start | bytes 2293760 | tf_op jit(solution)/shard_map/all_to_all | solution.py:521
  147.5 23.0 %collective-permute-start.8 = (bf16[64,3584]{1,0:T(8,128)(2,1)}, bf16[64,3584]{1,0:T(8,128)(2,1)}, u32[]{:S(2)}, u32[]{:S(2)}) collective-permute-start(bf16[64,3584]{1,0:T(8,128)(2,1)} %get-tuple-element.32.refs_4_), channel_id=1, source_target_pairs={{0,8},{1,9},{2,10},{3,11},{4,12},{5,13},{6,14},{7,15},{8,0},{9,1},... | collective-permute-start | bytes 1376264 | tf_op jit(solution)/shard_map/ppermute | solution.py:18
  148.2 44.2 %collective-permute-start.7 = (bf16[512,448]{1,0:T(8,128)(2,1)}, bf16[512,448]{1,0:T(8,128)(2,1)}, u32[]{:S(2)}, u32[]{:S(2)}) collective-permute-start(bf16[512,448]{1,0:T(8,128)(2,1)} %get-tuple-element.37), channel_id=1, source_target_pairs={{0,16},{16,0},{1,17},{17,1},{2,18},{18,2},{3,19},{19,3},{4,20},{20... | collective-permute-start | bytes 1376264 | tf_op jit(solution)/shard_map/ppermute | solution.py:18
  148.2 45.0 %collective-permute-start.9 = (bf16[384,3584]{1,0:T(8,128)(2,1)}, bf16[384,3584]{1,0:T(8,128)(2,1)}, u32[]{:S(2)}, u32[]{:S(2)}) collective-permute-start(bf16[384,3584]{1,0:T(8,128)(2,1)} %get-tuple-element.38.refs_0_.refs_2_), channel_id=1, source_target_pairs={{0,16},{16,0},{1,17},{17,1},{2,18},{18,2},{3,19},{19,3},{4,20},{20... | collective-permute-start | bytes 8257544 | tf_op jit(solution)/shard_map/ppermute | solution.py:18
  170.5 22.6 %collective-permute-start.10 = (bf16[64,3584]{1,0:T(8,128)(2,1)}, bf16[64,3584]{1,0:T(8,128)(2,1)}, u32[]{:S(2)}, u32[]{:S(2)}) collective-permute-start(bf16[64,3584]{1,0:T(8,128)(2,1)} %collective-permute-done.8.refs_1_.refs_3_), channel_id=1, source_target_pairs={{0,16},{16,0},{1,17},{17,1},{2,18},{18,2},{3,19},{19,3},{4,20},{20... | collective-permute-start | bytes 1376264 | tf_op jit(solution)/shard_map/ppermute | solution.py:18
  173.2 48.2 %collective-permute-start.5 = (bf16[128,1792]{1,0:T(8,128)(2,1)}, bf16[128,1792]{1,0:T(8,128)(2,1)}, u32[]{:S(2)}, u32[]{:S(2)}) collective-permute-start(bf16[128,1792]{1,0:T(8,128)(2,1)} %shard_map.96.refs_2_), channel_id=1, source_target_pairs={{0,8},{1,9},{2,10},{3,11},{4,12},{5,13},{6,14},{7,15},{8,0},{9,1},... | collective-permute-start | bytes 1376264 | tf_op jit(solution)/shard_map/ppermute | solution.py:18
  173.2 1.0 copy-start.1
  174.2 55.0 %all-to-all-start.3 = ((bf16[8,40,3584]{2,1,0:T(8,128)(2,1)}), bf16[8,40,3584]{2,1,0:T(8,128)(2,1)}, u32[]{:S(2)}, u32[]{:S(2)}) async-start(bf16[8,40,3584]{2,1,0:T(8,128)(2,1)} %bitcast.11), calls=%async_computation.3 | async-start | bytes 4587520 | tf_op jit(solution)/shard_map/all_to_all | solution.py:521
  181.9 39.4 %collective-permute-start.6 = (bf16[128,1792]{1,0:T(8,128)(2,1)}, bf16[128,1792]{1,0:T(8,128)(2,1)}, u32[]{:S(2)}, u32[]{:S(2)}) collective-permute-start(bf16[128,1792]{1,0:T(8,128)(2,1)} %shard_map.97.refs_4_), channel_id=1, source_target_pairs={{0,8},{1,9},{2,10},{3,11},{4,12},{5,13},{6,14},{7,15},{8,0},{9,1},... | collective-permute-start | bytes 1376264 | tf_op jit(solution)/shard_map/ppermute | solution.py:18
  192.4 41.5 %collective-permute-start.11 = (bf16[64,1024]{1,0:T(8,128)(2,1)}, bf16[64,1024]{1,0:T(8,128)(2,1)S(1)}, u32[]{:S(2)}, u32[]{:S(2)}) collective-permute-start(bf16[64,1024]{1,0:T(8,128)(2,1)} %get-tuple-element.40), channel_id=1, source_target_pairs={{0,8},{1,9},{2,10},{3,11},{4,12},{5,13},{6,14},{7,15},{8,0},{9,1},... | collective-permute-start | bytes 393224 | tf_op jit(solution)/shard_map/ppermute | solution.py:18
  233.9 0.6 copy-start.5

commit v3 on v0

--- a/solution.py
+++ b/solution.py
@@ -8,6 +8,7 @@
 
 F32, BF16, I32 = jnp.float32, jnp.bfloat16, jnp.int32
 LANES = 128
+LONG = 4_000_000_000_000
 VMEM_LIMIT = 60 * 1024 * 1024
 
 
@@ -44,7 +45,7 @@
     return jax.ShapeDtypeStruct(shape, F32)
 
 
-def call(body, grid, ins, outs, scratch=(), after=(), alias=None):
+def call(body, grid, ins, outs, scratch=(), after=(), alias=None, cost=0):
     single = not isinstance(outs, list)
     pairs = [outs] if single else outs
     specs = [spec for _, spec in pairs]
@@ -63,7 +64,7 @@
         scratch_shapes=list(scratch),
         input_output_aliases=alias or {},
         compiler_params=pltpu.CompilerParams(vmem_limit_bytes=VMEM_LIMIT),
-        cost_estimate=pl.CostEstimate(flops=0, bytes_accessed=0, transcendentals=0),
+        cost_estimate=pl.CostEstimate(flops=cost, bytes_accessed=0, transcendentals=0),
     )(*[array for array, _ in ins], *after)
 
 
@@ -104,17 +105,22 @@
     return call(head_kernel, 1, entire(devices, flags, gates) + [(hidden, last)], outs)
 
 
-def copy_kernel(source_ref, target_ref, done):
-    copy = pltpu.make_async_copy(source_ref, target_ref, done)
-    copy.start()
-    copy.wait()
-
-
-def copied(array, *after):
+def copy_kernel(source_ref, target_ref):
+    target_ref[...] = source_ref[...]
+
+
+def copied(array, tile, *after):
+    ins, outs = by_columns(tile, array), by_columns(tile, bf16(*array.shape))[0]
+    return call(copy_kernel, array.shape[1] // tile, ins, outs, (), after)
+
+
+def touch_kernel(source_ref, target_ref):
+    pass
+
+
+def touched(array, *after):
     shape = jax.ShapeDtypeStruct(array.shape, array.dtype)
-    return call(
-        copy_kernel, 1, [(array, anywhere())], (shape, anywhere()), [pltpu.SemaphoreType.DMA], after
-    )
+    return call(touch_kernel, 1, [(array, anywhere())], (shape, anywhere()), (), after, {0: 0})
 
 
 def plan_rows(meta, cap, half, sel_ref, gate_ref, mix_ref):
@@ -183,6 +189,7 @@
         entire(sel, gate) + by_columns(tile, tokens),
         by_columns(tile, bf16(rows, width))[0],
         after=after,
+        cost=LONG,
     )
 
 
@@ -243,35 +250,65 @@
     return call(functools.partial(plan_kernel, cap, half, main), 1, entire(metas), outs)
 
 
-def project_kernel(hidden_ref, spare_ref, near_ref, far_ref, main_out, spare_out, near_turned, far_turned, stack_ref):
-    main, half = main_out.shape[0], near_ref.shape[0]
-
+def side_by_side(source, target_ref):
+    half = target_ref.shape[1] // 2
+    core = lax.axis_index("dp")
+    for at, which in ((0, core), (half, 1 - core)):
+        start = pl.multiple_of(which * half, LANES)
+        target_ref[:, at : at + half] = source[: target_ref.shape[0], pl.ds(start, half)]
+
+
+def projected(stack_ref, near_ref, far_ref, out_ref):
+    half = near_ref.shape[0]
+    total = dot(stack_ref[:, :half], near_ref[...]) + dot(stack_ref[:, half:], far_ref[...])
+    out_ref[...] = total.astype(BF16)
+
+
+def project_spare_kernel(spare_ref, near_ref, far_ref, out_ref, stack_ref):
     @pl.when(pl.program_id(0) == 0)
     def _():
-        core = lax.axis_index("dp")
-        for at, which, turned_ref in ((0, core, near_turned), (half, 1 - core, far_turned)):
-            start = pl.multiple_of(which * half, LANES)
-            stack_ref[:main, at : at + half] = hidden_ref[:main, pl.ds(start, half)]
-            stack_ref[main:, at : at + half] = spare_ref[:, pl.ds(start, half)]
-            turned_ref[...] = stack_ref[:, at : at + half].T
-
-    total = dot(stack_ref[:, :half], near_ref[...]) + dot(stack_ref[:, half:], far_ref[...])
-    total = total.astype(BF16)
-    main_out[...] = total[:main]
-    spare_out[...] = total[main:]
+        side_by_side(spare_ref, stack_ref)
+
+    projected(stack_ref, near_ref, far_ref, out_ref)
+
+
+def project_spare(spare_hidden, near, far, tile, *after):
+    width = near.shape[1]
+    return call(
+        project_spare_kernel,
+        width // tile,
+        entire(spare_hidden) + by_columns(tile, near, far),
+        by_columns(tile, bf16(spare_hidden.shape[0], width))[0],
+        [pltpu.VMEM(spare_hidden.shape, BF16)],
+        after,
+    )
+
+
+def project_kernel(hidden_ref, spare_ref, near_ref, far_ref, out_ref, near_turned, far_turned, stack_ref, side_ref):
+    main, half = out_ref.shape[0], near_ref.shape[0]
+
+    @pl.when(pl.program_id(0) == 0)
+    def _():
+        side_by_side(hidden_ref, stack_ref)
+        side_by_side(spare_ref, side_ref)
+        for at, turned_ref in ((0, near_turned), (half, far_turned)):
+            turned_ref[:, :main] = stack_ref[:, at : at + half].T
+            turned_ref[:, main:] = side_ref[:, at : at + half].T
+
+    projected(stack_ref, near_ref, far_ref, out_ref)
 
 
 def project(hidden, spare_hidden, near, far, tile, *after):
     half, width = near.shape
     spare = spare_hidden.shape[0]
-    slots = hidden.shape[0]
+    slots, hid = hidden.shape
     turned = [bf16(half, slots), bf16(half, slots)]
     return call(
         project_kernel,
         width // tile,
         entire(hidden, spare_hidden) + by_columns(tile, near, far),
-        by_columns(tile, bf16(slots - spare, width), bf16(spare, width)) + entire(*turned),
-        [pltpu.VMEM(hidden.shape, BF16)],
+        by_columns(tile, bf16(slots - spare, width)) + entire(*turned),
+        [pltpu.VMEM((slots - spare, hid), BF16), pltpu.VMEM((spare, hid), BF16)],
         after,
     )
 
@@ -437,37 +474,33 @@
     )
     spare_hidden = swapped(spare_hidden, "expert", half)
     metas = lax.all_to_all(meta, "expert", 0, 0, tiled=True)
-    mirror = swapped(copied(grad_out, metas, spare_hidden), "expert", half)
     packed_own, mix_own = pack_own(meta, grad_out, cap, half, tile)
-    arrived_own = to_half(packed_own)
+    arrived_own = to_half(touched(packed_own, metas, spare_hidden, far))
+    out_spare = project_spare(spare_hidden, near, far, tile, mix_own)
     sel, gate, mix_mirror, give_own, take_own, give_mirror, take_mirror = plan(
         metas, cap, half, main, slots
     )
-    out_main, out_spare, turned, far_turned = project(
-        hidden, spare_hidden, near, far, tile, mix_own
-    )
+    out_main, turned, far_turned = project(hidden, spare_hidden, near, far, tile, out_spare)
+    out_spare = swapped(out_spare, "expert", half)
+    mirror = swapped(touched(copied(grad_out, width // 2), out_spare, out_main, sel), "expert", half)
     other_turned = swapped(far_turned, "dp", 1)
-    packed_mirror = pack(sel, gate, mirror, tile, out_spare)
-    out_spare = swapped(out_spare, "expert", half)
-    arrived_mirror = to_half(packed_mirror)
     given_own, given_mirror = give(give_own, give_mirror, out_main, out_spare, tile)
-    returned_mirror = to_half(given_mirror)
-    grads_main, grads_spare = take(
-        take_own, take_mirror, arrived_own, arrived_mirror, main, tile, given_mirror
-    )
-    returned_own = to_half(given_own)
+    returned_mirror = to_half(touched(given_mirror, arrived_own))
+    packed_mirror = pack(sel, gate, mirror, tile, given_own)
+    arrived_mirror = to_half(touched(packed_mirror, returned_mirror))
+    part = swapped(combine(mix_mirror, returned_mirror, [], tile), "expert", half)
+    grads_main, grads_spare = take(take_own, take_mirror, arrived_own, arrived_mirror, main, tile)
+    returned_own = to_half(touched(given_own, arrived_mirror, part))
     other_main = swapped(grads_main, "dp", 1)
     grads_spare = swapped(grads_spare, "expert", half)
     other_spare = swapped(grads_spare, "dp", 1)
-    part = combine(mix_mirror, returned_mirror, [], tile)
-    back, back_spare = project_back(grads_main, grads_spare, near, far, tile, part)
+    layer_out = combine(mix_own, returned_own, [part], tile)
+    back, back_spare = project_back(grads_main, grads_spare, near, far, tile)
+    back_spare = swapped(back_spare, "expert", half)
     grad_weight = weight_grad(
         turned, other_turned, (grads_main, grads_spare), (other_main, other_spare), tile, back
     )
-    part = swapped(part, "expert", half)
-    back_spare = swapped(back_spare, "expert", half)
-    layer_out = combine(mix_own, returned_own, [part], tile, grad_weight)
-    grad_hidden = with_spare(back, back_spare, layer_out)
+    grad_hidden = with_spare(back, back_spare, layer_out, grad_weight)
     return (layer_out, grad_hidden[None, None], grad_weight[None])
 
 

time: 294 us -> 238 us (0.81)
  blocking collectives: 37.2 us -> 0 us
  Pallas kernels: 92 us -> 69.7 us
  starting transfers between devices: 34 us -> 45.5 us
  waiting for transfers between devices: 123 us -> 112 us
    all_to_all x1 -> x0, blocking collectives: 37.2 us -> none  [to_half(): lax.all_to_all(rows.reshape(half, cap, width), 'expert', 0, 0, axis_index...]
    ppermute x10, waiting for transfers between devices: 120 us -> 93.8 us  [swapped(): return lax.ppermute(value, axis, pairs)]
    pallas_call x13 -> x19, Pallas kernels: 92 us -> 69.7 us  [call(): pl.pallas_call(kernel, grid=(grid,), in_specs=[spec for _, spec in ins] +...]
    all_to_all x3 -> x4, waiting for transfers between devices: 0.01 us -> 15.1 us  [to_half(): lax.all_to_all(rows.reshape(half, cap, width), 'expert', 0, 0, axis_index...]
    all_to_all x3 -> x4, starting transfers between devices: 12.2 us -> 21.7 us  [to_half(): lax.all_to_all(rows.reshape(half, cap, width), 'expert', 0, 0, axis_index...]
    ppermute x10, starting transfers between devices: 13.5 us -> 18.9 us  [swapped(): return lax.ppermute(value, axis, pairs)]
    all_to_all x1, starting transfers between devices: 8.31 us -> 4.84 us  [local(): metas = lax.all_to_all(meta, 'expert', 0, 0, tiled=True)]
    unnamed x22 -> x24, local copies, waits for them, and re-layouts: 6.29 us -> 8.91 us
  transfers between devices with their start and end apart: 14 -> 15, of which waited for: 6 -> 7; matrix products, arithmetic and copies ran while one was open for 0% -> 0% of each run, Pallas kernels for 30% -> 29%
where the time goes in v3:
time: 238 us; the launch traced here: 236 us
  waiting for transfers between devices  112 us (47%)
  Pallas kernels  69.7 us (29%)
  starting transfers between devices  45.5 us (19%)
  local copies, waits for them, and re-layouts  8.91 us (4%)
    ppermute x10, waiting for transfers between devices, swapped(): return lax.ppermute(value, axis, pairs)  93.8 us
    pallas_call x19, Pallas kernels, call(): pl.pallas_call(kernel, grid=(grid,), in_specs=[spec for _, spec in ins] +...  69.7 us
    all_to_all x4, starting transfers between devices, to_half(): lax.all_to_all(rows.reshape(half, cap, width), 'expert', 0, 0, axis_index...  21.7 us
    ppermute x10, starting transfers between devices, swapped(): return lax.ppermute(value, axis, pairs)  18.9 us
    all_to_all x4, waiting for transfers between devices, to_half(): lax.all_to_all(rows.reshape(half, cap, width), 'expert', 0, 0, axis_index...  15.1 us
    unnamed x24, local copies, waits for them, and re-layouts  8.91 us
    all_to_all x1, starting transfers between devices, local(): metas = lax.all_to_all(meta, 'expert', 0, 0, tiled=True)  4.84 us
  transfers between devices with their start and end apart: 15, of which 7 were waited for; matrix products, arithmetic and copies ran while one was open for 0% of the time, Pallas kernels for 29%

profile of v3, /device:TPU:0, one launch (start us, length us, event | category | flops | bytes accessed | tf_op | source)
XLA Modules:
  0.0 236.5 jit_solution(5723945692816495237)
XLA Ops:
  0.6 0.5 collective-permute-start.1
  1.1 1.6 shard_map.85
  2.8 3.6 %collective-permute-start = (bf16[64,1024]{1,0:T(8,128)(2,1)}, bf16[64,1024]{1,0:T(8,128)(2,1)S(1)}, u32[]{:S(2)}, u32[]{:S(2)}) collective-permute-start(bf16[64,1024]{1,0:T(8,128)(2,1)} %get-tuple-element.27), channel_id=1, source_target_pairs={{0,8},{1,9},{2,10},{3,11},{4,12},{5,13},{6,14},{7,15},{8,0},{9,1},... | collective-permute-start | bytes 393224 | tf_op jit(solution)/shard_map/ppermute | solution.py:18
  6.4 4.8 %all-to-all-start = ((f32[16,8,128]{2,1,0:T(8,128)}), f32[16,8,128]{2,1,0:T(8,128)S(1)}, u32[]{:S(2)}, u32[]{:S(2)}) async-start(f32[16,8,128]{2,1,0:T(8,128)} %get-tuple-element.23.refs_0_), calls=%async_computation | async-start | bytes 131072 | tf_op jit(solution)/shard_map/all_to_all | solution.py:476
  11.2 4.8 %shard_map.86 = (bf16[320,3584]{1,0:T(8,128)(2,1)}, bf16[256,320]{1,0:T(8,128)(2,1)}) custom-call(f32[16,8,128]{2,1,0:T(8,128)} %get-tuple-element.23.refs_0_, bf16[128,3584]{1,0:T(8,128)(2,1)} %refs_0_.1), custom_call_target="tpu_custom_call" | custom-call | tf_op jit(solution)/shard_map/pallas_call | solution.py:58
  16.1 2.7 %all-to-all-done.refs_0_.refs_1_ = f32[16,8,128]{2,1,0:T(8,128)S(1)} async-done(((f32[16,8,128]{2,1,0:T(8,128)}), f32[16,8,128]{2,1,0:T(8,128)S(1)}, u32[]{:S(2)}, u32[]{:S(2)}) %all-to-all-start) | async-done | bytes 65568 | tf_op jit(solution)/shard_map/all_to_all | solution.py:476
  18.8 0.0 copy-start.7
  18.8 0.0 collective-permute-done.refs_0_.refs_1_.refs_2_
  18.8 0.0 copy-start.6
  18.8 0.0 collective-permute-done.1.refs_2_.refs_3_
  18.8 0.6 copy-done.7
  19.4 0.1 copy-done.6
  19.5 3.6 %all-to-all-start.1 = ((bf16[8,40,3584]{2,1,0:T(8,128)(2,1)}), bf16[8,40,3584]{2,1,0:T(8,128)(2,1)S(1)}, u32[]{:S(2)}, u32[]{:S(2)}) async-start(bf16[8,40,3584]{2,1,0:T(8,128)(2,1)} %bitcast.26), calls=%async_computation.1 | async-start | bytes 4587520 | tf_op jit(solution)/shard_map/all_to_all | solution.py:467
  23.1 5.3 %shard_map.88.refs_4_ = bf16[64,3584]{1,0:T(8,128)(2,1)} custom-call(bf16[64,1024]{1,0:T(8,128)(2,1)} %copy-done.6, bf16[512,3584]{1,0:T(8,128)(2,1)} %bitcast.16, bf16[512,3584]{1,0:T(8,128)(2,1)} %collective-permute-done.1.refs_2_.refs_3_, bf16[256,320]{1,0:T(8,128)(2,1)} %get-tuple-element.24.refs_3_.refs_0_), custom_call_target="tpu_custom_call" | custom-call | tf_op jit(solution)/shard_map/pallas_call | solution.py:58
  28.4 1.0 collective-permute-start.2
  29.4 2.0 shard_map.91.refs_0_
  31.4 2.9 %shard_map.87 = (bf16[320,128]{1,0:T(8,128)(2,1)}, f32[320,128]{1,0:T(8,128)}, bf16[256,320]{1,0:T(8,128)(2,1)}, bf16[320,448]{1,0:T(8,128)(2,1)}, bf16[448,320]...) custom-call(f32[16,8,128]{2,1,0:T(8,128)} %copy-done.7), custom_call_target="tpu_custom_call" | custom-call | tf_op jit(solution)/shard_map/pallas_call | solution.py:58
  34.2 7.8 %shard_map.89 = (bf16[384,3584]{1,0:T(8,128)(2,1)}, bf16[512,448]{1,0:T(8,128)(2,1)}, bf16[512,448]{1,0:T(8,128)(2,1)}) custom-call(bf16[448,1024]{1,0:T(8,128)(2,1)} %bitcast.31, bf16[64,1024]{1,0:T(8,128)(2,1)} %copy-done.6, bf16[512,3584]{1,0:T(8,128)(2,1)} %bitcast.17, bf16[512,3584]{1,0:T(8,128)(2,1)} %collective-permute-done.1.refs_2_.refs_3_, ...), custom_call_target="tpu_custom_call" | custom-call | tf_op jit(solution)/shard_map/pallas_call | solution.py:58
  42.1 15.1 %collective-permute-done.2.refs_3_.refs_1_ = bf16[64,3584]{1,0:T(8,128)(2,1)S(1)} collective-permute-done((bf16[64,3584]{1,0:T(8,128)(2,1)}, bf16[64,3584]{1,0:T(8,128)(2,1)S(1)}, u32[]{:S(2)}, u32[]{:S(2)}) %collective-permute-start.2) | collective-permute-done | bytes 458784 | tf_op jit(solution)/shard_map/ppermute | solution.py:18
  57.2 0.0 copy-start.4
  57.2 0.8 copy-done.4
  57.9 3.3 %collective-permute-start.3 = (bf16[128,3584]{1,0:T(8,128)(2,1)}, bf16[128,3584]{1,0:T(8,128)(2,1)S(1)}, u32[]{:S(2)}, u32[]{:S(2)}) collective-permute-start(bf16[128,3584]{1,0:T(8,128)(2,1)} %shard_map.92), channel_id=1, source_target_pairs={{0,8},{1,9},{2,10},{3,11},{4,12},{5,13},{6,14},{7,15},{8,0},{9,1},... | collective-permute-start | bytes 2752520 | tf_op jit(solution)/shard_map/ppermute | solution.py:18
  61.2 6.8 %shard_map.90 = (bf16[320,3584]{1,0:T(8,128)(2,1)}, bf16[320,3584]{1,0:T(8,128)(2,1)}) custom-call(bf16[320,448]{1,0:T(8,128)(2,1)} %get-tuple-element.25.refs_0_, bf16[320,448]{1,0:T(8,128)(2,1)} %get-tuple-element.26.refs_1_, bf16[384,3584]{1,0:T(8,128)(2,1)} %get-tuple-element.28.refs_2_, bf16[64,3584]{1,0:T(8,128)(2,1)} %copy-done.4), custom_call_target="tpu_custom_call" | custom-call | tf_op jit(solution)/shard_map/pallas_call | solution.py:58
  68.0 0.0 all-to-all-done.1
  68.0 0.0 copy-start
  68.0 1.4 copy-done
  69.4 6.2 %all-to-all-start.2 = ((bf16[8,40,3584]{2,1,0:T(8,128)(2,1)}), bf16[8,40,3584]{2,1,0:T(8,128)(2,1)}, u32[]{:S(2)}, u32[]{:S(2)}) async-start(bf16[8,40,3584]{2,1,0:T(8,128)(2,1)} %bitcast.27), calls=%async_computation.2 | async-start | bytes 4587520 | tf_op jit(solution)/shard_map/all_to_all | solution.py:467
  75.6 24.3 %collective-permute-done.3.refs_2_ = bf16[128,3584]{1,0:T(8,128)(2,1)S(1)} collective-permute-done((bf16[128,3584]{1,0:T(8,128)(2,1)}, bf16[128,3584]{1,0:T(8,128)(2,1)S(1)}, u32[]{:S(2)}, u32[]{:S(2)}) %collective-permute-start.3) | collective-permute-done | bytes 917536 | tf_op jit(solution)/shard_map/ppermute | solution.py:18
  99.9 0.0 copy-start.11
  99.9 0.9 copy-done.11
  100.8 4.3 %shard_map.93.refs_0_ = bf16[320,3584]{1,0:T(8,128)(2,1)} custom-call(bf16[320,128]{1,0:T(8,128)(2,1)} %get-tuple-element.30.refs_3_.refs_0_, f32[320,128]{1,0:T(8,128)} %get-tuple-element.31.refs_1_, bf16[128,3584]{1,0:T(8,128)(2,1)} %copy-done.11, bf16[320,3584]{1,0:T(8,128)(2,1)} %get-tuple-element.29.refs_3_.refs_0_), custom_call_target="tpu_custom_call" | custom-call | flops 3999999983616 | tf_op jit(solution)/shard_map/pallas_call | solution.py:58
  105.1 13.1 %all-to-all-done.2 = bf16[8,40,3584]{2,1,0:T(8,128)(2,1)} async-done(((bf16[8,40,3584]{2,1,0:T(8,128)(2,1)}), bf16[8,40,3584]{2,1,0:T(8,128)(2,1)}, u32[]{:S(2)}, u32[]{:S(2)}) %all-to-all-start.2) | async-done | bytes 2293792 | tf_op jit(solution)/shard_map/all_to_all | solution.py:467
  118.2 3.6 %all-to-all-start.3 = ((bf16[8,40,3584]{2,1,0:T(8,128)(2,1)}), bf16[8,40,3584]{2,1,0:T(8,128)(2,1)S(1)}, u32[]{:S(2)}, u32[]{:S(2)}) async-start(bf16[8,40,3584]{2,1,0:T(8,128)(2,1)} %bitcast.28), calls=%async_computation.3 | async-start | bytes 4587520 | tf_op jit(solution)/shard_map/all_to_all | solution.py:467
  121.8 4.4 %shard_map.97 = bf16[128,3584]{1,0:T(8,128)(2,1)} custom-call(bf16[256,320]{1,0:T(8,128)(2,1)} %get-tuple-element.34.refs_0_, bf16[320,3584]{1,0:T(8,128)(2,1)} %bitcast.8.refs_1_), custom_call_target="tpu_custom_call" | custom-call | tf_op jit(solution)/shard_map/pallas_call | solution.py:58
  126.2 5.3 %collective-permute-start.4 = (bf16[128,3584]{1,0:T(8,128)(2,1)}, bf16[128,3584]{1,0:T(8,128)(2,1)S(1)}, u32[]{:S(2)}, u32[]{:S(2)}) collective-permute-start(bf16[128,3584]{1,0:T(8,128)(2,1)} %shard_map.97), channel_id=1, source_target_pairs={{0,8},{1,9},{2,10},{3,11},{4,12},{5,13},{6,14},{7,15},{8,0},{9,1},... | collective-permute-start | bytes 2752520 | tf_op jit(solution)/shard_map/ppermute | solution.py:18
  131.5 32.6 %collective-permute-done.4.refs_2_ = bf16[128,3584]{1,0:T(8,128)(2,1)S(1)} collective-permute-done((bf16[128,3584]{1,0:T(8,128)(2,1)}, bf16[128,3584]{1,0:T(8,128)(2,1)S(1)}, u32[]{:S(2)}, u32[]{:S(2)}) %collective-permute-start.4) | collective-permute-done | bytes 917536 | tf_op jit(solution)/shard_map/ppermute | solution.py:18
  164.1 0.0 copy-start.3
  164.1 2.0 all-to-all-done.3
  166.2 0.0 copy-start.1
  166.2 0.0 copy-done.3
  166.2 1.4 copy-done.1
  167.5 8.3 %all-to-all-start.4 = ((bf16[8,40,3584]{2,1,0:T(8,128)(2,1)}), bf16[8,40,3584]{2,1,0:T(8,128)(2,1)S(1)}, u32[]{:S(2)}, u32[]{:S(2)}) async-start(bf16[8,40,3584]{2,1,0:T(8,128)(2,1)} %bitcast.25), calls=%async_computation.4 | async-start | bytes 4587520 | tf_op jit(solution)/shard_map/all_to_all | solution.py:467
  175.8 7.1 %shard_map.100 = (bf16[384,3584]{1,0:T(8,128)(2,1)}, bf16[64,3584]{1,0:T(8,128)(2,1)}) custom-call(bf16[448,320]{1,0:T(8,128)(2,1)} %get-tuple-element.35.refs_0_, bf16[448,320]{1,0:T(8,128)(2,1)} %get-tuple-element.36.refs_1_, bf16[320,3584]{1,0:T(8,128)(2,1)} %bitcast.20, bf16[320,3584]{1,0:T(8,128)(2,1)} %bitcast.22), custom_call_target="tpu_custom_call" | custom-call | tf_op jit(solution)/shard_map/pallas_call | solution.py:58
  182.9 0.0 collective-permute-start.8
  182.9 1.8 collective-permute-start.5
  184.7 0.2 collective-permute-start.7
  184.9 21.8 %collective-permute-done.5.refs_1_.refs_3_ = bf16[64,3584]{1,0:T(8,128)(2,1)S(1)} collective-permute-done((bf16[64,3584]{1,0:T(8,128)(2,1)}, bf16[64,3584]{1,0:T(8,128)(2,1)S(1)}, u32[]{:S(2)}, u32[]{:S(2)}) %collective-permute-start.5) | collective-permute-done | bytes 458784 | tf_op jit(solution)/shard_map/ppermute | solution.py:18
  206.7 0.0 collective-permute-start.9
  206.7 0.8 copy-done.5
  207.4 8.3 %shard_map.101 = (bf16[448,1024]{1,0:T(8,128)(2,1)}, bf16[64,1024]{1,0:T(8,128)(2,1)}) custom-call(bf16[384,3584]{1,0:T(8,128)(2,1)} %get-tuple-element.37.refs_0_.refs_2_, bf16[64,3584]{1,0:T(8,128)(2,1)} %copy-done.5, bf16[512,3584]{1,0:T(8,128)(2,1)} %bitcast.18, bf16[512,3584]{1,0:T(8,128)(2,1)} %collective-permute-done.1.refs_2_.refs_3_), custom_call_target="tpu_custom_call" | custom-call | tf_op jit(solution)/shard_map/pallas_call | solution.py:58
  215.7 3.3 %collective-permute-start.6 = (bf16[64,1024]{1,0:T(8,128)(2,1)}, bf16[64,1024]{1,0:T(8,128)(2,1)S(1)}, u32[]{:S(2)}, u32[]{:S(2)}) collective-permute-start(bf16[64,1024]{1,0:T(8,128)(2,1)} %get-tuple-element.40), channel_id=1, source_target_pairs={{0,8},{1,9},{2,10},{3,11},{4,12},{5,13},{6,14},{7,15},{8,0},{9,1},... | collective-permute-start | bytes 393224 | tf_op jit(solution)/shard_map/ppermute | solution.py:18
  219.0 0.0 collective-permute-done.7.refs_1_
  219.0 0.0 collective-permute-done.9.refs_5_
  219.0 0.0 copy-start.9
  219.0 0.0 collective-permute-done.8.refs_4_
  219.0 0.8 copy-done.8
  219.8 0.2 copy-done.9
  220.0 8.3 %shard_map.102.refs_3_ = bf16[512,3584]{1,0:T(8,128)(2,1)} custom-call(bf16[512,448]{1,0:T(8,128)(2,1)} %get-tuple-element.41.refs_0_, bf16[512,448]{1,0:T(8,128)(2,1)} %copy-done.8, bf16[384,3584]{1,0:T(8,128)(2,1)} %get-tuple-element.37.refs_0_.refs_2_, bf16[64,3584]{1,0:T(8,128)(2,1)} %copy-done.5, bf16[384,3584]{1,0:T(8,128)(2,1)} %collective-permute-done.8.refs_4_, ...), custom_call_target="tpu_custom_call" | custom-call | tf_op jit(solution)/shard_map/pallas_call | solution.py:58
  228.3 0.0 all-to-all-done.4
  228.3 1.4 copy-done.2
  229.7 4.5 %shard_map.99.refs_2_ = bf16[128,3584]{1,0:T(8,128)(2,1)} custom-call(bf16[256,320]{1,0:T(8,128)(2,1)} %get-tuple-element.24.refs_3_.refs_0_, bf16[320,3584]{1,0:T(8,128)(2,1)} %bitcast.24, bf16[128,3584]{1,0:T(8,128)(2,1)} %copy-done.3), custom_call_target="tpu_custom_call" | custom-call | tf_op jit(solution)/shard_map/pallas_call | solution.py:58
  234.3 0.0 collective-permute-done.6.refs_1_
  234.3 0.6 copy-done.10
  234.9 1.6 shard_map.103
  (9 shorter events, 0.0 us)
Async XLA Ops:
  0.6 18.2 %collective-permute-start.1 = (bf16[512,3584]{1,0:T(8,128)(2,1)}, bf16[512,3584]{1,0:T(8,128)(2,1)}, u32[]{:S(2)}, u32[]{:S(2)}) collective-permute-start(bf16[512,3584]{1,0:T(8,128)(2,1)} %bitcast.15), channel_id=1, source_target_pairs={{0,16},{16,0},{1,17},{17,1},{2,18},{18,2},{3,19},{19,3},{4,20},{20... | collective-permute-start | bytes 11010056 | tf_op jit(solution)/shard_map/ppermute | solution.py:18
  2.8 16.0 %collective-permute-start = (bf16[64,1024]{1,0:T(8,128)(2,1)}, bf16[64,1024]{1,0:T(8,128)(2,1)S(1)}, u32[]{:S(2)}, u32[]{:S(2)}) collective-permute-start(bf16[64,1024]{1,0:T(8,128)(2,1)} %get-tuple-element.27), channel_id=1, source_target_pairs={{0,8},{1,9},{2,10},{3,11},{4,12},{5,13},{6,14},{7,15},{8,0},{9,1},... | collective-permute-start | bytes 393224 | tf_op jit(solution)/shard_map/ppermute | solution.py:18
  6.4 12.4 %all-to-all-start = ((f32[16,8,128]{2,1,0:T(8,128)}), f32[16,8,128]{2,1,0:T(8,128)S(1)}, u32[]{:S(2)}, u32[]{:S(2)}) async-start(f32[16,8,128]{2,1,0:T(8,128)} %get-tuple-element.23.refs_0_), calls=%async_computation | async-start | bytes 131072 | tf_op jit(solution)/shard_map/all_to_all | solution.py:476
  18.8 0.6 copy-start.7
  18.8 0.7 copy-start.6
  19.5 48.6 %all-to-all-start.1 = ((bf16[8,40,3584]{2,1,0:T(8,128)(2,1)}), bf16[8,40,3584]{2,1,0:T(8,128)(2,1)S(1)}, u32[]{:S(2)}, u32[]{:S(2)}) async-start(bf16[8,40,3584]{2,1,0:T(8,128)(2,1)} %bitcast.26), calls=%async_computation.1 | async-start | bytes 4587520 | tf_op jit(solution)/shard_map/all_to_all | solution.py:467
  28.4 28.8 %collective-permute-start.2 = (bf16[64,3584]{1,0:T(8,128)(2,1)}, bf16[64,3584]{1,0:T(8,128)(2,1)S(1)}, u32[]{:S(2)}, u32[]{:S(2)}) collective-permute-start(bf16[64,3584]{1,0:T(8,128)(2,1)} %shard_map.88.refs_4_), channel_id=1, source_target_pairs={{0,8},{1,9},{2,10},{3,11},{4,12},{5,13},{6,14},{7,15},{8,0},{9,1},... | collective-permute-start | bytes 1376264 | tf_op jit(solution)/shard_map/ppermute | solution.py:18
  57.2 0.8 copy-start.4
  57.9 42.0 %collective-permute-start.3 = (bf16[128,3584]{1,0:T(8,128)(2,1)}, bf16[128,3584]{1,0:T(8,128)(2,1)S(1)}, u32[]{:S(2)}, u32[]{:S(2)}) collective-permute-start(bf16[128,3584]{1,0:T(8,128)(2,1)} %shard_map.92), channel_id=1, source_target_pairs={{0,8},{1,9},{2,10},{3,11},{4,12},{5,13},{6,14},{7,15},{8,0},{9,1},... | collective-permute-start | bytes 2752520 | tf_op jit(solution)/shard_map/ppermute | solution.py:18
  68.0 1.4 copy-start
  69.4 48.8 %all-to-all-start.2 = ((bf16[8,40,3584]{2,1,0:T(8,128)(2,1)}), bf16[8,40,3584]{2,1,0:T(8,128)(2,1)}, u32[]{:S(2)}, u32[]{:S(2)}) async-start(bf16[8,40,3584]{2,1,0:T(8,128)(2,1)} %bitcast.27), calls=%async_computation.2 | async-start | bytes 4587520 | tf_op jit(solution)/shard_map/all_to_all | solution.py:467
  99.9 0.9 copy-start.11
  118.2 48.0 %all-to-all-start.3 = ((bf16[8,40,3584]{2,1,0:T(8,128)(2,1)}), bf16[8,40,3584]{2,1,0:T(8,128)(2,1)S(1)}, u32[]{:S(2)}, u32[]{:S(2)}) async-start(bf16[8,40,3584]{2,1,0:T(8,128)(2,1)} %bitcast.28), calls=%async_computation.3 | async-start | bytes 4587520 | tf_op jit(solution)/shard_map/all_to_all | solution.py:467
  126.2 37.9 %collective-permute-start.4 = (bf16[128,3584]{1,0:T(8,128)(2,1)}, bf16[128,3584]{1,0:T(8,128)(2,1)S(1)}, u32[]{:S(2)}, u32[]{:S(2)}) collective-permute-start(bf16[128,3584]{1,0:T(8,128)(2,1)} %shard_map.97), channel_id=1, source_target_pairs={{0,8},{1,9},{2,10},{3,11},{4,12},{5,13},{6,14},{7,15},{8,0},{9,1},... | collective-permute-start | bytes 2752520 | tf_op jit(solution)/shard_map/ppermute | solution.py:18
  164.1 2.0 copy-start.3
  166.2 1.4 copy-start.1
  167.5 60.8 %all-to-all-start.4 = ((bf16[8,40,3584]{2,1,0:T(8,128)(2,1)}), bf16[8,40,3584]{2,1,0:T(8,128)(2,1)S(1)}, u32[]{:S(2)}, u32[]{:S(2)}) async-start(bf16[8,40,3584]{2,1,0:T(8,128)(2,1)} %bitcast.25), calls=%async_computation.4 | async-start | bytes 4587520 | tf_op jit(solution)/shard_map/all_to_all | solution.py:467
  182.9 36.1 %collective-permute-start.8 = (bf16[384,3584]{1,0:T(8,128)(2,1)}, bf16[384,3584]{1,0:T(8,128)(2,1)}, u32[]{:S(2)}, u32[]{:S(2)}) collective-permute-start(bf16[384,3584]{1,0:T(8,128)(2,1)} %get-tuple-element.37.refs_0_.refs_2_), channel_id=1, source_target_pairs={{0,16},{16,0},{1,17},{17,1},{2,18},{18,2},{3,19},{19,3},{4,20},{20... | collective-permute-start | bytes 8257544 | tf_op jit(solution)/shard_map/ppermute | solution.py:18
  182.9 23.7 %collective-permute-start.5 = (bf16[64,3584]{1,0:T(8,128)(2,1)}, bf16[64,3584]{1,0:T(8,128)(2,1)S(1)}, u32[]{:S(2)}, u32[]{:S(2)}) collective-permute-start(bf16[64,3584]{1,0:T(8,128)(2,1)} %get-tuple-element.38), channel_id=1, source_target_pairs={{0,8},{1,9},{2,10},{3,11},{4,12},{5,13},{6,14},{7,15},{8,0},{9,1},... | collective-permute-start | bytes 1376264 | tf_op jit(solution)/shard_map/ppermute | solution.py:18
  184.7 34.3 %collective-permute-start.7 = (bf16[512,448]{1,0:T(8,128)(2,1)}, bf16[512,448]{1,0:T(8,128)(2,1)S(1)}, u32[]{:S(2)}, u32[]{:S(2)}) collective-permute-start(bf16[512,448]{1,0:T(8,128)(2,1)} %get-tuple-element.42), channel_id=1, source_target_pairs={{0,16},{16,0},{1,17},{17,1},{2,18},{18,2},{3,19},{19,3},{4,20},{20... | collective-permute-start | bytes 1376264 | tf_op jit(solution)/shard_map/ppermute | solution.py:18
  206.7 0.8 copy-start.5
  206.7 12.3 %collective-permute-start.9 = (bf16[64,3584]{1,0:T(8,128)(2,1)S(1)}, bf16[64,3584]{1,0:T(8,128)(2,1)S(1)}, u32[]{:S(2)}, u32[]{:S(2)}) collective-permute-start(bf16[64,3584]{1,0:T(8,128)(2,1)S(1)} %collective-permute-done.5.refs_1_.refs_3_), channel_id=1, source_target_pairs={{0,16},{16,0},{1,17},{17,1},{2,18},{18,2},{3,19},{19,3},{4,20},{20... | collective-permute-start | bytes 1376264 | tf_op jit(solution)/shard_map/ppermute | solution.py:18
  215.7 18.6 %collective-permute-start.6 = (bf16[64,1024]{1,0:T(8,128)(2,1)}, bf16[64,1024]{1,0:T(8,128)(2,1)S(1)}, u32[]{:S(2)}, u32[]{:S(2)}) collective-permute-start(bf16[64,1024]{1,0:T(8,128)(2,1)} %get-tuple-element.40), channel_id=1, source_target_pairs={{0,8},{1,9},{2,10},{3,11},{4,12},{5,13},{6,14},{7,15},{8,0},{9,1},... | collective-permute-start | bytes 393224 | tf_op jit(solution)/shard_map/ppermute | solution.py:18
  219.0 0.8 copy-start.8
  219.0 1.0 copy-start.9
  228.3 1.4 copy-start.2
  234.3 0.6 copy-start.10

commit v4 on v3

--- a/solution.py
+++ b/solution.py
@@ -9,6 +9,8 @@
 F32, BF16, I32 = jnp.float32, jnp.bfloat16, jnp.int32
 LANES = 128
 LONG = 4_000_000_000_000
+GIVE_COST = 5_000_000_000
+BACK_COST = 40_000_000_000
 VMEM_LIMIT = 60 * 1024 * 1024
 
 
@@ -327,24 +329,22 @@
         width // tile,
         entire(own_slot, mirror_slot) + by_columns(tile, out_main, out_spare),
         by_columns(tile, bf16(rows, width), bf16(rows, width)),
-    )
-
-
-def take_kernel(own_slot, mirror_slot, own_ref, mirror_ref, main_ref, spare_ref):
-    total = dot(own_slot[...], own_ref[...]) + dot(mirror_slot[...], mirror_ref[...])
-    total = total.astype(BF16)
-    main = main_ref.shape[0]
-    main_ref[...] = total[:main]
-    spare_ref[...] = total[main:]
-
-
-def take(own_slot, mirror_slot, own, mirror, main, tile, *after):
-    slots, width = own_slot.shape[0], own.shape[1]
-    return call(
-        take_kernel,
-        width // tile,
+        cost=GIVE_COST,
+    )
+
+
+def take_kernel(first, own_slot, mirror_slot, own_ref, mirror_ref, out_ref):
+    rows = pl.ds(first, out_ref.shape[0])
+    total = dot(own_slot[rows, :], own_ref[...]) + dot(mirror_slot[rows, :], mirror_ref[...])
+    out_ref[...] = total.astype(BF16)
+
+
+def take(own_slot, mirror_slot, own, mirror, first, count, tile, *after):
+    return call(
+        functools.partial(take_kernel, first),
+        own.shape[1] // tile,
         entire(own_slot, mirror_slot) + by_columns(tile, own, mirror),
-        by_columns(tile, bf16(main, width), bf16(slots - main, width)),
+        by_columns(tile, bf16(count, own.shape[1]))[0],
         after=after,
     )
 
@@ -435,6 +435,7 @@
         entire(bf16(slots, 2 * half), bf16(spare, 2 * half)),
         [pltpu.VMEM((slots, 2 * half), F32), pltpu.VMEM((slots, tile), BF16)],
         after,
+        cost=BACK_COST,
     )
 
 
@@ -482,15 +483,17 @@
     )
     out_main, turned, far_turned = project(hidden, spare_hidden, near, far, tile, out_spare)
     out_spare = swapped(out_spare, "expert", half)
-    mirror = swapped(touched(copied(grad_out, width // 2), out_spare, out_main, sel), "expert", half)
+    mirror = swapped(touched(copied(grad_out, width // 2), out_main, sel), "expert", half)
     other_turned = swapped(far_turned, "dp", 1)
     given_own, given_mirror = give(give_own, give_mirror, out_main, out_spare, tile)
     returned_mirror = to_half(touched(given_mirror, arrived_own))
     packed_mirror = pack(sel, gate, mirror, tile, given_own)
     arrived_mirror = to_half(touched(packed_mirror, returned_mirror))
     part = swapped(combine(mix_mirror, returned_mirror, [], tile), "expert", half)
-    grads_main, grads_spare = take(take_own, take_mirror, arrived_own, arrived_mirror, main, tile)
-    returned_own = to_half(touched(given_own, arrived_mirror, part))
+    arrived = (take_own, take_mirror, arrived_own, arrived_mirror)
+    grads_spare = take(*arrived, main, slots - main, tile)
+    returned_own = to_half(touched(given_own, part, grads_spare))
+    grads_main = take(*arrived, 0, main, tile, grads_spare)
     other_main = swapped(grads_main, "dp", 1)
     grads_spare = swapped(grads_spare, "expert", half)
     other_spare = swapped(grads_spare, "dp", 1)

time: 238 us -> 218 us (0.916)
  waiting for transfers between devices: 112 us -> 98.7 us
  starting transfers between devices: 45.5 us -> 33.9 us
  Pallas kernels: 69.7 us -> 74.2 us
    ppermute x10, waiting for transfers between devices: 93.8 us -> 37.3 us  [swapped(): return lax.ppermute(value, axis, pairs)]
    all_to_all x4, waiting for transfers between devices: 15.1 us -> 58.7 us  [to_half(): lax.all_to_all(rows.reshape(half, cap, width), 'expert', 0, 0, axis_index...]
    ppermute x10, starting transfers between devices: 18.9 us -> 7.6 us  [swapped(): return lax.ppermute(value, axis, pairs)]
    pallas_call x19 -> x20, Pallas kernels: 69.7 us -> 74.2 us  [call(): pl.pallas_call(kernel, grid=(grid,), in_specs=[spec for _, spec in ins] +...]
  transfers between devices with their start and end apart: 15 -> 15, of which waited for: 7 -> 7; matrix products, arithmetic and copies ran while one was open for 0% -> 0% of each run, Pallas kernels for 29% -> 34%
where the time goes in v4:
time: 218 us; the launch traced here: 217 us
  waiting for transfers between devices  98.7 us (45%)
  Pallas kernels  74.2 us (34%)
  starting transfers between devices  33.9 us (16%)
  local copies, waits for them, and re-layouts  9.11 us (4%)
    pallas_call x20, Pallas kernels, call(): pl.pallas_call(kernel, grid=(grid,), in_specs=[spec for _, spec in ins] +...  74.2 us
    all_to_all x4, waiting for transfers between devices, to_half(): lax.all_to_all(rows.reshape(half, cap, width), 'expert', 0, 0, axis_index...  58.7 us
    ppermute x10, waiting for transfers between devices, swapped(): return lax.ppermute(value, axis, pairs)  37.3 us
    all_to_all x4, starting transfers between devices, to_half(): lax.all_to_all(rows.reshape(half, cap, width), 'expert', 0, 0, axis_index...  21.4 us
    unnamed x24, local copies, waits for them, and re-layouts  9.11 us
    ppermute x10, starting transfers between devices, swapped(): return lax.ppermute(value, axis, pairs)  7.6 us
    all_to_all x1, starting transfers between devices, local(): metas = lax.all_to_all(meta, 'expert', 0, 0, tiled=True)  4.84 us
  transfers between devices with their start and end apart: 15, of which 7 were waited for; matrix products, arithmetic and copies ran while one was open for 0% of the time, Pallas kernels for 34%

profile of v4, /device:TPU:0, one launch (start us, length us, event | category | flops | bytes accessed | tf_op | source)
XLA Modules:
  0.0 216.6 jit_solution(7234312064852356602)
XLA Ops:
  0.6 0.5 collective-permute-start.1
  1.1 1.6 shard_map.85
  2.8 3.6 %collective-permute-start = (bf16[64,1024]{1,0:T(8,128)(2,1)}, bf16[64,1024]{1,0:T(8,128)(2,1)S(1)}, u32[]{:S(2)}, u32[]{:S(2)}) collective-permute-start(bf16[64,1024]{1,0:T(8,128)(2,1)} %get-tuple-element.25), channel_id=1, source_target_pairs={{0,8},{1,9},{2,10},{3,11},{4,12},{5,13},{6,14},{7,15},{8,0},{9,1},... | collective-permute-start | bytes 393224 | tf_op jit(solution)/shard_map/ppermute | solution.py:20
  6.4 4.8 %all-to-all-start = ((f32[16,8,128]{2,1,0:T(8,128)}), f32[16,8,128]{2,1,0:T(8,128)S(1)}, u32[]{:S(2)}, u32[]{:S(2)}) async-start(f32[16,8,128]{2,1,0:T(8,128)} %get-tuple-element.21.refs_0_), calls=%async_computation | async-start | bytes 131072 | tf_op jit(solution)/shard_map/all_to_all | solution.py:477
  11.2 4.8 %shard_map.86 = (bf16[320,3584]{1,0:T(8,128)(2,1)}, bf16[256,320]{1,0:T(8,128)(2,1)}) custom-call(f32[16,8,128]{2,1,0:T(8,128)} %get-tuple-element.21.refs_0_, bf16[128,3584]{1,0:T(8,128)(2,1)} %refs_0_.1), custom_call_target="tpu_custom_call" | custom-call | tf_op jit(solution)/shard_map/pallas_call | solution.py:60
  16.0 2.7 %all-to-all-done.refs_0_.refs_1_ = f32[16,8,128]{2,1,0:T(8,128)S(1)} async-done(((f32[16,8,128]{2,1,0:T(8,128)}), f32[16,8,128]{2,1,0:T(8,128)S(1)}, u32[]{:S(2)}, u32[]{:S(2)}) %all-to-all-start) | async-done | bytes 65568 | tf_op jit(solution)/shard_map/all_to_all | solution.py:477
  18.8 0.0 copy-start.5
  18.8 0.0 collective-permute-done.refs_0_.refs_1_.refs_2_
  18.8 0.0 copy-start.4
  18.8 0.0 collective-permute-done.1.refs_2_.refs_3_
  18.8 0.6 copy-done.5
  19.4 0.0 copy-done.4
  19.4 3.6 %all-to-all-start.1 = ((bf16[8,40,3584]{2,1,0:T(8,128)(2,1)}), bf16[8,40,3584]{2,1,0:T(8,128)(2,1)S(1)}, u32[]{:S(2)}, u32[]{:S(2)}) async-start(bf16[8,40,3584]{2,1,0:T(8,128)(2,1)} %bitcast.27), calls=%async_computation.1 | async-start | bytes 4587520 | tf_op jit(solution)/shard_map/all_to_all | solution.py:468
  23.1 5.3 %shard_map.88.refs_4_ = bf16[64,3584]{1,0:T(8,128)(2,1)} custom-call(bf16[64,1024]{1,0:T(8,128)(2,1)} %copy-done.4, bf16[512,3584]{1,0:T(8,128)(2,1)} %bitcast.22, bf16[512,3584]{1,0:T(8,128)(2,1)} %collective-permute-done.1.refs_2_.refs_3_, bf16[256,320]{1,0:T(8,128)(2,1)} %get-tuple-element.22.refs_3_.refs_0_), custom_call_target="tpu_custom_call" | custom-call | tf_op jit(solution)/shard_map/pallas_call | solution.py:60
  28.3 1.0 collective-permute-start.2
  29.3 2.0 shard_map.94.refs_0_
  31.3 2.9 %shard_map.87 = (bf16[320,128]{1,0:T(8,128)(2,1)}, f32[320,128]{1,0:T(8,128)}, bf16[256,320]{1,0:T(8,128)(2,1)}, bf16[320,448]{1,0:T(8,128)(2,1)}, bf16[448,320]...) custom-call(f32[16,8,128]{2,1,0:T(8,128)} %copy-done.5), custom_call_target="tpu_custom_call" | custom-call | tf_op jit(solution)/shard_map/pallas_call | solution.py:60
  34.2 7.8 %shard_map.89 = (bf16[384,3584]{1,0:T(8,128)(2,1)}, bf16[512,448]{1,0:T(8,128)(2,1)}, bf16[512,448]{1,0:T(8,128)(2,1)}) custom-call(bf16[448,1024]{1,0:T(8,128)(2,1)} %bitcast.32, bf16[64,1024]{1,0:T(8,128)(2,1)} %copy-done.4, bf16[512,3584]{1,0:T(8,128)(2,1)} %bitcast.23, bf16[512,3584]{1,0:T(8,128)(2,1)} %collective-permute-done.1.refs_2_.refs_3_, ...), custom_call_target="tpu_custom_call" | custom-call | tf_op jit(solution)/shard_map/pallas_call | solution.py:60
  42.0 1.9 collective-permute-start.4
  44.0 15.1 %collective-permute-done.2.refs_3_ = bf16[64,3584]{1,0:T(8,128)(2,1)S(1)} collective-permute-done((bf16[64,3584]{1,0:T(8,128)(2,1)}, bf16[64,3584]{1,0:T(8,128)(2,1)S(1)}, u32[]{:S(2)}, u32[]{:S(2)}) %collective-permute-start.2) | collective-permute-done | bytes 458784 | tf_op jit(solution)/shard_map/ppermute | solution.py:20
  59.0 0.0 copy-start.11
  59.0 0.8 copy-done.11
  59.9 6.8 %shard_map.90 = (bf16[320,3584]{1,0:T(8,128)(2,1)}, bf16[320,3584]{1,0:T(8,128)(2,1)}) custom-call(bf16[320,448]{1,0:T(8,128)(2,1)} %get-tuple-element.23.refs_0_, bf16[320,448]{1,0:T(8,128)(2,1)} %get-tuple-element.24.refs_1_, bf16[384,3584]{1,0:T(8,128)(2,1)} %get-tuple-element.26.refs_2_.refs_1_, bf16[64,3584]{1,0:T(8,128)(2,1)} %copy-done.11), custom_call_target="tpu_custom_call" | custom-call | flops 5000000000 | tf_op jit(solution)/shard_map/pallas_call | solution.py:60
  66.7 0.0 all-to-all-done.1
  66.7 0.0 copy-start
  66.7 1.4 copy-done
  68.1 9.1 %all-to-all-start.2 = ((bf16[8,40,3584]{2,1,0:T(8,128)(2,1)}), bf16[8,40,3584]{2,1,0:T(8,128)(2,1)}, u32[]{:S(2)}, u32[]{:S(2)}) async-start(bf16[8,40,3584]{2,1,0:T(8,128)(2,1)} %bitcast.28), calls=%async_computation.2 | async-start | bytes 4587520 | tf_op jit(solution)/shard_map/all_to_all | solution.py:468
  77.2 16.9 %collective-permute-done.4.refs_2_ = bf16[128,3584]{1,0:T(8,128)(2,1)S(1)} collective-permute-done((bf16[128,3584]{1,0:T(8,128)(2,1)}, bf16[128,3584]{1,0:T(8,128)(2,1)S(1)}, u32[]{:S(2)}, u32[]{:S(2)}) %collective-permute-start.4) | collective-permute-done | bytes 917536 | tf_op jit(solution)/shard_map/ppermute | solution.py:20
  94.1 0.9 copy-done.9
  95.0 4.4 %shard_map.96.refs_0_ = bf16[320,3584]{1,0:T(8,128)(2,1)} custom-call(bf16[320,128]{1,0:T(8,128)(2,1)} %get-tuple-element.33.refs_2_.refs_0_, f32[320,128]{1,0:T(8,128)} %get-tuple-element.34.refs_1_, bf16[128,3584]{1,0:T(8,128)(2,1)} %copy-done.9, bf16[320,3584]{1,0:T(8,128)(2,1)} %get-tuple-element.27.refs_3_.refs_0_), custom_call_target="tpu_custom_call" | custom-call | flops 3999999983616 | tf_op jit(solution)/shard_map/pallas_call | solution.py:60
  99.5 16.0 %all-to-all-done.2 = bf16[8,40,3584]{2,1,0:T(8,128)(2,1)} async-done(((bf16[8,40,3584]{2,1,0:T(8,128)(2,1)}), bf16[8,40,3584]{2,1,0:T(8,128)(2,1)}, u32[]{:S(2)}, u32[]{:S(2)}) %all-to-all-start.2) | async-done | bytes 2293792 | tf_op jit(solution)/shard_map/all_to_all | solution.py:468
  115.4 3.6 %all-to-all-start.3 = ((bf16[8,40,3584]{2,1,0:T(8,128)(2,1)}), bf16[8,40,3584]{2,1,0:T(8,128)(2,1)S(1)}, u32[]{:S(2)}, u32[]{:S(2)}) async-start(bf16[8,40,3584]{2,1,0:T(8,128)(2,1)} %bitcast.29), calls=%async_computation.3 | async-start | bytes 4587520 | tf_op jit(solution)/shard_map/all_to_all | solution.py:468
  119.1 4.4 %shard_map.93 = bf16[128,3584]{1,0:T(8,128)(2,1)} custom-call(bf16[256,320]{1,0:T(8,128)(2,1)} %get-tuple-element.28.refs_0_, bf16[320,3584]{1,0:T(8,128)(2,1)} %bitcast.8.refs_1_), custom_call_target="tpu_custom_call" | custom-call | tf_op jit(solution)/shard_map/pallas_call | solution.py:60
  123.5 0.0 collective-permute-start.3
  123.5 37.9 %all-to-all-done.3 = bf16[8,40,3584]{2,1,0:T(8,128)(2,1)S(1)} async-done(((bf16[8,40,3584]{2,1,0:T(8,128)(2,1)}), bf16[8,40,3584]{2,1,0:T(8,128)(2,1)S(1)}, u32[]{:S(2)}, u32[]{:S(2)}) %all-to-all-start.3) | async-done | bytes 2293792 | tf_op jit(solution)/shard_map/all_to_all | solution.py:468
  161.4 1.4 copy-done.1
  162.8 4.7 %shard_map.98.refs_2_.refs_4_ = bf16[64,3584]{1,0:T(8,128)(2,1)} custom-call(bf16[448,320]{1,0:T(8,128)(2,1)} %get-tuple-element.31.refs_0_, bf16[448,320]{1,0:T(8,128)(2,1)} %get-tuple-element.32.refs_1_, bf16[320,3584]{1,0:T(8,128)(2,1)} %bitcast.16, bf16[320,3584]{1,0:T(8,128)(2,1)} %bitcast.18), custom_call_target="tpu_custom_call" | custom-call | tf_op jit(solution)/shard_map/pallas_call | solution.py:60
  167.5 0.0 collective-permute-start.5
  167.5 0.0 collective-permute-done.3.refs_1_.refs_2_
  167.5 0.0 copy-start.3
  167.6 0.9 copy-done.3
  168.5 5.0 %all-to-all-start.4 = ((bf16[8,40,3584]{2,1,0:T(8,128)(2,1)}), bf16[8,40,3584]{2,1,0:T(8,128)(2,1)S(1)}, u32[]{:S(2)}, u32[]{:S(2)}) async-start(bf16[8,40,3584]{2,1,0:T(8,128)(2,1)} %bitcast.25), calls=%async_computation.4 | async-start | bytes 4587520 | tf_op jit(solution)/shard_map/all_to_all | solution.py:468
  173.5 0.0 copy-done.10
  173.5 0.1 collective-permute-start.7
  173.6 6.7 %shard_map.101.refs_0_.refs_2_ = bf16[384,3584]{1,0:T(8,128)(2,1)} custom-call(bf16[448,320]{1,0:T(8,128)(2,1)} %get-tuple-element.31.refs_0_, bf16[448,320]{1,0:T(8,128)(2,1)} %get-tuple-element.32.refs_1_, bf16[320,3584]{1,0:T(8,128)(2,1)} %bitcast.17, bf16[320,3584]{1,0:T(8,128)(2,1)} %bitcast.19, bf16[64,3584]{1,0:T(8,128)(2,1)} %shard_map.98.refs_2_.refs_4_), custom_call_target="tpu_custom_call" | custom-call | tf_op jit(solution)/shard_map/pallas_call | solution.py:60
  180.3 0.5 collective-permute-start.8
  180.8 5.3 %collective-permute-done.5.refs_1_.refs_3_ = bf16[64,3584]{1,0:T(8,128)(2,1)} collective-permute-done((bf16[64,3584]{1,0:T(8,128)(2,1)}, bf16[64,3584]{1,0:T(8,128)(2,1)}, u32[]{:S(2)}, u32[]{:S(2)}) %collective-permute-start.5) | collective-permute-done | bytes 458784 | tf_op jit(solution)/shard_map/ppermute | solution.py:20
  186.1 0.0 collective-permute-start.9
  186.1 8.3 %shard_map.102 = (bf16[448,1024]{1,0:T(8,128)(2,1)}, bf16[64,1024]{1,0:T(8,128)(2,1)}) custom-call(bf16[384,3584]{1,0:T(8,128)(2,1)} %shard_map.101.refs_0_.refs_2_, bf16[64,3584]{1,0:T(8,128)(2,1)} %collective-permute-done.5.refs_1_.refs_3_, bf16[512,3584]{1,0:T(8,128)(2,1)} %bitcast.24, bf16[512,3584]{1,0:T(8,128)(2,1)} %collective-permute-done.1.refs_2_.refs_3_), custom_call_target="tpu_custom_call" | custom-call | flops 40000000000 | tf_op jit(solution)/shard_map/pallas_call | solution.py:60
  194.4 0.0 collective-permute-start.6
  194.4 0.0 collective-permute-done.7.refs_1_
  194.4 0.0 copy-start.6
  194.4 0.0 collective-permute-done.9.refs_5_
  194.4 0.0 copy-start.7
  194.4 0.0 collective-permute-done.8.refs_4_
  194.4 0.8 copy-done.6
  195.2 0.2 copy-done.7
  195.3 8.3 %shard_map.103.refs_3_ = bf16[512,3584]{1,0:T(8,128)(2,1)} custom-call(bf16[512,448]{1,0:T(8,128)(2,1)} %get-tuple-element.37.refs_0_, bf16[512,448]{1,0:T(8,128)(2,1)} %copy-done.6, bf16[384,3584]{1,0:T(8,128)(2,1)} %shard_map.101.refs_0_.refs_2_, bf16[64,3584]{1,0:T(8,128)(2,1)} %collective-permute-done.5.refs_1_.refs_3_, ...), custom_call_target="tpu_custom_call" | custom-call | tf_op jit(solution)/shard_map/pallas_call | solution.py:60
  203.7 4.8 %all-to-all-done.4 = bf16[8,40,3584]{2,1,0:T(8,128)(2,1)S(1)} async-done(((bf16[8,40,3584]{2,1,0:T(8,128)(2,1)}), bf16[8,40,3584]{2,1,0:T(8,128)(2,1)S(1)}, u32[]{:S(2)}, u32[]{:S(2)}) %all-to-all-start.4) | async-done | bytes 2293792 | tf_op jit(solution)/shard_map/all_to_all | solution.py:468
  208.5 1.4 copy-done.2
  209.9 4.5 %shard_map.100.refs_2_ = bf16[128,3584]{1,0:T(8,128)(2,1)} custom-call(bf16[256,320]{1,0:T(8,128)(2,1)} %get-tuple-element.22.refs_3_.refs_0_, bf16[320,3584]{1,0:T(8,128)(2,1)} %bitcast.26, bf16[128,3584]{1,0:T(8,128)(2,1)} %copy-done.3), custom_call_target="tpu_custom_call" | custom-call | tf_op jit(solution)/shard_map/pallas_call | solution.py:60
  214.4 0.0 collective-permute-done.6.refs_1_
  214.4 0.6 copy-done.8
  215.1 1.6 shard_map.104
  (10 shorter events, 0.0 us)
Async XLA Ops:
  0.6 18.2 %collective-permute-start.1 = (bf16[512,3584]{1,0:T(8,128)(2,1)}, bf16[512,3584]{1,0:T(8,128)(2,1)}, u32[]{:S(2)}, u32[]{:S(2)}) collective-permute-start(bf16[512,3584]{1,0:T(8,128)(2,1)} %bitcast.21), channel_id=1, source_target_pairs={{0,16},{16,0},{1,17},{17,1},{2,18},{18,2},{3,19},{19,3},{4,20},{20... | collective-permute-start | bytes 11010056 | tf_op jit(solution)/shard_map/ppermute | solution.py:20
  2.8 16.0 %collective-permute-start = (bf16[64,1024]{1,0:T(8,128)(2,1)}, bf16[64,1024]{1,0:T(8,128)(2,1)S(1)}, u32[]{:S(2)}, u32[]{:S(2)}) collective-permute-start(bf16[64,1024]{1,0:T(8,128)(2,1)} %get-tuple-element.25), channel_id=1, source_target_pairs={{0,8},{1,9},{2,10},{3,11},{4,12},{5,13},{6,14},{7,15},{8,0},{9,1},... | collective-permute-start | bytes 393224 | tf_op jit(solution)/shard_map/ppermute | solution.py:20
  6.4 12.4 %all-to-all-start = ((f32[16,8,128]{2,1,0:T(8,128)}), f32[16,8,128]{2,1,0:T(8,128)S(1)}, u32[]{:S(2)}, u32[]{:S(2)}) async-start(f32[16,8,128]{2,1,0:T(8,128)} %get-tuple-element.21.refs_0_), calls=%async_computation | async-start | bytes 131072 | tf_op jit(solution)/shard_map/all_to_all | solution.py:477
  18.8 0.6 copy-start.5
  18.8 0.7 copy-start.4
  19.4 47.3 %all-to-all-start.1 = ((bf16[8,40,3584]{2,1,0:T(8,128)(2,1)}), bf16[8,40,3584]{2,1,0:T(8,128)(2,1)S(1)}, u32[]{:S(2)}, u32[]{:S(2)}) async-start(bf16[8,40,3584]{2,1,0:T(8,128)(2,1)} %bitcast.27), calls=%async_computation.1 | async-start | bytes 4587520 | tf_op jit(solution)/shard_map/all_to_all | solution.py:468
  28.3 30.7 %collective-permute-start.2 = (bf16[64,3584]{1,0:T(8,128)(2,1)}, bf16[64,3584]{1,0:T(8,128)(2,1)S(1)}, u32[]{:S(2)}, u32[]{:S(2)}) collective-permute-start(bf16[64,3584]{1,0:T(8,128)(2,1)} %shard_map.88.refs_4_), channel_id=1, source_target_pairs={{0,8},{1,9},{2,10},{3,11},{4,12},{5,13},{6,14},{7,15},{8,0},{9,1},... | collective-permute-start | bytes 1376264 | tf_op jit(solution)/shard_map/ppermute | solution.py:20
  42.0 52.1 %collective-permute-start.4 = (bf16[128,3584]{1,0:T(8,128)(2,1)}, bf16[128,3584]{1,0:T(8,128)(2,1)S(1)}, u32[]{:S(2)}, u32[]{:S(2)}) collective-permute-start(bf16[128,3584]{1,0:T(8,128)(2,1)} %shard_map.95), channel_id=1, source_target_pairs={{0,8},{1,9},{2,10},{3,11},{4,12},{5,13},{6,14},{7,15},{8,0},{9,1},... | collective-permute-start | bytes 2752520 | tf_op jit(solution)/shard_map/ppermute | solution.py:20
  59.0 0.8 copy-start.11
  66.7 1.4 copy-start
  68.1 47.3 %all-to-all-start.2 = ((bf16[8,40,3584]{2,1,0:T(8,128)(2,1)}), bf16[8,40,3584]{2,1,0:T(8,128)(2,1)}, u32[]{:S(2)}, u32[]{:S(2)}) async-start(bf16[8,40,3584]{2,1,0:T(8,128)(2,1)} %bitcast.28), calls=%async_computation.2 | async-start | bytes 4587520 | tf_op jit(solution)/shard_map/all_to_all | solution.py:468
  94.1 0.9 copy-start.9
  115.4 45.9 %all-to-all-start.3 = ((bf16[8,40,3584]{2,1,0:T(8,128)(2,1)}), bf16[8,40,3584]{2,1,0:T(8,128)(2,1)S(1)}, u32[]{:S(2)}, u32[]{:S(2)}) async-start(bf16[8,40,3584]{2,1,0:T(8,128)(2,1)} %bitcast.29), calls=%async_computation.3 | async-start | bytes 4587520 | tf_op jit(solution)/shard_map/all_to_all | solution.py:468
  123.5 44.1 %collective-permute-start.3 = (bf16[128,3584]{1,0:T(8,128)(2,1)}, bf16[128,3584]{1,0:T(8,128)(2,1)S(1)}, u32[]{:S(2)}, u32[]{:S(2)}) collective-permute-start(bf16[128,3584]{1,0:T(8,128)(2,1)} %shard_map.93), channel_id=1, source_target_pairs={{0,8},{1,9},{2,10},{3,11},{4,12},{5,13},{6,14},{7,15},{8,0},{9,1},... | collective-permute-start | bytes 2752520 | tf_op jit(solution)/shard_map/ppermute | solution.py:20
  161.4 1.4 copy-start.1
  167.5 18.6 %collective-permute-start.5 = (bf16[64,3584]{1,0:T(8,128)(2,1)}, bf16[64,3584]{1,0:T(8,128)(2,1)}, u32[]{:S(2)}, u32[]{:S(2)}) collective-permute-start(bf16[64,3584]{1,0:T(8,128)(2,1)} %shard_map.98.refs_2_.refs_4_), channel_id=1, source_target_pairs={{0,8},{1,9},{2,10},{3,11},{4,12},{5,13},{6,14},{7,15},{8,0},{9,1},... | collective-permute-start | bytes 1376264 | tf_op jit(solution)/shard_map/ppermute | solution.py:20
  167.5 0.9 copy-start.3
  168.5 5.1 %copy-start.10 = (bf16[512,448]{1,0:T(8,128)(2,1)S(1)}, bf16[512,448]{1,0:T(8,128)(2,1)}, u32[]{:S(2)}) copy-start(bf16[512,448]{1,0:T(8,128)(2,1)} %get-tuple-element.38) | copy-start | bytes 1376260
  168.5 40.0 %all-to-all-start.4 = ((bf16[8,40,3584]{2,1,0:T(8,128)(2,1)}), bf16[8,40,3584]{2,1,0:T(8,128)(2,1)S(1)}, u32[]{:S(2)}, u32[]{:S(2)}) async-start(bf16[8,40,3584]{2,1,0:T(8,128)(2,1)} %bitcast.25), calls=%async_computation.4 | async-start | bytes 4587520 | tf_op jit(solution)/shard_map/all_to_all | solution.py:468
  173.5 20.8 %collective-permute-start.7 = (bf16[512,448]{1,0:T(8,128)(2,1)S(1)}, bf16[512,448]{1,0:T(8,128)(2,1)S(1)}, u32[]{:S(2)}, u32[]{:S(2)}) collective-permute-start(bf16[512,448]{1,0:T(8,128)(2,1)S(1)} %copy-done.10), channel_id=1, source_target_pairs={{0,16},{16,0},{1,17},{17,1},{2,18},{18,2},{3,19},{19,3},{4,20},{20... | collective-permute-start | bytes 1376264 | tf_op jit(solution)/shard_map/ppermute | solution.py:20
  180.3 14.1 %collective-permute-start.8 = (bf16[384,3584]{1,0:T(8,128)(2,1)}, bf16[384,3584]{1,0:T(8,128)(2,1)}, u32[]{:S(2)}, u32[]{:S(2)}) collective-permute-start(bf16[384,3584]{1,0:T(8,128)(2,1)} %shard_map.101.refs_0_.refs_2_), channel_id=1, source_target_pairs={{0,16},{16,0},{1,17},{17,1},{2,18},{18,2},{3,19},{19,3},{4,20},{20... | collective-permute-start | bytes 8257544 | tf_op jit(solution)/shard_map/ppermute | solution.py:20
  186.1 8.3 %collective-permute-start.9 = (bf16[64,3584]{1,0:T(8,128)(2,1)}, bf16[64,3584]{1,0:T(8,128)(2,1)S(1)}, u32[]{:S(2)}, u32[]{:S(2)}) collective-permute-start(bf16[64,3584]{1,0:T(8,128)(2,1)} %collective-permute-done.5.refs_1_.refs_3_), channel_id=1, source_target_pairs={{0,16},{16,0},{1,17},{17,1},{2,18},{18,2},{3,19},{19,3},{4,20},{20... | collective-permute-start | bytes 1376264 | tf_op jit(solution)/shard_map/ppermute | solution.py:20
  194.4 20.0 %collective-permute-start.6 = (bf16[64,1024]{1,0:T(8,128)(2,1)}, bf16[64,1024]{1,0:T(8,128)(2,1)S(1)}, u32[]{:S(2)}, u32[]{:S(2)}) collective-permute-start(bf16[64,1024]{1,0:T(8,128)(2,1)} %get-tuple-element.36), channel_id=1, source_target_pairs={{0,8},{1,9},{2,10},{3,11},{4,12},{5,13},{6,14},{7,15},{8,0},{9,1},... | collective-permute-start | bytes 393224 | tf_op jit(solution)/shard_map/ppermute | solution.py:20
  194.4 0.8 copy-start.6
  194.4 0.9 copy-start.7
  208.5 1.4 copy-start.2
  214.4 0.6 copy-start.8

commit v5 on v4

--- a/solution.py
+++ b/solution.py
@@ -9,7 +9,7 @@
 F32, BF16, I32 = jnp.float32, jnp.bfloat16, jnp.int32
 LANES = 128
 LONG = 4_000_000_000_000
-GIVE_COST = 5_000_000_000
+GIVE_COST = 40_000_000_000
 BACK_COST = 40_000_000_000
 VMEM_LIMIT = 60 * 1024 * 1024
 
@@ -315,21 +315,21 @@
     )
 
 
-def give_kernel(own_slot, mirror_slot, main_ref, spare_ref, own_ref, mirror_ref):
+def give_kernel(slot_ref, main_ref, spare_ref, out_ref):
     main = main_ref.shape[0]
-    for slot_ref, out_ref in ((own_slot, own_ref), (mirror_slot, mirror_ref)):
-        packed = dot(slot_ref[:, :main], main_ref[...]) + dot(slot_ref[:, main:], spare_ref[...])
-        out_ref[...] = packed.astype(BF16)
-
-
-def give(own_slot, mirror_slot, out_main, out_spare, tile):
-    rows, width = own_slot.shape[0], out_main.shape[1]
+    packed = dot(slot_ref[:, :main], main_ref[...]) + dot(slot_ref[:, main:], spare_ref[...])
+    out_ref[...] = packed.astype(BF16)
+
+
+def give(slot, out_main, out_spare, tile, cost, *after):
+    rows, width = slot.shape[0], out_main.shape[1]
     return call(
         give_kernel,
         width // tile,
-        entire(own_slot, mirror_slot) + by_columns(tile, out_main, out_spare),
-        by_columns(tile, bf16(rows, width), bf16(rows, width)),
-        cost=GIVE_COST,
+        entire(slot) + by_columns(tile, out_main, out_spare),
+        by_columns(tile, bf16(rows, width))[0],
+        after=after,
+        cost=cost,
     )
 
 
@@ -476,8 +476,8 @@
     spare_hidden = swapped(spare_hidden, "expert", half)
     metas = lax.all_to_all(meta, "expert", 0, 0, tiled=True)
     packed_own, mix_own = pack_own(meta, grad_out, cap, half, tile)
-    arrived_own = to_half(touched(packed_own, metas, spare_hidden, far))
-    out_spare = project_spare(spare_hidden, near, far, tile, mix_own)
+    out_spare = project_spare(spare_hidden, near, far, width // 7, mix_own, metas)
+    arrived_own = to_half(touched(packed_own, metas, out_spare))
     sel, gate, mix_mirror, give_own, take_own, give_mirror, take_mirror = plan(
         metas, cap, half, main, slots
     )
@@ -485,7 +485,8 @@
     out_spare = swapped(out_spare, "expert", half)
     mirror = swapped(touched(copied(grad_out, width // 2), out_main, sel), "expert", half)
     other_turned = swapped(far_turned, "dp", 1)
-    given_own, given_mirror = give(give_own, give_mirror, out_main, out_spare, tile)
+    given_mirror = give(give_mirror, out_main, out_spare, tile, GIVE_COST)
+    given_own = give(give_own, out_main, out_spare, tile, 0, given_mirror)
     returned_mirror = to_half(touched(given_mirror, arrived_own))
     packed_mirror = pack(sel, gate, mirror, tile, given_own)
     arrived_mirror = to_half(touched(packed_mirror, returned_mirror))
@@ -503,7 +504,7 @@
     grad_weight = weight_grad(
         turned, other_turned, (grads_main, grads_spare), (other_main, other_spare), tile, back
     )
-    grad_hidden = with_spare(back, back_spare, layer_out, grad_weight)
+    grad_hidden = with_spare(back, back_spare, grad_weight)
     return (layer_out, grad_hidden[None, None], grad_weight[None])
 
 

time: 218 us -> 224 us (1.028)
  Pallas kernels: 74.2 us -> 79.7 us
  waiting for transfers between devices: 98.7 us -> 103 us
  starting transfers between devices: 33.9 us -> 31.2 us
    all_to_all x4, waiting for transfers between devices: 58.7 us -> 88.4 us  [to_half(): lax.all_to_all(rows.reshape(half, cap, width), 'expert', 0, 0, axis_index...]
    ppermute x10, waiting for transfers between devices: 37.3 us -> 12 us  [swapped(): return lax.ppermute(value, axis, pairs)]
    pallas_call x20 -> x21, Pallas kernels: 74.2 us -> 79.7 us  [call(): pl.pallas_call(kernel, grid=(grid,), in_specs=[spec for _, spec in ins] +...]
    all_to_all x4, starting transfers between devices: 21.4 us -> 17.8 us  [to_half(): lax.all_to_all(rows.reshape(half, cap, width), 'expert', 0, 0, axis_index...]
    unnamed x24 -> x22, local copies, waits for them, and re-layouts: 9.11 us -> 8.16 us
  transfers between devices with their start and end apart: 15 -> 15, of which waited for: 7 -> 8; matrix products, arithmetic and copies ran while one was open for 0% -> 0% of each run, Pallas kernels for 34% -> 31%
where the time goes in v5:
time: 224 us; the launch traced here: 223 us
  waiting for transfers between devices  103 us (46%)
  Pallas kernels  79.7 us (36%)
  starting transfers between devices  31.2 us (14%)
  local copies, waits for them, and re-layouts  8.16 us (4%)
    all_to_all x4, waiting for transfers between devices, to_half(): lax.all_to_all(rows.reshape(half, cap, width), 'expert', 0, 0, axis_index...  88.4 us
    pallas_call x21, Pallas kernels, call(): pl.pallas_call(kernel, grid=(grid,), in_specs=[spec for _, spec in ins] +...  79.7 us
    all_to_all x4, starting transfers between devices, to_half(): lax.all_to_all(rows.reshape(half, cap, width), 'expert', 0, 0, axis_index...  17.8 us
    ppermute x10, waiting for transfers between devices, swapped(): return lax.ppermute(value, axis, pairs)  12 us
    ppermute x10, starting transfers between devices, swapped(): return lax.ppermute(value, axis, pairs)  8.61 us
    unnamed x22, local copies, waits for them, and re-layouts  8.16 us
    all_to_all x1, starting transfers between devices, local(): metas = lax.all_to_all(meta, 'expert', 0, 0, tiled=True)  4.84 us
  transfers between devices with their start and end apart: 15, of which 8 were waited for; matrix products, arithmetic and copies ran while one was open for 0% of the time, Pallas kernels for 31%

profile of v5, /device:TPU:0, one launch (start us, length us, event | category | flops | bytes accessed | tf_op | source)
XLA Modules:
  0.0 222.9 jit_solution(2859586072371189525)
XLA Ops:
  0.6 0.5 collective-permute-start.1
  1.1 1.6 shard_map.85
  2.8 3.6 %collective-permute-start = (bf16[64,1024]{1,0:T(8,128)(2,1)}, bf16[64,1024]{1,0:T(8,128)(2,1)S(1)}, u32[]{:S(2)}, u32[]{:S(2)}) collective-permute-start(bf16[64,1024]{1,0:T(8,128)(2,1)} %get-tuple-element.22), channel_id=1, source_target_pairs={{0,8},{1,9},{2,10},{3,11},{4,12},{5,13},{6,14},{7,15},{8,0},{9,1},... | collective-permute-start | bytes 393224 | tf_op jit(solution)/shard_map/ppermute | solution.py:20
  6.4 4.8 %all-to-all-start = ((f32[16,8,128]{2,1,0:T(8,128)}), f32[16,8,128]{2,1,0:T(8,128)S(1)}, u32[]{:S(2)}, u32[]{:S(2)}) async-start(f32[16,8,128]{2,1,0:T(8,128)} %get-tuple-element.19.refs_0_), calls=%async_computation | async-start | bytes 131072 | tf_op jit(solution)/shard_map/all_to_all | solution.py:477
  11.2 4.8 %shard_map.86 = (bf16[320,3584]{1,0:T(8,128)(2,1)}, bf16[256,320]{1,0:T(8,128)(2,1)}) custom-call(f32[16,8,128]{2,1,0:T(8,128)} %get-tuple-element.19.refs_0_, bf16[128,3584]{1,0:T(8,128)(2,1)} %refs_0_.1), custom_call_target="tpu_custom_call" | custom-call | tf_op jit(solution)/shard_map/pallas_call | solution.py:60
  16.0 2.7 %all-to-all-done.refs_0_.refs_4_.refs_1_ = f32[16,8,128]{2,1,0:T(8,128)S(1)} async-done(((f32[16,8,128]{2,1,0:T(8,128)}), f32[16,8,128]{2,1,0:T(8,128)S(1)}, u32[]{:S(2)}, u32[]{:S(2)}) %all-to-all-start) | async-done | bytes 65568 | tf_op jit(solution)/shard_map/all_to_all | solution.py:477
  18.8 0.0 copy-start.4
  18.8 0.0 collective-permute-done.refs_0_.refs_1_
  18.8 0.0 copy-start.5
  18.8 0.0 collective-permute-done.1.refs_2_.refs_3_
  18.8 0.6 copy-done.4
  19.4 0.0 copy-done.5
  19.4 7.0 %shard_map.88.refs_4_.refs_2_ = bf16[64,3584]{1,0:T(8,128)(2,1)} custom-call(bf16[64,1024]{1,0:T(8,128)(2,1)} %copy-done.5, bf16[512,3584]{1,0:T(8,128)(2,1)} %bitcast.23, bf16[512,3584]{1,0:T(8,128)(2,1)} %collective-permute-done.1.refs_2_.refs_3_, bf16[256,320]{1,0:T(8,128)(2,1)} %get-tuple-element.20.refs_3_.refs_0_, f32[16,8,128]{2,1,0:T(8,128)} %copy-done.4), custom_call_target="tpu_custom_call" | custom-call | tf_op jit(solution)/shard_map/pallas_call | solution.py:60
  26.4 0.7 collective-permute-start.2
  27.2 3.9 %all-to-all-start.1 = ((bf16[8,40,3584]{2,1,0:T(8,128)(2,1)}), bf16[8,40,3584]{2,1,0:T(8,128)(2,1)S(1)}, u32[]{:S(2)}, u32[]{:S(2)}) async-start(bf16[8,40,3584]{2,1,0:T(8,128)(2,1)} %bitcast.27), calls=%async_computation.1 | async-start | bytes 4587520 | tf_op jit(solution)/shard_map/all_to_all | solution.py:468
  31.0 2.0 shard_map.95.refs_0_
  33.0 2.9 %shard_map.87 = (bf16[320,128]{1,0:T(8,128)(2,1)}, f32[320,128]{1,0:T(8,128)}, bf16[256,320]{1,0:T(8,128)(2,1)}, bf16[320,448]{1,0:T(8,128)(2,1)}, bf16[448,320]...) custom-call(f32[16,8,128]{2,1,0:T(8,128)} %copy-done.4), custom_call_target="tpu_custom_call" | custom-call | tf_op jit(solution)/shard_map/pallas_call | solution.py:60
  35.9 7.8 %shard_map.89 = (bf16[384,3584]{1,0:T(8,128)(2,1)}, bf16[512,448]{1,0:T(8,128)(2,1)}, bf16[512,448]{1,0:T(8,128)(2,1)}) custom-call(bf16[448,1024]{1,0:T(8,128)(2,1)} %bitcast.31, bf16[64,1024]{1,0:T(8,128)(2,1)} %copy-done.5, bf16[512,3584]{1,0:T(8,128)(2,1)} %bitcast.24, bf16[512,3584]{1,0:T(8,128)(2,1)} %collective-permute-done.1.refs_2_.refs_3_, ...), custom_call_target="tpu_custom_call" | custom-call | tf_op jit(solution)/shard_map/pallas_call | solution.py:60
  43.7 1.9 collective-permute-start.4
  45.6 3.3 %collective-permute-done.2.refs_2_ = bf16[64,3584]{1,0:T(8,128)(2,1)S(1)} collective-permute-done((bf16[64,3584]{1,0:T(8,128)(2,1)}, bf16[64,3584]{1,0:T(8,128)(2,1)S(1)}, u32[]{:S(2)}, u32[]{:S(2)}) %collective-permute-start.2) | collective-permute-done | bytes 458784 | tf_op jit(solution)/shard_map/ppermute | solution.py:20
  48.9 0.8 copy-done.7
  49.7 5.4 %shard_map.90.refs_3_.refs_0_ = bf16[320,3584]{1,0:T(8,128)(2,1)} custom-call(bf16[320,448]{1,0:T(8,128)(2,1)} %get-tuple-element.24.refs_0_, bf16[384,3584]{1,0:T(8,128)(2,1)} %get-tuple-element.23.refs_1_, bf16[64,3584]{1,0:T(8,128)(2,1)} %copy-done.7), custom_call_target="tpu_custom_call" | custom-call | flops 40000000000 | tf_op jit(solution)/shard_map/pallas_call | solution.py:60
  55.1 5.3 %shard_map.91.refs_3_.refs_0_ = bf16[320,3584]{1,0:T(8,128)(2,1)} custom-call(bf16[320,448]{1,0:T(8,128)(2,1)} %get-tuple-element.21.refs_0_, bf16[384,3584]{1,0:T(8,128)(2,1)} %get-tuple-element.23.refs_1_, bf16[64,3584]{1,0:T(8,128)(2,1)} %copy-done.7, bf16[320,3584]{1,0:T(8,128)(2,1)} %shard_map.90.refs_3_.refs_0_), custom_call_target="tpu_custom_call" | custom-call | tf_op jit(solution)/shard_map/pallas_call | solution.py:60
  60.4 22.4 %all-to-all-done.1 = bf16[8,40,3584]{2,1,0:T(8,128)(2,1)S(1)} async-done(((bf16[8,40,3584]{2,1,0:T(8,128)(2,1)}), bf16[8,40,3584]{2,1,0:T(8,128)(2,1)S(1)}, u32[]{:S(2)}, u32[]{:S(2)}) %all-to-all-start.1) | async-done | bytes 2293792 | tf_op jit(solution)/shard_map/all_to_all | solution.py:468
  82.9 0.0 copy-start
  82.9 1.4 copy-done
  84.2 4.9 %all-to-all-start.2 = ((bf16[8,40,3584]{2,1,0:T(8,128)(2,1)}), bf16[8,40,3584]{2,1,0:T(8,128)(2,1)}, u32[]{:S(2)}, u32[]{:S(2)}) async-start(bf16[8,40,3584]{2,1,0:T(8,128)(2,1)} %bitcast.21), calls=%async_computation.2 | async-start | bytes 4587520 | tf_op jit(solution)/shard_map/all_to_all | solution.py:468
  89.1 0.0 collective-permute-done.4.refs_2_
  89.1 4.4 %shard_map.97.refs_0_ = bf16[320,3584]{1,0:T(8,128)(2,1)} custom-call(bf16[320,128]{1,0:T(8,128)(2,1)} %get-tuple-element.29.refs_2_.refs_0_, f32[320,128]{1,0:T(8,128)} %get-tuple-element.30.refs_1_, bf16[128,3584]{1,0:T(8,128)(2,1)} %collective-permute-done.4.refs_2_, bf16[320,3584]{1,0:T(8,128)(2,1)} %shard_map.91.refs_3_.refs_0_), custom_call_target="tpu_custom_call" | custom-call | flops 3999999983616 | tf_op jit(solution)/shard_map/pallas_call | solution.py:60
  93.5 22.7 %all-to-all-done.2 = bf16[8,40,3584]{2,1,0:T(8,128)(2,1)} async-done(((bf16[8,40,3584]{2,1,0:T(8,128)(2,1)}), bf16[8,40,3584]{2,1,0:T(8,128)(2,1)}, u32[]{:S(2)}, u32[]{:S(2)}) %all-to-all-start.2) | async-done | bytes 2293792 | tf_op jit(solution)/shard_map/all_to_all | solution.py:468
  116.2 4.0 %all-to-all-start.3 = ((bf16[8,40,3584]{2,1,0:T(8,128)(2,1)}), bf16[8,40,3584]{2,1,0:T(8,128)(2,1)S(1)}, u32[]{:S(2)}, u32[]{:S(2)}) async-start(bf16[8,40,3584]{2,1,0:T(8,128)(2,1)} %bitcast.29), calls=%async_computation.3 | async-start | bytes 4587520 | tf_op jit(solution)/shard_map/all_to_all | solution.py:468
  120.2 4.4 %shard_map.94 = bf16[128,3584]{1,0:T(8,128)(2,1)} custom-call(bf16[256,320]{1,0:T(8,128)(2,1)} %get-tuple-element.25.refs_0_, bf16[320,3584]{1,0:T(8,128)(2,1)} %bitcast.8.refs_1_), custom_call_target="tpu_custom_call" | custom-call | tf_op jit(solution)/shard_map/pallas_call | solution.py:60
  124.6 1.3 collective-permute-start.3
  125.9 41.0 %all-to-all-done.3 = bf16[8,40,3584]{2,1,0:T(8,128)(2,1)S(1)} async-done(((bf16[8,40,3584]{2,1,0:T(8,128)(2,1)}), bf16[8,40,3584]{2,1,0:T(8,128)(2,1)S(1)}, u32[]{:S(2)}, u32[]{:S(2)}) %all-to-all-start.3) | async-done | bytes 2293792 | tf_op jit(solution)/shard_map/all_to_all | solution.py:468
  166.9 0.0 copy-start.1
  166.9 1.4 copy-done.1
  168.3 4.7 %shard_map.99.refs_2_.refs_4_ = bf16[64,3584]{1,0:T(8,128)(2,1)} custom-call(bf16[448,320]{1,0:T(8,128)(2,1)} %get-tuple-element.27.refs_0_, bf16[448,320]{1,0:T(8,128)(2,1)} %get-tuple-element.28.refs_1_, bf16[320,3584]{1,0:T(8,128)(2,1)} %bitcast.16, bf16[320,3584]{1,0:T(8,128)(2,1)} %bitcast.19), custom_call_target="tpu_custom_call" | custom-call | tf_op jit(solution)/shard_map/pallas_call | solution.py:60
  173.1 0.0 collective-permute-start.5
  173.1 0.0 collective-permute-done.3.refs_1_.refs_2_
  173.1 0.0 copy-start.3
  173.1 0.9 copy-done.3
  174.0 5.0 %all-to-all-start.4 = ((bf16[8,40,3584]{2,1,0:T(8,128)(2,1)}), bf16[8,40,3584]{2,1,0:T(8,128)(2,1)S(1)}, u32[]{:S(2)}, u32[]{:S(2)}) async-start(bf16[8,40,3584]{2,1,0:T(8,128)(2,1)} %bitcast.18), calls=%async_computation.4 | async-start | bytes 4587520 | tf_op jit(solution)/shard_map/all_to_all | solution.py:468
  179.0 0.0 copy-done.10
  179.0 0.1 collective-permute-start.7
  179.0 6.7 %shard_map.102.refs_0_.refs_2_ = bf16[384,3584]{1,0:T(8,128)(2,1)} custom-call(bf16[448,320]{1,0:T(8,128)(2,1)} %get-tuple-element.27.refs_0_, bf16[448,320]{1,0:T(8,128)(2,1)} %get-tuple-element.28.refs_1_, bf16[320,3584]{1,0:T(8,128)(2,1)} %bitcast.17, bf16[320,3584]{1,0:T(8,128)(2,1)} %bitcast.20, bf16[64,3584]{1,0:T(8,128)(2,1)} %shard_map.99.refs_2_.refs_4_), custom_call_target="tpu_custom_call" | custom-call | tf_op jit(solution)/shard_map/pallas_call | solution.py:60
  185.8 0.5 collective-permute-start.8
  186.2 8.2 %collective-permute-done.5.refs_1_.refs_3_ = bf16[64,3584]{1,0:T(8,128)(2,1)} collective-permute-done((bf16[64,3584]{1,0:T(8,128)(2,1)}, bf16[64,3584]{1,0:T(8,128)(2,1)}, u32[]{:S(2)}, u32[]{:S(2)}) %collective-permute-start.5) | collective-permute-done | bytes 458784 | tf_op jit(solution)/shard_map/ppermute | solution.py:20
  194.4 0.0 collective-permute-start.9
  194.4 8.3 %shard_map.103 = (bf16[448,1024]{1,0:T(8,128)(2,1)}, bf16[64,1024]{1,0:T(8,128)(2,1)}) custom-call(bf16[384,3584]{1,0:T(8,128)(2,1)} %shard_map.102.refs_0_.refs_2_, bf16[64,3584]{1,0:T(8,128)(2,1)} %collective-permute-done.5.refs_1_.refs_3_, bf16[512,3584]{1,0:T(8,128)(2,1)} %bitcast.25, bf16[512,3584]{1,0:T(8,128)(2,1)} %collective-permute-done.1.refs_2_.refs_3_), custom_call_target="tpu_custom_call" | custom-call | flops 40000000000 | tf_op jit(solution)/shard_map/pallas_call | solution.py:60
  202.7 0.0 collective-permute-start.6
  202.7 0.0 collective-permute-done.7.refs_1_
  202.7 0.0 copy-start.6
  202.7 0.0 collective-permute-done.9.refs_5_
  202.7 0.0 copy-start.8
  202.7 0.0 collective-permute-done.8.refs_4_
  202.7 0.7 copy-done.6
  203.5 0.2 copy-done.8
  203.6 8.3 %shard_map.104.refs_2_ = bf16[512,3584]{1,0:T(8,128)(2,1)} custom-call(bf16[512,448]{1,0:T(8,128)(2,1)} %get-tuple-element.33.refs_0_, bf16[512,448]{1,0:T(8,128)(2,1)} %copy-done.6, bf16[384,3584]{1,0:T(8,128)(2,1)} %shard_map.102.refs_0_.refs_2_, bf16[64,3584]{1,0:T(8,128)(2,1)} %collective-permute-done.5.refs_1_.refs_3_, ...), custom_call_target="tpu_custom_call" | custom-call | tf_op jit(solution)/shard_map/pallas_call | solution.py:60
  212.0 0.5 collective-permute-done.6.refs_1_
  212.5 0.7 copy-done.9
  213.2 1.6 shard_map.105
  214.8 2.2 %all-to-all-done.4 = bf16[8,40,3584]{2,1,0:T(8,128)(2,1)S(1)} async-done(((bf16[8,40,3584]{2,1,0:T(8,128)(2,1)}), bf16[8,40,3584]{2,1,0:T(8,128)(2,1)S(1)}, u32[]{:S(2)}, u32[]{:S(2)}) %all-to-all-start.4) | async-done | bytes 2293792 | tf_op jit(solution)/shard_map/all_to_all | solution.py:468
  217.0 1.4 copy-done.2
  218.4 4.5 %shard_map.101 = bf16[128,3584]{1,0:T(8,128)(2,1)} custom-call(bf16[256,320]{1,0:T(8,128)(2,1)} %get-tuple-element.20.refs_3_.refs_0_, bf16[320,3584]{1,0:T(8,128)(2,1)} %bitcast.28, bf16[128,3584]{1,0:T(8,128)(2,1)} %copy-done.3), custom_call_target="tpu_custom_call" | custom-call | tf_op jit(solution)/shard_map/pallas_call | solution.py:60
  (9 shorter events, 0.0 us)
Async XLA Ops:
  0.6 18.2 %collective-permute-start.1 = (bf16[512,3584]{1,0:T(8,128)(2,1)}, bf16[512,3584]{1,0:T(8,128)(2,1)}, u32[]{:S(2)}, u32[]{:S(2)}) collective-permute-start(bf16[512,3584]{1,0:T(8,128)(2,1)} %bitcast.22), channel_id=1, source_target_pairs={{0,16},{16,0},{1,17},{17,1},{2,18},{18,2},{3,19},{19,3},{4,20},{20... | collective-permute-start | bytes 11010056 | tf_op jit(solution)/shard_map/ppermute | solution.py:20
  2.8 16.0 %collective-permute-start = (bf16[64,1024]{1,0:T(8,128)(2,1)}, bf16[64,1024]{1,0:T(8,128)(2,1)S(1)}, u32[]{:S(2)}, u32[]{:S(2)}) collective-permute-start(bf16[64,1024]{1,0:T(8,128)(2,1)} %get-tuple-element.22), channel_id=1, source_target_pairs={{0,8},{1,9},{2,10},{3,11},{4,12},{5,13},{6,14},{7,15},{8,0},{9,1},... | collective-permute-start | bytes 393224 | tf_op jit(solution)/shard_map/ppermute | solution.py:20
  6.4 12.4 %all-to-all-start = ((f32[16,8,128]{2,1,0:T(8,128)}), f32[16,8,128]{2,1,0:T(8,128)S(1)}, u32[]{:S(2)}, u32[]{:S(2)}) async-start(f32[16,8,128]{2,1,0:T(8,128)} %get-tuple-element.19.refs_0_), calls=%async_computation | async-start | bytes 131072 | tf_op jit(solution)/shard_map/all_to_all | solution.py:477
  18.8 0.6 copy-start.4
  18.8 0.7 copy-start.5
  26.4 22.5 %collective-permute-start.2 = (bf16[64,3584]{1,0:T(8,128)(2,1)}, bf16[64,3584]{1,0:T(8,128)(2,1)S(1)}, u32[]{:S(2)}, u32[]{:S(2)}) collective-permute-start(bf16[64,3584]{1,0:T(8,128)(2,1)} %shard_map.88.refs_4_.refs_2_), channel_id=1, source_target_pairs={{0,8},{1,9},{2,10},{3,11},{4,12},{5,13},{6,14},{7,15},{8,0},{9,1},... | collective-permute-start | bytes 1376264 | tf_op jit(solution)/shard_map/ppermute | solution.py:20
  27.2 55.7 %all-to-all-start.1 = ((bf16[8,40,3584]{2,1,0:T(8,128)(2,1)}), bf16[8,40,3584]{2,1,0:T(8,128)(2,1)S(1)}, u32[]{:S(2)}, u32[]{:S(2)}) async-start(bf16[8,40,3584]{2,1,0:T(8,128)(2,1)} %bitcast.27), calls=%async_computation.1 | async-start | bytes 4587520 | tf_op jit(solution)/shard_map/all_to_all | solution.py:468
  43.7 45.4 %collective-permute-start.4 = (bf16[128,3584]{1,0:T(8,128)(2,1)}, bf16[128,3584]{1,0:T(8,128)(2,1)}, u32[]{:S(2)}, u32[]{:S(2)}) collective-permute-start(bf16[128,3584]{1,0:T(8,128)(2,1)} %shard_map.96), channel_id=1, source_target_pairs={{0,8},{1,9},{2,10},{3,11},{4,12},{5,13},{6,14},{7,15},{8,0},{9,1},... | collective-permute-start | bytes 2752520 | tf_op jit(solution)/shard_map/ppermute | solution.py:20
  48.9 0.8 copy-start.7
  82.9 1.4 copy-start
  84.2 31.9 %all-to-all-start.2 = ((bf16[8,40,3584]{2,1,0:T(8,128)(2,1)}), bf16[8,40,3584]{2,1,0:T(8,128)(2,1)}, u32[]{:S(2)}, u32[]{:S(2)}) async-start(bf16[8,40,3584]{2,1,0:T(8,128)(2,1)} %bitcast.21), calls=%async_computation.2 | async-start | bytes 4587520 | tf_op jit(solution)/shard_map/all_to_all | solution.py:468
  116.2 50.7 %all-to-all-start.3 = ((bf16[8,40,3584]{2,1,0:T(8,128)(2,1)}), bf16[8,40,3584]{2,1,0:T(8,128)(2,1)S(1)}, u32[]{:S(2)}, u32[]{:S(2)}) async-start(bf16[8,40,3584]{2,1,0:T(8,128)(2,1)} %bitcast.29), calls=%async_computation.3 | async-start | bytes 4587520 | tf_op jit(solution)/shard_map/all_to_all | solution.py:468
  124.6 48.5 %collective-permute-start.3 = (bf16[128,3584]{1,0:T(8,128)(2,1)}, bf16[128,3584]{1,0:T(8,128)(2,1)S(1)}, u32[]{:S(2)}, u32[]{:S(2)}) collective-permute-start(bf16[128,3584]{1,0:T(8,128)(2,1)} %shard_map.94), channel_id=1, source_target_pairs={{0,8},{1,9},{2,10},{3,11},{4,12},{5,13},{6,14},{7,15},{8,0},{9,1},... | collective-permute-start | bytes 2752520 | tf_op jit(solution)/shard_map/ppermute | solution.py:20
  166.9 1.4 copy-start.1
  173.1 21.3 %collective-permute-start.5 = (bf16[64,3584]{1,0:T(8,128)(2,1)}, bf16[64,3584]{1,0:T(8,128)(2,1)}, u32[]{:S(2)}, u32[]{:S(2)}) collective-permute-start(bf16[64,3584]{1,0:T(8,128)(2,1)} %shard_map.99.refs_2_.refs_4_), channel_id=1, source_target_pairs={{0,8},{1,9},{2,10},{3,11},{4,12},{5,13},{6,14},{7,15},{8,0},{9,1},... | collective-permute-start | bytes 1376264 | tf_op jit(solution)/shard_map/ppermute | solution.py:20
  173.1 0.9 copy-start.3
  174.0 5.0 %copy-start.10 = (bf16[512,448]{1,0:T(8,128)(2,1)S(1)}, bf16[512,448]{1,0:T(8,128)(2,1)}, u32[]{:S(2)}) copy-start(bf16[512,448]{1,0:T(8,128)(2,1)} %get-tuple-element.34) | copy-start | bytes 1376260
  174.0 43.0 %all-to-all-start.4 = ((bf16[8,40,3584]{2,1,0:T(8,128)(2,1)}), bf16[8,40,3584]{2,1,0:T(8,128)(2,1)S(1)}, u32[]{:S(2)}, u32[]{:S(2)}) async-start(bf16[8,40,3584]{2,1,0:T(8,128)(2,1)} %bitcast.18), calls=%async_computation.4 | async-start | bytes 4587520 | tf_op jit(solution)/shard_map/all_to_all | solution.py:468
  179.0 23.7 %collective-permute-start.7 = (bf16[512,448]{1,0:T(8,128)(2,1)S(1)}, bf16[512,448]{1,0:T(8,128)(2,1)S(1)}, u32[]{:S(2)}, u32[]{:S(2)}) collective-permute-start(bf16[512,448]{1,0:T(8,128)(2,1)S(1)} %copy-done.10), channel_id=1, source_target_pairs={{0,16},{16,0},{1,17},{17,1},{2,18},{18,2},{3,19},{19,3},{4,20},{20... | collective-permute-start | bytes 1376264 | tf_op jit(solution)/shard_map/ppermute | solution.py:20
  185.8 17.0 %collective-permute-start.8 = (bf16[384,3584]{1,0:T(8,128)(2,1)}, bf16[384,3584]{1,0:T(8,128)(2,1)}, u32[]{:S(2)}, u32[]{:S(2)}) collective-permute-start(bf16[384,3584]{1,0:T(8,128)(2,1)} %shard_map.102.refs_0_.refs_2_), channel_id=1, source_target_pairs={{0,16},{16,0},{1,17},{17,1},{2,18},{18,2},{3,19},{19,3},{4,20},{20... | collective-permute-start | bytes 8257544 | tf_op jit(solution)/shard_map/ppermute | solution.py:20
  194.4 8.3 %collective-permute-start.9 = (bf16[64,3584]{1,0:T(8,128)(2,1)}, bf16[64,3584]{1,0:T(8,128)(2,1)S(1)}, u32[]{:S(2)}, u32[]{:S(2)}) collective-permute-start(bf16[64,3584]{1,0:T(8,128)(2,1)} %collective-permute-done.5.refs_1_.refs_3_), channel_id=1, source_target_pairs={{0,16},{16,0},{1,17},{17,1},{2,18},{18,2},{3,19},{19,3},{4,20},{20... | collective-permute-start | bytes 1376264 | tf_op jit(solution)/shard_map/ppermute | solution.py:20
  202.7 9.9 %collective-permute-start.6 = (bf16[64,1024]{1,0:T(8,128)(2,1)}, bf16[64,1024]{1,0:T(8,128)(2,1)S(1)}, u32[]{:S(2)}, u32[]{:S(2)}) collective-permute-start(bf16[64,1024]{1,0:T(8,128)(2,1)} %get-tuple-element.32), channel_id=1, source_target_pairs={{0,8},{1,9},{2,10},{3,11},{4,12},{5,13},{6,14},{7,15},{8,0},{9,1},... | collective-permute-start | bytes 393224 | tf_op jit(solution)/shard_map/ppermute | solution.py:20
  202.7 0.8 copy-start.6
  202.7 0.9 copy-start.8
  212.5 0.7 copy-start.9
  217.0 1.4 copy-start.2

commit v6 on v5

--- a/solution.py
+++ b/solution.py
@@ -9,9 +9,9 @@
 F32, BF16, I32 = jnp.float32, jnp.bfloat16, jnp.int32
 LANES = 128
 LONG = 4_000_000_000_000
-GIVE_COST = 40_000_000_000
+GIVE_COST = 5_000_000_000
 BACK_COST = 40_000_000_000
-VMEM_LIMIT = 60 * 1024 * 1024
+VMEM_LIMIT = 64 * 1024 * 1024 - 65536
 
 
 def swapped(value, axis, distance):
@@ -476,8 +476,8 @@
     spare_hidden = swapped(spare_hidden, "expert", half)
     metas = lax.all_to_all(meta, "expert", 0, 0, tiled=True)
     packed_own, mix_own = pack_own(meta, grad_out, cap, half, tile)
-    out_spare = project_spare(spare_hidden, near, far, width // 7, mix_own, metas)
-    arrived_own = to_half(touched(packed_own, metas, out_spare))
+    arrived_own = to_half(touched(packed_own, metas, spare_hidden, far))
+    out_spare = project_spare(spare_hidden, near, far, tile, mix_own)
     sel, gate, mix_mirror, give_own, take_own, give_mirror, take_mirror = plan(
         metas, cap, half, main, slots
     )
@@ -486,10 +486,10 @@
     mirror = swapped(touched(copied(grad_out, width // 2), out_main, sel), "expert", half)
     other_turned = swapped(far_turned, "dp", 1)
     given_mirror = give(give_mirror, out_main, out_spare, tile, GIVE_COST)
-    given_own = give(give_own, out_main, out_spare, tile, 0, given_mirror)
     returned_mirror = to_half(touched(given_mirror, arrived_own))
-    packed_mirror = pack(sel, gate, mirror, tile, given_own)
-    arrived_mirror = to_half(touched(packed_mirror, returned_mirror))
+    packed_mirror = pack(sel, gate, mirror, tile)
+    given_own = give(give_own, out_main, out_spare, tile, 0, packed_mirror)
+    arrived_mirror = to_half(touched(packed_mirror, returned_mirror, given_own))
     part = swapped(combine(mix_mirror, returned_mirror, [], tile), "expert", half)
     arrived = (take_own, take_mirror, arrived_own, arrived_mirror)
     grads_spare = take(*arrived, main, slots - main, tile)

time: 224 us -> 208 us (0.929)
  waiting for transfers between devices: 103 us -> 92.5 us
  local copies, waits for them, and re-layouts: 8.16 us -> 0 us
  starting transfers between devices: 31.2 us -> 35.2 us
    all_to_all x4, waiting for transfers between devices: 88.4 us -> 49.4 us  [to_half(): lax.all_to_all(rows.reshape(half, cap, width), 'expert', 0, 0, axis_index...]
    ppermute x10, waiting for transfers between devices: 12 us -> 40.2 us  [swapped(): return lax.ppermute(value, axis, pairs)]
    unnamed x22 -> x0, local copies, waits for them, and re-layouts: 8.16 us -> none
    all_to_all x4, starting transfers between devices: 17.8 us -> 22.8 us  [to_half(): lax.all_to_all(rows.reshape(half, cap, width), 'expert', 0, 0, axis_index...]
  transfers between devices with their start and end apart: 15 -> 15, of which waited for: 8 -> 8; matrix products, arithmetic and copies ran while one was open for 0% -> 0% of each run, Pallas kernels for 31% -> 36%
where the time goes in v6:
time: 208 us; the launch traced here: 206 us
  waiting for transfers between devices  92.5 us (44%)
  Pallas kernels  78 us (38%)
  starting transfers between devices  35.2 us (17%)
    pallas_call x21, Pallas kernels, call(): pl.pallas_call(kernel, grid=(grid,), in_specs=[spec for _, spec in ins] +...  78 us
    all_to_all x4, waiting for transfers between devices, to_half(): lax.all_to_all(rows.reshape(half, cap, width), 'expert', 0, 0, axis_index...  49.4 us
    ppermute x10, waiting for transfers between devices, swapped(): return lax.ppermute(value, axis, pairs)  40.2 us
    all_to_all x4, starting transfers between devices, to_half(): lax.all_to_all(rows.reshape(half, cap, width), 'expert', 0, 0, axis_index...  22.8 us
    ppermute x10, starting transfers between devices, swapped(): return lax.ppermute(value, axis, pairs)  7.54 us
    all_to_all x1, starting transfers between devices, local(): metas = lax.all_to_all(meta, 'expert', 0, 0, tiled=True)  4.89 us
  transfers between devices with their start and end apart: 15, of which 8 were waited for; matrix products, arithmetic and copies ran while one was open for 0% of the time, Pallas kernels for 36%

profile of v6, /device:TPU:0, one launch (start us, length us, event | category | flops | bytes accessed | tf_op | source)
XLA Modules:
  0.0 206.4 jit_solution(875900374827508827)
XLA Ops:
  0.6 0.5 collective-permute-start.1
  1.1 1.6 shard_map.85
  2.8 3.6 %collective-permute-start = (bf16[64,1024]{1,0:T(8,128)(2,1)}, bf16[64,1024]{1,0:T(8,128)(2,1)}, u32[]{:S(2)}, u32[]{:S(2)}) collective-permute-start(bf16[64,1024]{1,0:T(8,128)(2,1)} %get-tuple-element.22), channel_id=1, source_target_pairs={{0,8},{1,9},{2,10},{3,11},{4,12},{5,13},{6,14},{7,15},{8,0},{9,1},... | collective-permute-start | bytes 393224 | tf_op jit(solution)/shard_map/ppermute | solution.py:20
  6.4 4.9 %all-to-all-start = ((f32[16,8,128]{2,1,0:T(8,128)}), f32[16,8,128]{2,1,0:T(8,128)}, u32[]{:S(2)}, u32[]{:S(2)}) async-start(f32[16,8,128]{2,1,0:T(8,128)} %get-tuple-element.19.refs_0_), calls=%async_computation | async-start | bytes 131072 | tf_op jit(solution)/shard_map/all_to_all | solution.py:477
  11.3 4.8 %shard_map.86 = (bf16[320,3584]{1,0:T(8,128)(2,1)}, bf16[256,320]{1,0:T(8,128)(2,1)}) custom-call(f32[16,8,128]{2,1,0:T(8,128)} %get-tuple-element.19.refs_0_, bf16[128,3584]{1,0:T(8,128)(2,1)} %refs_0_.1), custom_call_target="tpu_custom_call" | custom-call | tf_op jit(solution)/shard_map/pallas_call | solution.py:60
  16.1 2.8 %all-to-all-done.refs_0_.refs_1_ = f32[16,8,128]{2,1,0:T(8,128)} async-done(((f32[16,8,128]{2,1,0:T(8,128)}), f32[16,8,128]{2,1,0:T(8,128)}, u32[]{:S(2)}, u32[]{:S(2)}) %all-to-all-start) | async-done | bytes 65568 | tf_op jit(solution)/shard_map/all_to_all | solution.py:477
  18.9 0.0 collective-permute-done.refs_0_.refs_1_.refs_2_
  18.9 0.0 collective-permute-done.1.refs_2_.refs_3_
  18.9 4.4 %all-to-all-start.1 = ((bf16[8,40,3584]{2,1,0:T(8,128)(2,1)}), bf16[8,40,3584]{2,1,0:T(8,128)(2,1)}, u32[]{:S(2)}, u32[]{:S(2)}) async-start(bf16[8,40,3584]{2,1,0:T(8,128)(2,1)} %bitcast.22), calls=%async_computation.1 | async-start | bytes 4587520 | tf_op jit(solution)/shard_map/all_to_all | solution.py:468
  23.3 5.3 %shard_map.88.refs_4_ = bf16[64,3584]{1,0:T(8,128)(2,1)} custom-call(bf16[64,1024]{1,0:T(8,128)(2,1)} %collective-permute-done.refs_0_.refs_1_.refs_2_, bf16[512,3584]{1,0:T(8,128)(2,1)} %bitcast.18, bf16[512,3584]{1,0:T(8,128)(2,1)} %collective-permute-done.1.refs_2_.refs_3_, bf16[256,320]{1,0:T(8,128)(2,1)} %get-tuple-element.20.refs_3_.refs_0_), custom_call_target="tpu_custom_call" | custom-call | tf_op jit(solution)/shard_map/pallas_call | solution.py:60
  28.5 0.7 collective-permute-start.2
  29.3 2.0 shard_map.90.refs_0_
  31.3 2.9 %shard_map.87 = (bf16[320,128]{1,0:T(8,128)(2,1)}, f32[320,128]{1,0:T(8,128)}, bf16[256,320]{1,0:T(8,128)(2,1)}, bf16[320,448]{1,0:T(8,128)(2,1)}, bf16[448,320]...) custom-call(f32[16,8,128]{2,1,0:T(8,128)} %all-to-all-done.refs_0_.refs_1_), custom_call_target="tpu_custom_call" | custom-call | tf_op jit(solution)/shard_map/pallas_call | solution.py:60
  34.1 7.8 %shard_map.89 = (bf16[384,3584]{1,0:T(8,128)(2,1)}, bf16[512,448]{1,0:T(8,128)(2,1)}, bf16[512,448]{1,0:T(8,128)(2,1)}) custom-call(bf16[448,1024]{1,0:T(8,128)(2,1)} %bitcast.25, bf16[64,1024]{1,0:T(8,128)(2,1)} %collective-permute-done.refs_0_.refs_1_.refs_2_, bf16[512,3584]{1,0:T(8,128)(2,1)} %bitcast.19, ...), custom_call_target="tpu_custom_call" | custom-call | tf_op jit(solution)/shard_map/pallas_call | solution.py:60
  42.0 2.2 %collective-permute-start.3 = (bf16[128,3584]{1,0:T(8,128)(2,1)}, bf16[128,3584]{1,0:T(8,128)(2,1)}, u32[]{:S(2)}, u32[]{:S(2)}) collective-permute-start(bf16[128,3584]{1,0:T(8,128)(2,1)} %shard_map.91), channel_id=1, source_target_pairs={{0,8},{1,9},{2,10},{3,11},{4,12},{5,13},{6,14},{7,15},{8,0},{9,1},... | collective-permute-start | bytes 2752520 | tf_op jit(solution)/shard_map/ppermute | solution.py:20
  44.1 15.1 %collective-permute-done.2.refs_2_ = bf16[64,3584]{1,0:T(8,128)(2,1)} collective-permute-done((bf16[64,3584]{1,0:T(8,128)(2,1)}, bf16[64,3584]{1,0:T(8,128)(2,1)}, u32[]{:S(2)}, u32[]{:S(2)}) %collective-permute-start.2) | collective-permute-done | bytes 458784 | tf_op jit(solution)/shard_map/ppermute | solution.py:20
  59.3 5.3 %shard_map.94.refs_0_ = bf16[320,3584]{1,0:T(8,128)(2,1)} custom-call(bf16[320,448]{1,0:T(8,128)(2,1)} %get-tuple-element.27.refs_0_, bf16[384,3584]{1,0:T(8,128)(2,1)} %get-tuple-element.23.refs_1_, bf16[64,3584]{1,0:T(8,128)(2,1)} %collective-permute-done.2.refs_2_), custom_call_target="tpu_custom_call" | custom-call | flops 5000000000 | tf_op jit(solution)/shard_map/pallas_call | solution.py:60
  64.6 0.7 all-to-all-done.1
  65.3 8.2 %all-to-all-start.2 = ((bf16[8,40,3584]{2,1,0:T(8,128)(2,1)}), bf16[8,40,3584]{2,1,0:T(8,128)(2,1)}, u32[]{:S(2)}, u32[]{:S(2)}) async-start(bf16[8,40,3584]{2,1,0:T(8,128)(2,1)} %bitcast.23), calls=%async_computation.2 | async-start | bytes 4587520 | tf_op jit(solution)/shard_map/all_to_all | solution.py:468
  73.5 20.7 %collective-permute-done.3.refs_2_ = bf16[128,3584]{1,0:T(8,128)(2,1)} collective-permute-done((bf16[128,3584]{1,0:T(8,128)(2,1)}, bf16[128,3584]{1,0:T(8,128)(2,1)}, u32[]{:S(2)}, u32[]{:S(2)}) %collective-permute-start.3) | collective-permute-done | bytes 917536 | tf_op jit(solution)/shard_map/ppermute | solution.py:20
  94.2 4.4 %shard_map.92.refs_3_.refs_0_ = bf16[320,3584]{1,0:T(8,128)(2,1)} custom-call(bf16[320,128]{1,0:T(8,128)(2,1)} %get-tuple-element.24.refs_2_.refs_0_, f32[320,128]{1,0:T(8,128)} %get-tuple-element.25.refs_1_, bf16[128,3584]{1,0:T(8,128)(2,1)} %collective-permute-done.3.refs_2_), custom_call_target="tpu_custom_call" | custom-call | flops 3999999983616 | tf_op jit(solution)/shard_map/pallas_call | solution.py:60
  98.6 5.4 %shard_map.93.refs_2_.refs_0_ = bf16[320,3584]{1,0:T(8,128)(2,1)} custom-call(bf16[320,448]{1,0:T(8,128)(2,1)} %get-tuple-element.21.refs_0_, bf16[384,3584]{1,0:T(8,128)(2,1)} %get-tuple-element.23.refs_1_, bf16[64,3584]{1,0:T(8,128)(2,1)} %collective-permute-done.2.refs_2_, bf16[320,3584]{1,0:T(8,128)(2,1)} %shard_map.92.refs_3_.refs_0_), custom_call_target="tpu_custom_call" | custom-call | tf_op jit(solution)/shard_map/pallas_call | solution.py:60
  104.0 8.0 %all-to-all-done.2 = bf16[8,40,3584]{2,1,0:T(8,128)(2,1)} async-done(((bf16[8,40,3584]{2,1,0:T(8,128)(2,1)}), bf16[8,40,3584]{2,1,0:T(8,128)(2,1)}, u32[]{:S(2)}, u32[]{:S(2)}) %all-to-all-start.2) | async-done | bytes 2293792 | tf_op jit(solution)/shard_map/all_to_all | solution.py:468
  111.9 4.4 %all-to-all-start.3 = ((bf16[8,40,3584]{2,1,0:T(8,128)(2,1)}), bf16[8,40,3584]{2,1,0:T(8,128)(2,1)}, u32[]{:S(2)}, u32[]{:S(2)}) async-start(bf16[8,40,3584]{2,1,0:T(8,128)(2,1)} %bitcast.16), calls=%async_computation.3 | async-start | bytes 4587520 | tf_op jit(solution)/shard_map/all_to_all | solution.py:468
  116.3 4.4 %shard_map.97 = bf16[128,3584]{1,0:T(8,128)(2,1)} custom-call(bf16[256,320]{1,0:T(8,128)(2,1)} %get-tuple-element.26.refs_0_, bf16[320,3584]{1,0:T(8,128)(2,1)} %bitcast.8.refs_1_), custom_call_target="tpu_custom_call" | custom-call | tf_op jit(solution)/shard_map/pallas_call | solution.py:60
  120.7 0.0 collective-permute-start.4
  120.7 36.6 %all-to-all-done.3 = bf16[8,40,3584]{2,1,0:T(8,128)(2,1)} async-done(((bf16[8,40,3584]{2,1,0:T(8,128)(2,1)}), bf16[8,40,3584]{2,1,0:T(8,128)(2,1)}, u32[]{:S(2)}, u32[]{:S(2)}) %all-to-all-start.3) | async-done | bytes 2293792 | tf_op jit(solution)/shard_map/all_to_all | solution.py:468
  157.3 4.7 %shard_map.99.refs_2_.refs_4_ = bf16[64,3584]{1,0:T(8,128)(2,1)} custom-call(bf16[448,320]{1,0:T(8,128)(2,1)} %get-tuple-element.29.refs_0_, bf16[448,320]{1,0:T(8,128)(2,1)} %get-tuple-element.30.refs_1_, bf16[320,3584]{1,0:T(8,128)(2,1)} %bitcast.6.refs_1_.refs_2_, bf16[320,3584]{1,0:T(8,128)(2,1)} %bitcast.10.refs_3_), custom_call_target="tpu_custom_call" | custom-call | tf_op jit(solution)/shard_map/pallas_call | solution.py:60
  162.0 0.0 collective-permute-start.5
  162.0 0.0 collective-permute-done.4.refs_1_.refs_2_
  162.0 5.8 %all-to-all-start.4 = ((bf16[8,40,3584]{2,1,0:T(8,128)(2,1)}), bf16[8,40,3584]{2,1,0:T(8,128)(2,1)}, u32[]{:S(2)}, u32[]{:S(2)}) async-start(bf16[8,40,3584]{2,1,0:T(8,128)(2,1)} %bitcast.15), calls=%async_computation.4 | async-start | bytes 4587520 | tf_op jit(solution)/shard_map/all_to_all | solution.py:468
  167.8 0.0 collective-permute-start.7
  167.8 6.7 %shard_map.102.refs_0_.refs_2_ = bf16[384,3584]{1,0:T(8,128)(2,1)} custom-call(bf16[448,320]{1,0:T(8,128)(2,1)} %get-tuple-element.29.refs_0_, bf16[448,320]{1,0:T(8,128)(2,1)} %get-tuple-element.30.refs_1_, bf16[320,3584]{1,0:T(8,128)(2,1)} %bitcast.6.refs_1_.refs_2_, bf16[320,3584]{1,0:T(8,128)(2,1)} %bitcast.10.refs_3_, ...), custom_call_target="tpu_custom_call" | custom-call | tf_op jit(solution)/shard_map/pallas_call | solution.py:60
  174.5 0.5 collective-permute-start.8
  175.0 4.5 %collective-permute-done.5.refs_1_.refs_3_ = bf16[64,3584]{1,0:T(8,128)(2,1)} collective-permute-done((bf16[64,3584]{1,0:T(8,128)(2,1)}, bf16[64,3584]{1,0:T(8,128)(2,1)}, u32[]{:S(2)}, u32[]{:S(2)}) %collective-permute-start.5) | collective-permute-done | bytes 458784 | tf_op jit(solution)/shard_map/ppermute | solution.py:20
  179.4 0.0 collective-permute-start.9
  179.4 8.3 %shard_map.103 = (bf16[448,1024]{1,0:T(8,128)(2,1)}, bf16[64,1024]{1,0:T(8,128)(2,1)}) custom-call(bf16[384,3584]{1,0:T(8,128)(2,1)} %shard_map.102.refs_0_.refs_2_, bf16[64,3584]{1,0:T(8,128)(2,1)} %collective-permute-done.5.refs_1_.refs_3_, bf16[512,3584]{1,0:T(8,128)(2,1)} %bitcast.20, bf16[512,3584]{1,0:T(8,128)(2,1)} %collective-permute-done.1.refs_2_.refs_3_), custom_call_target="tpu_custom_call" | custom-call | flops 40000000000 | tf_op jit(solution)/shard_map/pallas_call | solution.py:60
  187.7 0.0 collective-permute-start.6
  187.7 0.0 collective-permute-done.7.refs_1_
  187.7 0.0 collective-permute-done.9.refs_5_
  187.7 0.0 collective-permute-done.8.refs_4_
  187.8 8.4 %shard_map.104.refs_2_ = bf16[512,3584]{1,0:T(8,128)(2,1)} custom-call(bf16[512,448]{1,0:T(8,128)(2,1)} %get-tuple-element.33.refs_0_, bf16[512,448]{1,0:T(8,128)(2,1)} %collective-permute-done.7.refs_1_, bf16[384,3584]{1,0:T(8,128)(2,1)} %shard_map.102.refs_0_.refs_2_, bf16[64,3584]{1,0:T(8,128)(2,1)} %collective-permute-done.5.refs_1_.refs_3_, ...), custom_call_target="tpu_custom_call" | custom-call | tf_op jit(solution)/shard_map/pallas_call | solution.py:60
  196.1 0.0 collective-permute-done.6.refs_1_
  196.1 1.6 shard_map.105
  197.7 4.2 %all-to-all-done.4 = bf16[8,40,3584]{2,1,0:T(8,128)(2,1)} async-done(((bf16[8,40,3584]{2,1,0:T(8,128)(2,1)}), bf16[8,40,3584]{2,1,0:T(8,128)(2,1)}, u32[]{:S(2)}, u32[]{:S(2)}) %all-to-all-start.4) | async-done | bytes 2293792 | tf_op jit(solution)/shard_map/all_to_all | solution.py:468
  201.8 4.5 %shard_map.101 = bf16[128,3584]{1,0:T(8,128)(2,1)} custom-call(bf16[256,320]{1,0:T(8,128)(2,1)} %get-tuple-element.20.refs_3_.refs_0_, bf16[320,3584]{1,0:T(8,128)(2,1)} %bitcast.12.refs_1_, bf16[128,3584]{1,0:T(8,128)(2,1)} %collective-permute-done.4.refs_1_.refs_2_), custom_call_target="tpu_custom_call" | custom-call | tf_op jit(solution)/shard_map/pallas_call | solution.py:60
  (5 shorter events, 0.0 us)
Async XLA Ops:
  0.6 18.3 %collective-permute-start.1 = (bf16[512,3584]{1,0:T(8,128)(2,1)}, bf16[512,3584]{1,0:T(8,128)(2,1)}, u32[]{:S(2)}, u32[]{:S(2)}) collective-permute-start(bf16[512,3584]{1,0:T(8,128)(2,1)} %bitcast.17), channel_id=1, source_target_pairs={{0,16},{16,0},{1,17},{17,1},{2,18},{18,2},{3,19},{19,3},{4,20},{20... | collective-permute-start | bytes 11010056 | tf_op jit(solution)/shard_map/ppermute | solution.py:20
  2.8 16.1 %collective-permute-start = (bf16[64,1024]{1,0:T(8,128)(2,1)}, bf16[64,1024]{1,0:T(8,128)(2,1)}, u32[]{:S(2)}, u32[]{:S(2)}) collective-permute-start(bf16[64,1024]{1,0:T(8,128)(2,1)} %get-tuple-element.22), channel_id=1, source_target_pairs={{0,8},{1,9},{2,10},{3,11},{4,12},{5,13},{6,14},{7,15},{8,0},{9,1},... | collective-permute-start | bytes 393224 | tf_op jit(solution)/shard_map/ppermute | solution.py:20
  6.4 12.5 %all-to-all-start = ((f32[16,8,128]{2,1,0:T(8,128)}), f32[16,8,128]{2,1,0:T(8,128)}, u32[]{:S(2)}, u32[]{:S(2)}) async-start(f32[16,8,128]{2,1,0:T(8,128)} %get-tuple-element.19.refs_0_), calls=%async_computation | async-start | bytes 131072 | tf_op jit(solution)/shard_map/all_to_all | solution.py:477
  18.9 46.4 %all-to-all-start.1 = ((bf16[8,40,3584]{2,1,0:T(8,128)(2,1)}), bf16[8,40,3584]{2,1,0:T(8,128)(2,1)}, u32[]{:S(2)}, u32[]{:S(2)}) async-start(bf16[8,40,3584]{2,1,0:T(8,128)(2,1)} %bitcast.22), calls=%async_computation.1 | async-start | bytes 4587520 | tf_op jit(solution)/shard_map/all_to_all | solution.py:468
  28.5 30.7 %collective-permute-start.2 = (bf16[64,3584]{1,0:T(8,128)(2,1)}, bf16[64,3584]{1,0:T(8,128)(2,1)}, u32[]{:S(2)}, u32[]{:S(2)}) collective-permute-start(bf16[64,3584]{1,0:T(8,128)(2,1)} %shard_map.88.refs_4_), channel_id=1, source_target_pairs={{0,8},{1,9},{2,10},{3,11},{4,12},{5,13},{6,14},{7,15},{8,0},{9,1},... | collective-permute-start | bytes 1376264 | tf_op jit(solution)/shard_map/ppermute | solution.py:20
  42.0 52.2 %collective-permute-start.3 = (bf16[128,3584]{1,0:T(8,128)(2,1)}, bf16[128,3584]{1,0:T(8,128)(2,1)}, u32[]{:S(2)}, u32[]{:S(2)}) collective-permute-start(bf16[128,3584]{1,0:T(8,128)(2,1)} %shard_map.91), channel_id=1, source_target_pairs={{0,8},{1,9},{2,10},{3,11},{4,12},{5,13},{6,14},{7,15},{8,0},{9,1},... | collective-permute-start | bytes 2752520 | tf_op jit(solution)/shard_map/ppermute | solution.py:20
  65.3 46.6 %all-to-all-start.2 = ((bf16[8,40,3584]{2,1,0:T(8,128)(2,1)}), bf16[8,40,3584]{2,1,0:T(8,128)(2,1)}, u32[]{:S(2)}, u32[]{:S(2)}) async-start(bf16[8,40,3584]{2,1,0:T(8,128)(2,1)} %bitcast.23), calls=%async_computation.2 | async-start | bytes 4587520 | tf_op jit(solution)/shard_map/all_to_all | solution.py:468
  111.9 45.4 %all-to-all-start.3 = ((bf16[8,40,3584]{2,1,0:T(8,128)(2,1)}), bf16[8,40,3584]{2,1,0:T(8,128)(2,1)}, u32[]{:S(2)}, u32[]{:S(2)}) async-start(bf16[8,40,3584]{2,1,0:T(8,128)(2,1)} %bitcast.16), calls=%async_computation.3 | async-start | bytes 4587520 | tf_op jit(solution)/shard_map/all_to_all | solution.py:468
  120.7 41.3 %collective-permute-start.4 = (bf16[128,3584]{1,0:T(8,128)(2,1)}, bf16[128,3584]{1,0:T(8,128)(2,1)}, u32[]{:S(2)}, u32[]{:S(2)}) collective-permute-start(bf16[128,3584]{1,0:T(8,128)(2,1)} %shard_map.97), channel_id=1, source_target_pairs={{0,8},{1,9},{2,10},{3,11},{4,12},{5,13},{6,14},{7,15},{8,0},{9,1},... | collective-permute-start | bytes 2752520 | tf_op jit(solution)/shard_map/ppermute | solution.py:20
  162.0 17.4 %collective-permute-start.5 = (bf16[64,3584]{1,0:T(8,128)(2,1)}, bf16[64,3584]{1,0:T(8,128)(2,1)}, u32[]{:S(2)}, u32[]{:S(2)}) collective-permute-start(bf16[64,3584]{1,0:T(8,128)(2,1)} %shard_map.99.refs_2_.refs_4_), channel_id=1, source_target_pairs={{0,8},{1,9},{2,10},{3,11},{4,12},{5,13},{6,14},{7,15},{8,0},{9,1},... | collective-permute-start | bytes 1376264 | tf_op jit(solution)/shard_map/ppermute | solution.py:20
  162.0 39.8 %all-to-all-start.4 = ((bf16[8,40,3584]{2,1,0:T(8,128)(2,1)}), bf16[8,40,3584]{2,1,0:T(8,128)(2,1)}, u32[]{:S(2)}, u32[]{:S(2)}) async-start(bf16[8,40,3584]{2,1,0:T(8,128)(2,1)} %bitcast.15), calls=%async_computation.4 | async-start | bytes 4587520 | tf_op jit(solution)/shard_map/all_to_all | solution.py:468
  167.8 19.9 %collective-permute-start.7 = (bf16[512,448]{1,0:T(8,128)(2,1)}, bf16[512,448]{1,0:T(8,128)(2,1)}, u32[]{:S(2)}, u32[]{:S(2)}) collective-permute-start(bf16[512,448]{1,0:T(8,128)(2,1)} %get-tuple-element.34), channel_id=1, source_target_pairs={{0,16},{16,0},{1,17},{17,1},{2,18},{18,2},{3,19},{19,3},{4,20},{20... | collective-permute-start | bytes 1376264 | tf_op jit(solution)/shard_map/ppermute | solution.py:20
  174.5 13.2 %collective-permute-start.8 = (bf16[384,3584]{1,0:T(8,128)(2,1)}, bf16[384,3584]{1,0:T(8,128)(2,1)}, u32[]{:S(2)}, u32[]{:S(2)}) collective-permute-start(bf16[384,3584]{1,0:T(8,128)(2,1)} %shard_map.102.refs_0_.refs_2_), channel_id=1, source_target_pairs={{0,16},{16,0},{1,17},{17,1},{2,18},{18,2},{3,19},{19,3},{4,20},{20... | collective-permute-start | bytes 8257544 | tf_op jit(solution)/shard_map/ppermute | solution.py:20
  179.4 8.3 %collective-permute-start.9 = (bf16[64,3584]{1,0:T(8,128)(2,1)}, bf16[64,3584]{1,0:T(8,128)(2,1)}, u32[]{:S(2)}, u32[]{:S(2)}) collective-permute-start(bf16[64,3584]{1,0:T(8,128)(2,1)} %collective-permute-done.5.refs_1_.refs_3_), channel_id=1, source_target_pairs={{0,16},{16,0},{1,17},{17,1},{2,18},{18,2},{3,19},{19,3},{4,20},{20... | collective-permute-start | bytes 1376264 | tf_op jit(solution)/shard_map/ppermute | solution.py:20
  187.7 8.4 %collective-permute-start.6 = (bf16[64,1024]{1,0:T(8,128)(2,1)}, bf16[64,1024]{1,0:T(8,128)(2,1)}, u32[]{:S(2)}, u32[]{:S(2)}) collective-permute-start(bf16[64,1024]{1,0:T(8,128)(2,1)} %get-tuple-element.32), channel_id=1, source_target_pairs={{0,8},{1,9},{2,10},{3,11},{4,12},{5,13},{6,14},{7,15},{8,0},{9,1},... | collective-permute-start | bytes 393224 | tf_op jit(solution)/shard_map/ppermute | solution.py:20

commit v7 on v6

--- a/solution.py
+++ b/solution.py
@@ -11,6 +11,7 @@
 LONG = 4_000_000_000_000
 GIVE_COST = 5_000_000_000
 BACK_COST = 40_000_000_000
+HEAD_COST = 5_000_000_000
 VMEM_LIMIT = 64 * 1024 * 1024 - 65536
 
 
@@ -120,9 +121,9 @@
     pass
 
 
-def touched(array, *after):
+def touched(array, *after, cost=0):
     shape = jax.ShapeDtypeStruct(array.shape, array.dtype)
-    return call(touch_kernel, 1, [(array, anywhere())], (shape, anywhere()), (), after, {0: 0})
+    return call(touch_kernel, 1, [(array, anywhere())], (shape, anywhere()), (), after, {0: 0}, cost)
 
 
 def plan_rows(meta, cap, half, sel_ref, gate_ref, mix_ref):
@@ -333,6 +334,35 @@
     )
 
 
+def give_main_kernel(slot_ref, main_ref, out_ref):
+    out_ref[...] = dot(slot_ref[:, : main_ref.shape[0]], main_ref[...]).astype(BF16)
+
+
+def give_main(slot, out_main, tile):
+    rows, width = slot.shape[0], out_main.shape[1]
+    return call(
+        give_main_kernel,
+        width // tile,
+        entire(slot) + by_columns(tile, out_main),
+        by_columns(tile, bf16(rows, width))[0],
+    )
+
+
+def give_rest_kernel(slot_ref, given_ref, spare_ref, out_ref):
+    rest = dot(slot_ref[:, slot_ref.shape[1] - spare_ref.shape[0] :], spare_ref[...])
+    out_ref[...] = given_ref[...] + rest.astype(BF16)
+
+
+def give_rest(slot, given, out_spare, tile, cost):
+    return call(
+        give_rest_kernel,
+        given.shape[1] // tile,
+        entire(slot) + by_columns(tile, given, out_spare),
+        by_columns(tile, bf16(*given.shape))[0],
+        cost=cost,
+    )
+
+
 def take_kernel(first, own_slot, mirror_slot, own_ref, mirror_ref, out_ref):
     rows = pl.ds(first, out_ref.shape[0])
     total = dot(own_slot[rows, :], own_ref[...]) + dot(mirror_slot[rows, :], mirror_ref[...])
@@ -461,7 +491,7 @@
     hidden = hidden_saved[0, 0]
     near = down_weight[0]
     slots = hidden.shape[0]
-    tile = width // 4
+    tile = width // 2
     groups = [list(range(half)), list(range(half, count))]
 
     def to_half(rows):
@@ -476,16 +506,17 @@
     spare_hidden = swapped(spare_hidden, "expert", half)
     metas = lax.all_to_all(meta, "expert", 0, 0, tiled=True)
     packed_own, mix_own = pack_own(meta, grad_out, cap, half, tile)
-    arrived_own = to_half(touched(packed_own, metas, spare_hidden, far))
+    arrived_own = to_half(touched(touched(packed_own, metas, cost=HEAD_COST), spare_hidden, far))
     out_spare = project_spare(spare_hidden, near, far, tile, mix_own)
     sel, gate, mix_mirror, give_own, take_own, give_mirror, take_mirror = plan(
         metas, cap, half, main, slots
     )
     out_main, turned, far_turned = project(hidden, spare_hidden, near, far, tile, out_spare)
     out_spare = swapped(out_spare, "expert", half)
-    mirror = swapped(touched(copied(grad_out, width // 2), out_main, sel), "expert", half)
+    given_main = give_main(give_mirror, out_main, tile)
+    mirror = swapped(touched(copied(grad_out, tile), out_main, sel), "expert", half)
     other_turned = swapped(far_turned, "dp", 1)
-    given_mirror = give(give_mirror, out_main, out_spare, tile, GIVE_COST)
+    given_mirror = give_rest(give_mirror, given_main, out_spare, tile, GIVE_COST)
     returned_mirror = to_half(touched(given_mirror, arrived_own))
     packed_mirror = pack(sel, gate, mirror, tile)
     given_own = give(give_own, out_main, out_spare, tile, 0, packed_mirror)

time: 208 us -> 213 us (1.024)
  waiting for transfers between devices: 92.5 us -> 107 us
  Pallas kernels: 78 us -> 70.1 us
    all_to_all x4, waiting for transfers between devices: 49.4 us -> 61 us  [to_half(): lax.all_to_all(rows.reshape(half, cap, width), 'expert', 0, 0, axis_index...]
    pallas_call x21 -> x23, Pallas kernels: 78 us -> 70.1 us  [call(): pl.pallas_call(kernel, grid=(grid,), in_specs=[spec for _, spec in ins] +...]
    ppermute x10, waiting for transfers between devices: 40.2 us -> 44.1 us  [swapped(): return lax.ppermute(value, axis, pairs)]
    all_to_all x4, starting transfers between devices: 22.8 us -> 19.7 us  [to_half(): lax.all_to_all(rows.reshape(half, cap, width), 'expert', 0, 0, axis_index...]
    all_to_all x1, starting transfers between devices: 4.89 us -> 7.93 us  [local(): metas = lax.all_to_all(meta, 'expert', 0, 0, tiled=True)]
  transfers between devices with their start and end apart: 15 -> 15, of which waited for: 8 -> 10; matrix products, arithmetic and copies ran while one was open for 0% -> 0% of each run, Pallas kernels for 36% -> 31%
where the time goes in v7:
time: 213 us; the launch traced here: 212 us
  waiting for transfers between devices  107 us (50%)
  Pallas kernels  70.1 us (33%)
  starting transfers between devices  34.5 us (16%)
    pallas_call x23, Pallas kernels, call(): pl.pallas_call(kernel, grid=(grid,), in_specs=[spec for _, spec in ins] +...  70.1 us
    all_to_all x4, waiting for transfers between devices, to_half(): lax.all_to_all(rows.reshape(half, cap, width), 'expert', 0, 0, axis_index...  61 us
    ppermute x10, waiting for transfers between devices, swapped(): return lax.ppermute(value, axis, pairs)  44.1 us
    all_to_all x4, starting transfers between devices, to_half(): lax.all_to_all(rows.reshape(half, cap, width), 'expert', 0, 0, axis_index...  19.7 us
    all_to_all x1, starting transfers between devices, local(): metas = lax.all_to_all(meta, 'expert', 0, 0, tiled=True)  7.93 us
    ppermute x10, starting transfers between devices, swapped(): return lax.ppermute(value, axis, pairs)  6.91 us
  transfers between devices with their start and end apart: 15, of which 10 were waited for; matrix products, arithmetic and copies ran while one was open for 0% of the time, Pallas kernels for 31%

profile of v7, /device:TPU:0, one launch (start us, length us, event | category | flops | bytes accessed | tf_op | source)
XLA Modules:
  0.0 212.0 jit_solution(4142461071668645258)
XLA Ops:
  0.6 0.5 collective-permute-start.1
  1.1 1.6 shard_map.85
  2.8 7.9 %all-to-all-start = ((f32[16,8,128]{2,1,0:T(8,128)}), f32[16,8,128]{2,1,0:T(8,128)}, u32[]{:S(2)}, u32[]{:S(2)}) async-start(f32[16,8,128]{2,1,0:T(8,128)} %get-tuple-element.19.refs_0_), calls=%async_computation | async-start | bytes 131072 | tf_op jit(solution)/shard_map/all_to_all | solution.py:507
  10.7 2.8 %collective-permute-start = (bf16[64,1024]{1,0:T(8,128)(2,1)}, bf16[64,1024]{1,0:T(8,128)(2,1)}, u32[]{:S(2)}, u32[]{:S(2)}) collective-permute-start(bf16[64,1024]{1,0:T(8,128)(2,1)} %get-tuple-element.22), channel_id=1, source_target_pairs={{0,8},{1,9},{2,10},{3,11},{4,12},{5,13},{6,14},{7,15},{8,0},{9,1},... | collective-permute-start | bytes 393224 | tf_op jit(solution)/shard_map/ppermute | solution.py:21
  13.5 3.5 %shard_map.86 = (bf16[320,3584]{1,0:T(8,128)(2,1)}, bf16[256,320]{1,0:T(8,128)(2,1)}) custom-call(f32[16,8,128]{2,1,0:T(8,128)} %get-tuple-element.19.refs_0_, bf16[128,3584]{1,0:T(8,128)(2,1)} %refs_0_.1), custom_call_target="tpu_custom_call" | custom-call | tf_op jit(solution)/shard_map/pallas_call | solution.py:61
  17.0 1.5 all-to-all-done.refs_0_.refs_1_
  18.5 3.1 %collective-permute-done.refs_0_.refs_1_ = bf16[64,1024]{1,0:T(8,128)(2,1)} collective-permute-done((bf16[64,1024]{1,0:T(8,128)(2,1)}, bf16[64,1024]{1,0:T(8,128)(2,1)}, u32[]{:S(2)}, u32[]{:S(2)}) %collective-permute-start) | collective-permute-done | bytes 131104 | tf_op jit(solution)/shard_map/ppermute | solution.py:21
  21.6 0.0 collective-permute-done.1.refs_2_.refs_3_
  21.6 4.4 %all-to-all-start.1 = ((bf16[8,40,3584]{2,1,0:T(8,128)(2,1)}), bf16[8,40,3584]{2,1,0:T(8,128)(2,1)}, u32[]{:S(2)}, u32[]{:S(2)}) async-start(bf16[8,40,3584]{2,1,0:T(8,128)(2,1)} %bitcast.22), calls=%async_computation.1 | async-start | bytes 4587520 | tf_op jit(solution)/shard_map/all_to_all | solution.py:498
  26.0 4.7 %shard_map.88.refs_4_ = bf16[64,3584]{1,0:T(8,128)(2,1)} custom-call(bf16[64,1024]{1,0:T(8,128)(2,1)} %collective-permute-done.refs_0_.refs_1_, bf16[512,3584]{1,0:T(8,128)(2,1)} %bitcast.18, bf16[512,3584]{1,0:T(8,128)(2,1)} %collective-permute-done.1.refs_2_.refs_3_, bf16[256,320]{1,0:T(8,128)(2,1)} %get-tuple-element.20.refs_3_.refs_0_), custom_call_target="tpu_custom_call" | custom-call | tf_op jit(solution)/shard_map/pallas_call | solution.py:61
  30.7 1.4 collective-permute-start.2
  32.1 2.0 shard_map.90.refs_0_
  34.1 2.9 %shard_map.87 = (bf16[320,128]{1,0:T(8,128)(2,1)}, f32[320,128]{1,0:T(8,128)}, bf16[256,320]{1,0:T(8,128)(2,1)}, bf16[320,448]{1,0:T(8,128)(2,1)}, bf16[448,320]...) custom-call(f32[16,8,128]{2,1,0:T(8,128)} %all-to-all-done.refs_0_.refs_1_), custom_call_target="tpu_custom_call" | custom-call | tf_op jit(solution)/shard_map/pallas_call | solution.py:61
  36.9 7.0 %shard_map.89 = (bf16[384,3584]{1,0:T(8,128)(2,1)}, bf16[512,448]{1,0:T(8,128)(2,1)}, bf16[512,448]{1,0:T(8,128)(2,1)}) custom-call(bf16[448,1024]{1,0:T(8,128)(2,1)} %bitcast.25, bf16[64,1024]{1,0:T(8,128)(2,1)} %collective-permute-done.refs_0_.refs_1_, bf16[512,3584]{1,0:T(8,128)(2,1)} %bitcast.19, ...), custom_call_target="tpu_custom_call" | custom-call | tf_op jit(solution)/shard_map/pallas_call | solution.py:61
  43.9 1.5 collective-permute-start.3
  45.5 4.0 %shard_map.94.refs_1_ = bf16[320,3584]{1,0:T(8,128)(2,1)} custom-call(bf16[320,448]{1,0:T(8,128)(2,1)} %get-tuple-element.27.refs_0_, bf16[384,3584]{1,0:T(8,128)(2,1)} %get-tuple-element.23.refs_1_), custom_call_target="tpu_custom_call" | custom-call | tf_op jit(solution)/shard_map/pallas_call | solution.py:61
  49.4 12.5 %collective-permute-done.2.refs_2_ = bf16[64,3584]{1,0:T(8,128)(2,1)} collective-permute-done((bf16[64,3584]{1,0:T(8,128)(2,1)}, bf16[64,3584]{1,0:T(8,128)(2,1)}, u32[]{:S(2)}, u32[]{:S(2)}) %collective-permute-start.2) | collective-permute-done | bytes 458784 | tf_op jit(solution)/shard_map/ppermute | solution.py:21
  62.0 3.4 %shard_map.95.refs_0_ = bf16[320,3584]{1,0:T(8,128)(2,1)} custom-call(bf16[320,448]{1,0:T(8,128)(2,1)} %get-tuple-element.27.refs_0_, bf16[320,3584]{1,0:T(8,128)(2,1)} %shard_map.94.refs_1_, bf16[64,3584]{1,0:T(8,128)(2,1)} %collective-permute-done.2.refs_2_), custom_call_target="tpu_custom_call" | custom-call | flops 5000000000 | tf_op jit(solution)/shard_map/pallas_call | solution.py:61
  65.3 4.8 %all-to-all-done.1 = bf16[8,40,3584]{2,1,0:T(8,128)(2,1)} async-done(((bf16[8,40,3584]{2,1,0:T(8,128)(2,1)}), bf16[8,40,3584]{2,1,0:T(8,128)(2,1)}, u32[]{:S(2)}, u32[]{:S(2)}) %all-to-all-start.1) | async-done | bytes 2293792 | tf_op jit(solution)/shard_map/all_to_all | solution.py:498
  70.1 6.4 %all-to-all-start.2 = ((bf16[8,40,3584]{2,1,0:T(8,128)(2,1)}), bf16[8,40,3584]{2,1,0:T(8,128)(2,1)}, u32[]{:S(2)}, u32[]{:S(2)}) async-start(bf16[8,40,3584]{2,1,0:T(8,128)(2,1)} %bitcast.23), calls=%async_computation.2 | async-start | bytes 4587520 | tf_op jit(solution)/shard_map/all_to_all | solution.py:498
  76.5 20.0 %collective-permute-done.3.refs_2_ = bf16[128,3584]{1,0:T(8,128)(2,1)} collective-permute-done((bf16[128,3584]{1,0:T(8,128)(2,1)}, bf16[128,3584]{1,0:T(8,128)(2,1)}, u32[]{:S(2)}, u32[]{:S(2)}) %collective-permute-start.3) | collective-permute-done | bytes 917536 | tf_op jit(solution)/shard_map/ppermute | solution.py:21
  96.5 3.1 %shard_map.92.refs_3_.refs_0_ = bf16[320,3584]{1,0:T(8,128)(2,1)} custom-call(bf16[320,128]{1,0:T(8,128)(2,1)} %get-tuple-element.24.refs_2_.refs_0_, f32[320,128]{1,0:T(8,128)} %get-tuple-element.25.refs_1_, bf16[128,3584]{1,0:T(8,128)(2,1)} %collective-permute-done.3.refs_2_), custom_call_target="tpu_custom_call" | custom-call | flops 3999999983616 | tf_op jit(solution)/shard_map/pallas_call | solution.py:61
  99.6 4.7 %shard_map.93.refs_2_.refs_0_ = bf16[320,3584]{1,0:T(8,128)(2,1)} custom-call(bf16[320,448]{1,0:T(8,128)(2,1)} %get-tuple-element.21.refs_0_, bf16[384,3584]{1,0:T(8,128)(2,1)} %get-tuple-element.23.refs_1_, bf16[64,3584]{1,0:T(8,128)(2,1)} %collective-permute-done.2.refs_2_, bf16[320,3584]{1,0:T(8,128)(2,1)} %shard_map.92.refs_3_.refs_0_), custom_call_target="tpu_custom_call" | custom-call | tf_op jit(solution)/shard_map/pallas_call | solution.py:61
  104.2 10.8 %all-to-all-done.2 = bf16[8,40,3584]{2,1,0:T(8,128)(2,1)} async-done(((bf16[8,40,3584]{2,1,0:T(8,128)(2,1)}), bf16[8,40,3584]{2,1,0:T(8,128)(2,1)}, u32[]{:S(2)}, u32[]{:S(2)}) %all-to-all-start.2) | async-done | bytes 2293792 | tf_op jit(solution)/shard_map/all_to_all | solution.py:498
  115.0 4.4 %all-to-all-start.3 = ((bf16[8,40,3584]{2,1,0:T(8,128)(2,1)}), bf16[8,40,3584]{2,1,0:T(8,128)(2,1)}, u32[]{:S(2)}, u32[]{:S(2)}) async-start(bf16[8,40,3584]{2,1,0:T(8,128)(2,1)} %bitcast.16), calls=%async_computation.3 | async-start | bytes 4587520 | tf_op jit(solution)/shard_map/all_to_all | solution.py:498
  119.3 3.3 %shard_map.99 = bf16[128,3584]{1,0:T(8,128)(2,1)} custom-call(bf16[256,320]{1,0:T(8,128)(2,1)} %get-tuple-element.26.refs_0_, bf16[320,3584]{1,0:T(8,128)(2,1)} %bitcast.8.refs_1_), custom_call_target="tpu_custom_call" | custom-call | tf_op jit(solution)/shard_map/pallas_call | solution.py:61
  122.7 0.1 collective-permute-start.4
  122.8 41.0 %all-to-all-done.3 = bf16[8,40,3584]{2,1,0:T(8,128)(2,1)} async-done(((bf16[8,40,3584]{2,1,0:T(8,128)(2,1)}), bf16[8,40,3584]{2,1,0:T(8,128)(2,1)}, u32[]{:S(2)}, u32[]{:S(2)}) %all-to-all-start.3) | async-done | bytes 2293792 | tf_op jit(solution)/shard_map/all_to_all | solution.py:498
  163.9 3.7 %shard_map.101.refs_2_.refs_4_ = bf16[64,3584]{1,0:T(8,128)(2,1)} custom-call(bf16[448,320]{1,0:T(8,128)(2,1)} %get-tuple-element.29.refs_0_, bf16[448,320]{1,0:T(8,128)(2,1)} %get-tuple-element.30.refs_1_, bf16[320,3584]{1,0:T(8,128)(2,1)} %bitcast.6.refs_1_.refs_2_, bf16[320,3584]{1,0:T(8,128)(2,1)} %bitcast.10.refs_3_), custom_call_target="tpu_custom_call" | custom-call | tf_op jit(solution)/shard_map/pallas_call | solution.py:61
  167.6 0.0 collective-permute-start.5
  167.6 0.0 collective-permute-done.4.refs_1_.refs_2_
  167.6 4.6 %all-to-all-start.4 = ((bf16[8,40,3584]{2,1,0:T(8,128)(2,1)}), bf16[8,40,3584]{2,1,0:T(8,128)(2,1)}, u32[]{:S(2)}, u32[]{:S(2)}) async-start(bf16[8,40,3584]{2,1,0:T(8,128)(2,1)} %bitcast.15), calls=%async_computation.4 | async-start | bytes 4587520 | tf_op jit(solution)/shard_map/all_to_all | solution.py:498
  172.1 0.1 collective-permute-start.7
  172.2 6.1 %shard_map.104.refs_0_.refs_2_ = bf16[384,3584]{1,0:T(8,128)(2,1)} custom-call(bf16[448,320]{1,0:T(8,128)(2,1)} %get-tuple-element.29.refs_0_, bf16[448,320]{1,0:T(8,128)(2,1)} %get-tuple-element.30.refs_1_, bf16[320,3584]{1,0:T(8,128)(2,1)} %bitcast.6.refs_1_.refs_2_, bf16[320,3584]{1,0:T(8,128)(2,1)} %bitcast.10.refs_3_, ...), custom_call_target="tpu_custom_call" | custom-call | tf_op jit(solution)/shard_map/pallas_call | solution.py:61
  178.3 0.5 collective-permute-start.8
  178.8 7.9 %collective-permute-done.5.refs_1_.refs_3_ = bf16[64,3584]{1,0:T(8,128)(2,1)} collective-permute-done((bf16[64,3584]{1,0:T(8,128)(2,1)}, bf16[64,3584]{1,0:T(8,128)(2,1)}, u32[]{:S(2)}, u32[]{:S(2)}) %collective-permute-start.5) | collective-permute-done | bytes 458784 | tf_op jit(solution)/shard_map/ppermute | solution.py:21
  186.7 0.0 collective-permute-start.9
  186.7 7.5 %shard_map.105 = (bf16[448,1024]{1,0:T(8,128)(2,1)}, bf16[64,1024]{1,0:T(8,128)(2,1)}) custom-call(bf16[384,3584]{1,0:T(8,128)(2,1)} %shard_map.104.refs_0_.refs_2_, bf16[64,3584]{1,0:T(8,128)(2,1)} %collective-permute-done.5.refs_1_.refs_3_, bf16[512,3584]{1,0:T(8,128)(2,1)} %bitcast.20, bf16[512,3584]{1,0:T(8,128)(2,1)} %collective-permute-done.1.refs_2_.refs_3_), custom_call_target="tpu_custom_call" | custom-call | flops 40000000000 | tf_op jit(solution)/shard_map/pallas_call | solution.py:61
  194.2 0.0 collective-permute-start.6
  194.2 0.0 collective-permute-done.7.refs_1_
  194.2 0.0 collective-permute-done.9.refs_5_
  194.2 0.0 collective-permute-done.8.refs_4_
  194.2 7.7 %shard_map.106.refs_2_ = bf16[512,3584]{1,0:T(8,128)(2,1)} custom-call(bf16[512,448]{1,0:T(8,128)(2,1)} %get-tuple-element.33.refs_0_, bf16[512,448]{1,0:T(8,128)(2,1)} %collective-permute-done.7.refs_1_, bf16[384,3584]{1,0:T(8,128)(2,1)} %shard_map.104.refs_0_.refs_2_, bf16[64,3584]{1,0:T(8,128)(2,1)} %collective-permute-done.5.refs_1_.refs_3_, ...), custom_call_target="tpu_custom_call" | custom-call | tf_op jit(solution)/shard_map/pallas_call | solution.py:61
  202.0 0.6 collective-permute-done.6.refs_1_
  202.6 1.6 shard_map.107
  204.1 4.4 %all-to-all-done.4 = bf16[8,40,3584]{2,1,0:T(8,128)(2,1)} async-done(((bf16[8,40,3584]{2,1,0:T(8,128)(2,1)}), bf16[8,40,3584]{2,1,0:T(8,128)(2,1)}, u32[]{:S(2)}, u32[]{:S(2)}) %all-to-all-start.4) | async-done | bytes 2293792 | tf_op jit(solution)/shard_map/all_to_all | solution.py:498
  208.5 3.5 %shard_map.103 = bf16[128,3584]{1,0:T(8,128)(2,1)} custom-call(bf16[256,320]{1,0:T(8,128)(2,1)} %get-tuple-element.20.refs_3_.refs_0_, bf16[320,3584]{1,0:T(8,128)(2,1)} %bitcast.12.refs_1_, bf16[128,3584]{1,0:T(8,128)(2,1)} %collective-permute-done.4.refs_1_.refs_2_), custom_call_target="tpu_custom_call" | custom-call | tf_op jit(solution)/shard_map/pallas_call | solution.py:61
  (6 shorter events, 0.0 us)
Async XLA Ops:
  0.6 21.0 %collective-permute-start.1 = (bf16[512,3584]{1,0:T(8,128)(2,1)}, bf16[512,3584]{1,0:T(8,128)(2,1)}, u32[]{:S(2)}, u32[]{:S(2)}) collective-permute-start(bf16[512,3584]{1,0:T(8,128)(2,1)} %bitcast.17), channel_id=1, source_target_pairs={{0,16},{16,0},{1,17},{17,1},{2,18},{18,2},{3,19},{19,3},{4,20},{20... | collective-permute-start | bytes 11010056 | tf_op jit(solution)/shard_map/ppermute | solution.py:21
  2.8 15.8 %all-to-all-start = ((f32[16,8,128]{2,1,0:T(8,128)}), f32[16,8,128]{2,1,0:T(8,128)}, u32[]{:S(2)}, u32[]{:S(2)}) async-start(f32[16,8,128]{2,1,0:T(8,128)} %get-tuple-element.19.refs_0_), calls=%async_computation | async-start | bytes 131072 | tf_op jit(solution)/shard_map/all_to_all | solution.py:507
  10.7 10.9 %collective-permute-start = (bf16[64,1024]{1,0:T(8,128)(2,1)}, bf16[64,1024]{1,0:T(8,128)(2,1)}, u32[]{:S(2)}, u32[]{:S(2)}) collective-permute-start(bf16[64,1024]{1,0:T(8,128)(2,1)} %get-tuple-element.22), channel_id=1, source_target_pairs={{0,8},{1,9},{2,10},{3,11},{4,12},{5,13},{6,14},{7,15},{8,0},{9,1},... | collective-permute-start | bytes 393224 | tf_op jit(solution)/shard_map/ppermute | solution.py:21
  21.6 48.5 %all-to-all-start.1 = ((bf16[8,40,3584]{2,1,0:T(8,128)(2,1)}), bf16[8,40,3584]{2,1,0:T(8,128)(2,1)}, u32[]{:S(2)}, u32[]{:S(2)}) async-start(bf16[8,40,3584]{2,1,0:T(8,128)(2,1)} %bitcast.22), calls=%async_computation.1 | async-start | bytes 4587520 | tf_op jit(solution)/shard_map/all_to_all | solution.py:498
  30.7 31.3 %collective-permute-start.2 = (bf16[64,3584]{1,0:T(8,128)(2,1)}, bf16[64,3584]{1,0:T(8,128)(2,1)}, u32[]{:S(2)}, u32[]{:S(2)}) collective-permute-start(bf16[64,3584]{1,0:T(8,128)(2,1)} %shard_map.88.refs_4_), channel_id=1, source_target_pairs={{0,8},{1,9},{2,10},{3,11},{4,12},{5,13},{6,14},{7,15},{8,0},{9,1},... | collective-permute-start | bytes 1376264 | tf_op jit(solution)/shard_map/ppermute | solution.py:21
  43.9 52.6 %collective-permute-start.3 = (bf16[128,3584]{1,0:T(8,128)(2,1)}, bf16[128,3584]{1,0:T(8,128)(2,1)}, u32[]{:S(2)}, u32[]{:S(2)}) collective-permute-start(bf16[128,3584]{1,0:T(8,128)(2,1)} %shard_map.91), channel_id=1, source_target_pairs={{0,8},{1,9},{2,10},{3,11},{4,12},{5,13},{6,14},{7,15},{8,0},{9,1},... | collective-permute-start | bytes 2752520 | tf_op jit(solution)/shard_map/ppermute | solution.py:21
  70.1 44.8 %all-to-all-start.2 = ((bf16[8,40,3584]{2,1,0:T(8,128)(2,1)}), bf16[8,40,3584]{2,1,0:T(8,128)(2,1)}, u32[]{:S(2)}, u32[]{:S(2)}) async-start(bf16[8,40,3584]{2,1,0:T(8,128)(2,1)} %bitcast.23), calls=%async_computation.2 | async-start | bytes 4587520 | tf_op jit(solution)/shard_map/all_to_all | solution.py:498
  115.0 48.9 %all-to-all-start.3 = ((bf16[8,40,3584]{2,1,0:T(8,128)(2,1)}), bf16[8,40,3584]{2,1,0:T(8,128)(2,1)}, u32[]{:S(2)}, u32[]{:S(2)}) async-start(bf16[8,40,3584]{2,1,0:T(8,128)(2,1)} %bitcast.16), calls=%async_computation.3 | async-start | bytes 4587520 | tf_op jit(solution)/shard_map/all_to_all | solution.py:498
  122.7 44.9 %collective-permute-start.4 = (bf16[128,3584]{1,0:T(8,128)(2,1)}, bf16[128,3584]{1,0:T(8,128)(2,1)}, u32[]{:S(2)}, u32[]{:S(2)}) collective-permute-start(bf16[128,3584]{1,0:T(8,128)(2,1)} %shard_map.99), channel_id=1, source_target_pairs={{0,8},{1,9},{2,10},{3,11},{4,12},{5,13},{6,14},{7,15},{8,0},{9,1},... | collective-permute-start | bytes 2752520 | tf_op jit(solution)/shard_map/ppermute | solution.py:21
  167.6 19.1 %collective-permute-start.5 = (bf16[64,3584]{1,0:T(8,128)(2,1)}, bf16[64,3584]{1,0:T(8,128)(2,1)}, u32[]{:S(2)}, u32[]{:S(2)}) collective-permute-start(bf16[64,3584]{1,0:T(8,128)(2,1)} %shard_map.101.refs_2_.refs_4_), channel_id=1, source_target_pairs={{0,8},{1,9},{2,10},{3,11},{4,12},{5,13},{6,14},{7,15},{8,0},{9,1},... | collective-permute-start | bytes 1376264 | tf_op jit(solution)/shard_map/ppermute | solution.py:21
  167.6 41.0 %all-to-all-start.4 = ((bf16[8,40,3584]{2,1,0:T(8,128)(2,1)}), bf16[8,40,3584]{2,1,0:T(8,128)(2,1)}, u32[]{:S(2)}, u32[]{:S(2)}) async-start(bf16[8,40,3584]{2,1,0:T(8,128)(2,1)} %bitcast.15), calls=%async_computation.4 | async-start | bytes 4587520 | tf_op jit(solution)/shard_map/all_to_all | solution.py:498
  172.1 22.1 %collective-permute-start.7 = (bf16[512,448]{1,0:T(8,128)(2,1)}, bf16[512,448]{1,0:T(8,128)(2,1)}, u32[]{:S(2)}, u32[]{:S(2)}) collective-permute-start(bf16[512,448]{1,0:T(8,128)(2,1)} %get-tuple-element.34), channel_id=1, source_target_pairs={{0,16},{16,0},{1,17},{17,1},{2,18},{18,2},{3,19},{19,3},{4,20},{20... | collective-permute-start | bytes 1376264 | tf_op jit(solution)/shard_map/ppermute | solution.py:21
  178.3 16.0 %collective-permute-start.8 = (bf16[384,3584]{1,0:T(8,128)(2,1)}, bf16[384,3584]{1,0:T(8,128)(2,1)}, u32[]{:S(2)}, u32[]{:S(2)}) collective-permute-start(bf16[384,3584]{1,0:T(8,128)(2,1)} %shard_map.104.refs_0_.refs_2_), channel_id=1, source_target_pairs={{0,16},{16,0},{1,17},{17,1},{2,18},{18,2},{3,19},{19,3},{4,20},{20... | collective-permute-start | bytes 8257544 | tf_op jit(solution)/shard_map/ppermute | solution.py:21
  186.7 7.5 %collective-permute-start.9 = (bf16[64,3584]{1,0:T(8,128)(2,1)}, bf16[64,3584]{1,0:T(8,128)(2,1)}, u32[]{:S(2)}, u32[]{:S(2)}) collective-permute-start(bf16[64,3584]{1,0:T(8,128)(2,1)} %collective-permute-done.5.refs_1_.refs_3_), channel_id=1, source_target_pairs={{0,16},{16,0},{1,17},{17,1},{2,18},{18,2},{3,19},{19,3},{4,20},{20... | collective-permute-start | bytes 1376264 | tf_op jit(solution)/shard_map/ppermute | solution.py:21
  194.2 8.4 %collective-permute-start.6 = (bf16[64,1024]{1,0:T(8,128)(2,1)}, bf16[64,1024]{1,0:T(8,128)(2,1)}, u32[]{:S(2)}, u32[]{:S(2)}) collective-permute-start(bf16[64,1024]{1,0:T(8,128)(2,1)} %get-tuple-element.32), channel_id=1, source_target_pairs={{0,8},{1,9},{2,10},{3,11},{4,12},{5,13},{6,14},{7,15},{8,0},{9,1},... | collective-permute-start | bytes 393224 | tf_op jit(solution)/shard_map/ppermute | solution.py:21

commit v8 on v7

--- a/solution.py
+++ b/solution.py
@@ -11,7 +11,6 @@
 LONG = 4_000_000_000_000
 GIVE_COST = 5_000_000_000
 BACK_COST = 40_000_000_000
-HEAD_COST = 5_000_000_000
 VMEM_LIMIT = 64 * 1024 * 1024 - 65536
 
 
@@ -121,9 +120,9 @@
     pass
 
 
-def touched(array, *after, cost=0):
+def touched(array, *after):
     shape = jax.ShapeDtypeStruct(array.shape, array.dtype)
-    return call(touch_kernel, 1, [(array, anywhere())], (shape, anywhere()), (), after, {0: 0}, cost)
+    return call(touch_kernel, 1, [(array, anywhere())], (shape, anywhere()), (), after, {0: 0})
 
 
 def plan_rows(meta, cap, half, sel_ref, gate_ref, mix_ref):
@@ -506,7 +505,7 @@
     spare_hidden = swapped(spare_hidden, "expert", half)
     metas = lax.all_to_all(meta, "expert", 0, 0, tiled=True)
     packed_own, mix_own = pack_own(meta, grad_out, cap, half, tile)
-    arrived_own = to_half(touched(touched(packed_own, metas, cost=HEAD_COST), spare_hidden, far))
+    arrived_own = to_half(touched(packed_own, metas, spare_hidden, far))
     out_spare = project_spare(spare_hidden, near, far, tile, mix_own)
     sel, gate, mix_mirror, give_own, take_own, give_mirror, take_mirror = plan(
         metas, cap, half, main, slots

time: 213 us -> 207 us (0.972)
  waiting for transfers between devices: 107 us -> 104 us
  starting transfers between devices: 34.5 us -> 31.7 us
    ppermute x10, waiting for transfers between devices: 44.1 us -> 40.6 us  [swapped(): return lax.ppermute(value, axis, pairs)]
    all_to_all x1, starting transfers between devices: 7.93 us -> 4.89 us  [local(): metas = lax.all_to_all(meta, 'expert', 0, 0, tiled=True)]
    all_to_all x1, waiting for transfers between devices: 1.53 us -> 4.06 us  [local(): metas = lax.all_to_all(meta, 'expert', 0, 0, tiled=True)]
    pallas_call x23 -> x22, Pallas kernels: 70.1 us -> 70.1 us  [call(): pl.pallas_call(kernel, grid=(grid,), in_specs=[spec for _, spec in ins] +...]
  transfers between devices with their start and end apart: 15 -> 15, of which waited for: 10 -> 9; matrix products, arithmetic and copies ran while one was open for 0% -> 0% of each run, Pallas kernels for 31% -> 32%
where the time goes in v8:
time: 207 us; the launch traced here: 206 us
  waiting for transfers between devices  104 us (50%)
  Pallas kernels  70.1 us (34%)
  starting transfers between devices  31.7 us (15%)
    pallas_call x22, Pallas kernels, call(): pl.pallas_call(kernel, grid=(grid,), in_specs=[spec for _, spec in ins] +...  70.1 us
    all_to_all x4, waiting for transfers between devices, to_half(): lax.all_to_all(rows.reshape(half, cap, width), 'expert', 0, 0, axis_index...  58.9 us
    ppermute x10, waiting for transfers between devices, swapped(): return lax.ppermute(value, axis, pairs)  40.6 us
    all_to_all x4, starting transfers between devices, to_half(): lax.all_to_all(rows.reshape(half, cap, width), 'expert', 0, 0, axis_index...  19.2 us
    ppermute x10, starting transfers between devices, swapped(): return lax.ppermute(value, axis, pairs)  7.6 us
    all_to_all x1, starting transfers between devices, local(): metas = lax.all_to_all(meta, 'expert', 0, 0, tiled=True)  4.89 us
  transfers between devices with their start and end apart: 15, of which 9 were waited for; matrix products, arithmetic and copies ran while one was open for 0% of the time, Pallas kernels for 32%

profile of v8, /device:TPU:0, one launch (start us, length us, event | category | flops | bytes accessed | tf_op | source)
XLA Modules:
  0.0 206.1 jit_solution(7057993943089848607)
XLA Ops:
  0.6 0.5 collective-permute-start.1
  1.1 1.6 shard_map.85
  2.8 3.6 %collective-permute-start = (bf16[64,1024]{1,0:T(8,128)(2,1)}, bf16[64,1024]{1,0:T(8,128)(2,1)}, u32[]{:S(2)}, u32[]{:S(2)}) collective-permute-start(bf16[64,1024]{1,0:T(8,128)(2,1)} %get-tuple-element.22), channel_id=1, source_target_pairs={{0,8},{1,9},{2,10},{3,11},{4,12},{5,13},{6,14},{7,15},{8,0},{9,1},... | collective-permute-start | bytes 393224 | tf_op jit(solution)/shard_map/ppermute | solution.py:20
  6.4 4.9 %all-to-all-start = ((f32[16,8,128]{2,1,0:T(8,128)}), f32[16,8,128]{2,1,0:T(8,128)}, u32[]{:S(2)}, u32[]{:S(2)}) async-start(f32[16,8,128]{2,1,0:T(8,128)} %get-tuple-element.19.refs_0_), calls=%async_computation | async-start | bytes 131072 | tf_op jit(solution)/shard_map/all_to_all | solution.py:506
  11.3 3.5 %shard_map.86 = (bf16[320,3584]{1,0:T(8,128)(2,1)}, bf16[256,320]{1,0:T(8,128)(2,1)}) custom-call(f32[16,8,128]{2,1,0:T(8,128)} %get-tuple-element.19.refs_0_, bf16[128,3584]{1,0:T(8,128)(2,1)} %refs_0_.1), custom_call_target="tpu_custom_call" | custom-call | tf_op jit(solution)/shard_map/pallas_call | solution.py:60
  14.8 4.1 %all-to-all-done.refs_0_.refs_1_ = f32[16,8,128]{2,1,0:T(8,128)} async-done(((f32[16,8,128]{2,1,0:T(8,128)}), f32[16,8,128]{2,1,0:T(8,128)}, u32[]{:S(2)}, u32[]{:S(2)}) %all-to-all-start) | async-done | bytes 65568 | tf_op jit(solution)/shard_map/all_to_all | solution.py:506
  18.9 0.0 collective-permute-done.refs_0_.refs_1_.refs_2_
  18.9 0.0 collective-permute-done.1.refs_2_.refs_3_
  18.9 4.4 %all-to-all-start.1 = ((bf16[8,40,3584]{2,1,0:T(8,128)(2,1)}), bf16[8,40,3584]{2,1,0:T(8,128)(2,1)}, u32[]{:S(2)}, u32[]{:S(2)}) async-start(bf16[8,40,3584]{2,1,0:T(8,128)(2,1)} %bitcast.22), calls=%async_computation.1 | async-start | bytes 4587520 | tf_op jit(solution)/shard_map/all_to_all | solution.py:497
  23.3 4.7 %shard_map.88.refs_4_ = bf16[64,3584]{1,0:T(8,128)(2,1)} custom-call(bf16[64,1024]{1,0:T(8,128)(2,1)} %collective-permute-done.refs_0_.refs_1_.refs_2_, bf16[512,3584]{1,0:T(8,128)(2,1)} %bitcast.18, bf16[512,3584]{1,0:T(8,128)(2,1)} %collective-permute-done.1.refs_2_.refs_3_, bf16[256,320]{1,0:T(8,128)(2,1)} %get-tuple-element.20.refs_3_.refs_0_), custom_call_target="tpu_custom_call" | custom-call | tf_op jit(solution)/shard_map/pallas_call | solution.py:60
  28.0 0.7 collective-permute-start.2
  28.7 2.0 shard_map.90.refs_0_
  30.7 2.9 %shard_map.87 = (bf16[320,128]{1,0:T(8,128)(2,1)}, f32[320,128]{1,0:T(8,128)}, bf16[256,320]{1,0:T(8,128)(2,1)}, bf16[320,448]{1,0:T(8,128)(2,1)}, bf16[448,320]...) custom-call(f32[16,8,128]{2,1,0:T(8,128)} %all-to-all-done.refs_0_.refs_1_), custom_call_target="tpu_custom_call" | custom-call | tf_op jit(solution)/shard_map/pallas_call | solution.py:60
  33.6 7.0 %shard_map.89 = (bf16[384,3584]{1,0:T(8,128)(2,1)}, bf16[512,448]{1,0:T(8,128)(2,1)}, bf16[512,448]{1,0:T(8,128)(2,1)}) custom-call(bf16[448,1024]{1,0:T(8,128)(2,1)} %bitcast.25, bf16[64,1024]{1,0:T(8,128)(2,1)} %collective-permute-done.refs_0_.refs_1_.refs_2_, bf16[512,3584]{1,0:T(8,128)(2,1)} %bitcast.19, ...), custom_call_target="tpu_custom_call" | custom-call | tf_op jit(solution)/shard_map/pallas_call | solution.py:60
  40.5 2.2 %collective-permute-start.3 = (bf16[128,3584]{1,0:T(8,128)(2,1)}, bf16[128,3584]{1,0:T(8,128)(2,1)}, u32[]{:S(2)}, u32[]{:S(2)}) collective-permute-start(bf16[128,3584]{1,0:T(8,128)(2,1)} %shard_map.91), channel_id=1, source_target_pairs={{0,8},{1,9},{2,10},{3,11},{4,12},{5,13},{6,14},{7,15},{8,0},{9,1},... | collective-permute-start | bytes 2752520 | tf_op jit(solution)/shard_map/ppermute | solution.py:20
  42.7 4.0 %shard_map.94.refs_1_ = bf16[320,3584]{1,0:T(8,128)(2,1)} custom-call(bf16[320,448]{1,0:T(8,128)(2,1)} %get-tuple-element.27.refs_0_, bf16[384,3584]{1,0:T(8,128)(2,1)} %get-tuple-element.23.refs_1_), custom_call_target="tpu_custom_call" | custom-call | tf_op jit(solution)/shard_map/pallas_call | solution.py:60
  46.7 12.6 %collective-permute-done.2.refs_2_ = bf16[64,3584]{1,0:T(8,128)(2,1)} collective-permute-done((bf16[64,3584]{1,0:T(8,128)(2,1)}, bf16[64,3584]{1,0:T(8,128)(2,1)}, u32[]{:S(2)}, u32[]{:S(2)}) %collective-permute-start.2) | collective-permute-done | bytes 458784 | tf_op jit(solution)/shard_map/ppermute | solution.py:20
  59.3 3.4 %shard_map.95.refs_0_ = bf16[320,3584]{1,0:T(8,128)(2,1)} custom-call(bf16[320,448]{1,0:T(8,128)(2,1)} %get-tuple-element.27.refs_0_, bf16[320,3584]{1,0:T(8,128)(2,1)} %shard_map.94.refs_1_, bf16[64,3584]{1,0:T(8,128)(2,1)} %collective-permute-done.2.refs_2_), custom_call_target="tpu_custom_call" | custom-call | flops 5000000000 | tf_op jit(solution)/shard_map/pallas_call | solution.py:60
  62.6 4.1 %all-to-all-done.1 = bf16[8,40,3584]{2,1,0:T(8,128)(2,1)} async-done(((bf16[8,40,3584]{2,1,0:T(8,128)(2,1)}), bf16[8,40,3584]{2,1,0:T(8,128)(2,1)}, u32[]{:S(2)}, u32[]{:S(2)}) %all-to-all-start.1) | async-done | bytes 2293792 | tf_op jit(solution)/shard_map/all_to_all | solution.py:497
  66.7 5.9 %all-to-all-start.2 = ((bf16[8,40,3584]{2,1,0:T(8,128)(2,1)}), bf16[8,40,3584]{2,1,0:T(8,128)(2,1)}, u32[]{:S(2)}, u32[]{:S(2)}) async-start(bf16[8,40,3584]{2,1,0:T(8,128)(2,1)} %bitcast.23), calls=%async_computation.2 | async-start | bytes 4587520 | tf_op jit(solution)/shard_map/all_to_all | solution.py:497
  72.6 20.2 %collective-permute-done.3.refs_2_ = bf16[128,3584]{1,0:T(8,128)(2,1)} collective-permute-done((bf16[128,3584]{1,0:T(8,128)(2,1)}, bf16[128,3584]{1,0:T(8,128)(2,1)}, u32[]{:S(2)}, u32[]{:S(2)}) %collective-permute-start.3) | collective-permute-done | bytes 917536 | tf_op jit(solution)/shard_map/ppermute | solution.py:20
  92.8 3.1 %shard_map.92.refs_3_.refs_0_ = bf16[320,3584]{1,0:T(8,128)(2,1)} custom-call(bf16[320,128]{1,0:T(8,128)(2,1)} %get-tuple-element.24.refs_2_.refs_0_, f32[320,128]{1,0:T(8,128)} %get-tuple-element.25.refs_1_, bf16[128,3584]{1,0:T(8,128)(2,1)} %collective-permute-done.3.refs_2_), custom_call_target="tpu_custom_call" | custom-call | flops 3999999983616 | tf_op jit(solution)/shard_map/pallas_call | solution.py:60
  95.9 4.7 %shard_map.93.refs_2_.refs_0_ = bf16[320,3584]{1,0:T(8,128)(2,1)} custom-call(bf16[320,448]{1,0:T(8,128)(2,1)} %get-tuple-element.21.refs_0_, bf16[384,3584]{1,0:T(8,128)(2,1)} %get-tuple-element.23.refs_1_, bf16[64,3584]{1,0:T(8,128)(2,1)} %collective-permute-done.2.refs_2_, bf16[320,3584]{1,0:T(8,128)(2,1)} %shard_map.92.refs_3_.refs_0_), custom_call_target="tpu_custom_call" | custom-call | tf_op jit(solution)/shard_map/pallas_call | solution.py:60
  100.5 10.1 %all-to-all-done.2 = bf16[8,40,3584]{2,1,0:T(8,128)(2,1)} async-done(((bf16[8,40,3584]{2,1,0:T(8,128)(2,1)}), bf16[8,40,3584]{2,1,0:T(8,128)(2,1)}, u32[]{:S(2)}, u32[]{:S(2)}) %all-to-all-start.2) | async-done | bytes 2293792 | tf_op jit(solution)/shard_map/all_to_all | solution.py:497
  110.6 4.4 %all-to-all-start.3 = ((bf16[8,40,3584]{2,1,0:T(8,128)(2,1)}), bf16[8,40,3584]{2,1,0:T(8,128)(2,1)}, u32[]{:S(2)}, u32[]{:S(2)}) async-start(bf16[8,40,3584]{2,1,0:T(8,128)(2,1)} %bitcast.16), calls=%async_computation.3 | async-start | bytes 4587520 | tf_op jit(solution)/shard_map/all_to_all | solution.py:497
  115.0 3.3 %shard_map.98 = bf16[128,3584]{1,0:T(8,128)(2,1)} custom-call(bf16[256,320]{1,0:T(8,128)(2,1)} %get-tuple-element.26.refs_0_, bf16[320,3584]{1,0:T(8,128)(2,1)} %bitcast.8.refs_1_), custom_call_target="tpu_custom_call" | custom-call | tf_op jit(solution)/shard_map/pallas_call | solution.py:60
  118.3 0.0 collective-permute-start.4
  118.3 40.4 %all-to-all-done.3 = bf16[8,40,3584]{2,1,0:T(8,128)(2,1)} async-done(((bf16[8,40,3584]{2,1,0:T(8,128)(2,1)}), bf16[8,40,3584]{2,1,0:T(8,128)(2,1)}, u32[]{:S(2)}, u32[]{:S(2)}) %all-to-all-start.3) | async-done | bytes 2293792 | tf_op jit(solution)/shard_map/all_to_all | solution.py:497
  158.7 3.7 %shard_map.100.refs_2_.refs_4_ = bf16[64,3584]{1,0:T(8,128)(2,1)} custom-call(bf16[448,320]{1,0:T(8,128)(2,1)} %get-tuple-element.29.refs_0_, bf16[448,320]{1,0:T(8,128)(2,1)} %get-tuple-element.30.refs_1_, bf16[320,3584]{1,0:T(8,128)(2,1)} %bitcast.6.refs_1_.refs_2_, bf16[320,3584]{1,0:T(8,128)(2,1)} %bitcast.10.refs_3_), custom_call_target="tpu_custom_call" | custom-call | tf_op jit(solution)/shard_map/pallas_call | solution.py:60
  162.4 0.0 collective-permute-start.5
  162.4 0.0 collective-permute-done.4.refs_1_.refs_2_
  162.5 4.6 %all-to-all-start.4 = ((bf16[8,40,3584]{2,1,0:T(8,128)(2,1)}), bf16[8,40,3584]{2,1,0:T(8,128)(2,1)}, u32[]{:S(2)}, u32[]{:S(2)}) async-start(bf16[8,40,3584]{2,1,0:T(8,128)(2,1)} %bitcast.15), calls=%async_computation.4 | async-start | bytes 4587520 | tf_op jit(solution)/shard_map/all_to_all | solution.py:497
  167.0 0.1 collective-permute-start.7
  167.1 6.1 %shard_map.103.refs_0_.refs_2_ = bf16[384,3584]{1,0:T(8,128)(2,1)} custom-call(bf16[448,320]{1,0:T(8,128)(2,1)} %get-tuple-element.29.refs_0_, bf16[448,320]{1,0:T(8,128)(2,1)} %get-tuple-element.30.refs_1_, bf16[320,3584]{1,0:T(8,128)(2,1)} %bitcast.6.refs_1_.refs_2_, bf16[320,3584]{1,0:T(8,128)(2,1)} %bitcast.10.refs_3_, ...), custom_call_target="tpu_custom_call" | custom-call | tf_op jit(solution)/shard_map/pallas_call | solution.py:60
  173.2 0.5 collective-permute-start.8
  173.6 7.2 %collective-permute-done.5.refs_1_.refs_3_ = bf16[64,3584]{1,0:T(8,128)(2,1)} collective-permute-done((bf16[64,3584]{1,0:T(8,128)(2,1)}, bf16[64,3584]{1,0:T(8,128)(2,1)}, u32[]{:S(2)}, u32[]{:S(2)}) %collective-permute-start.5) | collective-permute-done | bytes 458784 | tf_op jit(solution)/shard_map/ppermute | solution.py:20
  180.8 0.0 collective-permute-start.9
  180.8 7.5 %shard_map.104 = (bf16[448,1024]{1,0:T(8,128)(2,1)}, bf16[64,1024]{1,0:T(8,128)(2,1)}) custom-call(bf16[384,3584]{1,0:T(8,128)(2,1)} %shard_map.103.refs_0_.refs_2_, bf16[64,3584]{1,0:T(8,128)(2,1)} %collective-permute-done.5.refs_1_.refs_3_, bf16[512,3584]{1,0:T(8,128)(2,1)} %bitcast.20, bf16[512,3584]{1,0:T(8,128)(2,1)} %collective-permute-done.1.refs_2_.refs_3_), custom_call_target="tpu_custom_call" | custom-call | flops 40000000000 | tf_op jit(solution)/shard_map/pallas_call | solution.py:60
  188.3 0.0 collective-permute-start.6
  188.3 0.0 collective-permute-done.7.refs_1_
  188.3 0.0 collective-permute-done.9.refs_5_
  188.3 0.0 collective-permute-done.8.refs_4_
  188.4 7.7 %shard_map.105.refs_2_ = bf16[512,3584]{1,0:T(8,128)(2,1)} custom-call(bf16[512,448]{1,0:T(8,128)(2,1)} %get-tuple-element.33.refs_0_, bf16[512,448]{1,0:T(8,128)(2,1)} %collective-permute-done.7.refs_1_, bf16[384,3584]{1,0:T(8,128)(2,1)} %shard_map.103.refs_0_.refs_2_, bf16[64,3584]{1,0:T(8,128)(2,1)} %collective-permute-done.5.refs_1_.refs_3_, ...), custom_call_target="tpu_custom_call" | custom-call | tf_op jit(solution)/shard_map/pallas_call | solution.py:60
  196.1 0.6 collective-permute-done.6.refs_1_
  196.7 1.6 shard_map.106
  198.3 4.3 %all-to-all-done.4 = bf16[8,40,3584]{2,1,0:T(8,128)(2,1)} async-done(((bf16[8,40,3584]{2,1,0:T(8,128)(2,1)}), bf16[8,40,3584]{2,1,0:T(8,128)(2,1)}, u32[]{:S(2)}, u32[]{:S(2)}) %all-to-all-start.4) | async-done | bytes 2293792 | tf_op jit(solution)/shard_map/all_to_all | solution.py:497
  202.6 3.5 %shard_map.102 = bf16[128,3584]{1,0:T(8,128)(2,1)} custom-call(bf16[256,320]{1,0:T(8,128)(2,1)} %get-tuple-element.20.refs_3_.refs_0_, bf16[320,3584]{1,0:T(8,128)(2,1)} %bitcast.12.refs_1_, bf16[128,3584]{1,0:T(8,128)(2,1)} %collective-permute-done.4.refs_1_.refs_2_), custom_call_target="tpu_custom_call" | custom-call | tf_op jit(solution)/shard_map/pallas_call | solution.py:60
  (5 shorter events, 0.0 us)
Async XLA Ops:
  0.6 18.3 %collective-permute-start.1 = (bf16[512,3584]{1,0:T(8,128)(2,1)}, bf16[512,3584]{1,0:T(8,128)(2,1)}, u32[]{:S(2)}, u32[]{:S(2)}) collective-permute-start(bf16[512,3584]{1,0:T(8,128)(2,1)} %bitcast.17), channel_id=1, source_target_pairs={{0,16},{16,0},{1,17},{17,1},{2,18},{18,2},{3,19},{19,3},{4,20},{20... | collective-permute-start | bytes 11010056 | tf_op jit(solution)/shard_map/ppermute | solution.py:20
  2.8 16.1 %collective-permute-start = (bf16[64,1024]{1,0:T(8,128)(2,1)}, bf16[64,1024]{1,0:T(8,128)(2,1)}, u32[]{:S(2)}, u32[]{:S(2)}) collective-permute-start(bf16[64,1024]{1,0:T(8,128)(2,1)} %get-tuple-element.22), channel_id=1, source_target_pairs={{0,8},{1,9},{2,10},{3,11},{4,12},{5,13},{6,14},{7,15},{8,0},{9,1},... | collective-permute-start | bytes 393224 | tf_op jit(solution)/shard_map/ppermute | solution.py:20
  6.4 12.5 %all-to-all-start = ((f32[16,8,128]{2,1,0:T(8,128)}), f32[16,8,128]{2,1,0:T(8,128)}, u32[]{:S(2)}, u32[]{:S(2)}) async-start(f32[16,8,128]{2,1,0:T(8,128)} %get-tuple-element.19.refs_0_), calls=%async_computation | async-start | bytes 131072 | tf_op jit(solution)/shard_map/all_to_all | solution.py:506
  18.9 47.8 %all-to-all-start.1 = ((bf16[8,40,3584]{2,1,0:T(8,128)(2,1)}), bf16[8,40,3584]{2,1,0:T(8,128)(2,1)}, u32[]{:S(2)}, u32[]{:S(2)}) async-start(bf16[8,40,3584]{2,1,0:T(8,128)(2,1)} %bitcast.22), calls=%async_computation.1 | async-start | bytes 4587520 | tf_op jit(solution)/shard_map/all_to_all | solution.py:497
  28.0 31.3 %collective-permute-start.2 = (bf16[64,3584]{1,0:T(8,128)(2,1)}, bf16[64,3584]{1,0:T(8,128)(2,1)}, u32[]{:S(2)}, u32[]{:S(2)}) collective-permute-start(bf16[64,3584]{1,0:T(8,128)(2,1)} %shard_map.88.refs_4_), channel_id=1, source_target_pairs={{0,8},{1,9},{2,10},{3,11},{4,12},{5,13},{6,14},{7,15},{8,0},{9,1},... | collective-permute-start | bytes 1376264 | tf_op jit(solution)/shard_map/ppermute | solution.py:20
  40.5 52.2 %collective-permute-start.3 = (bf16[128,3584]{1,0:T(8,128)(2,1)}, bf16[128,3584]{1,0:T(8,128)(2,1)}, u32[]{:S(2)}, u32[]{:S(2)}) collective-permute-start(bf16[128,3584]{1,0:T(8,128)(2,1)} %shard_map.91), channel_id=1, source_target_pairs={{0,8},{1,9},{2,10},{3,11},{4,12},{5,13},{6,14},{7,15},{8,0},{9,1},... | collective-permute-start | bytes 2752520 | tf_op jit(solution)/shard_map/ppermute | solution.py:20
  66.7 43.9 %all-to-all-start.2 = ((bf16[8,40,3584]{2,1,0:T(8,128)(2,1)}), bf16[8,40,3584]{2,1,0:T(8,128)(2,1)}, u32[]{:S(2)}, u32[]{:S(2)}) async-start(bf16[8,40,3584]{2,1,0:T(8,128)(2,1)} %bitcast.23), calls=%async_computation.2 | async-start | bytes 4587520 | tf_op jit(solution)/shard_map/all_to_all | solution.py:497
  110.6 48.1 %all-to-all-start.3 = ((bf16[8,40,3584]{2,1,0:T(8,128)(2,1)}), bf16[8,40,3584]{2,1,0:T(8,128)(2,1)}, u32[]{:S(2)}, u32[]{:S(2)}) async-start(bf16[8,40,3584]{2,1,0:T(8,128)(2,1)} %bitcast.16), calls=%async_computation.3 | async-start | bytes 4587520 | tf_op jit(solution)/shard_map/all_to_all | solution.py:497
  118.3 44.1 %collective-permute-start.4 = (bf16[128,3584]{1,0:T(8,128)(2,1)}, bf16[128,3584]{1,0:T(8,128)(2,1)}, u32[]{:S(2)}, u32[]{:S(2)}) collective-permute-start(bf16[128,3584]{1,0:T(8,128)(2,1)} %shard_map.98), channel_id=1, source_target_pairs={{0,8},{1,9},{2,10},{3,11},{4,12},{5,13},{6,14},{7,15},{8,0},{9,1},... | collective-permute-start | bytes 2752520 | tf_op jit(solution)/shard_map/ppermute | solution.py:20
  162.4 18.4 %collective-permute-start.5 = (bf16[64,3584]{1,0:T(8,128)(2,1)}, bf16[64,3584]{1,0:T(8,128)(2,1)}, u32[]{:S(2)}, u32[]{:S(2)}) collective-permute-start(bf16[64,3584]{1,0:T(8,128)(2,1)} %shard_map.100.refs_2_.refs_4_), channel_id=1, source_target_pairs={{0,8},{1,9},{2,10},{3,11},{4,12},{5,13},{6,14},{7,15},{8,0},{9,1},... | collective-permute-start | bytes 1376264 | tf_op jit(solution)/shard_map/ppermute | solution.py:20
  162.5 40.1 %all-to-all-start.4 = ((bf16[8,40,3584]{2,1,0:T(8,128)(2,1)}), bf16[8,40,3584]{2,1,0:T(8,128)(2,1)}, u32[]{:S(2)}, u32[]{:S(2)}) async-start(bf16[8,40,3584]{2,1,0:T(8,128)(2,1)} %bitcast.15), calls=%async_computation.4 | async-start | bytes 4587520 | tf_op jit(solution)/shard_map/all_to_all | solution.py:497
  167.0 21.3 %collective-permute-start.7 = (bf16[512,448]{1,0:T(8,128)(2,1)}, bf16[512,448]{1,0:T(8,128)(2,1)}, u32[]{:S(2)}, u32[]{:S(2)}) collective-permute-start(bf16[512,448]{1,0:T(8,128)(2,1)} %get-tuple-element.34), channel_id=1, source_target_pairs={{0,16},{16,0},{1,17},{17,1},{2,18},{18,2},{3,19},{19,3},{4,20},{20... | collective-permute-start | bytes 1376264 | tf_op jit(solution)/shard_map/ppermute | solution.py:20
  173.2 15.2 %collective-permute-start.8 = (bf16[384,3584]{1,0:T(8,128)(2,1)}, bf16[384,3584]{1,0:T(8,128)(2,1)}, u32[]{:S(2)}, u32[]{:S(2)}) collective-permute-start(bf16[384,3584]{1,0:T(8,128)(2,1)} %shard_map.103.refs_0_.refs_2_), channel_id=1, source_target_pairs={{0,16},{16,0},{1,17},{17,1},{2,18},{18,2},{3,19},{19,3},{4,20},{20... | collective-permute-start | bytes 8257544 | tf_op jit(solution)/shard_map/ppermute | solution.py:20
  180.8 7.5 %collective-permute-start.9 = (bf16[64,3584]{1,0:T(8,128)(2,1)}, bf16[64,3584]{1,0:T(8,128)(2,1)}, u32[]{:S(2)}, u32[]{:S(2)}) collective-permute-start(bf16[64,3584]{1,0:T(8,128)(2,1)} %collective-permute-done.5.refs_1_.refs_3_), channel_id=1, source_target_pairs={{0,16},{16,0},{1,17},{17,1},{2,18},{18,2},{3,19},{19,3},{4,20},{20... | collective-permute-start | bytes 1376264 | tf_op jit(solution)/shard_map/ppermute | solution.py:20
  188.3 8.4 %collective-permute-start.6 = (bf16[64,1024]{1,0:T(8,128)(2,1)}, bf16[64,1024]{1,0:T(8,128)(2,1)}, u32[]{:S(2)}, u32[]{:S(2)}) collective-permute-start(bf16[64,1024]{1,0:T(8,128)(2,1)} %get-tuple-element.32), channel_id=1, source_target_pairs={{0,8},{1,9},{2,10},{3,11},{4,12},{5,13},{6,14},{7,15},{8,0},{9,1},... | collective-permute-start | bytes 393224 | tf_op jit(solution)/shard_map/ppermute | solution.py:20

commit v9 on v8

--- a/solution.py
+++ b/solution.py
@@ -161,28 +161,6 @@
     packed_ref[...] = (dot(sel_ref[...], tokens_ref[...]) * gate_ref[:, :1]).astype(BF16)
 
 
-def pack_own_kernel(cap, half, meta_ref, tokens_ref, packed_ref, mix_ref, sel_ref, gate_ref):
-    @pl.when(pl.program_id(0) == 0)
-    def _():
-        plan_rows(meta_ref[0], cap, half, sel_ref, gate_ref, mix_ref)
-
-    packed_rows(sel_ref, gate_ref, tokens_ref, packed_ref)
-
-
-def pack_own(meta, tokens, cap, half, tile, *after):
-    tok, width = tokens.shape
-    rows = half * cap
-    first = pl.BlockSpec((1, *meta.shape[1:]), lambda step: (0, 0, 0))
-    return call(
-        functools.partial(pack_own_kernel, cap, half),
-        width // tile,
-        [(meta, first)] + by_columns(tile, tokens),
-        by_columns(tile, bf16(rows, width)) + entire(bf16(2 * tok, rows)),
-        [pltpu.VMEM((rows, tok), BF16), pltpu.VMEM((rows, LANES), F32)],
-        after,
-    )
-
-
 def pack(sel, gate, tokens, tile, *after):
     rows, width = sel.shape[0], tokens.shape[1]
     return call(
@@ -195,13 +173,55 @@
     )
 
 
-def plan_kernel(cap, half, main, metas_ref, sel_ref, gate_ref, mix_ref, *slot_refs):
+def plan_plane(metas_ref, cap, turned, sel_ref, gate_ref):
+    count, tops, tok = metas_ref.shape
+    rows = sel_ref.shape[0]
+    top = tops // 2
+    size = count // 4
+    me = lax.axis_index("expert")
+    plane, mine = lax.div(me, size), lax.rem(me, size)
+    index = lax.broadcasted_iota(I32, (LANES, tok), 0)
+    inside = index < size
+    dest = ((index ^ mine if turned else index) + plane * size).astype(F32)
+    group, at = row_of(rows, cap, LANES)
+    block = jnp.floor(group * 0.5)
+    side = group - 2.0 * block
+    scale = jnp.zeros((rows, 1), F32)
+    for which, source in enumerate((me, (plane ^ 1) * size + mine)):
+        meta = metas_ref[source]
+        hit = jnp.zeros((LANES, tok), F32)
+        gate = jnp.zeros((LANES, tok), F32)
+        for k in range(top):
+            named = (dest == jnp.floor(meta[k : k + 1] * 0.5)) & inside
+            hit = jnp.where(named, 1.0, hit)
+            gate = jnp.where(named, meta[top + k : top + k + 1], gate)
+        place = dot(hit.astype(BF16), before_mask(tok))
+        place = jnp.where(hit > 0.5, place + 1.0, 0.0)
+        spread = ((iota((rows, LANES), 1) == block) & (side == 1.0 * which)).astype(BF16)
+        to_rows = lambda table: dot(spread, table.astype(BF16))
+        chosen = jnp.where(to_rows(place) == at + 1.0, 1.0, jnp.zeros((rows, tok), F32))
+        high = gate.astype(BF16).astype(F32)
+        mid = (gate - high).astype(BF16).astype(F32)
+        low = gate - high - mid
+        total = to_rows(high) + to_rows(mid) + to_rows(low)
+        scale = scale + jnp.sum(chosen * total, axis=1, keepdims=True)
+        sel_ref[:, which * tok : (which + 1) * tok] = chosen.astype(BF16)
+    gate_ref[...] = jnp.broadcast_to(scale, (rows, LANES))
+
+
+def plan_kernel(cap, half, main, turned, metas_ref, *refs):
+    sel_ref, gate_ref, mix_ref, plane_sel, plane_gate, mix_own = refs[:6]
+    give_own, take_plane, give_mirror, take_mirror = refs[6:10]
+    spare_sel, spare_gate = refs[10:]
     count, tops, tok = metas_ref.shape
     top = tops // 2
-    rows, slots = slot_refs[0].shape
+    rows, slots = give_own.shape
     spare = slots - main
+    size = count // 4
     me = lax.axis_index("expert")
     mirror = lax.rem(me + half, count)
+    plan_plane(metas_ref, cap, turned, plane_sel, plane_gate)
+    plan_rows(metas_ref[me], cap, half, spare_sel, spare_gate, mix_own)
     plan_rows(metas_ref[mirror], cap, half, sel_ref, gate_ref, mix_ref)
 
     mine, other = me.astype(F32), mirror.astype(F32)
@@ -232,24 +252,59 @@
     tens = tens.astype(BF16)
     group, _ = row_of(rows, cap, count)
     _, at = row_of(rows, cap, tok)
-    start = lax.div(me, half) * half
-    for side, base in enumerate((start, lax.rem(start + half, count))):
-        spread = (iota((rows, count), 1) == group + base.astype(F32)).astype(BF16)
+
+    def numbers(sources):
+        spread = (iota((rows, count), 1) == sources).astype(BF16)
         chosen = dot(spread, place) == at
         number = dot(spread, tens) * 32.0 + dot(spread, units)
-        number = jnp.sum(jnp.where(chosen, number, 0.0), axis=1, keepdims=True)
-        give_ref, take_ref = slot_refs[2 * side : 2 * side + 2]
-        give_ref[...] = (iota((rows, slots), 1) + 1.0 == number).astype(BF16)
+        return jnp.sum(jnp.where(chosen, number, 0.0), axis=1, keepdims=True)
+
+    def give_to(ref, number):
+        ref[...] = (iota((rows, slots), 1) + 1.0 == number).astype(BF16)
+
+    def take_to(ref, number):
         number = jnp.broadcast_to(number, (rows, LANES)).T[0:1]
-        take_ref[...] = (iota((slots, rows), 0) + 1.0 == number).astype(BF16)
-
-
-def plan(metas, cap, half, main, slots):
+        ref[...] = (iota((slots, rows), 0) + 1.0 == number).astype(BF16)
+
+    start = lax.div(me, half) * half
+    give_to(give_own, numbers(group + start.astype(F32)))
+    number = numbers(group + lax.rem(start + half, count).astype(F32))
+    give_to(give_mirror, number)
+    take_to(take_mirror, number)
+    block = jnp.floor(group * 0.5)
+    side = group - 2.0 * block
+    plane = lax.div(me, size)
+    holder = block.astype(I32)
+    holder = (holder ^ lax.rem(me, size) if turned else holder).astype(F32)
+    start = jnp.where(side == 0.0, (plane * size).astype(F32), ((plane ^ 1) * size).astype(F32))
+    take_to(take_plane, numbers(holder + start))
+
+
+def plan(metas, cap, half, main, slots, turned):
     tok = metas.shape[2]
     rows = half * cap
-    sides = [bf16(rows, slots), bf16(slots, rows)] * 2
-    outs = entire(bf16(rows, tok), f32(rows, LANES), bf16(2 * tok, rows), *sides)
-    return call(functools.partial(plan_kernel, cap, half, main), 1, entire(metas), outs)
+    outs = [bf16(rows, tok), f32(rows, LANES), bf16(2 * tok, rows)]
+    outs += [bf16(rows, 2 * tok), f32(rows, LANES), bf16(2 * tok, rows)]
+    outs += [bf16(rows, slots), bf16(slots, rows)] * 2
+    scratch = [pltpu.VMEM((rows, tok), BF16), pltpu.VMEM((rows, LANES), F32)]
+    body = functools.partial(plan_kernel, cap, half, main, turned)
+    return call(body, 1, entire(metas), entire(*outs), scratch)
+
+
+def pack_plane_kernel(sel_ref, gate_ref, own_ref, neighbour_ref, *outs):
+    tok = own_ref.shape[0]
+    packed = dot(sel_ref[:, :tok], own_ref[...]) + dot(sel_ref[:, tok:], neighbour_ref[...])
+    packed = (packed * gate_ref[:, :1]).astype(BF16)
+    rows = outs[0].shape[0]
+    for index, out_ref in enumerate(outs):
+        out_ref[...] = packed[index * rows : (index + 1) * rows]
+
+
+def pack_plane(sel, gate, own, neighbour, blocks, tile):
+    width = own.shape[1]
+    shapes = [bf16(sel.shape[0] // blocks, width)] * blocks
+    ins = entire(sel, gate) + by_columns(tile, own, neighbour)
+    return call(pack_plane_kernel, width // tile, ins, by_columns(tile, *shapes))
 
 
 def side_by_side(source, target_ref):
@@ -362,19 +417,25 @@
     )
 
 
-def take_kernel(first, own_slot, mirror_slot, own_ref, mirror_ref, out_ref):
+def take_kernel(first, own_slot, mirror_slot, mirror_ref, *rest):
+    blocks, (out_ref, stack_ref) = rest[:-2], rest[-2:]
+    size = blocks[0].shape[0]
+    for index, block_ref in enumerate(blocks):
+        stack_ref[index * size : (index + 1) * size] = block_ref[...]
     rows = pl.ds(first, out_ref.shape[0])
-    total = dot(own_slot[rows, :], own_ref[...]) + dot(mirror_slot[rows, :], mirror_ref[...])
+    total = dot(own_slot[rows, :], stack_ref[...]) + dot(mirror_slot[rows, :], mirror_ref[...])
     out_ref[...] = total.astype(BF16)
 
 
-def take(own_slot, mirror_slot, own, mirror, first, count, tile, *after):
+def take(own_slot, mirror_slot, mirror, own, first, count, tile, *after):
+    rows, width = mirror.shape
     return call(
         functools.partial(take_kernel, first),
-        own.shape[1] // tile,
-        entire(own_slot, mirror_slot) + by_columns(tile, own, mirror),
-        by_columns(tile, bf16(count, own.shape[1]))[0],
-        after=after,
+        width // tile,
+        entire(own_slot, mirror_slot) + by_columns(tile, mirror, *own),
+        by_columns(tile, bf16(count, width))[0],
+        [pltpu.VMEM((rows, tile), BF16)],
+        after,
     )
 
 
@@ -504,24 +565,38 @@
     )
     spare_hidden = swapped(spare_hidden, "expert", half)
     metas = lax.all_to_all(meta, "expert", 0, 0, tiled=True)
-    packed_own, mix_own = pack_own(meta, grad_out, cap, half, tile)
-    arrived_own = to_half(touched(packed_own, metas, spare_hidden, far))
-    out_spare = project_spare(spare_hidden, near, far, tile, mix_own)
-    sel, gate, mix_mirror, give_own, take_own, give_mirror, take_mirror = plan(
-        metas, cap, half, main, slots
-    )
-    out_main, turned, far_turned = project(hidden, spare_hidden, near, far, tile, out_spare)
+    size = count // 4
+    turned_blocks = size == 4
+    place_of = lambda plane, index: plane * size + index
+    across = [(d, place_of(d // size ^ 1, d % size)) for d in range(count)]
+    neighbour = lax.ppermute(grad_out, "expert", across)
+    out_spare = project_spare(spare_hidden, near, far, tile)
+    plans = plan(metas, cap, half, main, slots, turned_blocks)
+    sel, gate, mix_mirror, plane_sel, plane_gate, mix_own = plans[:6]
+    give_own, take_own, give_mirror, take_mirror = plans[6:]
+    blocks = 4 if turned_blocks else 1
+    packed_own = pack_plane(plane_sel, plane_gate, grad_out, neighbour, blocks, tile)
+    if turned_blocks:
+        ways = [[(d, d // size * size + (d % size ^ way)) for d in range(count)] for way in range(blocks)]
+        arrived_own = [packed_own[0]]
+        arrived_own += [lax.ppermute(packed_own[way], "expert", ways[way]) for way in range(1, blocks)]
+    else:
+        planes = [[place_of(plane, index) for index in range(size)] for plane in range(4)]
+        rows = packed_own[0].reshape(size, 2 * cap, width)
+        rows = lax.all_to_all(rows, "expert", 0, 0, axis_index_groups=planes, tiled=True)
+        arrived_own = [rows.reshape(half * cap, width)]
+    out_main, turned, far_turned = project(hidden, spare_hidden, near, far, tile, out_spare, packed_own[0])
     out_spare = swapped(out_spare, "expert", half)
     given_main = give_main(give_mirror, out_main, tile)
     mirror = swapped(touched(copied(grad_out, tile), out_main, sel), "expert", half)
     other_turned = swapped(far_turned, "dp", 1)
     given_mirror = give_rest(give_mirror, given_main, out_spare, tile, GIVE_COST)
-    returned_mirror = to_half(touched(given_mirror, arrived_own))
-    packed_mirror = pack(sel, gate, mirror, tile)
+    returned_mirror = to_half(given_mirror)
+    packed_mirror = pack(sel, gate, mirror, tile, *arrived_own[1:])
     given_own = give(give_own, out_main, out_spare, tile, 0, packed_mirror)
     arrived_mirror = to_half(touched(packed_mirror, returned_mirror, given_own))
     part = swapped(combine(mix_mirror, returned_mirror, [], tile), "expert", half)
-    arrived = (take_own, take_mirror, arrived_own, arrived_mirror)
+    arrived = (take_own, take_mirror, arrived_mirror, arrived_own)
     grads_spare = take(*arrived, main, slots - main, tile)
     returned_own = to_half(touched(given_own, part, grads_spare))
     grads_main = take(*arrived, 0, main, tile, grads_spare)

time: 207 us -> 223 us (1.077)
  waiting for transfers between devices: 104 us -> 117 us
    ppermute x10, waiting for transfers between devices: 40.6 us -> 54.1 us  [swapped(): return lax.ppermute(value, axis, pairs)]
    ppermute x0 -> x4, starting transfers between devices: none -> 6.2 us  [the longest x3 3.55 us: local(): lax.ppermute(packed_own[way], 'expert', ways[way])]
    all_to_all x4 -> x3, starting transfers between devices: 19.2 us -> 14 us  [to_half(): lax.all_to_all(rows.reshape(half, cap, width), 'expert', 0, 0, axis_index...]
    all_to_all x1, waiting for transfers between devices: 4.06 us -> 0.01 us  [local(): metas = lax.all_to_all(meta, 'expert', 0, 0, tiled=True)]
    all_to_all x4 -> x3, waiting for transfers between devices: 58.9 us -> 62.5 us  [to_half(): lax.all_to_all(rows.reshape(half, cap, width), 'expert', 0, 0, axis_index...]
    pallas_call x22 -> x20, Pallas kernels: 70.1 us -> 71.4 us  [call(): pl.pallas_call(kernel, grid=(grid,), in_specs=[spec for _, spec in ins] +...]
  transfers between devices with their start and end apart: 15 -> 18, of which waited for: 9 -> 8; matrix products, arithmetic and copies ran while one was open for 0% -> 0% of each run, Pallas kernels for 32% -> 31%
where the time goes in v9:
time: 223 us; the launch traced here: 222 us
  waiting for transfers between devices  117 us (52%)
  Pallas kernels  71.4 us (32%)
  starting transfers between devices  33.2 us (15%)
    pallas_call x20, Pallas kernels, call(): pl.pallas_call(kernel, grid=(grid,), in_specs=[spec for _, spec in ins] +...  71.4 us
    all_to_all x3, waiting for transfers between devices, to_half(): lax.all_to_all(rows.reshape(half, cap, width), 'expert', 0, 0, axis_index...  62.5 us
    ppermute x10, waiting for transfers between devices, swapped(): return lax.ppermute(value, axis, pairs)  54.1 us
    all_to_all x3, starting transfers between devices, to_half(): lax.all_to_all(rows.reshape(half, cap, width), 'expert', 0, 0, axis_index...  14 us
    ppermute x10, starting transfers between devices, swapped(): return lax.ppermute(value, axis, pairs)  8.86 us
  transfers between devices with their start and end apart: 18, of which 8 were waited for; matrix products, arithmetic and copies ran while one was open for 0% of the time, Pallas kernels for 31%

profile of v9, /device:TPU:0, one launch (start us, length us, event | category | flops | bytes accessed | tf_op | source)
XLA Modules:
  0.0 221.9 jit_solution(18183175010943143846)
XLA Ops:
  0.6 0.5 collective-permute-start.1
  1.1 2.7 %collective-permute-start.2 = (bf16[128,3584]{1,0:T(8,128)(2,1)}, bf16[128,3584]{1,0:T(8,128)(2,1)}, u32[]{:S(2)}, u32[]{:S(2)}) collective-permute-start(bf16[128,3584]{1,0:T(8,128)(2,1)} %refs_0_.1), channel_id=1, source_target_pairs={{0,4},{1,5},{2,6},{3,7},{4,0},{5,1},{6,2},{7,3},{8,12},{9,13},{10,... | collective-permute-start | bytes 2752520 | tf_op jit(solution)/shard_map/ppermute | solution.py:572
  3.8 1.6 shard_map.85
  5.4 2.6 %collective-permute-start = (bf16[64,1024]{1,0:T(8,128)(2,1)}, bf16[64,1024]{1,0:T(8,128)(2,1)}, u32[]{:S(2)}, u32[]{:S(2)}) collective-permute-start(bf16[64,1024]{1,0:T(8,128)(2,1)} %get-tuple-element.27), channel_id=1, source_target_pairs={{0,8},{1,9},{2,10},{3,11},{4,12},{5,13},{6,14},{7,15},{8,0},{9,1},... | collective-permute-start | bytes 393224 | tf_op jit(solution)/shard_map/ppermute | solution.py:20
  8.0 4.1 %all-to-all-start = ((f32[16,8,128]{2,1,0:T(8,128)}), f32[16,8,128]{2,1,0:T(8,128)}, u32[]{:S(2)}, u32[]{:S(2)}) async-start(f32[16,8,128]{2,1,0:T(8,128)} %get-tuple-element.24), calls=%async_computation | async-start | bytes 131072 | tf_op jit(solution)/shard_map/all_to_all | solution.py:567
  12.2 15.4 %collective-permute-done.refs_0_.refs_1_ = bf16[64,1024]{1,0:T(8,128)(2,1)} collective-permute-done((bf16[64,1024]{1,0:T(8,128)(2,1)}, bf16[64,1024]{1,0:T(8,128)(2,1)}, u32[]{:S(2)}, u32[]{:S(2)}) %collective-permute-start) | collective-permute-done | bytes 131104 | tf_op jit(solution)/shard_map/ppermute | solution.py:20
  27.6 0.0 collective-permute-done.1.refs_2_.refs_3_
  27.6 4.6 %shard_map.87.refs_4_ = bf16[64,3584]{1,0:T(8,128)(2,1)} custom-call(bf16[64,1024]{1,0:T(8,128)(2,1)} %collective-permute-done.refs_0_.refs_1_, bf16[512,3584]{1,0:T(8,128)(2,1)} %bitcast.16, bf16[512,3584]{1,0:T(8,128)(2,1)} %collective-permute-done.1.refs_2_.refs_3_), custom_call_target="tpu_custom_call" | custom-call | tf_op jit(solution)/shard_map/pallas_call | solution.py:60
  32.3 3.4 %collective-permute-start.3 = (bf16[64,3584]{1,0:T(8,128)(2,1)}, bf16[64,3584]{1,0:T(8,128)(2,1)}, u32[]{:S(2)}, u32[]{:S(2)}) collective-permute-start(bf16[64,3584]{1,0:T(8,128)(2,1)} %shard_map.87.refs_4_), channel_id=1, source_target_pairs={{0,8},{1,9},{2,10},{3,11},{4,12},{5,13},{6,14},{7,15},{8,0},{9,1},... | collective-permute-start | bytes 1376264 | tf_op jit(solution)/shard_map/ppermute | solution.py:20
  35.6 2.0 shard_map.90.refs_0_
  37.6 0.0 all-to-all-done.refs_0_
  37.6 3.7 %shard_map.86 = (bf16[320,128]{1,0:T(8,128)(2,1)}, f32[320,128]{1,0:T(8,128)}, bf16[256,320]{1,0:T(8,128)(2,1)}, bf16[320,256]{1,0:T(8,128)(2,1)}, f32[320,128]{...) custom-call(f32[16,8,128]{2,1,0:T(8,128)} %all-to-all-done.refs_0_), custom_call_target="tpu_custom_call" | custom-call | tf_op jit(solution)/shard_map/pallas_call | solution.py:60
  41.3 0.0 collective-permute-done.2.refs_3_
  41.3 3.7 %shard_map.88 = (bf16[80,3584]{1,0:T(8,128)(2,1)}, bf16[80,3584]{1,0:T(8,128)(2,1)}, bf16[80,3584]{1,0:T(8,128)(2,1)}, bf16[80,3584]{1,0:T(8,128)(2,1)}) custom-call(bf16[320,256]{1,0:T(8,128)(2,1)} %get-tuple-element.28.refs_0_, f32[320,128]{1,0:T(8,128)} %get-tuple-element.29.refs_1_, bf16[128,3584]{1,0:T(8,128)(2,1)} %refs_0_.1, ...), custom_call_target="tpu_custom_call" | custom-call | tf_op jit(solution)/shard_map/pallas_call | solution.py:60
  45.0 7.0 %shard_map.89 = (bf16[384,3584]{1,0:T(8,128)(2,1)}, bf16[512,448]{1,0:T(8,128)(2,1)}, bf16[512,448]{1,0:T(8,128)(2,1)}) custom-call(bf16[448,1024]{1,0:T(8,128)(2,1)} %bitcast.21, bf16[64,1024]{1,0:T(8,128)(2,1)} %collective-permute-done.refs_0_.refs_1_, bf16[512,3584]{1,0:T(8,128)(2,1)} %bitcast.17, ...), custom_call_target="tpu_custom_call" | custom-call | tf_op jit(solution)/shard_map/pallas_call | solution.py:60
  52.0 0.0 collective-permute-start.4
  52.0 1.6 collective-permute-start.5
  53.6 1.5 collective-permute-start.6
  55.1 0.5 collective-permute-start.7
  55.6 4.0 %shard_map.94.refs_1_ = bf16[320,3584]{1,0:T(8,128)(2,1)} custom-call(bf16[320,448]{1,0:T(8,128)(2,1)} %get-tuple-element.38.refs_0_, bf16[384,3584]{1,0:T(8,128)(2,1)} %get-tuple-element.31.refs_1_), custom_call_target="tpu_custom_call" | custom-call | tf_op jit(solution)/shard_map/pallas_call | solution.py:60
  59.5 16.7 %collective-permute-done.3.refs_2_ = bf16[64,3584]{1,0:T(8,128)(2,1)} collective-permute-done((bf16[64,3584]{1,0:T(8,128)(2,1)}, bf16[64,3584]{1,0:T(8,128)(2,1)}, u32[]{:S(2)}, u32[]{:S(2)}) %collective-permute-start.3) | collective-permute-done | bytes 458784 | tf_op jit(solution)/shard_map/ppermute | solution.py:20
  76.2 3.3 %shard_map.95 = bf16[320,3584]{1,0:T(8,128)(2,1)} custom-call(bf16[320,448]{1,0:T(8,128)(2,1)} %get-tuple-element.38.refs_0_, bf16[320,3584]{1,0:T(8,128)(2,1)} %shard_map.94.refs_1_, bf16[64,3584]{1,0:T(8,128)(2,1)} %collective-permute-done.3.refs_2_), custom_call_target="tpu_custom_call" | custom-call | flops 5000000000 | tf_op jit(solution)/shard_map/pallas_call | solution.py:60
  79.6 4.4 %all-to-all-start.1 = ((bf16[8,40,3584]{2,1,0:T(8,128)(2,1)}), bf16[8,40,3584]{2,1,0:T(8,128)(2,1)}, u32[]{:S(2)}, u32[]{:S(2)}) async-start(bf16[8,40,3584]{2,1,0:T(8,128)(2,1)} %bitcast.23), calls=%async_computation.1 | async-start | bytes 4587520 | tf_op jit(solution)/shard_map/all_to_all | solution.py:558
  83.9 0.0 collective-permute-done.5.refs_3_.refs_4_
  83.9 0.0 collective-permute-done.6.refs_4_.refs_5_
  83.9 0.0 collective-permute-done.7.refs_5_.refs_6_
  83.9 11.1 %collective-permute-done.4.refs_2_ = bf16[128,3584]{1,0:T(8,128)(2,1)} collective-permute-done((bf16[128,3584]{1,0:T(8,128)(2,1)}, bf16[128,3584]{1,0:T(8,128)(2,1)}, u32[]{:S(2)}, u32[]{:S(2)}) %collective-permute-start.4) | collective-permute-done | bytes 917536 | tf_op jit(solution)/shard_map/ppermute | solution.py:20
  95.1 3.1 %shard_map.92.refs_3_.refs_0_ = bf16[320,3584]{1,0:T(8,128)(2,1)} custom-call(bf16[320,128]{1,0:T(8,128)(2,1)} %get-tuple-element.32.refs_2_.refs_0_, f32[320,128]{1,0:T(8,128)} %get-tuple-element.33.refs_1_, bf16[128,3584]{1,0:T(8,128)(2,1)} %collective-permute-done.4.refs_2_, bf16[80,3584]{1,0:T(8,128)(2,1)} %collective-permute-done.5.refs_3_.refs_4_, ...), custom_call_target="tpu_custom_call" | custom-call | flops 3999999983616 | tf_op jit(solution)/shard_map/pallas_call | solution.py:60
  98.2 4.7 %shard_map.93.refs_2_.refs_0_ = bf16[320,3584]{1,0:T(8,128)(2,1)} custom-call(bf16[320,448]{1,0:T(8,128)(2,1)} %get-tuple-element.26.refs_0_, bf16[384,3584]{1,0:T(8,128)(2,1)} %get-tuple-element.31.refs_1_, bf16[64,3584]{1,0:T(8,128)(2,1)} %collective-permute-done.3.refs_2_, bf16[320,3584]{1,0:T(8,128)(2,1)} %shard_map.92.refs_3_.refs_0_), custom_call_target="tpu_custom_call" | custom-call | tf_op jit(solution)/shard_map/pallas_call | solution.py:60
  102.9 16.7 %all-to-all-done.1 = bf16[8,40,3584]{2,1,0:T(8,128)(2,1)} async-done(((bf16[8,40,3584]{2,1,0:T(8,128)(2,1)}), bf16[8,40,3584]{2,1,0:T(8,128)(2,1)}, u32[]{:S(2)}, u32[]{:S(2)}) %all-to-all-start.1) | async-done | bytes 2293792 | tf_op jit(solution)/shard_map/all_to_all | solution.py:558
  119.6 4.4 %all-to-all-start.2 = ((bf16[8,40,3584]{2,1,0:T(8,128)(2,1)}), bf16[8,40,3584]{2,1,0:T(8,128)(2,1)}, u32[]{:S(2)}, u32[]{:S(2)}) async-start(bf16[8,40,3584]{2,1,0:T(8,128)(2,1)} %bitcast.14), calls=%async_computation.2 | async-start | bytes 4587520 | tf_op jit(solution)/shard_map/all_to_all | solution.py:558
  123.9 3.3 %shard_map.96 = bf16[128,3584]{1,0:T(8,128)(2,1)} custom-call(bf16[256,320]{1,0:T(8,128)(2,1)} %get-tuple-element.37.refs_0_, bf16[320,3584]{1,0:T(8,128)(2,1)} %bitcast.6.refs_1_), custom_call_target="tpu_custom_call" | custom-call | tf_op jit(solution)/shard_map/pallas_call | solution.py:60
  127.3 1.9 collective-permute-start.8
  129.2 41.9 %all-to-all-done.2 = bf16[8,40,3584]{2,1,0:T(8,128)(2,1)} async-done(((bf16[8,40,3584]{2,1,0:T(8,128)(2,1)}), bf16[8,40,3584]{2,1,0:T(8,128)(2,1)}, u32[]{:S(2)}, u32[]{:S(2)}) %all-to-all-start.2) | async-done | bytes 2293792 | tf_op jit(solution)/shard_map/all_to_all | solution.py:558
  171.1 3.7 %shard_map.98.refs_2_.refs_7_ = bf16[64,3584]{1,0:T(8,128)(2,1)} custom-call(bf16[448,320]{1,0:T(8,128)(2,1)} %get-tuple-element.39.refs_0_, bf16[448,320]{1,0:T(8,128)(2,1)} %get-tuple-element.40.refs_1_, bf16[320,3584]{1,0:T(8,128)(2,1)} %bitcast.8.refs_2_, bf16[80,3584]{1,0:T(8,128)(2,1)} %get-tuple-element.30.refs_5_.refs_3_, ...), custom_call_target="tpu_custom_call" | custom-call | tf_op jit(solution)/shard_map/pallas_call | solution.py:60
  174.8 0.0 collective-permute-start.9
  174.8 0.0 collective-permute-done.8.refs_1_.refs_2_
  174.8 5.3 %all-to-all-start.3 = ((bf16[8,40,3584]{2,1,0:T(8,128)(2,1)}), bf16[8,40,3584]{2,1,0:T(8,128)(2,1)}, u32[]{:S(2)}, u32[]{:S(2)}) async-start(bf16[8,40,3584]{2,1,0:T(8,128)(2,1)} %bitcast.13), calls=%async_computation.3 | async-start | bytes 4587520 | tf_op jit(solution)/shard_map/all_to_all | solution.py:558
  180.1 0.0 collective-permute-start.11
  180.1 6.3 %shard_map.101.refs_0_.refs_2_ = bf16[384,3584]{1,0:T(8,128)(2,1)} custom-call(bf16[448,320]{1,0:T(8,128)(2,1)} %get-tuple-element.39.refs_0_, bf16[448,320]{1,0:T(8,128)(2,1)} %get-tuple-element.40.refs_1_, bf16[320,3584]{1,0:T(8,128)(2,1)} %bitcast.8.refs_2_, bf16[80,3584]{1,0:T(8,128)(2,1)} %get-tuple-element.30.refs_5_.refs_3_, ...), custom_call_target="tpu_custom_call" | custom-call | tf_op jit(solution)/shard_map/pallas_call | solution.py:60
  186.4 0.5 collective-permute-start.12
  186.9 9.6 %collective-permute-done.9.refs_1_.refs_3_ = bf16[64,3584]{1,0:T(8,128)(2,1)} collective-permute-done((bf16[64,3584]{1,0:T(8,128)(2,1)}, bf16[64,3584]{1,0:T(8,128)(2,1)}, u32[]{:S(2)}, u32[]{:S(2)}) %collective-permute-start.9) | collective-permute-done | bytes 458784 | tf_op jit(solution)/shard_map/ppermute | solution.py:20
  196.5 0.0 collective-permute-start.13
  196.5 7.5 %shard_map.102 = (bf16[448,1024]{1,0:T(8,128)(2,1)}, bf16[64,1024]{1,0:T(8,128)(2,1)}) custom-call(bf16[384,3584]{1,0:T(8,128)(2,1)} %shard_map.101.refs_0_.refs_2_, bf16[64,3584]{1,0:T(8,128)(2,1)} %collective-permute-done.9.refs_1_.refs_3_, bf16[512,3584]{1,0:T(8,128)(2,1)} %bitcast.18, bf16[512,3584]{1,0:T(8,128)(2,1)} %collective-permute-done.1.refs_2_.refs_3_), custom_call_target="tpu_custom_call" | custom-call | flops 40000000000 | tf_op jit(solution)/shard_map/pallas_call | solution.py:60
  204.0 0.0 collective-permute-start.10
  204.0 0.0 collective-permute-done.11.refs_1_
  204.0 0.0 collective-permute-done.13.refs_5_
  204.0 0.0 collective-permute-done.12.refs_4_
  204.0 7.7 %shard_map.103.refs_2_ = bf16[512,3584]{1,0:T(8,128)(2,1)} custom-call(bf16[512,448]{1,0:T(8,128)(2,1)} %get-tuple-element.43.refs_0_, bf16[512,448]{1,0:T(8,128)(2,1)} %collective-permute-done.11.refs_1_, bf16[384,3584]{1,0:T(8,128)(2,1)} %shard_map.101.refs_0_.refs_2_, bf16[64,3584]{1,0:T(8,128)(2,1)} %collective-permute-done.9.refs_1_.refs_3_, ...), custom_call_target="tpu_custom_call" | custom-call | tf_op jit(solution)/shard_map/pallas_call | solution.py:60
  211.8 1.2 collective-permute-done.10.refs_1_
  213.0 1.6 shard_map.104
  214.5 3.9 %all-to-all-done.3 = bf16[8,40,3584]{2,1,0:T(8,128)(2,1)} async-done(((bf16[8,40,3584]{2,1,0:T(8,128)(2,1)}), bf16[8,40,3584]{2,1,0:T(8,128)(2,1)}, u32[]{:S(2)}, u32[]{:S(2)}) %all-to-all-start.3) | async-done | bytes 2293792 | tf_op jit(solution)/shard_map/all_to_all | solution.py:558
  218.5 3.5 %shard_map.100 = bf16[128,3584]{1,0:T(8,128)(2,1)} custom-call(bf16[256,320]{1,0:T(8,128)(2,1)} %get-tuple-element.25.refs_0_, bf16[320,3584]{1,0:T(8,128)(2,1)} %bitcast.10.refs_1_, bf16[128,3584]{1,0:T(8,128)(2,1)} %collective-permute-done.8.refs_1_.refs_2_), custom_call_target="tpu_custom_call" | custom-call | tf_op jit(solution)/shard_map/pallas_call | solution.py:60
  (3 shorter events, 0.0 us)
Async XLA Ops:
  0.6 27.0 %collective-permute-start.1 = (bf16[512,3584]{1,0:T(8,128)(2,1)}, bf16[512,3584]{1,0:T(8,128)(2,1)}, u32[]{:S(2)}, u32[]{:S(2)}) collective-permute-start(bf16[512,3584]{1,0:T(8,128)(2,1)} %bitcast.15), channel_id=1, source_target_pairs={{0,16},{16,0},{1,17},{17,1},{2,18},{18,2},{3,19},{19,3},{4,20},{20... | collective-permute-start | bytes 11010056 | tf_op jit(solution)/shard_map/ppermute | solution.py:20
  1.1 40.1 %collective-permute-start.2 = (bf16[128,3584]{1,0:T(8,128)(2,1)}, bf16[128,3584]{1,0:T(8,128)(2,1)}, u32[]{:S(2)}, u32[]{:S(2)}) collective-permute-start(bf16[128,3584]{1,0:T(8,128)(2,1)} %refs_0_.1), channel_id=1, source_target_pairs={{0,4},{1,5},{2,6},{3,7},{4,0},{5,1},{6,2},{7,3},{8,12},{9,13},{10,... | collective-permute-start | bytes 2752520 | tf_op jit(solution)/shard_map/ppermute | solution.py:572
  5.4 22.2 %collective-permute-start = (bf16[64,1024]{1,0:T(8,128)(2,1)}, bf16[64,1024]{1,0:T(8,128)(2,1)}, u32[]{:S(2)}, u32[]{:S(2)}) collective-permute-start(bf16[64,1024]{1,0:T(8,128)(2,1)} %get-tuple-element.27), channel_id=1, source_target_pairs={{0,8},{1,9},{2,10},{3,11},{4,12},{5,13},{6,14},{7,15},{8,0},{9,1},... | collective-permute-start | bytes 393224 | tf_op jit(solution)/shard_map/ppermute | solution.py:20
  8.0 29.6 %all-to-all-start = ((f32[16,8,128]{2,1,0:T(8,128)}), f32[16,8,128]{2,1,0:T(8,128)}, u32[]{:S(2)}, u32[]{:S(2)}) async-start(f32[16,8,128]{2,1,0:T(8,128)} %get-tuple-element.24), calls=%async_computation | async-start | bytes 131072 | tf_op jit(solution)/shard_map/all_to_all | solution.py:567
  32.3 44.0 %collective-permute-start.3 = (bf16[64,3584]{1,0:T(8,128)(2,1)}, bf16[64,3584]{1,0:T(8,128)(2,1)}, u32[]{:S(2)}, u32[]{:S(2)}) collective-permute-start(bf16[64,3584]{1,0:T(8,128)(2,1)} %shard_map.87.refs_4_), channel_id=1, source_target_pairs={{0,8},{1,9},{2,10},{3,11},{4,12},{5,13},{6,14},{7,15},{8,0},{9,1},... | collective-permute-start | bytes 1376264 | tf_op jit(solution)/shard_map/ppermute | solution.py:20
  52.0 43.1 %collective-permute-start.4 = (bf16[128,3584]{1,0:T(8,128)(2,1)}, bf16[128,3584]{1,0:T(8,128)(2,1)}, u32[]{:S(2)}, u32[]{:S(2)}) collective-permute-start(bf16[128,3584]{1,0:T(8,128)(2,1)} %shard_map.91), channel_id=1, source_target_pairs={{0,8},{1,9},{2,10},{3,11},{4,12},{5,13},{6,14},{7,15},{8,0},{9,1},... | collective-permute-start | bytes 2752520 | tf_op jit(solution)/shard_map/ppermute | solution.py:20
  52.0 31.9 %collective-permute-start.5 = (bf16[80,3584]{1,0:T(8,128)(2,1)}, bf16[80,3584]{1,0:T(8,128)(2,1)}, u32[]{:S(2)}, u32[]{:S(2)}) collective-permute-start(bf16[80,3584]{1,0:T(8,128)(2,1)} %get-tuple-element.34), channel_id=1, source_target_pairs={{0,1},{1,0},{2,3},{3,2},{4,5},{5,4},{6,7},{7,6},{8,9},{9,8},{10,11... | collective-permute-start | bytes 1720328 | tf_op jit(solution)/shard_map/ppermute | solution.py:582
  53.6 30.4 %collective-permute-start.6 = (bf16[80,3584]{1,0:T(8,128)(2,1)}, bf16[80,3584]{1,0:T(8,128)(2,1)}, u32[]{:S(2)}, u32[]{:S(2)}) collective-permute-start(bf16[80,3584]{1,0:T(8,128)(2,1)} %get-tuple-element.35), channel_id=1, source_target_pairs={{0,2},{1,3},{2,0},{3,1},{4,6},{5,7},{6,4},{7,5},{8,10},{9,11},{10,... | collective-permute-start | bytes 1720328 | tf_op jit(solution)/shard_map/ppermute | solution.py:582
  55.1 28.8 %collective-permute-start.7 = (bf16[80,3584]{1,0:T(8,128)(2,1)}, bf16[80,3584]{1,0:T(8,128)(2,1)}, u32[]{:S(2)}, u32[]{:S(2)}) collective-permute-start(bf16[80,3584]{1,0:T(8,128)(2,1)} %get-tuple-element.36), channel_id=1, source_target_pairs={{0,3},{1,2},{2,1},{3,0},{4,7},{5,6},{6,5},{7,4},{8,11},{9,10},{10,... | collective-permute-start | bytes 1720328 | tf_op jit(solution)/shard_map/ppermute | solution.py:582
  79.6 40.0 %all-to-all-start.1 = ((bf16[8,40,3584]{2,1,0:T(8,128)(2,1)}), bf16[8,40,3584]{2,1,0:T(8,128)(2,1)}, u32[]{:S(2)}, u32[]{:S(2)}) async-start(bf16[8,40,3584]{2,1,0:T(8,128)(2,1)} %bitcast.23), calls=%async_computation.1 | async-start | bytes 4587520 | tf_op jit(solution)/shard_map/all_to_all | solution.py:558
  119.6 51.5 %all-to-all-start.2 = ((bf16[8,40,3584]{2,1,0:T(8,128)(2,1)}), bf16[8,40,3584]{2,1,0:T(8,128)(2,1)}, u32[]{:S(2)}, u32[]{:S(2)}) async-start(bf16[8,40,3584]{2,1,0:T(8,128)(2,1)} %bitcast.14), calls=%async_computation.2 | async-start | bytes 4587520 | tf_op jit(solution)/shard_map/all_to_all | solution.py:558
  127.3 47.5 %collective-permute-start.8 = (bf16[128,3584]{1,0:T(8,128)(2,1)}, bf16[128,3584]{1,0:T(8,128)(2,1)}, u32[]{:S(2)}, u32[]{:S(2)}) collective-permute-start(bf16[128,3584]{1,0:T(8,128)(2,1)} %shard_map.96), channel_id=1, source_target_pairs={{0,8},{1,9},{2,10},{3,11},{4,12},{5,13},{6,14},{7,15},{8,0},{9,1},... | collective-permute-start | bytes 2752520 | tf_op jit(solution)/shard_map/ppermute | solution.py:20
  174.8 21.7 %collective-permute-start.9 = (bf16[64,3584]{1,0:T(8,128)(2,1)}, bf16[64,3584]{1,0:T(8,128)(2,1)}, u32[]{:S(2)}, u32[]{:S(2)}) collective-permute-start(bf16[64,3584]{1,0:T(8,128)(2,1)} %shard_map.98.refs_2_.refs_7_), channel_id=1, source_target_pairs={{0,8},{1,9},{2,10},{3,11},{4,12},{5,13},{6,14},{7,15},{8,0},{9,1},... | collective-permute-start | bytes 1376264 | tf_op jit(solution)/shard_map/ppermute | solution.py:20
  174.8 43.7 %all-to-all-start.3 = ((bf16[8,40,3584]{2,1,0:T(8,128)(2,1)}), bf16[8,40,3584]{2,1,0:T(8,128)(2,1)}, u32[]{:S(2)}, u32[]{:S(2)}) async-start(bf16[8,40,3584]{2,1,0:T(8,128)(2,1)} %bitcast.13), calls=%async_computation.3 | async-start | bytes 4587520 | tf_op jit(solution)/shard_map/all_to_all | solution.py:558
  180.1 23.9 %collective-permute-start.11 = (bf16[512,448]{1,0:T(8,128)(2,1)}, bf16[512,448]{1,0:T(8,128)(2,1)}, u32[]{:S(2)}, u32[]{:S(2)}) collective-permute-start(bf16[512,448]{1,0:T(8,128)(2,1)} %get-tuple-element.44), channel_id=1, source_target_pairs={{0,16},{16,0},{1,17},{17,1},{2,18},{18,2},{3,19},{19,3},{4,20},{20... | collective-permute-start | bytes 1376264 | tf_op jit(solution)/shard_map/ppermute | solution.py:20
  186.4 17.6 %collective-permute-start.12 = (bf16[384,3584]{1,0:T(8,128)(2,1)}, bf16[384,3584]{1,0:T(8,128)(2,1)}, u32[]{:S(2)}, u32[]{:S(2)}) collective-permute-start(bf16[384,3584]{1,0:T(8,128)(2,1)} %shard_map.101.refs_0_.refs_2_), channel_id=1, source_target_pairs={{0,16},{16,0},{1,17},{17,1},{2,18},{18,2},{3,19},{19,3},{4,20},{20... | collective-permute-start | bytes 8257544 | tf_op jit(solution)/shard_map/ppermute | solution.py:20
  196.5 7.5 %collective-permute-start.13 = (bf16[64,3584]{1,0:T(8,128)(2,1)}, bf16[64,3584]{1,0:T(8,128)(2,1)}, u32[]{:S(2)}, u32[]{:S(2)}) collective-permute-start(bf16[64,3584]{1,0:T(8,128)(2,1)} %collective-permute-done.9.refs_1_.refs_3_), channel_id=1, source_target_pairs={{0,16},{16,0},{1,17},{17,1},{2,18},{18,2},{3,19},{19,3},{4,20},{20... | collective-permute-start | bytes 1376264 | tf_op jit(solution)/shard_map/ppermute | solution.py:20
  204.0 9.0 %collective-permute-start.10 = (bf16[64,1024]{1,0:T(8,128)(2,1)}, bf16[64,1024]{1,0:T(8,128)(2,1)}, u32[]{:S(2)}, u32[]{:S(2)}) collective-permute-start(bf16[64,1024]{1,0:T(8,128)(2,1)} %get-tuple-element.42), channel_id=1, source_target_pairs={{0,8},{1,9},{2,10},{3,11},{4,12},{5,13},{6,14},{7,15},{8,0},{9,1},... | collective-permute-start | bytes 393224 | tf_op jit(solution)/shard_map/ppermute | solution.py:20

commit v10 on v9

--- a/solution.py
+++ b/solution.py
@@ -300,11 +300,11 @@
         out_ref[...] = packed[index * rows : (index + 1) * rows]
 
 
-def pack_plane(sel, gate, own, neighbour, blocks, tile):
+def pack_plane(sel, gate, own, neighbour, blocks, tile, *after):
     width = own.shape[1]
     shapes = [bf16(sel.shape[0] // blocks, width)] * blocks
     ins = entire(sel, gate) + by_columns(tile, own, neighbour)
-    return call(pack_plane_kernel, width // tile, ins, by_columns(tile, *shapes))
+    return call(pack_plane_kernel, width // tile, ins, by_columns(tile, *shapes), (), after)
 
 
 def side_by_side(source, target_ref):
@@ -569,13 +569,15 @@
     turned_blocks = size == 4
     place_of = lambda plane, index: plane * size + index
     across = [(d, place_of(d // size ^ 1, d % size)) for d in range(count)]
-    neighbour = lax.ppermute(grad_out, "expert", across)
+    neighbour = lax.ppermute(touched(copied(grad_out, tile), spare_hidden, metas), "expert", across)
     out_spare = project_spare(spare_hidden, near, far, tile)
     plans = plan(metas, cap, half, main, slots, turned_blocks)
     sel, gate, mix_mirror, plane_sel, plane_gate, mix_own = plans[:6]
     give_own, take_own, give_mirror, take_mirror = plans[6:]
     blocks = 4 if turned_blocks else 1
-    packed_own = pack_plane(plane_sel, plane_gate, grad_out, neighbour, blocks, tile)
+    out_main, turned, far_turned = project(hidden, spare_hidden, near, far, tile, out_spare)
+    given_main = give_main(give_mirror, out_main, tile)
+    packed_own = pack_plane(plane_sel, plane_gate, grad_out, neighbour, blocks, tile, given_main)
     if turned_blocks:
         ways = [[(d, d // size * size + (d % size ^ way)) for d in range(count)] for way in range(blocks)]
         arrived_own = [packed_own[0]]
@@ -585,10 +587,8 @@
         rows = packed_own[0].reshape(size, 2 * cap, width)
         rows = lax.all_to_all(rows, "expert", 0, 0, axis_index_groups=planes, tiled=True)
         arrived_own = [rows.reshape(half * cap, width)]
-    out_main, turned, far_turned = project(hidden, spare_hidden, near, far, tile, out_spare, packed_own[0])
     out_spare = swapped(out_spare, "expert", half)
-    given_main = give_main(give_mirror, out_main, tile)
-    mirror = swapped(touched(copied(grad_out, tile), out_main, sel), "expert", half)
+    mirror = swapped(touched(copied(grad_out, tile, meta), out_main, packed_own[0]), "expert", half)
     other_turned = swapped(far_turned, "dp", 1)
     given_mirror = give_rest(give_mirror, given_main, out_spare, tile, GIVE_COST)
     returned_mirror = to_half(given_mirror)

time: 223 us -> 210 us (0.942)
  waiting for transfers between devices: 117 us -> 105 us
  starting transfers between devices: 33.2 us -> 29.6 us
    ppermute x10, waiting for transfers between devices: 54.1 us -> 14.6 us  [swapped(): return lax.ppermute(value, axis, pairs)]
    ppermute x3, waiting for transfers between devices: 0.01 us -> 23.9 us  [local(): lax.ppermute(packed_own[way], 'expert', ways[way])]
    all_to_all x3, waiting for transfers between devices: 62.5 us -> 53.1 us  [to_half(): lax.all_to_all(rows.reshape(half, cap, width), 'expert', 0, 0, axis_index...]
    ppermute x1, waiting for transfers between devices: 0.01 us -> 7.98 us  [local(): lax.ppermute(touched(copied(grad_out, tile), spare_hidden, metas), 'exper...]
    all_to_all x1, waiting for transfers between devices: 0.01 us -> 5.61 us  [local(): metas = lax.all_to_all(meta, 'expert', 0, 0, tiled=True)]
    pallas_call x20 -> x22, Pallas kernels: 71.4 us -> 73.4 us  [call(): pl.pallas_call(kernel, grid=(grid,), in_specs=[spec for _, spec in ins] +...]
  transfers between devices with their start and end apart: 18 -> 18, of which waited for: 8 -> 10; matrix products, arithmetic and copies ran while one was open for 0% -> 0% of each run, Pallas kernels for 31% -> 33%
where the time goes in v10:
time: 210 us; the launch traced here: 209 us
  waiting for transfers between devices  105 us (50%)
  Pallas kernels  73.4 us (35%)
  starting transfers between devices  29.6 us (14%)
    pallas_call x22, Pallas kernels, call(): pl.pallas_call(kernel, grid=(grid,), in_specs=[spec for _, spec in ins] +...  73.4 us
    all_to_all x3, waiting for transfers between devices, to_half(): lax.all_to_all(rows.reshape(half, cap, width), 'expert', 0, 0, axis_index...  53.1 us
    ppermute x3, waiting for transfers between devices, local(): lax.ppermute(packed_own[way], 'expert', ways[way])  23.9 us
    ppermute x10, waiting for transfers between devices, swapped(): return lax.ppermute(value, axis, pairs)  14.6 us
    all_to_all x3, starting transfers between devices, to_half(): lax.all_to_all(rows.reshape(half, cap, width), 'expert', 0, 0, axis_index...  13.3 us
    ppermute x1, waiting for transfers between devices, local(): lax.ppermute(touched(copied(grad_out, tile), spare_hidden, metas), 'exper...  7.98 us
    ppermute x10, starting transfers between devices, swapped(): return lax.ppermute(value, axis, pairs)  7.32 us
    all_to_all x1, waiting for transfers between devices, local(): metas = lax.all_to_all(meta, 'expert', 0, 0, tiled=True)  5.61 us
  transfers between devices with their start and end apart: 18, of which 10 were waited for; matrix products, arithmetic and copies ran while one was open for 0% of the time, Pallas kernels for 33%

profile of v10, /device:TPU:0, one launch (start us, length us, event | category | flops | bytes accessed | tf_op | source)
XLA Modules:
  0.0 209.0 jit_solution(16168007723944170747)
XLA Ops:
  0.6 0.5 collective-permute-start.1
  1.1 1.6 shard_map.85
  2.8 3.6 %collective-permute-start = (bf16[64,1024]{1,0:T(8,128)(2,1)}, bf16[64,1024]{1,0:T(8,128)(2,1)}, u32[]{:S(2)}, u32[]{:S(2)}) collective-permute-start(bf16[64,1024]{1,0:T(8,128)(2,1)} %get-tuple-element.27), channel_id=1, source_target_pairs={{0,8},{1,9},{2,10},{3,11},{4,12},{5,13},{6,14},{7,15},{8,0},{9,1},... | collective-permute-start | bytes 393224 | tf_op jit(solution)/shard_map/ppermute | solution.py:20
  6.4 4.9 %all-to-all-start = ((f32[16,8,128]{2,1,0:T(8,128)}), f32[16,8,128]{2,1,0:T(8,128)}, u32[]{:S(2)}, u32[]{:S(2)}) async-start(f32[16,8,128]{2,1,0:T(8,128)} %get-tuple-element.24.refs_1_), calls=%async_computation | async-start | bytes 131072 | tf_op jit(solution)/shard_map/all_to_all | solution.py:567
  11.3 2.0 shard_map.90.refs_0_
  13.3 5.6 %all-to-all-done.refs_0_.refs_2_ = f32[16,8,128]{2,1,0:T(8,128)} async-done(((f32[16,8,128]{2,1,0:T(8,128)}), f32[16,8,128]{2,1,0:T(8,128)}, u32[]{:S(2)}, u32[]{:S(2)}) %all-to-all-start) | async-done | bytes 65568 | tf_op jit(solution)/shard_map/all_to_all | solution.py:567
  18.9 0.0 collective-permute-done.refs_0_.refs_1_
  18.9 0.7 collective-permute-start.3
  19.5 0.0 collective-permute-done.1.refs_2_.refs_3_
  19.5 4.6 %shard_map.87.refs_4_ = bf16[64,3584]{1,0:T(8,128)(2,1)} custom-call(bf16[64,1024]{1,0:T(8,128)(2,1)} %collective-permute-done.refs_0_.refs_1_, bf16[512,3584]{1,0:T(8,128)(2,1)} %bitcast.16, bf16[512,3584]{1,0:T(8,128)(2,1)} %collective-permute-done.1.refs_2_.refs_3_), custom_call_target="tpu_custom_call" | custom-call | tf_op jit(solution)/shard_map/pallas_call | solution.py:60
  24.2 1.4 collective-permute-start.2
  25.6 2.0 shard_map.89.refs_0_
  27.6 3.7 %shard_map.86 = (bf16[320,128]{1,0:T(8,128)(2,1)}, f32[320,128]{1,0:T(8,128)}, bf16[256,320]{1,0:T(8,128)(2,1)}, bf16[320,256]{1,0:T(8,128)(2,1)}, f32[320,128]{...) custom-call(f32[16,8,128]{2,1,0:T(8,128)} %all-to-all-done.refs_0_.r, ...), custom_call_target="tpu_custom_call" | custom-call | tf_op jit(solution)/shard_map/pallas_call | solution.py:60
  31.2 7.0 %shard_map.88 = (bf16[384,3584]{1,0:T(8,128)(2,1)}, bf16[512,448]{1,0:T(8,128)(2,1)}, bf16[512,448]{1,0:T(8,128)(2,1)}) custom-call(bf16[448,1024]{1,0:T(8,128)(2,1)} %bitcast.21, bf16[64,1024]{1,0:T(8,128)(2,1)} %collective-permute-done.refs_0_.refs_1_, bf16[512,3584]{1,0:T(8,128)(2,1)} %bitcast.17, ...), custom_call_target="tpu_custom_call" | custom-call | tf_op jit(solution)/shard_map/pallas_call | solution.py:60
  38.2 4.0 %shard_map.92.refs_4_.refs_1_ = bf16[320,3584]{1,0:T(8,128)(2,1)} custom-call(bf16[320,448]{1,0:T(8,128)(2,1)} %get-tuple-element.33.refs_0_, bf16[384,3584]{1,0:T(8,128)(2,1)} %get-tuple-element.28.refs_1_), custom_call_target="tpu_custom_call" | custom-call | tf_op jit(solution)/shard_map/pallas_call | solution.py:60
  42.2 8.0 %collective-permute-done.3.refs_3_ = bf16[128,3584]{1,0:T(8,128)(2,1)} collective-permute-done((bf16[128,3584]{1,0:T(8,128)(2,1)}, bf16[128,3584]{1,0:T(8,128)(2,1)}, u32[]{:S(2)}, u32[]{:S(2)}) %collective-permute-start.3) | collective-permute-done | bytes 917536 | tf_op jit(solution)/shard_map/ppermute | solution.py:572
  50.2 3.7 %shard_map.93 = (bf16[80,3584]{1,0:T(8,128)(2,1)}, bf16[80,3584]{1,0:T(8,128)(2,1)}, bf16[80,3584]{1,0:T(8,128)(2,1)}, bf16[80,3584]{1,0:T(8,128)(2,1)}) custom-call(bf16[320,256]{1,0:T(8,128)(2,1)} %get-tuple-element.31.refs_0_, f32[320,128]{1,0:T(8,128)} %get-tuple-element.32.refs_1_, bf16[128,3584]{1,0:T(8,128)(2,1)} %refs_2_.1, ...), custom_call_target="tpu_custom_call" | custom-call | tf_op jit(solution)/shard_map/pallas_call | solution.py:60
  53.9 0.4 collective-permute-start.4
  54.3 0.7 collective-permute-start.5
  55.0 0.8 collective-permute-start.6
  55.8 2.0 collective-permute-start.7
  57.8 0.0 collective-permute-done.2.refs_2_
  57.8 3.3 %shard_map.97 = bf16[320,3584]{1,0:T(8,128)(2,1)} custom-call(bf16[320,448]{1,0:T(8,128)(2,1)} %get-tuple-element.33.refs_0_, bf16[320,3584]{1,0:T(8,128)(2,1)} %shard_map.92.refs_4_.refs_1_, bf16[64,3584]{1,0:T(8,128)(2,1)} %collective-permute-done.2.refs_2_), custom_call_target="tpu_custom_call" | custom-call | flops 5000000000 | tf_op jit(solution)/shard_map/pallas_call | solution.py:60
  61.1 4.4 %all-to-all-start.1 = ((bf16[8,40,3584]{2,1,0:T(8,128)(2,1)}), bf16[8,40,3584]{2,1,0:T(8,128)(2,1)}, u32[]{:S(2)}, u32[]{:S(2)}) async-start(bf16[8,40,3584]{2,1,0:T(8,128)(2,1)} %bitcast.23), calls=%async_computation.1 | async-start | bytes 4587520 | tf_op jit(solution)/shard_map/all_to_all | solution.py:558
  65.5 10.7 %collective-permute-done.5.refs_3_.refs_4_ = bf16[80,3584]{1,0:T(8,128)(2,1)} collective-permute-done((bf16[80,3584]{1,0:T(8,128)(2,1)}, bf16[80,3584]{1,0:T(8,128)(2,1)}, u32[]{:S(2)}, u32[]{:S(2)}) %collective-permute-start.5) | collective-permute-done | bytes 573472 | tf_op jit(solution)/shard_map/ppermute | solution.py:584
  76.2 0.0 collective-permute-done.6.refs_4_.refs_5_
  76.2 13.2 %collective-permute-done.7.refs_5_.refs_6_ = bf16[80,3584]{1,0:T(8,128)(2,1)} collective-permute-done((bf16[80,3584]{1,0:T(8,128)(2,1)}, bf16[80,3584]{1,0:T(8,128)(2,1)}, u32[]{:S(2)}, u32[]{:S(2)}) %collective-permute-start.7) | collective-permute-done | bytes 573472 | tf_op jit(solution)/shard_map/ppermute | solution.py:584
  89.4 5.7 %collective-permute-done.4.refs_2_ = bf16[128,3584]{1,0:T(8,128)(2,1)} collective-permute-done((bf16[128,3584]{1,0:T(8,128)(2,1)}, bf16[128,3584]{1,0:T(8,128)(2,1)}, u32[]{:S(2)}, u32[]{:S(2)}) %collective-permute-start.4) | collective-permute-done | bytes 917536 | tf_op jit(solution)/shard_map/ppermute | solution.py:20
  95.1 3.1 %shard_map.95.refs_3_.refs_0_ = bf16[320,3584]{1,0:T(8,128)(2,1)} custom-call(bf16[320,128]{1,0:T(8,128)(2,1)} %get-tuple-element.29.refs_0_, f32[320,128]{1,0:T(8,128)} %get-tuple-element.30.refs_1_, bf16[128,3584]{1,0:T(8,128)(2,1)} %collective-permute-done.4.refs_2_, bf16[80,3584]{1,0:T(8,128)(2,1)} %collective-permute-done.5.refs_3_.refs_4_, ...), custom_call_target="tpu_custom_call" | custom-call | flops 3999999983616 | tf_op jit(solution)/shard_map/pallas_call | solution.py:60
  98.2 4.7 %shard_map.96.refs_2_.refs_0_ = bf16[320,3584]{1,0:T(8,128)(2,1)} custom-call(bf16[320,448]{1,0:T(8,128)(2,1)} %get-tuple-element.26.refs_0_, bf16[384,3584]{1,0:T(8,128)(2,1)} %get-tuple-element.28.refs_1_, bf16[64,3584]{1,0:T(8,128)(2,1)} %collective-permute-done.2.refs_2_, bf16[320,3584]{1,0:T(8,128)(2,1)} %shard_map.95.refs_3_.refs_0_), custom_call_target="tpu_custom_call" | custom-call | tf_op jit(solution)/shard_map/pallas_call | solution.py:60
  102.9 7.4 %all-to-all-done.1 = bf16[8,40,3584]{2,1,0:T(8,128)(2,1)} async-done(((bf16[8,40,3584]{2,1,0:T(8,128)(2,1)}), bf16[8,40,3584]{2,1,0:T(8,128)(2,1)}, u32[]{:S(2)}, u32[]{:S(2)}) %all-to-all-start.1) | async-done | bytes 2293792 | tf_op jit(solution)/shard_map/all_to_all | solution.py:558
  110.4 4.4 %all-to-all-start.2 = ((bf16[8,40,3584]{2,1,0:T(8,128)(2,1)}), bf16[8,40,3584]{2,1,0:T(8,128)(2,1)}, u32[]{:S(2)}, u32[]{:S(2)}) async-start(bf16[8,40,3584]{2,1,0:T(8,128)(2,1)} %bitcast.14), calls=%async_computation.2 | async-start | bytes 4587520 | tf_op jit(solution)/shard_map/all_to_all | solution.py:558
  114.7 3.3 %shard_map.98 = bf16[128,3584]{1,0:T(8,128)(2,1)} custom-call(bf16[256,320]{1,0:T(8,128)(2,1)} %get-tuple-element.38.refs_0_, bf16[320,3584]{1,0:T(8,128)(2,1)} %bitcast.6.refs_1_), custom_call_target="tpu_custom_call" | custom-call | tf_op jit(solution)/shard_map/pallas_call | solution.py:60
  118.1 0.8 collective-permute-start.8
  118.9 41.3 %all-to-all-done.2 = bf16[8,40,3584]{2,1,0:T(8,128)(2,1)} async-done(((bf16[8,40,3584]{2,1,0:T(8,128)(2,1)}), bf16[8,40,3584]{2,1,0:T(8,128)(2,1)}, u32[]{:S(2)}, u32[]{:S(2)}) %all-to-all-start.2) | async-done | bytes 2293792 | tf_op jit(solution)/shard_map/all_to_all | solution.py:558
  160.2 3.7 %shard_map.100.refs_2_.refs_7_ = bf16[64,3584]{1,0:T(8,128)(2,1)} custom-call(bf16[448,320]{1,0:T(8,128)(2,1)} %get-tuple-element.39.refs_0_, bf16[448,320]{1,0:T(8,128)(2,1)} %get-tuple-element.40.refs_1_, bf16[320,3584]{1,0:T(8,128)(2,1)} %bitcast.8.refs_2_, bf16[80,3584]{1,0:T(8,128)(2,1)} %get-tuple-element.34.refs_2_.refs_3_, ...), custom_call_target="tpu_custom_call" | custom-call | tf_op jit(solution)/shard_map/pallas_call | solution.py:60
  163.9 0.0 collective-permute-start.9
  163.9 0.0 collective-permute-done.8.refs_1_.refs_2_
  163.9 4.6 %all-to-all-start.3 = ((bf16[8,40,3584]{2,1,0:T(8,128)(2,1)}), bf16[8,40,3584]{2,1,0:T(8,128)(2,1)}, u32[]{:S(2)}, u32[]{:S(2)}) async-start(bf16[8,40,3584]{2,1,0:T(8,128)(2,1)} %bitcast.13), calls=%async_computation.3 | async-start | bytes 4587520 | tf_op jit(solution)/shard_map/all_to_all | solution.py:558
  168.5 0.1 collective-permute-start.11
  168.6 6.3 %shard_map.103.refs_0_.refs_2_ = bf16[384,3584]{1,0:T(8,128)(2,1)} custom-call(bf16[448,320]{1,0:T(8,128)(2,1)} %get-tuple-element.39.refs_0_, bf16[448,320]{1,0:T(8,128)(2,1)} %get-tuple-element.40.refs_1_, bf16[320,3584]{1,0:T(8,128)(2,1)} %bitcast.8.refs_2_, bf16[80,3584]{1,0:T(8,128)(2,1)} %get-tuple-element.34.refs_2_.refs_3_, ...), custom_call_target="tpu_custom_call" | custom-call | tf_op jit(solution)/shard_map/pallas_call | solution.py:60
  174.9 0.5 collective-permute-start.12
  175.4 8.3 %collective-permute-done.9.refs_1_.refs_3_ = bf16[64,3584]{1,0:T(8,128)(2,1)} collective-permute-done((bf16[64,3584]{1,0:T(8,128)(2,1)}, bf16[64,3584]{1,0:T(8,128)(2,1)}, u32[]{:S(2)}, u32[]{:S(2)}) %collective-permute-start.9) | collective-permute-done | bytes 458784 | tf_op jit(solution)/shard_map/ppermute | solution.py:20
  183.7 0.0 collective-permute-start.13
  183.7 7.5 %shard_map.104 = (bf16[448,1024]{1,0:T(8,128)(2,1)}, bf16[64,1024]{1,0:T(8,128)(2,1)}) custom-call(bf16[384,3584]{1,0:T(8,128)(2,1)} %shard_map.103.refs_0_.refs_2_, bf16[64,3584]{1,0:T(8,128)(2,1)} %collective-permute-done.9.refs_1_.refs_3_, bf16[512,3584]{1,0:T(8,128)(2,1)} %bitcast.18, bf16[512,3584]{1,0:T(8,128)(2,1)} %collective-permute-done.1.refs_2_.refs_3_), custom_call_target="tpu_custom_call" | custom-call | flops 40000000000 | tf_op jit(solution)/shard_map/pallas_call | solution.py:60
  191.2 0.0 collective-permute-start.10
  191.2 0.0 collective-permute-done.11.refs_1_
  191.2 0.0 collective-permute-done.13.refs_5_
  191.2 0.0 collective-permute-done.12.refs_4_
  191.2 7.7 %shard_map.105.refs_2_ = bf16[512,3584]{1,0:T(8,128)(2,1)} custom-call(bf16[512,448]{1,0:T(8,128)(2,1)} %get-tuple-element.43.refs_0_, bf16[512,448]{1,0:T(8,128)(2,1)} %collective-permute-done.11.refs_1_, bf16[384,3584]{1,0:T(8,128)(2,1)} %shard_map.103.refs_0_.refs_2_, bf16[64,3584]{1,0:T(8,128)(2,1)} %collective-permute-done.9.refs_1_.refs_3_, ...), custom_call_target="tpu_custom_call" | custom-call | tf_op jit(solution)/shard_map/pallas_call | solution.py:60
  198.9 0.6 collective-permute-done.10.refs_1_
  199.6 1.6 shard_map.106
  201.1 4.4 %all-to-all-done.3 = bf16[8,40,3584]{2,1,0:T(8,128)(2,1)} async-done(((bf16[8,40,3584]{2,1,0:T(8,128)(2,1)}), bf16[8,40,3584]{2,1,0:T(8,128)(2,1)}, u32[]{:S(2)}, u32[]{:S(2)}) %all-to-all-start.3) | async-done | bytes 2293792 | tf_op jit(solution)/shard_map/all_to_all | solution.py:558
  205.5 3.5 %shard_map.102 = bf16[128,3584]{1,0:T(8,128)(2,1)} custom-call(bf16[256,320]{1,0:T(8,128)(2,1)} %get-tuple-element.25.refs_0_, bf16[320,3584]{1,0:T(8,128)(2,1)} %bitcast.10.refs_1_, bf16[128,3584]{1,0:T(8,128)(2,1)} %collective-permute-done.8.refs_1_.refs_2_), custom_call_target="tpu_custom_call" | custom-call | tf_op jit(solution)/shard_map/pallas_call | solution.py:60
  (4 shorter events, 0.0 us)
Async XLA Ops:
  0.6 18.9 %collective-permute-start.1 = (bf16[512,3584]{1,0:T(8,128)(2,1)}, bf16[512,3584]{1,0:T(8,128)(2,1)}, u32[]{:S(2)}, u32[]{:S(2)}) collective-permute-start(bf16[512,3584]{1,0:T(8,128)(2,1)} %bitcast.15), channel_id=1, source_target_pairs={{0,16},{16,0},{1,17},{17,1},{2,18},{18,2},{3,19},{19,3},{4,20},{20... | collective-permute-start | bytes 11010056 | tf_op jit(solution)/shard_map/ppermute | solution.py:20
  2.8 16.1 %collective-permute-start = (bf16[64,1024]{1,0:T(8,128)(2,1)}, bf16[64,1024]{1,0:T(8,128)(2,1)}, u32[]{:S(2)}, u32[]{:S(2)}) collective-permute-start(bf16[64,1024]{1,0:T(8,128)(2,1)} %get-tuple-element.27), channel_id=1, source_target_pairs={{0,8},{1,9},{2,10},{3,11},{4,12},{5,13},{6,14},{7,15},{8,0},{9,1},... | collective-permute-start | bytes 393224 | tf_op jit(solution)/shard_map/ppermute | solution.py:20
  6.4 12.5 %all-to-all-start = ((f32[16,8,128]{2,1,0:T(8,128)}), f32[16,8,128]{2,1,0:T(8,128)}, u32[]{:S(2)}, u32[]{:S(2)}) async-start(f32[16,8,128]{2,1,0:T(8,128)} %get-tuple-element.24.refs_1_), calls=%async_computation | async-start | bytes 131072 | tf_op jit(solution)/shard_map/all_to_all | solution.py:567
  18.9 31.3 %collective-permute-start.3 = (bf16[128,3584]{1,0:T(8,128)(2,1)}, bf16[128,3584]{1,0:T(8,128)(2,1)}, u32[]{:S(2)}, u32[]{:S(2)}) collective-permute-start(bf16[128,3584]{1,0:T(8,128)(2,1)} %shard_map.91), channel_id=1, source_target_pairs={{0,4},{1,5},{2,6},{3,7},{4,0},{5,1},{6,2},{7,3},{8,12},{9,13},{10,... | collective-permute-start | bytes 2752520 | tf_op jit(solution)/shard_map/ppermute | solution.py:572
  24.2 33.6 %collective-permute-start.2 = (bf16[64,3584]{1,0:T(8,128)(2,1)}, bf16[64,3584]{1,0:T(8,128)(2,1)}, u32[]{:S(2)}, u32[]{:S(2)}) collective-permute-start(bf16[64,3584]{1,0:T(8,128)(2,1)} %shard_map.87.refs_4_), channel_id=1, source_target_pairs={{0,8},{1,9},{2,10},{3,11},{4,12},{5,13},{6,14},{7,15},{8,0},{9,1},... | collective-permute-start | bytes 1376264 | tf_op jit(solution)/shard_map/ppermute | solution.py:20
  53.9 41.2 %collective-permute-start.4 = (bf16[128,3584]{1,0:T(8,128)(2,1)}, bf16[128,3584]{1,0:T(8,128)(2,1)}, u32[]{:S(2)}, u32[]{:S(2)}) collective-permute-start(bf16[128,3584]{1,0:T(8,128)(2,1)} %shard_map.94), channel_id=1, source_target_pairs={{0,8},{1,9},{2,10},{3,11},{4,12},{5,13},{6,14},{7,15},{8,0},{9,1},... | collective-permute-start | bytes 2752520 | tf_op jit(solution)/shard_map/ppermute | solution.py:20
  54.3 21.9 %collective-permute-start.5 = (bf16[80,3584]{1,0:T(8,128)(2,1)}, bf16[80,3584]{1,0:T(8,128)(2,1)}, u32[]{:S(2)}, u32[]{:S(2)}) collective-permute-start(bf16[80,3584]{1,0:T(8,128)(2,1)} %get-tuple-element.35), channel_id=1, source_target_pairs={{0,1},{1,0},{2,3},{3,2},{4,5},{5,4},{6,7},{7,6},{8,9},{9,8},{10,11... | collective-permute-start | bytes 1720328 | tf_op jit(solution)/shard_map/ppermute | solution.py:584
  55.0 21.2 %collective-permute-start.6 = (bf16[80,3584]{1,0:T(8,128)(2,1)}, bf16[80,3584]{1,0:T(8,128)(2,1)}, u32[]{:S(2)}, u32[]{:S(2)}) collective-permute-start(bf16[80,3584]{1,0:T(8,128)(2,1)} %get-tuple-element.36), channel_id=1, source_target_pairs={{0,2},{1,3},{2,0},{3,1},{4,6},{5,7},{6,4},{7,5},{8,10},{9,11},{10,... | collective-permute-start | bytes 1720328 | tf_op jit(solution)/shard_map/ppermute | solution.py:584
  55.8 33.6 %collective-permute-start.7 = (bf16[80,3584]{1,0:T(8,128)(2,1)}, bf16[80,3584]{1,0:T(8,128)(2,1)}, u32[]{:S(2)}, u32[]{:S(2)}) collective-permute-start(bf16[80,3584]{1,0:T(8,128)(2,1)} %get-tuple-element.37), channel_id=1, source_target_pairs={{0,3},{1,2},{2,1},{3,0},{4,7},{5,6},{6,5},{7,4},{8,11},{9,10},{10,... | collective-permute-start | bytes 1720328 | tf_op jit(solution)/shard_map/ppermute | solution.py:584
  61.1 49.2 %all-to-all-start.1 = ((bf16[8,40,3584]{2,1,0:T(8,128)(2,1)}), bf16[8,40,3584]{2,1,0:T(8,128)(2,1)}, u32[]{:S(2)}, u32[]{:S(2)}) async-start(bf16[8,40,3584]{2,1,0:T(8,128)(2,1)} %bitcast.23), calls=%async_computation.1 | async-start | bytes 4587520 | tf_op jit(solution)/shard_map/all_to_all | solution.py:558
  110.4 49.9 %all-to-all-start.2 = ((bf16[8,40,3584]{2,1,0:T(8,128)(2,1)}), bf16[8,40,3584]{2,1,0:T(8,128)(2,1)}, u32[]{:S(2)}, u32[]{:S(2)}) async-start(bf16[8,40,3584]{2,1,0:T(8,128)(2,1)} %bitcast.14), calls=%async_computation.2 | async-start | bytes 4587520 | tf_op jit(solution)/shard_map/all_to_all | solution.py:558
  118.1 45.8 %collective-permute-start.8 = (bf16[128,3584]{1,0:T(8,128)(2,1)}, bf16[128,3584]{1,0:T(8,128)(2,1)}, u32[]{:S(2)}, u32[]{:S(2)}) collective-permute-start(bf16[128,3584]{1,0:T(8,128)(2,1)} %shard_map.98), channel_id=1, source_target_pairs={{0,8},{1,9},{2,10},{3,11},{4,12},{5,13},{6,14},{7,15},{8,0},{9,1},... | collective-permute-start | bytes 2752520 | tf_op jit(solution)/shard_map/ppermute | solution.py:20
  163.9 19.7 %collective-permute-start.9 = (bf16[64,3584]{1,0:T(8,128)(2,1)}, bf16[64,3584]{1,0:T(8,128)(2,1)}, u32[]{:S(2)}, u32[]{:S(2)}) collective-permute-start(bf16[64,3584]{1,0:T(8,128)(2,1)} %shard_map.100.refs_2_.refs_7_), channel_id=1, source_target_pairs={{0,8},{1,9},{2,10},{3,11},{4,12},{5,13},{6,14},{7,15},{8,0},{9,1},... | collective-permute-start | bytes 1376264 | tf_op jit(solution)/shard_map/ppermute | solution.py:20
  163.9 41.6 %all-to-all-start.3 = ((bf16[8,40,3584]{2,1,0:T(8,128)(2,1)}), bf16[8,40,3584]{2,1,0:T(8,128)(2,1)}, u32[]{:S(2)}, u32[]{:S(2)}) async-start(bf16[8,40,3584]{2,1,0:T(8,128)(2,1)} %bitcast.13), calls=%async_computation.3 | async-start | bytes 4587520 | tf_op jit(solution)/shard_map/all_to_all | solution.py:558
  168.5 22.7 %collective-permute-start.11 = (bf16[512,448]{1,0:T(8,128)(2,1)}, bf16[512,448]{1,0:T(8,128)(2,1)}, u32[]{:S(2)}, u32[]{:S(2)}) collective-permute-start(bf16[512,448]{1,0:T(8,128)(2,1)} %get-tuple-element.44), channel_id=1, source_target_pairs={{0,16},{16,0},{1,17},{17,1},{2,18},{18,2},{3,19},{19,3},{4,20},{20... | collective-permute-start | bytes 1376264 | tf_op jit(solution)/shard_map/ppermute | solution.py:20
  174.9 16.3 %collective-permute-start.12 = (bf16[384,3584]{1,0:T(8,128)(2,1)}, bf16[384,3584]{1,0:T(8,128)(2,1)}, u32[]{:S(2)}, u32[]{:S(2)}) collective-permute-start(bf16[384,3584]{1,0:T(8,128)(2,1)} %shard_map.103.refs_0_.refs_2_), channel_id=1, source_target_pairs={{0,16},{16,0},{1,17},{17,1},{2,18},{18,2},{3,19},{19,3},{4,20},{20... | collective-permute-start | bytes 8257544 | tf_op jit(solution)/shard_map/ppermute | solution.py:20
  183.7 7.5 %collective-permute-start.13 = (bf16[64,3584]{1,0:T(8,128)(2,1)}, bf16[64,3584]{1,0:T(8,128)(2,1)}, u32[]{:S(2)}, u32[]{:S(2)}) collective-permute-start(bf16[64,3584]{1,0:T(8,128)(2,1)} %collective-permute-done.9.refs_1_.refs_3_), channel_id=1, source_target_pairs={{0,16},{16,0},{1,17},{17,1},{2,18},{18,2},{3,19},{19,3},{4,20},{20... | collective-permute-start | bytes 1376264 | tf_op jit(solution)/shard_map/ppermute | solution.py:20
  191.2 8.4 %collective-permute-start.10 = (bf16[64,1024]{1,0:T(8,128)(2,1)}, bf16[64,1024]{1,0:T(8,128)(2,1)}, u32[]{:S(2)}, u32[]{:S(2)}) collective-permute-start(bf16[64,1024]{1,0:T(8,128)(2,1)} %get-tuple-element.42), channel_id=1, source_target_pairs={{0,8},{1,9},{2,10},{3,11},{4,12},{5,13},{6,14},{7,15},{8,0},{9,1},... | collective-permute-start | bytes 393224 | tf_op jit(solution)/shard_map/ppermute | solution.py:20

commit v11 on v10

--- a/solution.py
+++ b/solution.py
@@ -592,7 +592,7 @@
     other_turned = swapped(far_turned, "dp", 1)
     given_mirror = give_rest(give_mirror, given_main, out_spare, tile, GIVE_COST)
     returned_mirror = to_half(given_mirror)
-    packed_mirror = pack(sel, gate, mirror, tile, *arrived_own[1:])
+    packed_mirror = pack(sel, gate, mirror, tile, *arrived_own[1:2])
     given_own = give(give_own, out_main, out_spare, tile, 0, packed_mirror)
     arrived_mirror = to_half(touched(packed_mirror, returned_mirror, given_own))
     part = swapped(combine(mix_mirror, returned_mirror, [], tile), "expert", half)

time: 210 us -> 213 us (1.014)
  starting transfers between devices: 29.6 us -> 32.2 us
    all_to_all x3, waiting for transfers between devices: 53.1 us -> 10.1 us  [to_half(): lax.all_to_all(rows.reshape(half, cap, width), 'expert', 0, 0, axis_index...]
    ppermute x3, waiting for transfers between devices: 23.9 us -> 55.4 us  [local(): lax.ppermute(packed_own[way], 'expert', ways[way])]
    ppermute x10, waiting for transfers between devices: 14.6 us -> 27.2 us  [swapped(): return lax.ppermute(value, axis, pairs)]
  transfers between devices with their start and end apart: 18 -> 18, of which waited for: 10 -> 9; matrix products, arithmetic and copies ran while one was open for 0% -> 0% of each run, Pallas kernels for 33% -> 33%
where the time goes in v11:
time: 213 us
  waiting for transfers between devices  106 us (50%)
  Pallas kernels  73.4 us (34%)
  starting transfers between devices  32.2 us (15%)
    pallas_call x22, Pallas kernels, call(): pl.pallas_call(kernel, grid=(grid,), in_specs=[spec for _, spec in ins] +...  73.4 us
    ppermute x3, waiting for transfers between devices, local(): lax.ppermute(packed_own[way], 'expert', ways[way])  55.4 us
    ppermute x10, waiting for transfers between devices, swapped(): return lax.ppermute(value, axis, pairs)  27.2 us
    all_to_all x3, starting transfers between devices, to_half(): lax.all_to_all(rows.reshape(half, cap, width), 'expert', 0, 0, axis_index...  13.8 us
    all_to_all x3, waiting for transfers between devices, to_half(): lax.all_to_all(rows.reshape(half, cap, width), 'expert', 0, 0, axis_index...  10.1 us
    ppermute x10, starting transfers between devices, swapped(): return lax.ppermute(value, axis, pairs)  8.69 us
    ppermute x1, waiting for transfers between devices, local(): lax.ppermute(touched(copied(grad_out, tile), spare_hidden, metas), 'exper...  7.99 us
    all_to_all x1, waiting for transfers between devices, local(): metas = lax.all_to_all(meta, 'expert', 0, 0, tiled=True)  5.61 us
  transfers between devices with their start and end apart: 18, of which 9 were waited for; matrix products, arithmetic and copies ran while one was open for 0% of the time, Pallas kernels for 33%

profile of v11, /device:TPU:0, one launch (start us, length us, event | category | flops | bytes accessed | tf_op | source)
XLA Modules:
  0.0 212.6 jit_solution(14073965219292701890)
XLA Ops:
  0.6 0.5 collective-permute-start.1
  1.1 1.6 shard_map.85
  2.8 3.6 %collective-permute-start = (bf16[64,1024]{1,0:T(8,128)(2,1)}, bf16[64,1024]{1,0:T(8,128)(2,1)}, u32[]{:S(2)}, u32[]{:S(2)}) collective-permute-start(bf16[64,1024]{1,0:T(8,128)(2,1)} %get-tuple-element.27), channel_id=1, source_target_pairs={{0,8},{1,9},{2,10},{3,11},{4,12},{5,13},{6,14},{7,15},{8,0},{9,1},... | collective-permute-start | bytes 393224 | tf_op jit(solution)/shard_map/ppermute | solution.py:20
  6.4 4.9 %all-to-all-start = ((f32[16,8,128]{2,1,0:T(8,128)}), f32[16,8,128]{2,1,0:T(8,128)}, u32[]{:S(2)}, u32[]{:S(2)}) async-start(f32[16,8,128]{2,1,0:T(8,128)} %get-tuple-element.24.refs_1_), calls=%async_computation | async-start | bytes 131072 | tf_op jit(solution)/shard_map/all_to_all | solution.py:567
  11.3 2.0 shard_map.90.refs_0_
  13.3 5.6 %all-to-all-done.refs_0_.refs_2_ = f32[16,8,128]{2,1,0:T(8,128)} async-done(((f32[16,8,128]{2,1,0:T(8,128)}), f32[16,8,128]{2,1,0:T(8,128)}, u32[]{:S(2)}, u32[]{:S(2)}) %all-to-all-start) | async-done | bytes 65568 | tf_op jit(solution)/shard_map/all_to_all | solution.py:567
  18.9 0.0 collective-permute-done.refs_0_.refs_1_
  18.9 0.7 collective-permute-start.3
  19.5 0.0 collective-permute-done.1.refs_2_.refs_3_
  19.5 4.6 %shard_map.87.refs_4_ = bf16[64,3584]{1,0:T(8,128)(2,1)} custom-call(bf16[64,1024]{1,0:T(8,128)(2,1)} %collective-permute-done.refs_0_.refs_1_, bf16[512,3584]{1,0:T(8,128)(2,1)} %bitcast.16, bf16[512,3584]{1,0:T(8,128)(2,1)} %collective-permute-done.1.refs_2_.refs_3_), custom_call_target="tpu_custom_call" | custom-call | tf_op jit(solution)/shard_map/pallas_call | solution.py:60
  24.2 1.4 collective-permute-start.2
  25.6 2.0 shard_map.89.refs_0_
  27.6 3.7 %shard_map.86 = (bf16[320,128]{1,0:T(8,128)(2,1)}, f32[320,128]{1,0:T(8,128)}, bf16[256,320]{1,0:T(8,128)(2,1)}, bf16[320,256]{1,0:T(8,128)(2,1)}, f32[320,128]{...) custom-call(f32[16,8,128]{2,1,0:T(8,128)} %all-to-all-done.refs_0_.r, ...), custom_call_target="tpu_custom_call" | custom-call | tf_op jit(solution)/shard_map/pallas_call | solution.py:60
  31.2 7.0 %shard_map.88 = (bf16[384,3584]{1,0:T(8,128)(2,1)}, bf16[512,448]{1,0:T(8,128)(2,1)}, bf16[512,448]{1,0:T(8,128)(2,1)}) custom-call(bf16[448,1024]{1,0:T(8,128)(2,1)} %bitcast.21, bf16[64,1024]{1,0:T(8,128)(2,1)} %collective-permute-done.refs_0_.refs_1_, bf16[512,3584]{1,0:T(8,128)(2,1)} %bitcast.17, ...), custom_call_target="tpu_custom_call" | custom-call | tf_op jit(solution)/shard_map/pallas_call | solution.py:60
  38.2 4.0 %shard_map.92.refs_4_.refs_1_ = bf16[320,3584]{1,0:T(8,128)(2,1)} custom-call(bf16[320,448]{1,0:T(8,128)(2,1)} %get-tuple-element.33.refs_0_, bf16[384,3584]{1,0:T(8,128)(2,1)} %get-tuple-element.28.refs_1_), custom_call_target="tpu_custom_call" | custom-call | tf_op jit(solution)/shard_map/pallas_call | solution.py:60
  42.2 8.0 %collective-permute-done.3.refs_3_ = bf16[128,3584]{1,0:T(8,128)(2,1)} collective-permute-done((bf16[128,3584]{1,0:T(8,128)(2,1)}, bf16[128,3584]{1,0:T(8,128)(2,1)}, u32[]{:S(2)}, u32[]{:S(2)}) %collective-permute-start.3) | collective-permute-done | bytes 917536 | tf_op jit(solution)/shard_map/ppermute | solution.py:572
  50.2 3.7 %shard_map.93 = (bf16[80,3584]{1,0:T(8,128)(2,1)}, bf16[80,3584]{1,0:T(8,128)(2,1)}, bf16[80,3584]{1,0:T(8,128)(2,1)}, bf16[80,3584]{1,0:T(8,128)(2,1)}) custom-call(bf16[320,256]{1,0:T(8,128)(2,1)} %get-tuple-element.31.refs_0_, f32[320,128]{1,0:T(8,128)} %get-tuple-element.32.refs_1_, bf16[128,3584]{1,0:T(8,128)(2,1)} %refs_2_.1, ...), custom_call_target="tpu_custom_call" | custom-call | tf_op jit(solution)/shard_map/pallas_call | solution.py:60
  53.9 0.4 collective-permute-start.4
  54.3 0.7 collective-permute-start.5
  55.0 0.0 collective-permute-done.2.refs_2_
  55.0 3.3 %shard_map.97 = bf16[320,3584]{1,0:T(8,128)(2,1)} custom-call(bf16[320,448]{1,0:T(8,128)(2,1)} %get-tuple-element.33.refs_0_, bf16[320,3584]{1,0:T(8,128)(2,1)} %shard_map.92.refs_4_.refs_1_, bf16[64,3584]{1,0:T(8,128)(2,1)} %collective-permute-done.2.refs_2_), custom_call_target="tpu_custom_call" | custom-call | flops 5000000000 | tf_op jit(solution)/shard_map/pallas_call | solution.py:60
  58.3 4.9 %all-to-all-start.1 = ((bf16[8,40,3584]{2,1,0:T(8,128)(2,1)}), bf16[8,40,3584]{2,1,0:T(8,128)(2,1)}, u32[]{:S(2)}, u32[]{:S(2)}) async-start(bf16[8,40,3584]{2,1,0:T(8,128)(2,1)} %bitcast.23), calls=%async_computation.1 | async-start | bytes 4587520 | tf_op jit(solution)/shard_map/all_to_all | solution.py:558
  63.3 13.7 %collective-permute-done.5.refs_3_.refs_4_ = bf16[80,3584]{1,0:T(8,128)(2,1)} collective-permute-done((bf16[80,3584]{1,0:T(8,128)(2,1)}, bf16[80,3584]{1,0:T(8,128)(2,1)}, u32[]{:S(2)}, u32[]{:S(2)}) %collective-permute-start.5) | collective-permute-done | bytes 573472 | tf_op jit(solution)/shard_map/ppermute | solution.py:584
  76.9 18.2 %collective-permute-done.4.refs_2_ = bf16[128,3584]{1,0:T(8,128)(2,1)} collective-permute-done((bf16[128,3584]{1,0:T(8,128)(2,1)}, bf16[128,3584]{1,0:T(8,128)(2,1)}, u32[]{:S(2)}, u32[]{:S(2)}) %collective-permute-start.4) | collective-permute-done | bytes 917536 | tf_op jit(solution)/shard_map/ppermute | solution.py:20
  95.1 3.1 %shard_map.95.refs_3_.refs_0_ = bf16[320,3584]{1,0:T(8,128)(2,1)} custom-call(bf16[320,128]{1,0:T(8,128)(2,1)} %get-tuple-element.29.refs_0_, f32[320,128]{1,0:T(8,128)} %get-tuple-element.30.refs_1_, bf16[128,3584]{1,0:T(8,128)(2,1)} %collective-permute-done.4.refs_2_, bf16[80,3584]{1,0:T(8,128)(2,1)} %collective-permute-done.5.refs_3_.refs_4_), custom_call_target="tpu_custom_call" | custom-call | flops 3999999983616 | tf_op jit(solution)/shard_map/pallas_call | solution.py:60
  98.2 4.7 %shard_map.96.refs_2_.refs_0_ = bf16[320,3584]{1,0:T(8,128)(2,1)} custom-call(bf16[320,448]{1,0:T(8,128)(2,1)} %get-tuple-element.26.refs_0_, bf16[384,3584]{1,0:T(8,128)(2,1)} %get-tuple-element.28.refs_1_, bf16[64,3584]{1,0:T(8,128)(2,1)} %collective-permute-done.2.refs_2_, bf16[320,3584]{1,0:T(8,128)(2,1)} %shard_map.95.refs_3_.refs_0_), custom_call_target="tpu_custom_call" | custom-call | tf_op jit(solution)/shard_map/pallas_call | solution.py:60
  102.9 5.2 %all-to-all-done.1 = bf16[8,40,3584]{2,1,0:T(8,128)(2,1)} async-done(((bf16[8,40,3584]{2,1,0:T(8,128)(2,1)}), bf16[8,40,3584]{2,1,0:T(8,128)(2,1)}, u32[]{:S(2)}, u32[]{:S(2)}) %all-to-all-start.1) | async-done | bytes 2293792 | tf_op jit(solution)/shard_map/all_to_all | solution.py:558
  108.1 4.4 %all-to-all-start.2 = ((bf16[8,40,3584]{2,1,0:T(8,128)(2,1)}), bf16[8,40,3584]{2,1,0:T(8,128)(2,1)}, u32[]{:S(2)}, u32[]{:S(2)}) async-start(bf16[8,40,3584]{2,1,0:T(8,128)(2,1)} %bitcast.14), calls=%async_computation.2 | async-start | bytes 4587520 | tf_op jit(solution)/shard_map/all_to_all | solution.py:558
  112.5 3.3 %shard_map.98 = bf16[128,3584]{1,0:T(8,128)(2,1)} custom-call(bf16[256,320]{1,0:T(8,128)(2,1)} %get-tuple-element.36.refs_0_, bf16[320,3584]{1,0:T(8,128)(2,1)} %bitcast.6.refs_1_), custom_call_target="tpu_custom_call" | custom-call | tf_op jit(solution)/shard_map/pallas_call | solution.py:60
  115.8 1.3 collective-permute-start.6
  117.1 2.0 collective-permute-start.7
  119.1 1.5 collective-permute-start.8
  120.6 41.7 %collective-permute-done.7.refs_5_ = bf16[80,3584]{1,0:T(8,128)(2,1)} collective-permute-done((bf16[80,3584]{1,0:T(8,128)(2,1)}, bf16[80,3584]{1,0:T(8,128)(2,1)}, u32[]{:S(2)}, u32[]{:S(2)}) %collective-permute-start.7) | collective-permute-done | bytes 573472 | tf_op jit(solution)/shard_map/ppermute | solution.py:584
  162.3 0.0 collective-permute-done.8.refs_6_
  162.3 0.0 all-to-all-done.2
  162.3 3.7 %shard_map.100.refs_2_.refs_7_ = bf16[64,3584]{1,0:T(8,128)(2,1)} custom-call(bf16[448,320]{1,0:T(8,128)(2,1)} %get-tuple-element.37.refs_0_, bf16[448,320]{1,0:T(8,128)(2,1)} %get-tuple-element.38.refs_1_, bf16[320,3584]{1,0:T(8,128)(2,1)} %bitcast.8.refs_2_, bf16[80,3584]{1,0:T(8,128)(2,1)} %get-tuple-element.34.refs_2_.refs_3_, ...), custom_call_target="tpu_custom_call" | custom-call | tf_op jit(solution)/shard_map/pallas_call | solution.py:60
  166.0 0.9 collective-permute-start.9
  166.9 0.0 collective-permute-done.6.refs_1_.refs_2_
  166.9 4.5 %all-to-all-start.3 = ((bf16[8,40,3584]{2,1,0:T(8,128)(2,1)}), bf16[8,40,3584]{2,1,0:T(8,128)(2,1)}, u32[]{:S(2)}, u32[]{:S(2)}) async-start(bf16[8,40,3584]{2,1,0:T(8,128)(2,1)} %bitcast.13), calls=%async_computation.3 | async-start | bytes 4587520 | tf_op jit(solution)/shard_map/all_to_all | solution.py:558
  171.5 0.1 collective-permute-start.11
  171.6 6.3 %shard_map.103.refs_0_.refs_2_ = bf16[384,3584]{1,0:T(8,128)(2,1)} custom-call(bf16[448,320]{1,0:T(8,128)(2,1)} %get-tuple-element.37.refs_0_, bf16[448,320]{1,0:T(8,128)(2,1)} %get-tuple-element.38.refs_1_, bf16[320,3584]{1,0:T(8,128)(2,1)} %bitcast.8.refs_2_, bf16[80,3584]{1,0:T(8,128)(2,1)} %get-tuple-element.34.refs_2_.refs_3_, ...), custom_call_target="tpu_custom_call" | custom-call | tf_op jit(solution)/shard_map/pallas_call | solution.py:60
  177.9 0.5 collective-permute-start.12
  178.4 8.2 %collective-permute-done.9.refs_1_.refs_3_ = bf16[64,3584]{1,0:T(8,128)(2,1)} collective-permute-done((bf16[64,3584]{1,0:T(8,128)(2,1)}, bf16[64,3584]{1,0:T(8,128)(2,1)}, u32[]{:S(2)}, u32[]{:S(2)}) %collective-permute-start.9) | collective-permute-done | bytes 458784 | tf_op jit(solution)/shard_map/ppermute | solution.py:20
  186.6 0.0 collective-permute-start.13
  186.6 7.5 %shard_map.104 = (bf16[448,1024]{1,0:T(8,128)(2,1)}, bf16[64,1024]{1,0:T(8,128)(2,1)}) custom-call(bf16[384,3584]{1,0:T(8,128)(2,1)} %shard_map.103.refs_0_.refs_2_, bf16[64,3584]{1,0:T(8,128)(2,1)} %collective-permute-done.9.refs_1_.refs_3_, bf16[512,3584]{1,0:T(8,128)(2,1)} %bitcast.18, bf16[512,3584]{1,0:T(8,128)(2,1)} %collective-permute-done.1.refs_2_.refs_3_), custom_call_target="tpu_custom_call" | custom-call | flops 40000000000 | tf_op jit(solution)/shard_map/pallas_call | solution.py:60
  194.1 0.0 collective-permute-start.10
  194.1 0.0 collective-permute-done.11.refs_1_
  194.1 0.0 collective-permute-done.13.refs_5_
  194.1 0.0 collective-permute-done.12.refs_4_
  194.1 7.7 %shard_map.105.refs_2_ = bf16[512,3584]{1,0:T(8,128)(2,1)} custom-call(bf16[512,448]{1,0:T(8,128)(2,1)} %get-tuple-element.43.refs_0_, bf16[512,448]{1,0:T(8,128)(2,1)} %collective-permute-done.11.refs_1_, bf16[384,3584]{1,0:T(8,128)(2,1)} %shard_map.103.refs_0_.refs_2_, bf16[64,3584]{1,0:T(8,128)(2,1)} %collective-permute-done.9.refs_1_.refs_3_, ...), custom_call_target="tpu_custom_call" | custom-call | tf_op jit(solution)/shard_map/pallas_call | solution.py:60
  201.8 0.8 collective-permute-done.10.refs_1_
  202.6 1.6 shard_map.106
  204.2 4.9 %all-to-all-done.3 = bf16[8,40,3584]{2,1,0:T(8,128)(2,1)} async-done(((bf16[8,40,3584]{2,1,0:T(8,128)(2,1)}), bf16[8,40,3584]{2,1,0:T(8,128)(2,1)}, u32[]{:S(2)}, u32[]{:S(2)}) %all-to-all-start.3) | async-done | bytes 2293792 | tf_op jit(solution)/shard_map/all_to_all | solution.py:558
  209.1 3.5 %shard_map.102 = bf16[128,3584]{1,0:T(8,128)(2,1)} custom-call(bf16[256,320]{1,0:T(8,128)(2,1)} %get-tuple-element.25.refs_0_, bf16[320,3584]{1,0:T(8,128)(2,1)} %bitcast.10.refs_1_, bf16[128,3584]{1,0:T(8,128)(2,1)} %collective-permute-done.6.refs_1_.refs_2_), custom_call_target="tpu_custom_call" | custom-call | tf_op jit(solution)/shard_map/pallas_call | solution.py:60
  (4 shorter events, 0.0 us)
Async XLA Ops:
  0.6 18.9 %collective-permute-start.1 = (bf16[512,3584]{1,0:T(8,128)(2,1)}, bf16[512,3584]{1,0:T(8,128)(2,1)}, u32[]{:S(2)}, u32[]{:S(2)}) collective-permute-start(bf16[512,3584]{1,0:T(8,128)(2,1)} %bitcast.15), channel_id=1, source_target_pairs={{0,16},{16,0},{1,17},{17,1},{2,18},{18,2},{3,19},{19,3},{4,20},{20... | collective-permute-start | bytes 11010056 | tf_op jit(solution)/shard_map/ppermute | solution.py:20
  2.8 16.1 %collective-permute-start = (bf16[64,1024]{1,0:T(8,128)(2,1)}, bf16[64,1024]{1,0:T(8,128)(2,1)}, u32[]{:S(2)}, u32[]{:S(2)}) collective-permute-start(bf16[64,1024]{1,0:T(8,128)(2,1)} %get-tuple-element.27), channel_id=1, source_target_pairs={{0,8},{1,9},{2,10},{3,11},{4,12},{5,13},{6,14},{7,15},{8,0},{9,1},... | collective-permute-start | bytes 393224 | tf_op jit(solution)/shard_map/ppermute | solution.py:20
  6.4 12.5 %all-to-all-start = ((f32[16,8,128]{2,1,0:T(8,128)}), f32[16,8,128]{2,1,0:T(8,128)}, u32[]{:S(2)}, u32[]{:S(2)}) async-start(f32[16,8,128]{2,1,0:T(8,128)} %get-tuple-element.24.refs_1_), calls=%async_computation | async-start | bytes 131072 | tf_op jit(solution)/shard_map/all_to_all | solution.py:567
  18.9 31.3 %collective-permute-start.3 = (bf16[128,3584]{1,0:T(8,128)(2,1)}, bf16[128,3584]{1,0:T(8,128)(2,1)}, u32[]{:S(2)}, u32[]{:S(2)}) collective-permute-start(bf16[128,3584]{1,0:T(8,128)(2,1)} %shard_map.91), channel_id=1, source_target_pairs={{0,4},{1,5},{2,6},{3,7},{4,0},{5,1},{6,2},{7,3},{8,12},{9,13},{10,... | collective-permute-start | bytes 2752520 | tf_op jit(solution)/shard_map/ppermute | solution.py:572
  24.2 30.8 %collective-permute-start.2 = (bf16[64,3584]{1,0:T(8,128)(2,1)}, bf16[64,3584]{1,0:T(8,128)(2,1)}, u32[]{:S(2)}, u32[]{:S(2)}) collective-permute-start(bf16[64,3584]{1,0:T(8,128)(2,1)} %shard_map.87.refs_4_), channel_id=1, source_target_pairs={{0,8},{1,9},{2,10},{3,11},{4,12},{5,13},{6,14},{7,15},{8,0},{9,1},... | collective-permute-start | bytes 1376264 | tf_op jit(solution)/shard_map/ppermute | solution.py:20
  53.9 41.2 %collective-permute-start.4 = (bf16[128,3584]{1,0:T(8,128)(2,1)}, bf16[128,3584]{1,0:T(8,128)(2,1)}, u32[]{:S(2)}, u32[]{:S(2)}) collective-permute-start(bf16[128,3584]{1,0:T(8,128)(2,1)} %shard_map.94), channel_id=1, source_target_pairs={{0,8},{1,9},{2,10},{3,11},{4,12},{5,13},{6,14},{7,15},{8,0},{9,1},... | collective-permute-start | bytes 2752520 | tf_op jit(solution)/shard_map/ppermute | solution.py:20
  54.3 22.6 %collective-permute-start.5 = (bf16[80,3584]{1,0:T(8,128)(2,1)}, bf16[80,3584]{1,0:T(8,128)(2,1)}, u32[]{:S(2)}, u32[]{:S(2)}) collective-permute-start(bf16[80,3584]{1,0:T(8,128)(2,1)} %get-tuple-element.35), channel_id=1, source_target_pairs={{0,1},{1,0},{2,3},{3,2},{4,5},{5,4},{6,7},{7,6},{8,9},{9,8},{10,11... | collective-permute-start | bytes 1720328 | tf_op jit(solution)/shard_map/ppermute | solution.py:584
  58.3 49.8 %all-to-all-start.1 = ((bf16[8,40,3584]{2,1,0:T(8,128)(2,1)}), bf16[8,40,3584]{2,1,0:T(8,128)(2,1)}, u32[]{:S(2)}, u32[]{:S(2)}) async-start(bf16[8,40,3584]{2,1,0:T(8,128)(2,1)} %bitcast.23), calls=%async_computation.1 | async-start | bytes 4587520 | tf_op jit(solution)/shard_map/all_to_all | solution.py:558
  108.1 54.2 %all-to-all-start.2 = ((bf16[8,40,3584]{2,1,0:T(8,128)(2,1)}), bf16[8,40,3584]{2,1,0:T(8,128)(2,1)}, u32[]{:S(2)}, u32[]{:S(2)}) async-start(bf16[8,40,3584]{2,1,0:T(8,128)(2,1)} %bitcast.14), calls=%async_computation.2 | async-start | bytes 4587520 | tf_op jit(solution)/shard_map/all_to_all | solution.py:558
  115.8 51.1 %collective-permute-start.6 = (bf16[128,3584]{1,0:T(8,128)(2,1)}, bf16[128,3584]{1,0:T(8,128)(2,1)}, u32[]{:S(2)}, u32[]{:S(2)}) collective-permute-start(bf16[128,3584]{1,0:T(8,128)(2,1)} %shard_map.98), channel_id=1, source_target_pairs={{0,8},{1,9},{2,10},{3,11},{4,12},{5,13},{6,14},{7,15},{8,0},{9,1},... | collective-permute-start | bytes 2752520 | tf_op jit(solution)/shard_map/ppermute | solution.py:20
  117.1 45.2 %collective-permute-start.7 = (bf16[80,3584]{1,0:T(8,128)(2,1)}, bf16[80,3584]{1,0:T(8,128)(2,1)}, u32[]{:S(2)}, u32[]{:S(2)}) collective-permute-start(bf16[80,3584]{1,0:T(8,128)(2,1)} %get-tuple-element.39), channel_id=1, source_target_pairs={{0,2},{1,3},{2,0},{3,1},{4,6},{5,7},{6,4},{7,5},{8,10},{9,11},{10,... | collective-permute-start | bytes 1720328 | tf_op jit(solution)/shard_map/ppermute | solution.py:584
  119.1 43.2 %collective-permute-start.8 = (bf16[80,3584]{1,0:T(8,128)(2,1)}, bf16[80,3584]{1,0:T(8,128)(2,1)}, u32[]{:S(2)}, u32[]{:S(2)}) collective-permute-start(bf16[80,3584]{1,0:T(8,128)(2,1)} %get-tuple-element.40), channel_id=1, source_target_pairs={{0,3},{1,2},{2,1},{3,0},{4,7},{5,6},{6,5},{7,4},{8,11},{9,10},{10,... | collective-permute-start | bytes 1720328 | tf_op jit(solution)/shard_map/ppermute | solution.py:584
  166.0 20.6 %collective-permute-start.9 = (bf16[64,3584]{1,0:T(8,128)(2,1)}, bf16[64,3584]{1,0:T(8,128)(2,1)}, u32[]{:S(2)}, u32[]{:S(2)}) collective-permute-start(bf16[64,3584]{1,0:T(8,128)(2,1)} %shard_map.100.refs_2_.refs_7_), channel_id=1, source_target_pairs={{0,8},{1,9},{2,10},{3,11},{4,12},{5,13},{6,14},{7,15},{8,0},{9,1},... | collective-permute-start | bytes 1376264 | tf_op jit(solution)/shard_map/ppermute | solution.py:20
  166.9 42.2 %all-to-all-start.3 = ((bf16[8,40,3584]{2,1,0:T(8,128)(2,1)}), bf16[8,40,3584]{2,1,0:T(8,128)(2,1)}, u32[]{:S(2)}, u32[]{:S(2)}) async-start(bf16[8,40,3584]{2,1,0:T(8,128)(2,1)} %bitcast.13), calls=%async_computation.3 | async-start | bytes 4587520 | tf_op jit(solution)/shard_map/all_to_all | solution.py:558
  171.5 22.6 %collective-permute-start.11 = (bf16[512,448]{1,0:T(8,128)(2,1)}, bf16[512,448]{1,0:T(8,128)(2,1)}, u32[]{:S(2)}, u32[]{:S(2)}) collective-permute-start(bf16[512,448]{1,0:T(8,128)(2,1)} %get-tuple-element.44), channel_id=1, source_target_pairs={{0,16},{16,0},{1,17},{17,1},{2,18},{18,2},{3,19},{19,3},{4,20},{20... | collective-permute-start | bytes 1376264 | tf_op jit(solution)/shard_map/ppermute | solution.py:20
  177.9 16.2 %collective-permute-start.12 = (bf16[384,3584]{1,0:T(8,128)(2,1)}, bf16[384,3584]{1,0:T(8,128)(2,1)}, u32[]{:S(2)}, u32[]{:S(2)}) collective-permute-start(bf16[384,3584]{1,0:T(8,128)(2,1)} %shard_map.103.refs_0_.refs_2_), channel_id=1, source_target_pairs={{0,16},{16,0},{1,17},{17,1},{2,18},{18,2},{3,19},{19,3},{4,20},{20... | collective-permute-start | bytes 8257544 | tf_op jit(solution)/shard_map/ppermute | solution.py:20
  186.6 7.5 %collective-permute-start.13 = (bf16[64,3584]{1,0:T(8,128)(2,1)}, bf16[64,3584]{1,0:T(8,128)(2,1)}, u32[]{:S(2)}, u32[]{:S(2)}) collective-permute-start(bf16[64,3584]{1,0:T(8,128)(2,1)} %collective-permute-done.9.refs_1_.refs_3_), channel_id=1, source_target_pairs={{0,16},{16,0},{1,17},{17,1},{2,18},{18,2},{3,19},{19,3},{4,20},{20... | collective-permute-start | bytes 1376264 | tf_op jit(solution)/shard_map/ppermute | solution.py:20
  194.1 8.5 %collective-permute-start.10 = (bf16[64,1024]{1,0:T(8,128)(2,1)}, bf16[64,1024]{1,0:T(8,128)(2,1)}, u32[]{:S(2)}, u32[]{:S(2)}) collective-permute-start(bf16[64,1024]{1,0:T(8,128)(2,1)} %get-tuple-element.42), channel_id=1, source_target_pairs={{0,8},{1,9},{2,10},{3,11},{4,12},{5,13},{6,14},{7,15},{8,0},{9,1},... | collective-permute-start | bytes 393224 | tf_op jit(solution)/shard_map/ppermute | solution.py:20

commit v12 on v8

--- a/solution.py
+++ b/solution.py
@@ -9,7 +9,7 @@
 F32, BF16, I32 = jnp.float32, jnp.bfloat16, jnp.int32
 LANES = 128
 LONG = 4_000_000_000_000
-GIVE_COST = 5_000_000_000
+GIVE_COST = 10_000_000_000
 BACK_COST = 40_000_000_000
 VMEM_LIMIT = 64 * 1024 * 1024 - 65536
 
@@ -505,8 +505,8 @@
     spare_hidden = swapped(spare_hidden, "expert", half)
     metas = lax.all_to_all(meta, "expert", 0, 0, tiled=True)
     packed_own, mix_own = pack_own(meta, grad_out, cap, half, tile)
-    arrived_own = to_half(touched(packed_own, metas, spare_hidden, far))
     out_spare = project_spare(spare_hidden, near, far, tile, mix_own)
+    arrived_own = to_half(touched(packed_own, metas, out_spare))
     sel, gate, mix_mirror, give_own, take_own, give_mirror, take_mirror = plan(
         metas, cap, half, main, slots
     )

time: 207 us -> 215 us (1.039)
  waiting for transfers between devices: 104 us -> 111 us
    all_to_all x4, waiting for transfers between devices: 58.9 us -> 72.2 us  [to_half(): lax.all_to_all(rows.reshape(half, cap, width), 'expert', 0, 0, axis_index...]
    all_to_all x1, waiting for transfers between devices: 4.06 us -> 0.01 us  [local(): metas = lax.all_to_all(meta, 'expert', 0, 0, tiled=True)]
  transfers between devices with their start and end apart: 15 -> 15, of which waited for: 9 -> 8; matrix products, arithmetic and copies ran while one was open for 0% -> 0% of each run, Pallas kernels for 32% -> 31%
where the time goes in v12:
time: 215 us; the launch traced here: 214 us
  waiting for transfers between devices  111 us (52%)
  Pallas kernels  70.1 us (33%)
  starting transfers between devices  32.7 us (15%)
    all_to_all x4, waiting for transfers between devices, to_half(): lax.all_to_all(rows.reshape(half, cap, width), 'expert', 0, 0, axis_index...  72.2 us
    pallas_call x22, Pallas kernels, call(): pl.pallas_call(kernel, grid=(grid,), in_specs=[spec for _, spec in ins] +...  70.1 us
    ppermute x10, waiting for transfers between devices, swapped(): return lax.ppermute(value, axis, pairs)  38.6 us
    all_to_all x4, starting transfers between devices, to_half(): lax.all_to_all(rows.reshape(half, cap, width), 'expert', 0, 0, axis_index...  20.2 us
    ppermute x10, starting transfers between devices, swapped(): return lax.ppermute(value, axis, pairs)  7.61 us
    all_to_all x1, starting transfers between devices, local(): metas = lax.all_to_all(meta, 'expert', 0, 0, tiled=True)  4.89 us
  transfers between devices with their start and end apart: 15, of which 8 were waited for; matrix products, arithmetic and copies ran while one was open for 0% of the time, Pallas kernels for 31%

profile of v12, /device:TPU:0, one launch (start us, length us, event | category | flops | bytes accessed | tf_op | source)
XLA Modules:
  0.0 214.3 jit_solution(7043573657375995562)
XLA Ops:
  0.6 0.5 collective-permute-start.1
  1.1 1.6 shard_map.85
  2.8 3.6 %collective-permute-start = (bf16[64,1024]{1,0:T(8,128)(2,1)}, bf16[64,1024]{1,0:T(8,128)(2,1)}, u32[]{:S(2)}, u32[]{:S(2)}) collective-permute-start(bf16[64,1024]{1,0:T(8,128)(2,1)} %get-tuple-element.22), channel_id=1, source_target_pairs={{0,8},{1,9},{2,10},{3,11},{4,12},{5,13},{6,14},{7,15},{8,0},{9,1},... | collective-permute-start | bytes 393224 | tf_op jit(solution)/shard_map/ppermute | solution.py:20
  6.4 4.9 %all-to-all-start = ((f32[16,8,128]{2,1,0:T(8,128)}), f32[16,8,128]{2,1,0:T(8,128)}, u32[]{:S(2)}, u32[]{:S(2)}) async-start(f32[16,8,128]{2,1,0:T(8,128)} %get-tuple-element.19.refs_0_), calls=%async_computation | async-start | bytes 131072 | tf_op jit(solution)/shard_map/all_to_all | solution.py:506
  11.3 3.6 %shard_map.86 = (bf16[320,3584]{1,0:T(8,128)(2,1)}, bf16[256,320]{1,0:T(8,128)(2,1)}) custom-call(f32[16,8,128]{2,1,0:T(8,128)} %get-tuple-element.19.refs_0_, bf16[128,3584]{1,0:T(8,128)(2,1)} %refs_0_.1), custom_call_target="tpu_custom_call" | custom-call | tf_op jit(solution)/shard_map/pallas_call | solution.py:60
  14.8 0.0 collective-permute-done.refs_0_.refs_1_
  14.9 0.0 collective-permute-done.1.refs_2_.refs_3_
  14.9 4.7 %shard_map.88.refs_4_.refs_2_ = bf16[64,3584]{1,0:T(8,128)(2,1)} custom-call(bf16[64,1024]{1,0:T(8,128)(2,1)} %collective-permute-done.refs_0_.refs_1_, bf16[512,3584]{1,0:T(8,128)(2,1)} %bitcast.18, bf16[512,3584]{1,0:T(8,128)(2,1)} %collective-permute-done.1.refs_2_.refs_3_, bf16[256,320]{1,0:T(8,128)(2,1)} %get-tuple-element.20.refs_3_.refs_0_), custom_call_target="tpu_custom_call" | custom-call | tf_op jit(solution)/shard_map/pallas_call | solution.py:60
  19.5 0.0 all-to-all-done.refs_0_.refs_1_
  19.5 4.9 %all-to-all-start.1 = ((bf16[8,40,3584]{2,1,0:T(8,128)(2,1)}), bf16[8,40,3584]{2,1,0:T(8,128)(2,1)}, u32[]{:S(2)}, u32[]{:S(2)}) async-start(bf16[8,40,3584]{2,1,0:T(8,128)(2,1)} %bitcast.22), calls=%async_computation.1 | async-start | bytes 4587520 | tf_op jit(solution)/shard_map/all_to_all | solution.py:497
  24.5 2.4 %collective-permute-start.2 = (bf16[64,3584]{1,0:T(8,128)(2,1)}, bf16[64,3584]{1,0:T(8,128)(2,1)}, u32[]{:S(2)}, u32[]{:S(2)}) collective-permute-start(bf16[64,3584]{1,0:T(8,128)(2,1)} %shard_map.88.refs_4_.refs_2_), channel_id=1, source_target_pairs={{0,8},{1,9},{2,10},{3,11},{4,12},{5,13},{6,14},{7,15},{8,0},{9,1},... | collective-permute-start | bytes 1376264 | tf_op jit(solution)/shard_map/ppermute | solution.py:20
  26.9 2.0 shard_map.90.refs_0_
  28.8 2.9 %shard_map.87 = (bf16[320,128]{1,0:T(8,128)(2,1)}, f32[320,128]{1,0:T(8,128)}, bf16[256,320]{1,0:T(8,128)(2,1)}, bf16[320,448]{1,0:T(8,128)(2,1)}, bf16[448,320]...) custom-call(f32[16,8,128]{2,1,0:T(8,128)} %all-to-all-done.refs_0_.refs_1_), custom_call_target="tpu_custom_call" | custom-call | tf_op jit(solution)/shard_map/pallas_call | solution.py:60
  31.7 7.0 %shard_map.89 = (bf16[384,3584]{1,0:T(8,128)(2,1)}, bf16[512,448]{1,0:T(8,128)(2,1)}, bf16[512,448]{1,0:T(8,128)(2,1)}) custom-call(bf16[448,1024]{1,0:T(8,128)(2,1)} %bitcast.25, bf16[64,1024]{1,0:T(8,128)(2,1)} %collective-permute-done.refs_0_.refs_1_, bf16[512,3584]{1,0:T(8,128)(2,1)} %bitcast.19, ...), custom_call_target="tpu_custom_call" | custom-call | tf_op jit(solution)/shard_map/pallas_call | solution.py:60
  38.7 0.6 collective-permute-start.3
  39.2 3.9 %shard_map.94.refs_1_ = bf16[320,3584]{1,0:T(8,128)(2,1)} custom-call(bf16[320,448]{1,0:T(8,128)(2,1)} %get-tuple-element.27.refs_0_, bf16[384,3584]{1,0:T(8,128)(2,1)} %get-tuple-element.23.refs_1_), custom_call_target="tpu_custom_call" | custom-call | tf_op jit(solution)/shard_map/pallas_call | solution.py:60
  43.2 17.3 %collective-permute-done.2.refs_2_ = bf16[64,3584]{1,0:T(8,128)(2,1)} collective-permute-done((bf16[64,3584]{1,0:T(8,128)(2,1)}, bf16[64,3584]{1,0:T(8,128)(2,1)}, u32[]{:S(2)}, u32[]{:S(2)}) %collective-permute-start.2) | collective-permute-done | bytes 458784 | tf_op jit(solution)/shard_map/ppermute | solution.py:20
  60.5 3.4 %shard_map.95.refs_0_ = bf16[320,3584]{1,0:T(8,128)(2,1)} custom-call(bf16[320,448]{1,0:T(8,128)(2,1)} %get-tuple-element.27.refs_0_, bf16[320,3584]{1,0:T(8,128)(2,1)} %shard_map.94.refs_1_, bf16[64,3584]{1,0:T(8,128)(2,1)} %collective-permute-done.2.refs_2_), custom_call_target="tpu_custom_call" | custom-call | flops 10000000000 | tf_op jit(solution)/shard_map/pallas_call | solution.py:60
  63.9 8.9 %all-to-all-done.1 = bf16[8,40,3584]{2,1,0:T(8,128)(2,1)} async-done(((bf16[8,40,3584]{2,1,0:T(8,128)(2,1)}), bf16[8,40,3584]{2,1,0:T(8,128)(2,1)}, u32[]{:S(2)}, u32[]{:S(2)}) %all-to-all-start.1) | async-done | bytes 2293792 | tf_op jit(solution)/shard_map/all_to_all | solution.py:497
  72.8 6.3 %all-to-all-start.2 = ((bf16[8,40,3584]{2,1,0:T(8,128)(2,1)}), bf16[8,40,3584]{2,1,0:T(8,128)(2,1)}, u32[]{:S(2)}, u32[]{:S(2)}) async-start(bf16[8,40,3584]{2,1,0:T(8,128)(2,1)} %bitcast.23), calls=%async_computation.2 | async-start | bytes 4587520 | tf_op jit(solution)/shard_map/all_to_all | solution.py:497
  79.1 12.0 %collective-permute-done.3.refs_2_ = bf16[128,3584]{1,0:T(8,128)(2,1)} collective-permute-done((bf16[128,3584]{1,0:T(8,128)(2,1)}, bf16[128,3584]{1,0:T(8,128)(2,1)}, u32[]{:S(2)}, u32[]{:S(2)}) %collective-permute-start.3) | collective-permute-done | bytes 917536 | tf_op jit(solution)/shard_map/ppermute | solution.py:20
  91.1 3.1 %shard_map.92.refs_3_.refs_0_ = bf16[320,3584]{1,0:T(8,128)(2,1)} custom-call(bf16[320,128]{1,0:T(8,128)(2,1)} %get-tuple-element.24.refs_2_.refs_0_, f32[320,128]{1,0:T(8,128)} %get-tuple-element.25.refs_1_, bf16[128,3584]{1,0:T(8,128)(2,1)} %collective-permute-done.3.refs_2_), custom_call_target="tpu_custom_call" | custom-call | flops 3999999983616 | tf_op jit(solution)/shard_map/pallas_call | solution.py:60
  94.2 4.7 %shard_map.93.refs_2_.refs_0_ = bf16[320,3584]{1,0:T(8,128)(2,1)} custom-call(bf16[320,448]{1,0:T(8,128)(2,1)} %get-tuple-element.21.refs_0_, bf16[384,3584]{1,0:T(8,128)(2,1)} %get-tuple-element.23.refs_1_, bf16[64,3584]{1,0:T(8,128)(2,1)} %collective-permute-done.2.refs_2_, bf16[320,3584]{1,0:T(8,128)(2,1)} %shard_map.92.refs_3_.refs_0_), custom_call_target="tpu_custom_call" | custom-call | tf_op jit(solution)/shard_map/pallas_call | solution.py:60
  98.8 16.7 %all-to-all-done.2 = bf16[8,40,3584]{2,1,0:T(8,128)(2,1)} async-done(((bf16[8,40,3584]{2,1,0:T(8,128)(2,1)}), bf16[8,40,3584]{2,1,0:T(8,128)(2,1)}, u32[]{:S(2)}, u32[]{:S(2)}) %all-to-all-start.2) | async-done | bytes 2293792 | tf_op jit(solution)/shard_map/all_to_all | solution.py:497
  115.5 4.4 %all-to-all-start.3 = ((bf16[8,40,3584]{2,1,0:T(8,128)(2,1)}), bf16[8,40,3584]{2,1,0:T(8,128)(2,1)}, u32[]{:S(2)}, u32[]{:S(2)}) async-start(bf16[8,40,3584]{2,1,0:T(8,128)(2,1)} %bitcast.16), calls=%async_computation.3 | async-start | bytes 4587520 | tf_op jit(solution)/shard_map/all_to_all | solution.py:497
  119.9 3.3 %shard_map.98 = bf16[128,3584]{1,0:T(8,128)(2,1)} custom-call(bf16[256,320]{1,0:T(8,128)(2,1)} %get-tuple-element.26.refs_0_, bf16[320,3584]{1,0:T(8,128)(2,1)} %bitcast.8.refs_1_), custom_call_target="tpu_custom_call" | custom-call | tf_op jit(solution)/shard_map/pallas_call | solution.py:60
  123.3 0.0 collective-permute-start.4
  123.3 42.2 %all-to-all-done.3 = bf16[8,40,3584]{2,1,0:T(8,128)(2,1)} async-done(((bf16[8,40,3584]{2,1,0:T(8,128)(2,1)}), bf16[8,40,3584]{2,1,0:T(8,128)(2,1)}, u32[]{:S(2)}, u32[]{:S(2)}) %all-to-all-start.3) | async-done | bytes 2293792 | tf_op jit(solution)/shard_map/all_to_all | solution.py:497
  165.5 3.7 %shard_map.100.refs_2_.refs_4_ = bf16[64,3584]{1,0:T(8,128)(2,1)} custom-call(bf16[448,320]{1,0:T(8,128)(2,1)} %get-tuple-element.29.refs_0_, bf16[448,320]{1,0:T(8,128)(2,1)} %get-tuple-element.30.refs_1_, bf16[320,3584]{1,0:T(8,128)(2,1)} %bitcast.6.refs_1_.refs_2_, bf16[320,3584]{1,0:T(8,128)(2,1)} %bitcast.10.refs_3_), custom_call_target="tpu_custom_call" | custom-call | tf_op jit(solution)/shard_map/pallas_call | solution.py:60
  169.1 0.0 collective-permute-start.5
  169.1 0.0 collective-permute-done.4.refs_1_.refs_2_
  169.2 4.6 %all-to-all-start.4 = ((bf16[8,40,3584]{2,1,0:T(8,128)(2,1)}), bf16[8,40,3584]{2,1,0:T(8,128)(2,1)}, u32[]{:S(2)}, u32[]{:S(2)}) async-start(bf16[8,40,3584]{2,1,0:T(8,128)(2,1)} %bitcast.15), calls=%async_computation.4 | async-start | bytes 4587520 | tf_op jit(solution)/shard_map/all_to_all | solution.py:497
  173.7 0.1 collective-permute-start.7
  173.8 6.1 %shard_map.103.refs_0_.refs_2_ = bf16[384,3584]{1,0:T(8,128)(2,1)} custom-call(bf16[448,320]{1,0:T(8,128)(2,1)} %get-tuple-element.29.refs_0_, bf16[448,320]{1,0:T(8,128)(2,1)} %get-tuple-element.30.refs_1_, bf16[320,3584]{1,0:T(8,128)(2,1)} %bitcast.6.refs_1_.refs_2_, bf16[320,3584]{1,0:T(8,128)(2,1)} %bitcast.10.refs_3_, ...), custom_call_target="tpu_custom_call" | custom-call | tf_op jit(solution)/shard_map/pallas_call | solution.py:60
  179.9 0.5 collective-permute-start.8
  180.3 8.6 %collective-permute-done.5.refs_1_.refs_3_ = bf16[64,3584]{1,0:T(8,128)(2,1)} collective-permute-done((bf16[64,3584]{1,0:T(8,128)(2,1)}, bf16[64,3584]{1,0:T(8,128)(2,1)}, u32[]{:S(2)}, u32[]{:S(2)}) %collective-permute-start.5) | collective-permute-done | bytes 458784 | tf_op jit(solution)/shard_map/ppermute | solution.py:20
  188.9 0.0 collective-permute-start.9
  188.9 7.5 %shard_map.104 = (bf16[448,1024]{1,0:T(8,128)(2,1)}, bf16[64,1024]{1,0:T(8,128)(2,1)}) custom-call(bf16[384,3584]{1,0:T(8,128)(2,1)} %shard_map.103.refs_0_.refs_2_, bf16[64,3584]{1,0:T(8,128)(2,1)} %collective-permute-done.5.refs_1_.refs_3_, bf16[512,3584]{1,0:T(8,128)(2,1)} %bitcast.20, bf16[512,3584]{1,0:T(8,128)(2,1)} %collective-permute-done.1.refs_2_.refs_3_), custom_call_target="tpu_custom_call" | custom-call | flops 40000000000 | tf_op jit(solution)/shard_map/pallas_call | solution.py:60
  196.5 0.0 collective-permute-start.6
  196.5 0.0 collective-permute-done.7.refs_1_
  196.5 0.0 collective-permute-done.9.refs_5_
  196.5 0.0 collective-permute-done.8.refs_4_
  196.5 7.7 %shard_map.105.refs_2_ = bf16[512,3584]{1,0:T(8,128)(2,1)} custom-call(bf16[512,448]{1,0:T(8,128)(2,1)} %get-tuple-element.33.refs_0_, bf16[512,448]{1,0:T(8,128)(2,1)} %collective-permute-done.7.refs_1_, bf16[384,3584]{1,0:T(8,128)(2,1)} %shard_map.103.refs_0_.refs_2_, bf16[64,3584]{1,0:T(8,128)(2,1)} %collective-permute-done.5.refs_1_.refs_3_, ...), custom_call_target="tpu_custom_call" | custom-call | tf_op jit(solution)/shard_map/pallas_call | solution.py:60
  204.2 0.6 collective-permute-done.6.refs_1_
  204.8 1.6 shard_map.106
  206.4 4.4 %all-to-all-done.4 = bf16[8,40,3584]{2,1,0:T(8,128)(2,1)} async-done(((bf16[8,40,3584]{2,1,0:T(8,128)(2,1)}), bf16[8,40,3584]{2,1,0:T(8,128)(2,1)}, u32[]{:S(2)}, u32[]{:S(2)}) %all-to-all-start.4) | async-done | bytes 2293792 | tf_op jit(solution)/shard_map/all_to_all | solution.py:497
  210.8 3.5 %shard_map.102 = bf16[128,3584]{1,0:T(8,128)(2,1)} custom-call(bf16[256,320]{1,0:T(8,128)(2,1)} %get-tuple-element.20.refs_3_.refs_0_, bf16[320,3584]{1,0:T(8,128)(2,1)} %bitcast.12.refs_1_, bf16[128,3584]{1,0:T(8,128)(2,1)} %collective-permute-done.4.refs_1_.refs_2_), custom_call_target="tpu_custom_call" | custom-call | tf_op jit(solution)/shard_map/pallas_call | solution.py:60
  (5 shorter events, 0.0 us)
Async XLA Ops:
  0.6 14.2 %collective-permute-start.1 = (bf16[512,3584]{1,0:T(8,128)(2,1)}, bf16[512,3584]{1,0:T(8,128)(2,1)}, u32[]{:S(2)}, u32[]{:S(2)}) collective-permute-start(bf16[512,3584]{1,0:T(8,128)(2,1)} %bitcast.17), channel_id=1, source_target_pairs={{0,16},{16,0},{1,17},{17,1},{2,18},{18,2},{3,19},{19,3},{4,20},{20... | collective-permute-start | bytes 11010056 | tf_op jit(solution)/shard_map/ppermute | solution.py:20
  2.8 12.1 %collective-permute-start = (bf16[64,1024]{1,0:T(8,128)(2,1)}, bf16[64,1024]{1,0:T(8,128)(2,1)}, u32[]{:S(2)}, u32[]{:S(2)}) collective-permute-start(bf16[64,1024]{1,0:T(8,128)(2,1)} %get-tuple-element.22), channel_id=1, source_target_pairs={{0,8},{1,9},{2,10},{3,11},{4,12},{5,13},{6,14},{7,15},{8,0},{9,1},... | collective-permute-start | bytes 393224 | tf_op jit(solution)/shard_map/ppermute | solution.py:20
  6.4 13.1 %all-to-all-start = ((f32[16,8,128]{2,1,0:T(8,128)}), f32[16,8,128]{2,1,0:T(8,128)}, u32[]{:S(2)}, u32[]{:S(2)}) async-start(f32[16,8,128]{2,1,0:T(8,128)} %get-tuple-element.19.refs_0_), calls=%async_computation | async-start | bytes 131072 | tf_op jit(solution)/shard_map/all_to_all | solution.py:506
  19.5 53.2 %all-to-all-start.1 = ((bf16[8,40,3584]{2,1,0:T(8,128)(2,1)}), bf16[8,40,3584]{2,1,0:T(8,128)(2,1)}, u32[]{:S(2)}, u32[]{:S(2)}) async-start(bf16[8,40,3584]{2,1,0:T(8,128)(2,1)} %bitcast.22), calls=%async_computation.1 | async-start | bytes 4587520 | tf_op jit(solution)/shard_map/all_to_all | solution.py:497
  24.5 36.0 %collective-permute-start.2 = (bf16[64,3584]{1,0:T(8,128)(2,1)}, bf16[64,3584]{1,0:T(8,128)(2,1)}, u32[]{:S(2)}, u32[]{:S(2)}) collective-permute-start(bf16[64,3584]{1,0:T(8,128)(2,1)} %shard_map.88.refs_4_.refs_2_), channel_id=1, source_target_pairs={{0,8},{1,9},{2,10},{3,11},{4,12},{5,13},{6,14},{7,15},{8,0},{9,1},... | collective-permute-start | bytes 1376264 | tf_op jit(solution)/shard_map/ppermute | solution.py:20
  38.7 52.4 %collective-permute-start.3 = (bf16[128,3584]{1,0:T(8,128)(2,1)}, bf16[128,3584]{1,0:T(8,128)(2,1)}, u32[]{:S(2)}, u32[]{:S(2)}) collective-permute-start(bf16[128,3584]{1,0:T(8,128)(2,1)} %shard_map.91), channel_id=1, source_target_pairs={{0,8},{1,9},{2,10},{3,11},{4,12},{5,13},{6,14},{7,15},{8,0},{9,1},... | collective-permute-start | bytes 2752520 | tf_op jit(solution)/shard_map/ppermute | solution.py:20
  72.8 42.8 %all-to-all-start.2 = ((bf16[8,40,3584]{2,1,0:T(8,128)(2,1)}), bf16[8,40,3584]{2,1,0:T(8,128)(2,1)}, u32[]{:S(2)}, u32[]{:S(2)}) async-start(bf16[8,40,3584]{2,1,0:T(8,128)(2,1)} %bitcast.23), calls=%async_computation.2 | async-start | bytes 4587520 | tf_op jit(solution)/shard_map/all_to_all | solution.py:497
  115.5 49.9 %all-to-all-start.3 = ((bf16[8,40,3584]{2,1,0:T(8,128)(2,1)}), bf16[8,40,3584]{2,1,0:T(8,128)(2,1)}, u32[]{:S(2)}, u32[]{:S(2)}) async-start(bf16[8,40,3584]{2,1,0:T(8,128)(2,1)} %bitcast.16), calls=%async_computation.3 | async-start | bytes 4587520 | tf_op jit(solution)/shard_map/all_to_all | solution.py:497
  123.3 45.9 %collective-permute-start.4 = (bf16[128,3584]{1,0:T(8,128)(2,1)}, bf16[128,3584]{1,0:T(8,128)(2,1)}, u32[]{:S(2)}, u32[]{:S(2)}) collective-permute-start(bf16[128,3584]{1,0:T(8,128)(2,1)} %shard_map.98), channel_id=1, source_target_pairs={{0,8},{1,9},{2,10},{3,11},{4,12},{5,13},{6,14},{7,15},{8,0},{9,1},... | collective-permute-start | bytes 2752520 | tf_op jit(solution)/shard_map/ppermute | solution.py:20
  169.1 19.8 %collective-permute-start.5 = (bf16[64,3584]{1,0:T(8,128)(2,1)}, bf16[64,3584]{1,0:T(8,128)(2,1)}, u32[]{:S(2)}, u32[]{:S(2)}) collective-permute-start(bf16[64,3584]{1,0:T(8,128)(2,1)} %shard_map.100.refs_2_.refs_4_), channel_id=1, source_target_pairs={{0,8},{1,9},{2,10},{3,11},{4,12},{5,13},{6,14},{7,15},{8,0},{9,1},... | collective-permute-start | bytes 1376264 | tf_op jit(solution)/shard_map/ppermute | solution.py:20
  169.2 41.6 %all-to-all-start.4 = ((bf16[8,40,3584]{2,1,0:T(8,128)(2,1)}), bf16[8,40,3584]{2,1,0:T(8,128)(2,1)}, u32[]{:S(2)}, u32[]{:S(2)}) async-start(bf16[8,40,3584]{2,1,0:T(8,128)(2,1)} %bitcast.15), calls=%async_computation.4 | async-start | bytes 4587520 | tf_op jit(solution)/shard_map/all_to_all | solution.py:497
  173.7 22.7 %collective-permute-start.7 = (bf16[512,448]{1,0:T(8,128)(2,1)}, bf16[512,448]{1,0:T(8,128)(2,1)}, u32[]{:S(2)}, u32[]{:S(2)}) collective-permute-start(bf16[512,448]{1,0:T(8,128)(2,1)} %get-tuple-element.34), channel_id=1, source_target_pairs={{0,16},{16,0},{1,17},{17,1},{2,18},{18,2},{3,19},{19,3},{4,20},{20... | collective-permute-start | bytes 1376264 | tf_op jit(solution)/shard_map/ppermute | solution.py:20
  179.9 16.6 %collective-permute-start.8 = (bf16[384,3584]{1,0:T(8,128)(2,1)}, bf16[384,3584]{1,0:T(8,128)(2,1)}, u32[]{:S(2)}, u32[]{:S(2)}) collective-permute-start(bf16[384,3584]{1,0:T(8,128)(2,1)} %shard_map.103.refs_0_.refs_2_), channel_id=1, source_target_pairs={{0,16},{16,0},{1,17},{17,1},{2,18},{18,2},{3,19},{19,3},{4,20},{20... | collective-permute-start | bytes 8257544 | tf_op jit(solution)/shard_map/ppermute | solution.py:20
  188.9 7.5 %collective-permute-start.9 = (bf16[64,3584]{1,0:T(8,128)(2,1)}, bf16[64,3584]{1,0:T(8,128)(2,1)}, u32[]{:S(2)}, u32[]{:S(2)}) collective-permute-start(bf16[64,3584]{1,0:T(8,128)(2,1)} %collective-permute-done.5.refs_1_.refs_3_), channel_id=1, source_target_pairs={{0,16},{16,0},{1,17},{17,1},{2,18},{18,2},{3,19},{19,3},{4,20},{20... | collective-permute-start | bytes 1376264 | tf_op jit(solution)/shard_map/ppermute | solution.py:20
  196.5 8.4 %collective-permute-start.6 = (bf16[64,1024]{1,0:T(8,128)(2,1)}, bf16[64,1024]{1,0:T(8,128)(2,1)}, u32[]{:S(2)}, u32[]{:S(2)}) collective-permute-start(bf16[64,1024]{1,0:T(8,128)(2,1)} %get-tuple-element.32), channel_id=1, source_target_pairs={{0,8},{1,9},{2,10},{3,11},{4,12},{5,13},{6,14},{7,15},{8,0},{9,1},... | collective-permute-start | bytes 393224 | tf_op jit(solution)/shard_map/ppermute | solution.py:20
